TPU v7x, 32 devices: a whole 2x2x4 slice. The times are simulated.
32 devices in a mesh: groups: 2 (over x), pat: 16 (over z, y, core), cov: 1.
Axes of the slice: x: 2, y: 2, z: 4, core: 2. Of those that a mesh axis runs over, the one named last changes fastest.
Arguments:
- covariates: bfloat16 [4096, 19968], P(('groups', 'pat'), 'cov'), parts along dimension 0, may hold values from -13 to 13
- weights: bfloat16 [4096, 16], P(('groups', 'pat')), parts along dimension 0, may hold values from 0.19921875 to 5
- arms: int32 [4096, 48], P(('groups', 'pat'), 'cov'), parts along dimension 0, may hold values from 0 to 1, as said below
- pick: int32 [48], replicated, may hold values from 0 to 15
Outputs:
- balance: float32 [96, 1, 19968], P('groups', 'cov', 'pat'), parts along dimension 0
There are 2 independent parts, one for each index of `groups`. A program takes and returns all parts, laid end to end along the dimension named above; an argument that names none is the same for every part. Nothing has to cross between parts.
Inputs may be any that keep to these rules, and one draw needn't show every extreme that they name: Every comparison has patients in both arms.
All inputs are finite; a program needn't handle non-finite values.
Results may differ from a plain program's by a relative error of at most 0.0003.
Values may be sent and summed in bfloat16 or wider, within the bound.
No kernel may reach another device: no remote copies, remote signals or barrier semaphores. Data moves between devices by JAX's collectives and lax.ppermute only.
A program may use at most 128 MiB of HBM per device.

v0:
```python
import jax
import jax.numpy as jnp
from jax import lax
from jax.sharding import PartitionSpec as P


def moment_pair(columns, covariates, squares):
    dims = (((0,), (0,)), ((), ()))
    first = lax.dot_general(columns, covariates, dims, preferred_element_type=jnp.float32)
    second = lax.dot_general(columns, squares, dims, preferred_element_type=jnp.float32)
    return (first, second)


def on_device(covariates, weights, arms, pick):
    patients_here = covariates.shape[0]
    comps_here = arms.shape[1]
    comps_all = pick.shape[0]
    weightings = weights.shape[1]
    cov_index = lax.axis_index("cov")
    my_pick = lax.dynamic_slice_in_dim(pick, cov_index * comps_here, comps_here)
    onehot_here = (jnp.arange(weightings)[:, None] == my_pick[None, :]).astype(weights.dtype)
    picked = jnp.dot(weights, onehot_here, preferred_element_type=jnp.float32).astype(weights.dtype)
    arm_vals = arms.astype(weights.dtype)
    target = picked * arm_vals
    comparator = picked * (1 - arm_vals)
    squares = (covariates.astype(jnp.float32) * covariates.astype(jnp.float32)).astype(
        covariates.dtype
    )
    local_totals = jnp.stack(
        [
            jnp.sum(target.astype(jnp.float32), axis=0),
            jnp.sum(comparator.astype(jnp.float32), axis=0),
        ]
    )
    placed = lax.dynamic_update_slice(
        jnp.zeros((2, comps_all), jnp.float32), local_totals, (jnp.int32(0), cov_index * comps_here)
    )
    totals = lax.psum(placed, ("pat", "cov"))
    panel = jnp.stack([target, comparator], axis=1)
    piece = lax.all_gather(panel, "cov", axis=2, tiled=True)
    count = piece.shape[2]
    flat = piece.reshape(patients_here, 2 * count)
    first, second = moment_pair(flat, covariates, squares)
    moments = jnp.stack([first.reshape(2, count, -1), second.reshape(2, count, -1)])
    tiles = lax.psum_scatter(moments, "pat", scatter_dimension=3, tiled=True)
    first_target, first_other = (tiles[0, 0], tiles[0, 1])
    second_target, second_other = (tiles[1, 0], tiles[1, 1])
    total_target = totals[0][:, None]
    total_other = totals[1][:, None]
    mean_target = first_target / total_target
    mean_other = first_other / total_other
    var_target = second_target / total_target - mean_target * mean_target
    var_other = second_other / total_other - mean_other * mean_other
    pooled = jnp.maximum((var_target + var_other) / 2.0, 0.01)
    balance = (mean_target - mean_other) / jnp.sqrt(pooled)
    return balance.reshape(comps_all, 1, balance.shape[1])


def solution(mesh):
    placed = (
        P(("groups", "pat"), "cov"),
        P(("groups", "pat"), None),
        P(("groups", "pat"), "cov"),
        P(),
    )
    return jax.shard_map(
        on_device, mesh=mesh, in_specs=placed, out_specs=P("groups", "cov", "pat"), check_vma=False
    )
```

profile of v0, /device:TPU:1, one launch (start us, length us, event | category | flops | bytes accessed | tf_op | source)
XLA Modules:
  0.0 349.3 jit_solution(3739592782603911319)
XLA Ops:
  6.5 0.0 copy-start
  6.5 0.0 reduce-scatter.4.cloned.1.call-start
  6.5 0.7 copy-done
  7.2 1.1 convert_reduce_fusion.1
  8.3 0.8 fusion.14
  9.0 6.8 %convolution_bitcast_fusion = f32[1,2,48,19968]{3,2,1,0:T(8,128)} fusion(bf16[128,19968]{1,0:T(8,128)(2,1)} %param.4, bf16[128,1,48]{0,2,1:T(8,128)(2,1)S(1)} %get-tuple-element.12, bf16[128,1,48]{0,2,1:T(8,128)(2,1)S(1)} %get-tuple-element.11), kind=kOutput, calls=%fused_computation | convolution fusion | flops 498413568 | bytes 12804096 | tf_op jit(solution)/shard_map/dot_general | solution.py:10
  15.9 0.0 slice-done
  15.9 0.0 slice-done.1
  15.9 4.3 %convolution_bitcast_fusion.1 = f32[1,2,48,19968]{3,2,1,0:T(8,128)} fusion(bf16[128,19968]{1,0:T(8,128)(2,1)S(1)} %bitcast.63, bf16[128,1,48]{0,2,1:T(8,128)(2,1)S(1)} %get-tuple-element.12, bf16[128,1,48]{0,2,1:T(8,128)(2,1)S(1)} %get-tuple-element.11), kind=kOutput, calls=%fused_computation.1 | convolution fusion | flops 490745856 | bytes 12804096 | tf_op jit(solution)/shard_map/dot_general | solution.py:9
  20.1 11.7 %pad_maximum_fusion = f32[2,2,48,19968]{3,2,1,0:T(8,128)} fusion(f32[1,2,48,19968]{3,2,1,0:T(8,128)} %convolution_bitcast_fusion, f32[1,2,48,19968]{3,2,1,0:T(8,128)} %convolution_bitcast_fusion.1), kind=kLoop, calls=%fused_computation.2 | loop fusion | flops 3833856 | bytes 30670848 | tf_op jit(solution)/shard_map/stack | solution.py:44
  31.8 47.1 %copy.7 = f32[2,2,48,19968]{2,1,0,3:T(2,128)} copy(f32[2,2,48,19968]{3,2,1,0:T(8,128)} %pad_maximum_fusion) | data formatting | bytes 30670848
  78.9 42.4 %reshape.203 = f32[19968,192]{1,0:T(8,128)} reshape(f32[19968,2,2,48]{3,2,1,0:T(2,128)} %bitcast.61) | data formatting | bytes 30670848
  121.3 0.0 reduce-scatter.4.cloned.1.call-update
  121.3 0.0 copy-start.1
  121.3 30.6 %psum.7 = f32[2,48]{1,0:T(2,128)S(1)} all-reduce(f32[2,48]{1,0:T(2,128)S(1)} %pad_maximum_fusion.1), channel_id=1, replica_groups=mesh['groups'=2,'pat'=16,'cov'=1] {'pat','cov'}, use_global_device_ids=true, to_apply=%region_3.0 | all-reduce | flops 96 | bytes 768 | tf_op jit(solution)/shard_map/psum | solution.py:38
  151.9 178.2 %reduce-scatter.4.cloned.1.call-done = f32[1248,192]{1,0:T(8,128)} async-done(((f32[19968,192]{1,0:T(8,128)}), f32[1248,192]{1,0:T(8,128)}) %reduce-scatter.4.cloned.1.call-update) | async-done | bytes 958480
  330.2 3.8 %reshape.204 = f32[1248,2,2,48]{3,2,1,0:T(2,128)S(1)} reshape(f32[1248,192]{1,0:T(8,128)} %reduce-scatter.4.cloned.1.call-done) | data formatting | bytes 1916928
  334.0 3.0 fusion.16
  336.9 1.3 copy.10
  338.2 1.3 copy.11
  339.5 1.3 copy.9
  340.8 0.5 copy.12
  341.3 0.2 fusion.9
  341.5 0.9 copy.6
  (6 shorter events, 0.0 us)
Async XLA Ops:
  6.5 0.7 copy-start
  6.5 9.3 %slice-start = ((s8[5111808]{0:T(1024)(128)(4,1)}), s8[917504]{0:T(1024)(128)(4,1)S(1)}, s32[]{:S(2)}) async-start(s8[5111808]{0:T(1024)(128)(4,1)} %bitcast.62), calls=%async_computation.2 | async-start | bytes 1835008
  6.5 323.6 %reduce-scatter.4.cloned.1.call-start = ((), (), s32[]{:S(2)}) async-start(), calls=%async_computation.1 | async-start | bytes 21725184
  9.0 6.8 %slice-start.1 = ((s8[5111808]{0:T(1024)(128)(4,1)}), s8[4194304]{0:T(1024)(128)(4,1)S(1)}, s32[]{:S(2)}) async-start(s8[5111808]{0:T(1024)(128)(4,1)} %bitcast.62), calls=%async_computation.3 | async-start | bytes 8388608
  121.3 221.1 %copy-start.1 = (bf16[128,16]{0,1:T(8,128)(2,1)S(1)}, bf16[128,16]{0,1:T(8,128)(2,1)}, u32[]{:S(2)}) copy-start(bf16[128,16]{0,1:T(8,128)(2,1)} %param.5) | copy-start | bytes 12292
Sparse Core Ops, SparseCore 0:
  121.4 208.7 reduce-scatter.3
where the time goes:
time: 352 us; the launch traced here: 349 us
  waiting for transfers between devices  178 us (51%)
  local copies, waits for them, and re-layouts  102 us (29%)
  blocking collectives  30.6 us (9%)
  between operations  13.5 us (4%)
  other arithmetic  12.6 us (4%)
  matrix products  12.1 us (3%)
    unnamed x2, waiting for transfers between devices  178 us
    unnamed x15, local copies, waits for them, and re-layouts  98.3 us
    psum x1, blocking collectives, on_device(): totals = lax.psum(placed, ('pat', 'cov'))  30.6 us
    another operation x1, other arithmetic, on_device(): jnp.stack([first.reshape(2, count, -1), second.reshape(2, count, -1)])  11.7 us
  transfers between devices with their start and end apart: 1, of which 1 were waited for; matrix products, arithmetic and copies ran while one was open for 0% of the time, Pallas kernels for 0%

commit v1 on v0

v1 whole, which is shorter than its diff:
```python
import functools

import jax
import jax.numpy as jnp
from jax import lax
from jax.experimental import pallas as pl
from jax.experimental.pallas import tpu as pltpu
from jax.sharding import PartitionSpec as P

LANES = 128
VMEM_BYTES = 48 * 1024 * 1024


def round_up(value, multiple):
    return -(-value // multiple) * multiple


def pick_bits(value, bits):
    result = 0
    for place, bit in enumerate(bits):
        result = result + ((value >> bit) & 1) * (1 << place)
    return result


def spread_bits(value, bits):
    result = 0
    for place, bit in enumerate(bits):
        result += ((value >> place) & 1) << bit
    return result


class Half:
    def __init__(self, start, width, raw_bits, all_bits):
        self.start = start
        self.width = width
        self.padded = round_up(width, LANES)
        self.raw_bits = raw_bits
        self.sum_bits = [bit for bit in all_bits if bit not in raw_bits]
        self.members = [spread_bits(r, raw_bits) for r in range(1 << len(raw_bits))]


def halves_of(n, block):
    all_bits = list(range(n.bit_length() - 1))
    first = min(round_up(block // 2, LANES), block)
    return [
        Half(0, first, [0, 1], all_bits),
        Half(first, block - first, [0, 2], all_bits),
    ]


def pack_kernel(n, block, group, halves, x_ref, *refs):
    members = [len(half.members) for half in halves]
    outs = [refs[:members[0]], refs[members[0]:sum(members)]]
    buffers = refs[sum(members):sum(members) + 2]
    sems = refs[-1]
    step = pl.program_id(0)
    me = lax.axis_index("pat")
    rows = x_ref.shape[0]
    for i in range(group):
        owner = step * group + i
        relative = owner ^ me
        for h, half in enumerate(halves):
            left = i * block + half.start
            for row in range(0, rows, 32):
                piece = x_ref[row:row + 32, left:left + half.width]
                if half.padded > half.width:
                    piece = jnp.concatenate(
                        [piece, jnp.zeros((32, half.padded - half.width), piece.dtype)], axis=1
                    )
                buffers[h][owner, row:row + 32, :] = piece
            member = pick_bits(relative, half.raw_bits)
            place = pick_bits(relative, half.sum_bits)
            for r in range(members[h]):

                @pl.when(member == r)
                def _():
                    pltpu.make_async_copy(
                        buffers[h].at[owner], outs[h][r].at[place], sems.at[h, owner]
                    ).start()

    @pl.when(step == pl.num_programs(0) - 1)
    def _():
        for h in range(2):
            for owner in range(n):
                pltpu.make_async_copy(
                    buffers[h].at[owner], outs[h][0].at[0], sems.at[h, owner]
                ).wait()


def pack(covariates, n, halves):
    rows, columns = covariates.shape
    block = columns // n
    group = 4
    while group < n and (group * block) % LANES:
        group *= 2
    out_shape = [
        jax.ShapeDtypeStruct((n // len(half.members), rows, half.padded), covariates.dtype)
        for half in halves
        for _ in half.members
    ]
    outs = pl.pallas_call(
        functools.partial(pack_kernel, n, block, group, halves),
        grid=(n // group,),
        in_specs=[pl.BlockSpec((rows, group * block), lambda s: (0, s))],
        out_specs=[pl.BlockSpec(memory_space=pl.ANY)] * len(out_shape),
        out_shape=out_shape,
        scratch_shapes=[
            pltpu.VMEM((n, rows, half.padded), covariates.dtype) for half in halves
        ]
        + [pltpu.SemaphoreType.DMA((2, n))],
        compiler_params=pltpu.CompilerParams(vmem_limit_bytes=VMEM_BYTES),
        cost_estimate=pl.CostEstimate(
            flops=0, bytes_accessed=4 * covariates.size, transcendentals=0
        ),
        name="pack",
    )(covariates)
    first = len(halves[0].members)
    return outs[:first], outs[first:]


def panel_kernel(n, weightings, halves, gathered_ref, pick_ref, *out_refs):
    panels, stats_ref = out_refs[:-1], out_refs[-1]
    me = lax.axis_index("pat")
    comps = pick_ref.shape[0]
    rows = gathered_ref.shape[2]
    index = lax.broadcasted_iota(jnp.int32, (comps, weightings), 1)
    onehot = jnp.where(index == pick_ref[...], 1.0, 0.0).astype(jnp.bfloat16)

    def columns_of(device):
        weights = gathered_ref[device, 0:weightings, :]
        arms = gathered_ref[device, weightings:weightings + comps, :].astype(jnp.float32)
        picked = jnp.dot(onehot, weights, preferred_element_type=jnp.float32)
        return weights, picked * arms, picked * (1.0 - arms)

    target_sum = jnp.zeros((comps, rows), jnp.float32)
    other_sum = jnp.zeros((comps, rows), jnp.float32)
    for device in range(n):
        _, target, other = columns_of(device)
        target_sum += target
        other_sum += other
    total_target = jnp.sum(target_sum, axis=1, keepdims=True)
    total_other = jnp.sum(other_sum, axis=1, keepdims=True)
    light = jnp.where(total_target <= total_other, 1.0, 0.0)
    stats_ref[0] = jnp.broadcast_to(1.0 / total_target, (comps, LANES))
    stats_ref[1] = jnp.broadcast_to(1.0 / total_other, (comps, LANES))
    stats_ref[2] = jnp.broadcast_to(light, (comps, LANES))
    for h, half in enumerate(halves):
        first_ref, second_ref = panels[2 * h], panels[2 * h + 1]
        for r, member in enumerate(half.members):
            weights, target, other = columns_of(me ^ member)
            here = slice(r * rows, (r + 1) * rows)
            lighter = light * target + (1.0 - light) * other
            first_ref[0:comps, here] = lighter.astype(jnp.bfloat16)
            first_ref[comps:comps + weightings, here] = weights
            second_ref[0:comps, here] = target.astype(jnp.bfloat16)
            second_ref[comps:2 * comps, here] = other.astype(jnp.bfloat16)


def make_panels(gathered, pick, weightings, halves):
    n, _, rows = gathered.shape
    comps = pick.shape[0]
    out_shape = []
    for half in halves:
        count = len(half.members) * rows
        out_shape.append(jax.ShapeDtypeStruct((comps + weightings, count), jnp.bfloat16))
        out_shape.append(jax.ShapeDtypeStruct((2 * comps, count), jnp.bfloat16))
    out_shape.append(jax.ShapeDtypeStruct((3, comps, LANES), jnp.float32))
    return pl.pallas_call(
        functools.partial(panel_kernel, n, weightings, halves),
        in_specs=[pl.BlockSpec(memory_space=pltpu.VMEM)] * 2,
        out_specs=[pl.BlockSpec(memory_space=pltpu.VMEM)] * len(out_shape),
        out_shape=out_shape,
        compiler_params=pltpu.CompilerParams(vmem_limit_bytes=VMEM_BYTES),
        cost_estimate=pl.CostEstimate(
            flops=2 * gathered.size * comps, bytes_accessed=4 * gathered.size, transcendentals=0
        ),
        name="panels",
    )(gathered, pick.reshape(comps, 1))


def moments_kernel(x_count, *refs):
    xs = refs[:x_count]
    first_ref, second_ref, stats_ref = refs[x_count:x_count + 3]
    outs = refs[x_count + 3:]
    first_rows = first_ref.shape[0]
    comps = second_ref.shape[0] // 2
    inverse_target = stats_ref[0][:, 0:1]
    inverse_other = stats_ref[1][:, 0:1]
    for place, out_ref in enumerate(outs):
        x = jnp.concatenate([ref[place] for ref in xs], axis=0)
        first = jnp.dot(first_ref[...], x, preferred_element_type=jnp.float32)
        squares = (x.astype(jnp.float32) * x.astype(jnp.float32)).astype(jnp.bfloat16)
        second = jnp.dot(second_ref[...], squares, preferred_element_type=jnp.float32)
        out_ref[0, 0:first_rows, :] = first
        out_ref[0, first_rows:first_rows + comps, :] = (
            second[0:comps] * inverse_target + second[comps:2 * comps] * inverse_other
        )


def moments(xs, first, second, stats):
    places, rows, width = xs[0].shape
    comps = second.shape[0] // 2
    out_rows = first.shape[0] + comps
    whole = lambda s: (0, 0)
    return pl.pallas_call(
        functools.partial(moments_kernel, len(xs)),
        grid=(places // 2,),
        in_specs=[pl.BlockSpec((2, rows, width), lambda s: (s, 0, 0))] * len(xs)
        + [
            pl.BlockSpec(first.shape, whole),
            pl.BlockSpec(second.shape, whole),
            pl.BlockSpec(stats.shape, lambda s: (0, 0, 0)),
        ],
        out_specs=[pl.BlockSpec((1, out_rows, width), lambda s: (s, 0, 0))] * 2,
        out_shape=[jax.ShapeDtypeStruct((places // 2, out_rows, width), jnp.float32)] * 2,
        compiler_params=pltpu.CompilerParams(vmem_limit_bytes=VMEM_BYTES),
        cost_estimate=pl.CostEstimate(
            flops=2 * places * len(xs) * rows * width * (first.shape[0] + second.shape[0]),
            bytes_accessed=places * width * (2 * len(xs) * rows + 4 * out_rows),
            transcendentals=0,
        ),
        name="moments",
    )(*xs, first, second, stats)


def finish_kernel(weightings, widths, pick_ref, stats_ref, *refs):
    out_ref = refs[-1]
    comps = pick_ref.shape[0]
    index = lax.broadcasted_iota(jnp.int32, (comps, weightings), 1)
    onehot = jnp.where(index == pick_ref[...], 1.0, 0.0)
    inverse_target = stats_ref[0][:, 0:1]
    inverse_other = stats_ref[1][:, 0:1]
    light = stats_ref[2][:, 0:1] > 0.5
    start = 0
    for h, width in enumerate(widths):
        kept, arrived = refs[2 * h], refs[2 * h + 1]
        sums = kept[...] + arrived[...]
        lighter = sums[0:comps]
        both = jnp.dot(
            onehot,
            sums[comps:comps + weightings],
            precision=lax.Precision.HIGHEST,
            preferred_element_type=jnp.float32,
        )
        spread = sums[comps + weightings:2 * comps + weightings]
        heavier = both - lighter
        mean_target = jnp.where(light, lighter, heavier) * inverse_target
        mean_other = jnp.where(light, heavier, lighter) * inverse_other
        variance = spread - mean_target * mean_target - mean_other * mean_other
        pooled = jnp.maximum(variance / 2.0, 0.01)
        balance = (mean_target - mean_other) / jnp.sqrt(pooled)
        out_ref[:, 0, start:start + width] = balance[:, 0:width]
        start += width


def finish(parts, pick, stats, weightings, widths):
    comps = pick.shape[0]
    operands = [array for pair in parts for array in pair]
    return pl.pallas_call(
        functools.partial(finish_kernel, weightings, widths),
        in_specs=[pl.BlockSpec(memory_space=pltpu.VMEM)] * (2 + len(operands)),
        out_specs=pl.BlockSpec(memory_space=pltpu.VMEM),
        out_shape=jax.ShapeDtypeStruct((comps, 1, sum(widths)), jnp.float32),
        compiler_params=pltpu.CompilerParams(vmem_limit_bytes=VMEM_BYTES),
        cost_estimate=pl.CostEstimate(
            flops=20 * comps * sum(widths),
            bytes_accessed=4 * sum(2 * part[0].size for part in parts),
            transcendentals=comps * sum(widths),
        ),
        name="finish",
    )(pick.reshape(comps, 1), stats, *operands)


def swap(array, n, mask):
    return lax.ppermute(array, "pat", [(d, d ^ mask) for d in range(n)])


def on_device(n, covs, covariates, weights, arms, pick):
    weightings = weights.shape[1]
    block = covariates.shape[1] // n
    halves = halves_of(n, block)
    arm_rows = arms.T.astype(weights.dtype)
    if covs > 1:
        arm_rows = lax.all_gather(arm_rows, "cov", axis=0, tiled=True)
    gathered = lax.all_gather(jnp.concatenate([weights.T, arm_rows], axis=0), "pat")
    packed = pack(covariates, n, halves)
    shares = [
        [arrays[0]] + [swap(arrays[r], n, half.members[r]) for r in range(1, len(arrays))]
        for half, arrays in zip(halves, packed)
    ]
    *panels, stats = make_panels(gathered, pick, weightings, halves)
    parts = []
    for h, half in enumerate(halves):
        kept, sent = moments(shares[h], panels[2 * h], panels[2 * h + 1], stats)
        arrived = swap(sent, n, 1 << half.sum_bits[0])
        parts.append((kept, arrived))
    for level in range(1, len(halves[0].sum_bits)):
        for h, half in enumerate(halves):
            kept, arrived = parts[h]
            sent = kept[1::2] + arrived[1::2]
            parts[h] = (kept[0::2] + arrived[0::2], swap(sent, n, 1 << half.sum_bits[level]))
    parts = [(kept[0], arrived[0]) for kept, arrived in parts]
    return finish(parts, pick, stats, weightings, [half.width for half in halves])


def solution(mesh):
    placed = (
        P(("groups", "pat"), "cov"),
        P(("groups", "pat"), None),
        P(("groups", "pat"), "cov"),
        P(),
    )
    body = functools.partial(on_device, mesh.shape["pat"], mesh.shape["cov"])
    return jax.shard_map(
        body, mesh=mesh, in_specs=placed, out_specs=P("groups", "cov", "pat"), check_vma=False
    )
```

time: 352 us -> 106 us (0.30)
  waiting for transfers between devices: 178 us -> 39.5 us
  local copies, waits for them, and re-layouts: 102 us -> 0.11 us
  blocking collectives: 30.6 us -> 45 us
  between operations: 13.5 us -> 0.13 us
  Pallas kernels: 0 us -> 13.2 us
  other arithmetic: 12.6 us -> 0.15 us
  matrix products: 12.1 us -> 0 us
  starting transfers between devices: 0.01 us -> 6.75 us
    unnamed x2 -> x0, waiting for transfers between devices: 178 us -> none
    unnamed x15 -> x8, local copies, waits for them, and re-layouts: 98.3 us -> 0.02 us
    all_gather x0 -> x1, blocking collectives: none -> 45 us  [on_device(): lax.all_gather(jnp.concatenate([weights.T, arm_rows], axis=0), 'pat')]
    ppermute x0 -> x10, waiting for transfers between devices: none -> 39.5 us  [swap(): return lax.ppermute(array, 'pat', [(d, d ^ mask) for d in range(n)])]
    psum x1 -> x0, blocking collectives: 30.6 us -> none  [on_device(): totals = lax.psum(placed, ('pat', 'cov'))]
    pallas_call x0 -> x5, Pallas kernels: none -> 13.2 us  [the longest x1 7.96 us: pack(): pl.pallas_call(functools.partial(pack_kernel, n, block, group, halves), g...]
    another operation x3 -> x0, other arithmetic: 12.4 us -> none  [the longest x1 11.7 us: on_device(): jnp.stack([first.reshape(2, count, -1), second.reshape(2, count, -1)])]
    dot_general x3 -> x0, matrix products: 12.1 us -> none  [the longest x1 6.82 us: moment_pair(): lax.dot_general(columns, squares, dims, preferred_element_type=jnp.float32)]
  transfers between devices with their start and end apart: 1 -> 10, of which waited for: 1 -> 4; matrix products, arithmetic and copies ran while one was open for 0% -> 0% of each run, Pallas kernels for 0% -> 4%
where the time goes in v1:
time: 106 us; the launch traced here: 105 us
  blocking collectives  45 us (42%)
  waiting for transfers between devices  39.5 us (37%)
  Pallas kernels  13.2 us (12%)
  starting transfers between devices  6.75 us (6%)
    all_gather x1, blocking collectives, on_device(): lax.all_gather(jnp.concatenate([weights.T, arm_rows], axis=0), 'pat')  45 us
    ppermute x10, waiting for transfers between devices, swap(): return lax.ppermute(array, 'pat', [(d, d ^ mask) for d in range(n)])  39.5 us
    pallas_call x1, Pallas kernels, pack(): pl.pallas_call(functools.partial(pack_kernel, n, block, group, halves), g...  7.96 us
    ppermute x10, starting transfers between devices, swap(): return lax.ppermute(array, 'pat', [(d, d ^ mask) for d in range(n)])  6.75 us
    pallas_call x2, Pallas kernels, moments(): pl.pallas_call(functools.partial(moments_kernel, len(xs)), grid=(places /...  3.65 us
  transfers between devices with their start and end apart: 10, of which 4 were waited for; matrix products, arithmetic and copies ran while one was open for 0% of the time, Pallas kernels for 4%

profile of v1, /device:TPU:1, one launch (start us, length us, event | category | flops | bytes accessed | tf_op | source)
XLA Modules:
  0.0 104.9 jit_solution(16355914386001513001)
XLA Ops:
  0.0 8.0 %pack.1 = (bf16[4,128,640]{2,1,0:T(8,128)(2,1)S(1)}, bf16[4,128,640]{2,1,0:T(8,128)(2,1)}, bf16[4,128,640]{2,1,0:T(8,128)(2,1)}, bf16[4,128,640]{2,1,0:T(8,128)(...) custom-call(bf16[128,19968]{1,0:T(8,128)(2,1)} %x_ref.1), custom_call_target="tpu_custom_call" | custom-call | bytes 10223616 | tf_op jit(solution)/shard_map/pack/pallas_call | solution.py:101
  8.0 0.1 collective-permute-start
  8.1 2.6 %collective-permute-start.1 = (bf16[4,128,640]{2,1,0:T(8,128)(2,1)}, bf16[4,128,640]{2,1,0:T(8,128)(2,1)}, u32[]{:S(2)}, u32[]{:S(2)}) collective-permute-start(bf16[4,128,640]{2,1,0:T(8,128)(2,1)} %get-tuple-element.25), channel_id=1, source_target_pairs={{0,2},{1,3},{2,0},{3,1},{4,6},{5,7},{6,4},{7,5},{8,10},{9,11},{10,... | collective-permute-start | bytes 1966088 | tf_op jit(solution)/shard_map/ppermute | solution.py:275
  10.7 0.1 collective-permute-start.2
  10.8 0.4 collective-permute-start.5
  11.1 1.6 %collective-permute-start.6 = (bf16[4,128,640]{2,1,0:T(8,128)(2,1)}, bf16[4,128,640]{2,1,0:T(8,128)(2,1)S(1)}, u32[]{:S(2)}, u32[]{:S(2)}) collective-permute-start(bf16[4,128,640]{2,1,0:T(8,128)(2,1)} %get-tuple-element.33), channel_id=1, source_target_pairs={{0,4},{1,5},{2,6},{3,7},{4,0},{5,1},{6,2},{7,3},{8,12},{9,13},{10,... | collective-permute-start | bytes 1966088 | tf_op jit(solution)/shard_map/ppermute | solution.py:275
  12.8 0.1 copy.6.pick_ref
  12.9 0.3 collective-permute-start.7
  13.2 45.0 %all-gather = bf16[1024,128]{1,0:T(8,128)(2,1)S(1)} all-gather(bf16[64,128]{1,0:T(8,128)(2,1)S(1)} %pad_maximum_fusion), channel_id=2, replica_groups=mesh['groups'=2,'pat'=16,'cov'=1] {'pat'}, dimensions={0}, use_global_device_ids=true | all-gather | bytes 278528 | tf_op jit(solution)/shard_map/all_gather | solution.py:285
  58.2 0.4 panels.1
  58.6 0.0 collective-permute-done.1.refs_2_
  58.6 2.4 %moments.2 = (f32[2,112,640]{2,1,0:T(8,128)S(1)}, f32[2,112,640]{2,1,0:T(8,128)S(1)}) custom-call(bf16[4,128,640]{2,1,0:T(8,128)(2,1)S(1)} %get-tuple-element.23.refs_0_, bf16[4,128,640]{2,1,0:T(8,128)(2,1)S(1)} %collective-permute-done.refs_1_, bf16[4,128,640]{2,1,0:T(8,128)(2,1)} %collective-permute-done.1.refs_2_, ...), custom_call_target="tpu_custom_call" | custom-call | flops 419430400 | bytes 3768320 | tf_op jit(solution)/shard_map/moments/pallas_call | solution.py:205
  61.0 0.1 collective-permute-start.3
  61.1 1.3 %moments.3 = (f32[2,112,640]{2,1,0:T(8,128)S(1)}, f32[2,112,640]{2,1,0:T(8,128)S(1)}) custom-call(bf16[4,128,640]{2,1,0:T(8,128)(2,1)S(1)} %get-tuple-element.31.refs_0_, bf16[4,128,640]{2,1,0:T(8,128)(2,1)S(1)} %collective-permute-done.5.refs_1_, bf16[4,128,640]{2,1,0:T(8,128)(2,1)S(1)} %collective-permute-done.6.refs_2_, ...), custom_call_target="tpu_custom_call" | custom-call | flops 419430400 | bytes 3768320 | tf_op jit(solution)/shard_map/moments/pallas_call | solution.py:205
  62.4 0.4 collective-permute-start.8
  62.8 12.7 %collective-permute-done.3 = f32[2,112,640]{2,1,0:T(8,128)S(1)} collective-permute-done((f32[2,112,640]{2,1,0:T(8,128)S(1)}, f32[2,112,640]{2,1,0:T(8,128)S(1)}, u32[]{:S(2)}, u32[]{:S(2)}) %collective-permute-start.3) | collective-permute-done | bytes 573472 | tf_op jit(solution)/shard_map/ppermute | solution.py:275
  75.5 0.1 slice_add_fusion.2
  75.5 0.1 collective-permute-start.4
  75.6 1.2 %collective-permute-done.8 = f32[2,112,640]{2,1,0:T(8,128)S(1)} collective-permute-done((f32[2,112,640]{2,1,0:T(8,128)S(1)}, f32[2,112,640]{2,1,0:T(8,128)S(1)}, u32[]{:S(2)}, u32[]{:S(2)}) %collective-permute-start.8) | collective-permute-done | bytes 573472 | tf_op jit(solution)/shard_map/ppermute | solution.py:275
  76.9 0.1 slice_add_fusion
  76.9 1.2 %collective-permute-start.9 = (f32[1,112,640]{2,1,0:T(8,128)S(1)}, f32[1,112,640]{2,1,0:T(8,128)S(1)}, u32[]{:S(2)}, u32[]{:S(2)}) collective-permute-start(f32[1,112,640]{2,1,0:T(8,128)S(1)} %get-tuple-element.39), channel_id=1, source_target_pairs={{0,8},{1,9},{2,10},{3,11},{4,12},{5,13},{6,14},{7,15},{8,0},{9,1},... | collective-permute-start | bytes 860168 | tf_op jit(solution)/shard_map/ppermute | solution.py:275
  78.1 19.4 %collective-permute-done.4 = f32[1,112,640]{2,1,0:T(8,128)S(1)} collective-permute-done((f32[1,112,640]{2,1,0:T(8,128)S(1)}, f32[1,112,640]{2,1,0:T(8,128)S(1)}, u32[]{:S(2)}, u32[]{:S(2)}) %collective-permute-start.4) | collective-permute-done | bytes 286752 | tf_op jit(solution)/shard_map/ppermute | solution.py:275
  97.5 6.1 %collective-permute-done.9 = f32[1,112,640]{2,1,0:T(8,128)S(1)} collective-permute-done((f32[1,112,640]{2,1,0:T(8,128)S(1)}, f32[1,112,640]{2,1,0:T(8,128)S(1)}, u32[]{:S(2)}, u32[]{:S(2)}) %collective-permute-start.9) | collective-permute-done | bytes 286752 | tf_op jit(solution)/shard_map/ppermute | solution.py:275
  103.6 1.2 %finish.1 = f32[48,1,1248]{2,1,0:T(1,128)} custom-call(s32[48,1]{1,0:T(8,128)S(1)} %copy.6.pick_ref, f32[3,48,128]{2,1,0:T(8,128)S(1)} %get-tuple-element.22.refs_6_.stats_ref, f32[112,640]{1,0:T(8,128)S(1)} %get-tuple-element.42.refs_0_, f32[112,640]{1,0:T(8,128)S(1)} %bitcast.12, f32[112,640]{1,0:T(8,128)S(1)} %get-tuple-element.40.refs_2_, ...), custom_call_target="tpu_custom_call" | custom-call | flops 1198080 | bytes 1146880 | tf_op jit(solution)/shard_map/finish/pallas_call | solution.py:259
  (15 shorter events, 0.0 us)
Async XLA Ops:
  0.0 12.8 %copy-start.3 = (s32[48]{0:T(128)S(1)}, s32[48]{0:T(128)}, u32[]{:S(2)}) copy-start(s32[48]{0:T(128)} %param.7) | copy-start | bytes 580
  0.0 13.1 %copy-start.1 = (s32[128,48]{0,1:T(8,128)S(1)}, s32[128,48]{0,1:T(8,128)}, u32[]{:S(2)}) copy-start(s32[128,48]{0,1:T(8,128)} %param.6) | copy-start | bytes 73732
  0.0 13.1 %copy-start.2 = (bf16[128,16]{0,1:T(8,128)(2,1)S(1)}, bf16[128,16]{0,1:T(8,128)(2,1)}, u32[]{:S(2)}) copy-start(bf16[128,16]{0,1:T(8,128)(2,1)} %param.5) | copy-start | bytes 12292
  8.0 4.8 %copy-start = (bf16[4,128,640]{2,1,0:T(8,128)(2,1)}, bf16[4,128,640]{2,1,0:T(8,128)(2,1)S(1)}, u32[]{:S(2)}) copy-start(bf16[4,128,640]{2,1,0:T(8,128)(2,1)S(1)} %get-tuple-element.34) | copy-start | bytes 1966084
  8.0 4.9 %collective-permute-start = (bf16[4,128,640]{2,1,0:T(8,128)(2,1)}, bf16[4,128,640]{2,1,0:T(8,128)(2,1)S(1)}, u32[]{:S(2)}, u32[]{:S(2)}) collective-permute-start(bf16[4,128,640]{2,1,0:T(8,128)(2,1)} %get-tuple-element.24), channel_id=1, source_target_pairs={{0,1},{1,0},{2,3},{3,2},{4,5},{5,4},{6,7},{7,6},{8,9},{9,8},{10,11... | collective-permute-start | bytes 1966088 | tf_op jit(solution)/shard_map/ppermute | solution.py:275
  8.1 50.5 %collective-permute-start.1 = (bf16[4,128,640]{2,1,0:T(8,128)(2,1)}, bf16[4,128,640]{2,1,0:T(8,128)(2,1)}, u32[]{:S(2)}, u32[]{:S(2)}) collective-permute-start(bf16[4,128,640]{2,1,0:T(8,128)(2,1)} %get-tuple-element.25), channel_id=1, source_target_pairs={{0,2},{1,3},{2,0},{3,1},{4,6},{5,7},{6,4},{7,5},{8,10},{9,11},{10,... | collective-permute-start | bytes 1966088 | tf_op jit(solution)/shard_map/ppermute | solution.py:275
  10.7 47.9 %collective-permute-start.2 = (bf16[4,128,640]{2,1,0:T(8,128)(2,1)}, bf16[4,128,640]{2,1,0:T(8,128)(2,1)}, u32[]{:S(2)}, u32[]{:S(2)}) collective-permute-start(bf16[4,128,640]{2,1,0:T(8,128)(2,1)} %get-tuple-element.26), channel_id=1, source_target_pairs={{0,3},{1,2},{2,1},{3,0},{4,7},{5,6},{6,5},{7,4},{8,11},{9,10},{10,... | collective-permute-start | bytes 1966088 | tf_op jit(solution)/shard_map/ppermute | solution.py:275
  10.8 50.3 %collective-permute-start.5 = (bf16[4,128,640]{2,1,0:T(8,128)(2,1)}, bf16[4,128,640]{2,1,0:T(8,128)(2,1)S(1)}, u32[]{:S(2)}, u32[]{:S(2)}) collective-permute-start(bf16[4,128,640]{2,1,0:T(8,128)(2,1)} %get-tuple-element.32), channel_id=1, source_target_pairs={{0,1},{1,0},{2,3},{3,2},{4,5},{5,4},{6,7},{7,6},{8,9},{9,8},{10,11... | collective-permute-start | bytes 1966088 | tf_op jit(solution)/shard_map/ppermute | solution.py:275
  11.1 49.9 %collective-permute-start.6 = (bf16[4,128,640]{2,1,0:T(8,128)(2,1)}, bf16[4,128,640]{2,1,0:T(8,128)(2,1)S(1)}, u32[]{:S(2)}, u32[]{:S(2)}) collective-permute-start(bf16[4,128,640]{2,1,0:T(8,128)(2,1)} %get-tuple-element.33), channel_id=1, source_target_pairs={{0,4},{1,5},{2,6},{3,7},{4,0},{5,1},{6,2},{7,3},{8,12},{9,13},{10,... | collective-permute-start | bytes 1966088 | tf_op jit(solution)/shard_map/ppermute | solution.py:275
  12.9 48.2 %collective-permute-start.7 = (bf16[4,128,640]{2,1,0:T(8,128)(2,1)}, bf16[4,128,640]{2,1,0:T(8,128)(2,1)S(1)}, u32[]{:S(2)}, u32[]{:S(2)}) collective-permute-start(bf16[4,128,640]{2,1,0:T(8,128)(2,1)} %copy-done), channel_id=1, source_target_pairs={{0,5},{1,4},{2,7},{3,6},{4,1},{5,0},{6,3},{7,2},{8,13},{9,12},{10,... | collective-permute-start | bytes 1966088 | tf_op jit(solution)/shard_map/ppermute | solution.py:275
  61.0 14.5 %collective-permute-start.3 = (f32[2,112,640]{2,1,0:T(8,128)S(1)}, f32[2,112,640]{2,1,0:T(8,128)S(1)}, u32[]{:S(2)}, u32[]{:S(2)}) collective-permute-start(f32[2,112,640]{2,1,0:T(8,128)S(1)} %get-tuple-element.30), channel_id=1, source_target_pairs={{0,4},{1,5},{2,6},{3,7},{4,0},{5,1},{6,2},{7,3},{8,12},{9,13},{10,... | collective-permute-start | bytes 1720328 | tf_op jit(solution)/shard_map/ppermute | solution.py:275
  62.4 14.5 %collective-permute-start.8 = (f32[2,112,640]{2,1,0:T(8,128)S(1)}, f32[2,112,640]{2,1,0:T(8,128)S(1)}, u32[]{:S(2)}, u32[]{:S(2)}) collective-permute-start(f32[2,112,640]{2,1,0:T(8,128)S(1)} %get-tuple-element.38), channel_id=1, source_target_pairs={{0,2},{1,3},{2,0},{3,1},{4,6},{5,7},{6,4},{7,5},{8,10},{9,11},{10,... | collective-permute-start | bytes 1720328 | tf_op jit(solution)/shard_map/ppermute | solution.py:275
  75.5 22.0 %collective-permute-start.4 = (f32[1,112,640]{2,1,0:T(8,128)S(1)}, f32[1,112,640]{2,1,0:T(8,128)S(1)}, u32[]{:S(2)}, u32[]{:S(2)}) collective-permute-start(f32[1,112,640]{2,1,0:T(8,128)S(1)} %get-tuple-element.41), channel_id=1, source_target_pairs={{0,8},{1,9},{2,10},{3,11},{4,12},{5,13},{6,14},{7,15},{8,0},{9,1},... | collective-permute-start | bytes 860168 | tf_op jit(solution)/shard_map/ppermute | solution.py:275
  76.9 26.7 %collective-permute-start.9 = (f32[1,112,640]{2,1,0:T(8,128)S(1)}, f32[1,112,640]{2,1,0:T(8,128)S(1)}, u32[]{:S(2)}, u32[]{:S(2)}) collective-permute-start(f32[1,112,640]{2,1,0:T(8,128)S(1)} %get-tuple-element.39), channel_id=1, source_target_pairs={{0,8},{1,9},{2,10},{3,11},{4,12},{5,13},{6,14},{7,15},{8,0},{9,1},... | collective-permute-start | bytes 860168 | tf_op jit(solution)/shard_map/ppermute | solution.py:275

commit v2 on v0

v2 whole, which is shorter than its diff:
```python
import functools

import jax
import jax.numpy as jnp
from jax import lax
from jax.experimental import pallas as pl
from jax.experimental.pallas import tpu as pltpu
from jax.sharding import PartitionSpec as P

LANES = 128
VMEM_BYTES = 48 * 1024 * 1024


def round_up(value, multiple):
    return -(-value // multiple) * multiple


def pick_bits(value, bits):
    result = 0
    for place, bit in enumerate(bits):
        result = result + ((value >> bit) & 1) * (1 << place)
    return result


def spread_bits(value, bits):
    result = 0
    for place, bit in enumerate(bits):
        result += ((value >> place) & 1) << bit
    return result


class Plan:
    def __init__(self, n, block):
        self.n = n
        self.block = block
        self.tiles = round_up(block, LANES) // LANES
        self.share = (self.tiles + 1) // 2
        self.high_bits = list(range(3, n.bit_length() - 1))
        first = (3 * self.share + 4) // 5
        self.chunks = [(0, first)]
        if self.share > first:
            self.chunks.append((first, self.share - first))

    def width(self, chunk):
        return self.chunks[chunk][1] * LANES

    def ring(self, side, chunk):
        start, count = self.chunks[chunk]
        low = side * self.share + start
        return range(low, min(low + count, self.tiles if side else self.share))

    def folded(self, owner):
        first = owner * self.block // LANES
        return (owner * self.block + self.block - 1) // LANES - first == self.tiles

    def folds(self, chunk):
        return [] if chunk else [owner for owner in range(self.n) if self.folded(owner)]

    def panel_rows(self, height):
        return round_up(-(-height // self.chunks[0][1]), 16)

    def place_bits(self, side):
        return [2 - side] + self.high_bits + [0]

    def by_rows(self):
        return [(d, d ^ (2 + 2 * (d & 1))) for d in range(self.n)]

    def by_sums(self):
        return [(d, d ^ (4 - 2 * (d & 1))) for d in range(self.n)]

    def by_mask(self, mask):
        return [(d, d ^ mask) for d in range(self.n)]


def pack_kernel(plan, chunk, x_ref, mine_ref, *refs):
    outs, (ends, fold, end_sems, sems) = refs[-8:-4], refs[-4:]
    me = lax.axis_index("pat")
    rows = x_ref.shape[0]
    folded = plan.folds(chunk)

    def tile(index, count=1):
        return x_ref.at[:, pl.ds(index * LANES, count * LANES)]

    def end_copies(number):
        first = folded[number] * plan.block // LANES
        return [
            pltpu.make_async_copy(
                tile(first + which * plan.tiles), ends.at[number, which], end_sems.at[number, which]
            )
            for which in range(2)
        ]

    def move(source, side, owner, lane, sem):
        away = (me & 1) ^ side
        relative = owner ^ me ^ away
        target = 2 * away + ((relative >> (1 + side)) & 1)
        place = pick_bits(relative, plan.place_bits(side))
        lanes = pl.ds(lane, source.shape[-1])
        for t in range(4):

            @pl.when(target == t)
            def _():
                here = pl.ds(pl.multiple_of(place * rows, rows), rows)
                pltpu.make_async_copy(source, outs[t].at[here, lanes], sem).start()

        return pltpu.make_async_copy(source, outs[0].at[pl.ds(0, rows), lanes], sem)

    for number in range(len(folded)):
        for copy in end_copies(number):
            copy.start()
    waits = []
    for owner in range(plan.n):
        first = owner * plan.block // LANES
        for side in range(2):
            places = plan.ring(side, chunk)
            skip = int(0 in places and owner in folded)
            if len(places) > skip:
                source = tile(first + places[skip], len(places) - skip)
                waits.append(move(source, side, owner, skip * LANES, sems.at[len(waits)]))
    if chunk == 0:
        height = plan.panel_rows(mine_ref.shape[0])
        for piece in range(mine_ref.shape[0] // height):
            for out in outs[1::2]:
                copy = pltpu.make_async_copy(
                    mine_ref.at[pl.ds(piece * height, height), :],
                    out.at[pl.ds(plan.n // 2 * rows, height), pl.ds(piece * LANES, LANES)],
                    sems.at[len(waits)],
                )
                copy.start()
                waits.append(copy)
    for number, owner in enumerate(folded):
        for copy in end_copies(number):
            copy.wait()
        edge = owner * plan.block % LANES
        lane = lax.broadcasted_iota(jnp.int32, (16, LANES), 1)
        for row in range(0, rows, 16):
            here = slice(row, row + 16)
            head = ends[number, 0, here, :].astype(jnp.float32)
            tail = ends[number, 1, here, :].astype(jnp.float32)
            fold[number, here, :] = jnp.where(lane >= edge, head, tail).astype(fold.dtype)
        waits.append(move(fold.at[number], 0, owner, 0, sems.at[len(waits)]))
    for copy in waits:
        copy.wait()


def pack(covariates, mine, plan, chunk, after):
    rows = covariates.shape[0]
    tail = 0 if chunk else plan.panel_rows(mine.shape[0])
    out_shape = [
        jax.ShapeDtypeStruct((plan.n // 2 * rows + sent * tail, plan.width(chunk)), covariates.dtype)
        for sent in (0, 1, 0, 1)
    ]
    folds = max(1, len(plan.folds(chunk)))
    moves = 2 * plan.n + folds + 2 * (mine.shape[0] // 16)
    return pl.pallas_call(
        functools.partial(pack_kernel, plan, chunk),
        in_specs=[pl.BlockSpec(memory_space=pl.ANY)] * (2 + len(after)),
        out_specs=[pl.BlockSpec(memory_space=pl.ANY)] * 4,
        out_shape=out_shape,
        scratch_shapes=[
            pltpu.VMEM((folds, 2, rows, LANES), covariates.dtype),
            pltpu.VMEM((folds, rows, LANES), covariates.dtype),
            pltpu.SemaphoreType.DMA((folds, 2)),
            pltpu.SemaphoreType.DMA((moves,)),
        ],
        compiler_params=pltpu.CompilerParams(vmem_limit_bytes=VMEM_BYTES),
        cost_estimate=pl.CostEstimate(
            flops=0, bytes_accessed=2 * covariates.size, transcendentals=0
        ),
        name="pack",
    )(covariates, mine, *after)


def onehot_of(pick_ref, weightings, dtype):
    index = lax.broadcasted_iota(jnp.int32, (pick_ref.shape[0], weightings), 1)
    return jnp.where(index == pick_ref[...], 1.0, 0.0).astype(dtype)


def arm_columns(tail_ref, onehot):
    comps, weightings = onehot.shape
    height, width = tail_ref.shape
    pieces = [tail_ref[:, lane:lane + LANES] for lane in range(0, width, LANES)]
    panel = jnp.concatenate(pieces[:(weightings + comps) // height], axis=0)
    weights = panel[0:weightings]
    arms = panel[weightings:weightings + comps].astype(jnp.float32)
    picked = jnp.dot(onehot, weights, preferred_element_type=jnp.float32)
    return weights, picked * arms, picked * (1.0 - arms)


def tail_specs(arrays, height):
    return [
        pl.BlockSpec((height, array.shape[1]), lambda s, at=array.shape[0] // height - 1: (at, 0))
        for array in arrays
    ]


def whole_spec(shape):
    return pl.BlockSpec(shape, lambda s: (0,) * len(shape))


def totals_kernel(weightings, pick_ref, *refs):
    tail_refs, out_ref = refs[:-1], refs[-1]
    onehot = onehot_of(pick_ref, weightings, jnp.bfloat16)
    target_sum, other_sum = 0.0, 0.0
    for ref in tail_refs:
        _, target, other = arm_columns(ref, onehot)
        target_sum += target
        other_sum += other
    lane = lax.broadcasted_iota(jnp.int32, out_ref.shape, 1)
    out_ref[...] = jnp.where(
        lane == 0,
        jnp.sum(target_sum, axis=1, keepdims=True),
        jnp.sum(other_sum, axis=1, keepdims=True),
    )


def group_totals(rows, pick_column, weightings, height):
    comps = pick_column.shape[0]
    return pl.pallas_call(
        functools.partial(totals_kernel, weightings),
        grid=(1,),
        in_specs=[whole_spec(pick_column.shape)] + tail_specs(rows, height),
        out_specs=whole_spec((comps, LANES)),
        out_shape=jax.ShapeDtypeStruct((comps, LANES), jnp.float32),
        cost_estimate=pl.CostEstimate(flops=0, bytes_accessed=1 << 18, transcendentals=0),
        name="totals",
    )(pick_column, *rows)


def panel_kernel(weightings, pick_ref, totals_ref, *refs):
    tail_refs, (first_ref, second_ref, stats_ref) = refs[:-3], refs[-3:]
    comps = pick_ref.shape[0]
    onehot = onehot_of(pick_ref, weightings, jnp.bfloat16)
    totals = totals_ref[...]
    total_target, total_other = totals[:, 0:1], totals[:, 1:2]
    light = jnp.where(total_target <= total_other, 1.0, 0.0)
    stats_ref[0] = jnp.broadcast_to(1.0 / total_target, (comps, LANES))
    stats_ref[1] = jnp.broadcast_to(1.0 / total_other, (comps, LANES))
    stats_ref[2] = jnp.broadcast_to(light, (comps, LANES))
    for place, ref in enumerate(tail_refs):
        weights, target, other = arm_columns(ref, onehot)
        lighter = light * target + (1.0 - light) * other
        here = slice(place * LANES, (place + 1) * LANES)
        first_ref[0:comps, here] = lighter.astype(jnp.bfloat16)
        first_ref[comps:comps + weightings, here] = weights
        second_ref[0:comps, here] = target.astype(jnp.bfloat16)
        second_ref[comps:2 * comps, here] = other.astype(jnp.bfloat16)


def make_panels(rows, totals, pick_column, weightings, height):
    comps = pick_column.shape[0]
    shapes = [
        ((comps + weightings, len(rows) * LANES), jnp.bfloat16),
        ((2 * comps, len(rows) * LANES), jnp.bfloat16),
        ((3, comps, LANES), jnp.float32),
    ]
    return pl.pallas_call(
        functools.partial(panel_kernel, weightings),
        grid=(1,),
        in_specs=[whole_spec(pick_column.shape), whole_spec(totals.shape)]
        + tail_specs(rows, height),
        out_specs=[whole_spec(shape) for shape, _ in shapes],
        out_shape=[jax.ShapeDtypeStruct(shape, dtype) for shape, dtype in shapes],
        cost_estimate=pl.CostEstimate(flops=0, bytes_accessed=1 << 19, transcendentals=0),
        name="panels",
    )(pick_column, totals, *rows)


def moments_kernel(rows, x_count, *refs):
    xs = refs[:x_count]
    first_ref, second_ref, stats_ref = refs[x_count:x_count + 3]
    outs = refs[-2:]
    first_rows = first_ref.shape[0]
    comps = second_ref.shape[0] // 2
    inverse_target = stats_ref[0][:, 0:1]
    inverse_other = stats_ref[1][:, 0:1]
    for place, out_ref in enumerate(outs):
        x = jnp.concatenate([ref[place * rows:(place + 1) * rows, :] for ref in xs], axis=0)
        first = jnp.dot(first_ref[...], x, preferred_element_type=jnp.float32)
        squares = (x.astype(jnp.float32) * x.astype(jnp.float32)).astype(jnp.bfloat16)
        second = jnp.dot(second_ref[...], squares, preferred_element_type=jnp.float32)
        out_ref[0, 0:first_rows, :] = first
        out_ref[0, first_rows:first_rows + comps, :] = (
            second[0:comps] * inverse_target + second[comps:2 * comps] * inverse_other
        )


def moments(xs, first, second, stats, places, after):
    rows = first.shape[1] // len(xs)
    width = xs[0].shape[1]
    comps = second.shape[0] // 2
    out_rows = first.shape[0] + comps
    return pl.pallas_call(
        functools.partial(moments_kernel, rows, len(xs)),
        grid=(places // 2,),
        in_specs=[pl.BlockSpec((2 * rows, width), lambda s: (s, 0))] * len(xs)
        + [whole_spec(array.shape) for array in (first, second, stats)]
        + [pl.BlockSpec(memory_space=pl.ANY)] * len(after),
        out_specs=[pl.BlockSpec((1, out_rows, width), lambda s: (s, 0, 0))] * 2,
        out_shape=[jax.ShapeDtypeStruct((places // 2, out_rows, width), jnp.float32)] * 2,
        compiler_params=pltpu.CompilerParams(vmem_limit_bytes=VMEM_BYTES),
        cost_estimate=pl.CostEstimate(
            flops=2 * places * len(xs) * rows * width * (first.shape[0] + second.shape[0]),
            bytes_accessed=places * width * (2 * len(xs) * rows + 4 * out_rows),
            transcendentals=0,
        ),
        name="moments",
    )(*xs, first, second, stats, *after)


def finish_kernel(plan, weightings, pick_ref, stats_ref, *refs):
    out_ref, ring_ref = refs[-2:]
    per_chunk = (len(refs) - 2) // len(plan.chunks)
    comps = pick_ref.shape[0]
    onehot = onehot_of(pick_ref, weightings, jnp.float32)
    inverse_target = stats_ref[0][:, 0:1]
    inverse_other = stats_ref[1][:, 0:1]
    light = stats_ref[2][:, 0:1] > 0.5
    me = lax.axis_index("pat")
    my_side = me & 1
    for chunk in range(len(plan.chunks)):
        arrays = refs[chunk * per_chunk:(chunk + 1) * per_chunk]
        for away in range(2):
            sums = arrays[away][...]
            for more in arrays[2 + away::2]:
                sums += more[...]
            lighter = sums[0:comps]
            both = jnp.dot(
                onehot,
                sums[comps:comps + weightings],
                precision=lax.Precision.HIGHEST,
                preferred_element_type=jnp.float32,
            )
            spread = sums[comps + weightings:2 * comps + weightings]
            heavier = both - lighter
            mean_target = jnp.where(light, lighter, heavier) * inverse_target
            mean_other = jnp.where(light, heavier, lighter) * inverse_other
            variance = spread - mean_target * mean_target - mean_other * mean_other
            pooled = jnp.maximum(variance / 2.0, 0.01)
            balance = (mean_target - mean_other) / jnp.sqrt(pooled)
            for side in range(2):
                places = plan.ring(side, chunk)
                if places:
                    lanes = slice(places[0] * LANES, places[-1] * LANES + LANES)

                    @pl.when(my_side ^ away == side)
                    def _():
                        ring_ref[:, lanes] = balance[:, 0:len(places) * LANES]
    width = plan.tiles * LANES
    shift = width - lax.rem(me * plan.block, LANES)
    out_ref[:, 0, :] = pltpu.roll(ring_ref[...], shift, 1)[:, 0:plan.block]


def finish(plan, parts, pick_column, stats, weightings):
    comps = pick_column.shape[0]
    operands = [array for part in parts for array in part]
    return pl.pallas_call(
        functools.partial(finish_kernel, plan, weightings),
        in_specs=[pl.BlockSpec(memory_space=pltpu.VMEM)] * (2 + len(operands)),
        out_specs=pl.BlockSpec(memory_space=pltpu.VMEM),
        out_shape=jax.ShapeDtypeStruct((comps, 1, plan.block), jnp.float32),
        scratch_shapes=[pltpu.VMEM((comps, plan.tiles * LANES), jnp.float32)],
        compiler_params=pltpu.CompilerParams(vmem_limit_bytes=VMEM_BYTES),
        cost_estimate=pl.CostEstimate(
            flops=20 * comps * plan.block,
            bytes_accessed=4 * sum(operand.size for operand in operands),
            transcendentals=comps * plan.block,
        ),
        name="finish",
    )(pick_column, stats, *operands)


def swap(array, pairs):
    return lax.ppermute(array, "pat", pairs)


def on_device(n, covs, covariates, weights, arms, pick):
    weightings = weights.shape[1]
    pick_column = pick.reshape(pick.shape[0], 1)
    plan = Plan(n, covariates.shape[1] // n)
    to_other_side = plan.by_mask(1)

    arm_rows = arms.T.astype(weights.dtype)
    if covs > 1:
        arm_rows = lax.all_gather(arm_rows, "cov", axis=0, tiled=True)
    mine = jnp.concatenate([weights.T, arm_rows], axis=0)

    rows, after = [], []
    for chunk in range(len(plan.chunks)):
        kept, sent, other_kept, other_sent = pack(covariates, mine, plan, chunk, after)
        passed = swap(other_sent, to_other_side)
        arrived = swap(sent, plan.by_rows())
        rows.append([kept, swap(other_kept, to_other_side), arrived, swap(passed, plan.by_rows())])
        if chunk == 0:
            tails = [sent, passed] + rows[0][2:]
        after = [passed]

    height = plan.panel_rows(mine.shape[0])
    totals = group_totals(tails, pick_column, weightings, height)
    totals += swap(totals, plan.by_sums())
    for bit in plan.high_bits:
        totals += swap(totals, plan.by_mask(1 << bit))
    first, second, stats = make_panels(tails, totals, pick_column, weightings, height)

    parts, after = [], []
    for chunk in range(len(plan.chunks)):
        kept, sent = moments(rows[chunk], first, second, stats, n // 2, after)
        after = [kept]
        arrived = swap(sent, plan.by_sums())
        for bit in plan.high_bits[:-1]:
            sent = kept[1::2] + arrived[1::2]
            kept = kept[0::2] + arrived[0::2]
            arrived = swap(sent, plan.by_mask(1 << bit))
        part = []
        for bit in plan.high_bits[-1:]:
            last = plan.by_mask(1 << bit)
            last_other = plan.by_mask((1 << bit) | 1)
            part = [
                swap(kept[1] + arrived[1], last),
                swap(kept[3] + arrived[3], last_other),
            ]
            kept, arrived = kept[0::2], arrived[0::2]
        part = [kept[0] + arrived[0], swap(kept[1] + arrived[1], to_other_side)] + part
        parts.append(part)
    return finish(plan, parts, pick_column, stats, weightings)


def solution(mesh):
    placed = (
        P(("groups", "pat"), "cov"),
        P(("groups", "pat"), None),
        P(("groups", "pat"), "cov"),
        P(),
    )
    body = functools.partial(on_device, mesh.shape["pat"], mesh.shape["cov"])
    return jax.shard_map(
        body, mesh=mesh, in_specs=placed, out_specs=P("groups", "cov", "pat"), check_vma=False
    )
```

time: 352 us -> 148 us (0.42)
  waiting for transfers between devices: 178 us -> 33.2 us
  local copies, waits for them, and re-layouts: 102 us -> 11.1 us
  Pallas kernels: 0 us -> 66.4 us
  starting transfers between devices: 0.01 us -> 33 us
  blocking collectives: 30.6 us -> 0 us
  between operations: 13.5 us -> 0.2 us
  matrix products: 12.1 us -> 0 us
  other arithmetic: 12.6 us -> 2.93 us
    unnamed x2 -> x0, waiting for transfers between devices: 178 us -> none
    unnamed x15 -> x38, local copies, waits for them, and re-layouts: 98.3 us -> 10.3 us
    pallas_call x0 -> x7, Pallas kernels: none -> 66.4 us  [the longest x2 54.8 us: pack(): pl.pallas_call(functools.partial(pack_kernel, plan, chunk), in_specs=[pl....]
    ppermute x0 -> x18, waiting for transfers between devices: none -> 33.2 us  [swap(): return lax.ppermute(array, 'pat', pairs)]
    ppermute x0 -> x18, starting transfers between devices: none -> 33 us  [swap(): return lax.ppermute(array, 'pat', pairs)]
    psum x1 -> x0, blocking collectives: 30.6 us -> none  [on_device(): totals = lax.psum(placed, ('pat', 'cov'))]
    another operation x3 -> x0, other arithmetic: 12.4 us -> none  [the longest x1 11.7 us: on_device(): jnp.stack([first.reshape(2, count, -1), second.reshape(2, count, -1)])]
    dot_general x3 -> x0, matrix products: 12.1 us -> none  [the longest x1 6.82 us: moment_pair(): lax.dot_general(columns, squares, dims, preferred_element_type=jnp.float32)]
  transfers between devices with their start and end apart: 1 -> 18, of which waited for: 1 -> 8; matrix products, arithmetic and copies ran while one was open for 0% -> 2% of each run, Pallas kernels for 0% -> 27%
where the time goes in v2:
time: 148 us; the launch traced here: 147 us
  Pallas kernels  66.4 us (45%)
  waiting for transfers between devices  33.2 us (22%)
  starting transfers between devices  33 us (22%)
  local copies, waits for them, and re-layouts  11.1 us (8%)
  other arithmetic  2.93 us (2%)
    pallas_call x2, Pallas kernels, pack(): pl.pallas_call(functools.partial(pack_kernel, plan, chunk), in_specs=[pl....  54.8 us
    ppermute x18, waiting for transfers between devices, swap(): return lax.ppermute(array, 'pat', pairs)  33.2 us
    ppermute x18, starting transfers between devices, swap(): return lax.ppermute(array, 'pat', pairs)  33 us
    unnamed x38, local copies, waits for them, and re-layouts  10.3 us
    pallas_call x2, Pallas kernels, moments(): pl.pallas_call(functools.partial(moments_kernel, rows, len(xs)), grid=(pl...  6.19 us
  transfers between devices with their start and end apart: 18, of which 8 were waited for; matrix products, arithmetic and copies ran while one was open for 2% of the time, Pallas kernels for 27%

profile of v2, /device:TPU:1, one launch (start us, length us, event | category | flops | bytes accessed | tf_op | source)
XLA Modules:
  0.0 146.8 jit_solution(8871809506229020489)
XLA Ops:
  1.4 21.6 %pack.2 = (bf16[1024,384]{1,0:T(8,128)(2,1)S(1)}, bf16[1056,384]{1,0:T(8,128)(2,1)S(1)}, bf16[1024,384]{1,0:T(8,128)(2,1)}, bf16[1056,384]{1,0:T(8,128)(2,1)S(1)}) custom-call(bf16[128,19968]{1,0:T(8,128)(2,1)} %x_ref.3, bf16[64,128]{1,0:T(8,128)(2,1)S(1)} %pad_maximum_fusion.mine_ref), custom_call_target="tpu_custom_call" | custom-call | bytes 5111808 | tf_op jit(solution)/shard_map/pack/pallas_call | solution.py:155
  23.0 4.1 %collective-permute-start = (bf16[1056,384]{1,0:T(8,128)(2,1)S(1)}, bf16[1056,384]{1,0:T(8,128)(2,1)S(1)}, u32[]{:S(2)}, u32[]{:S(2)}) collective-permute-start(bf16[1056,384]{1,0:T(8,128)(2,1)S(1)} %get-tuple-element.21), channel_id=1, source_target_pairs={{0,1},{1,0},{2,3},{3,2},{4,5},{5,4},{6,7},{7,6},{8,9},{9,8},{10,11... | collective-permute-start | bytes 2433032 | tf_op jit(solution)/shard_map/ppermute | solution.py:374
  27.1 2.8 %collective-permute-start.1 = (bf16[1056,384]{1,0:T(8,128)(2,1)S(1)}, bf16[1056,384]{1,0:T(8,128)(2,1)S(1)}, u32[]{:S(2)}, u32[]{:S(2)}) collective-permute-start(bf16[1056,384]{1,0:T(8,128)(2,1)S(1)} %get-tuple-element.20.refs_0_), channel_id=1, source_target_pairs={{0,2},{1,5},{2,0},{3,7},{4,6},{5,1},{6,4},{7,3},{8,10},{9,13},{10,... | collective-permute-start | bytes 2433032 | tf_op jit(solution)/shard_map/ppermute | solution.py:374
  30.0 33.2 %pack.3 = (bf16[1024,256]{1,0:T(8,128)(2,1)S(1)}, bf16[1024,256]{1,0:T(8,128)(2,1)}, bf16[1024,256]{1,0:T(8,128)(2,1)}, bf16[1024,256]{1,0:T(8,128)(2,1)S(1)}) custom-call(bf16[128,19968]{1,0:T(8,128)(2,1)} %x_ref.3, bf16[64,128]{1,0:T(8,128)(2,1)S(1)} %pad_maximum_fusion.mine_ref, bf16[1056,384]{1,0:T(8,128)(2,1)S(1)} %collective-permute-done.refs_1_.refs_0_), custom_call_target="tpu_custom_call" | custom-call | bytes 5111808 | tf_op jit(solution)/shard_map/pack/pallas_call | solution.py:155
  64.3 2.1 %collective-permute-start.2 = (bf16[1056,384]{1,0:T(8,128)(2,1)S(1)}, bf16[1056,384]{1,0:T(8,128)(2,1)S(1)}, u32[]{:S(2)}, u32[]{:S(2)}) collective-permute-start(bf16[1056,384]{1,0:T(8,128)(2,1)S(1)} %collective-permute-done.refs_1_.refs_0_), channel_id=1, source_target_pairs={{0,2},{1,5},{2,0},{3,7},{4,6},{5,1},{6,4},{7,3},{8,10},{9,13},{10,... | collective-permute-start | bytes 2433032 | tf_op jit(solution)/shard_map/ppermute | solution.py:374
  66.9 1.2 collective-permute-start.11
  69.1 7.2 %collective-permute-done.2.refs_3_ = bf16[1056,384]{1,0:T(8,128)(2,1)S(1)} collective-permute-done((bf16[1056,384]{1,0:T(8,128)(2,1)S(1)}, bf16[1056,384]{1,0:T(8,128)(2,1)S(1)}, u32[]{:S(2)}, u32[]{:S(2)}) %collective-permute-start.2) | collective-permute-done | bytes 811040 | tf_op jit(solution)/shard_map/ppermute | solution.py:374
  77.2 1.7 %totals.1 = f32[48,128]{1,0:T(8,128)} custom-call(s32[48,1]{1,0:T(8,128)} %copy.7.pick_ref, bf16[1056,384]{1,0:T(8,128)(2,1)} %copy-done.5, bf16[1056,384]{1,0:T(8,128)(2,1)} %copy-done.2, bf16[1056,384]{1,0:T(8,128)(2,1)} %copy-done, bf16[1056,384]{1,0:T(8,128)(2,1)} %copy-done.3), custom_call_target="tpu_custom_call" | custom-call | bytes 262144 | tf_op jit(solution)/shard_map/totals/pallas_call | solution.py:219
  78.9 1.3 collective-permute-start.3
  80.2 2.3 %collective-permute-done.3 = f32[48,128]{1,0:T(8,128)S(1)} collective-permute-done((f32[48,128]{1,0:T(8,128)}, f32[48,128]{1,0:T(8,128)S(1)}, u32[]{:S(2)}, u32[]{:S(2)}) %collective-permute-start.3) | collective-permute-done | bytes 24608 | tf_op jit(solution)/shard_map/ppermute | solution.py:374
  83.3 2.4 %collective-permute-start.4 = (f32[48,128]{1,0:T(8,128)S(1)}, f32[48,128]{1,0:T(8,128)S(1)}, u32[]{:S(2)}, u32[]{:S(2)}) collective-permute-start(f32[48,128]{1,0:T(8,128)S(1)} %add.52), channel_id=1, source_target_pairs={{0,8},{1,9},{2,10},{3,11},{4,12},{5,13},{6,14},{7,15},{8,0},{9,1},... | collective-permute-start | bytes 73736 | tf_op jit(solution)/shard_map/ppermute | solution.py:374
  85.7 1.7 %collective-permute-done.4 = f32[48,128]{1,0:T(8,128)S(1)} collective-permute-done((f32[48,128]{1,0:T(8,128)S(1)}, f32[48,128]{1,0:T(8,128)S(1)}, u32[]{:S(2)}, u32[]{:S(2)}) %collective-permute-start.4) | collective-permute-done | bytes 24608 | tf_op jit(solution)/shard_map/ppermute | solution.py:374
  88.0 1.7 %panels.1 = (bf16[64,512]{1,0:T(8,128)(2,1)}, bf16[96,512]{1,0:T(8,128)(2,1)}, f32[3,48,128]{2,1,0:T(8,128)}) custom-call(s32[48,1]{1,0:T(8,128)} %copy.7.pick_ref, f32[48,128]{1,0:T(8,128)} %add.53.totals_ref, bf16[1056,384]{1,0:T(8,128)(2,1)} %copy-done.5, bf16[1056,384]{1,0:T(8,128)(2,1)} %copy-done.2, bf16[1056,384]{1,0:T(8,128)(2,1)} %copy-done, ...), custom_call_target="tpu_custom_call" | custom-call | bytes 524288 | tf_op jit(solution)/shard_map/panels/pallas_call | solution.py:257
  90.8 1.1 copy-done.4
  95.7 3.1 %moments.2 = (f32[4,112,384]{2,1,0:T(8,128)S(1)}, f32[4,112,384]{2,1,0:T(8,128)S(1)}) custom-call(bf16[1024,384]{1,0:T(8,128)(2,1)S(1)} %copy-done.7, bf16[1024,384]{1,0:T(8,128)(2,1)} %collective-permute-done.5.refs_1_, bf16[1056,384]{1,0:T(8,128)(2,1)S(1)} %copy-done.1, bf16[1056,384]{1,0:T(8,128)(2,1)S(1)} %copy-done.4, bf16[64,512]{1,0:T(8,128)(2,1)S(1)} %copy-done.16, ...), custom_call_target="tpu_custom_call" | custom-call | flops 503316480 | bytes 4521984 | tf_op jit(solution)/shard_map/moments/pallas_call | solution.py:293
  101.5 3.1 %moments.3 = (f32[4,112,256]{2,1,0:T(8,128)S(1)}, f32[4,112,256]{2,1,0:T(8,128)S(1)}) custom-call(bf16[1024,256]{1,0:T(8,128)(2,1)S(1)} %copy-done.12, bf16[1024,256]{1,0:T(8,128)(2,1)} %collective-permute-done.10.refs_1_, bf16[1024,256]{1,0:T(8,128)(2,1)} %collective-permute-done.11.refs_2_, bf16[1024,256]{1,0:T(8,128)(2,1)} %collective-permute-done.13.refs_3_, ...), custom_call_target="tpu_custom_call" | custom-call | flops 335544320 | bytes 3014656 | tf_op jit(solution)/shard_map/moments/pallas_call | solution.py:293
  104.6 1.3 collective-permute-start.14
  106.2 6.1 %collective-permute-done.14 = f32[4,112,256]{2,1,0:T(8,128)S(1)} collective-permute-done((f32[4,112,256]{2,1,0:T(8,128)S(1)}, f32[4,112,256]{2,1,0:T(8,128)S(1)}, u32[]{:S(2)}, u32[]{:S(2)}) %collective-permute-start.14) | collective-permute-done | bytes 458784 | tf_op jit(solution)/shard_map/ppermute | solution.py:374
  112.3 5.6 %collective-permute-start.17 = (f32[112,256]{1,0:T(8,128)S(1)}, f32[112,256]{1,0:T(8,128)S(1)}, u32[]{:S(2)}, u32[]{:S(2)}) collective-permute-start(f32[112,256]{1,0:T(8,128)S(1)} %get-tuple-element.37), channel_id=1, source_target_pairs={{0,9},{1,8},{2,11},{3,10},{4,13},{5,12},{6,15},{7,14},{8,1},{9,0},... | collective-permute-start | bytes 344072 | tf_op jit(solution)/shard_map/ppermute | solution.py:374
  117.9 1.7 %collective-permute-done.6 = f32[4,112,384]{2,1,0:T(8,128)S(1)} collective-permute-done((f32[4,112,384]{2,1,0:T(8,128)S(1)}, f32[4,112,384]{2,1,0:T(8,128)S(1)}, u32[]{:S(2)}, u32[]{:S(2)}) %collective-permute-start.6) | collective-permute-done | bytes 688160 | tf_op jit(solution)/shard_map/ppermute | solution.py:374
  119.7 9.4 %collective-permute-start.9 = (f32[112,384]{1,0:T(8,128)S(1)}, f32[112,384]{1,0:T(8,128)S(1)}, u32[]{:S(2)}, u32[]{:S(2)}) collective-permute-start(f32[112,384]{1,0:T(8,128)S(1)} %get-tuple-element.35), channel_id=1, source_target_pairs={{0,9},{1,8},{2,11},{3,10},{4,13},{5,12},{6,15},{7,14},{8,1},{9,0},... | collective-permute-start | bytes 516104 | tf_op jit(solution)/shard_map/ppermute | solution.py:374
  131.7 9.5 %collective-permute-done.9.refs_3_ = f32[112,384]{1,0:T(8,128)S(1)} collective-permute-done((f32[112,384]{1,0:T(8,128)S(1)}, f32[112,384]{1,0:T(8,128)S(1)}, u32[]{:S(2)}, u32[]{:S(2)}) %collective-permute-start.9) | collective-permute-done | bytes 172064 | tf_op jit(solution)/shard_map/ppermute | solution.py:374
  141.2 3.7 %collective-permute-done.8.refs_2_ = f32[112,384]{1,0:T(8,128)S(1)} collective-permute-done((f32[112,384]{1,0:T(8,128)S(1)}, f32[112,384]{1,0:T(8,128)S(1)}, u32[]{:S(2)}, u32[]{:S(2)}) %collective-permute-start.8) | collective-permute-done | bytes 172064 | tf_op jit(solution)/shard_map/ppermute | solution.py:374
  144.9 2.0 %finish.1 = f32[48,1,1248]{2,1,0:T(1,128)} custom-call(s32[48,1]{1,0:T(8,128)S(1)} %copy-done.13, f32[3,48,128]{2,1,0:T(8,128)S(1)} %copy-done.10, f32[112,384]{1,0:T(8,128)S(1)} %get-tuple-element.40.refs_0_, f32[112,384]{1,0:T(8,128)S(1)} %collective-permute-done.7.refs_1_, f32[112,384]{1,0:T(8,128)S(1)} %collective-permute-done.8.refs_2_, ...), custom_call_target="tpu_custom_call" | custom-call | flops 1198080 | bytes 1146880 | tf_op jit(solution)/shard_map/finish/pallas_call | solution.py:357
  (70 shorter events, 16.6 us)
Async XLA Ops:
  1.4 67.0 %copy-start.18 = (s32[48]{0:T(128)S(1)}, s32[48]{0:T(128)}, u32[]{:S(2)}) copy-start(s32[48]{0:T(128)} %param.7) | copy-start | bytes 580
  23.0 43.9 %copy-start.6 = (bf16[1024,384]{1,0:T(8,128)(2,1)}, bf16[1024,384]{1,0:T(8,128)(2,1)S(1)}, u32[]{:S(2)}) copy-start(bf16[1024,384]{1,0:T(8,128)(2,1)S(1)} %get-tuple-element.23.refs_0_) | copy-start | bytes 2359300
  23.0 53.3 %copy-start.5 = (bf16[1056,384]{1,0:T(8,128)(2,1)}, bf16[1056,384]{1,0:T(8,128)(2,1)S(1)}, u32[]{:S(2)}) copy-start(bf16[1056,384]{1,0:T(8,128)(2,1)S(1)} %get-tuple-element.20.refs_0_) | copy-start | bytes 2433028
  23.0 7.0 %collective-permute-start = (bf16[1056,384]{1,0:T(8,128)(2,1)S(1)}, bf16[1056,384]{1,0:T(8,128)(2,1)S(1)}, u32[]{:S(2)}, u32[]{:S(2)}) collective-permute-start(bf16[1056,384]{1,0:T(8,128)(2,1)S(1)} %get-tuple-element.21), channel_id=1, source_target_pairs={{0,1},{1,0},{2,3},{3,2},{4,5},{5,4},{6,7},{7,6},{8,9},{9,8},{10,11... | collective-permute-start | bytes 2433032 | tf_op jit(solution)/shard_map/ppermute | solution.py:374
  27.1 39.7 %collective-permute-start.1 = (bf16[1056,384]{1,0:T(8,128)(2,1)S(1)}, bf16[1056,384]{1,0:T(8,128)(2,1)S(1)}, u32[]{:S(2)}, u32[]{:S(2)}) collective-permute-start(bf16[1056,384]{1,0:T(8,128)(2,1)S(1)} %get-tuple-element.20.refs_0_), channel_id=1, source_target_pairs={{0,2},{1,5},{2,0},{3,7},{4,6},{5,1},{6,4},{7,3},{8,10},{9,13},{10,... | collective-permute-start | bytes 2433032 | tf_op jit(solution)/shard_map/ppermute | solution.py:374
  30.0 46.3 %copy-start.2 = (bf16[1056,384]{1,0:T(8,128)(2,1)}, bf16[1056,384]{1,0:T(8,128)(2,1)S(1)}, u32[]{:S(2)}) copy-start(bf16[1056,384]{1,0:T(8,128)(2,1)S(1)} %collective-permute-done.refs_1_.refs_0_) | copy-start | bytes 2433028
  64.1 4.1 %collective-permute-start.12 = (bf16[1024,256]{1,0:T(8,128)(2,1)S(1)}, bf16[1024,256]{1,0:T(8,128)(2,1)}, u32[]{:S(2)}, u32[]{:S(2)}) collective-permute-start(bf16[1024,256]{1,0:T(8,128)(2,1)S(1)} %get-tuple-element.32), channel_id=1, source_target_pairs={{0,1},{1,0},{2,3},{3,2},{4,5},{5,4},{6,7},{7,6},{8,9},{9,8},{10,11... | collective-permute-start | bytes 1572872 | tf_op jit(solution)/shard_map/ppermute | solution.py:374
  64.3 12.0 %collective-permute-start.2 = (bf16[1056,384]{1,0:T(8,128)(2,1)S(1)}, bf16[1056,384]{1,0:T(8,128)(2,1)S(1)}, u32[]{:S(2)}, u32[]{:S(2)}) collective-permute-start(bf16[1056,384]{1,0:T(8,128)(2,1)S(1)} %collective-permute-done.refs_1_.refs_0_), channel_id=1, source_target_pairs={{0,2},{1,5},{2,0},{3,7},{4,6},{5,1},{6,4},{7,3},{8,10},{9,13},{10,... | collective-permute-start | bytes 2433032 | tf_op jit(solution)/shard_map/ppermute | solution.py:374
  66.4 23.3 %collective-permute-start.5 = (bf16[1024,384]{1,0:T(8,128)(2,1)}, bf16[1024,384]{1,0:T(8,128)(2,1)}, u32[]{:S(2)}, u32[]{:S(2)}) collective-permute-start(bf16[1024,384]{1,0:T(8,128)(2,1)} %get-tuple-element.24), channel_id=1, source_target_pairs={{0,1},{1,0},{2,3},{3,2},{4,5},{5,4},{6,7},{7,6},{8,9},{9,8},{10,11... | collective-permute-start | bytes 2359304 | tf_op jit(solution)/shard_map/ppermute | solution.py:374
  66.6 32.2 %collective-permute-start.10 = (bf16[1024,256]{1,0:T(8,128)(2,1)}, bf16[1024,256]{1,0:T(8,128)(2,1)}, u32[]{:S(2)}, u32[]{:S(2)}) collective-permute-start(bf16[1024,256]{1,0:T(8,128)(2,1)} %get-tuple-element.30), channel_id=1, source_target_pairs={{0,1},{1,0},{2,3},{3,2},{4,5},{5,4},{6,7},{7,6},{8,9},{9,8},{10,11... | collective-permute-start | bytes 1572872 | tf_op jit(solution)/shard_map/ppermute | solution.py:374
  66.9 32.0 %collective-permute-start.11 = (bf16[1024,256]{1,0:T(8,128)(2,1)}, bf16[1024,256]{1,0:T(8,128)(2,1)}, u32[]{:S(2)}, u32[]{:S(2)}) collective-permute-start(bf16[1024,256]{1,0:T(8,128)(2,1)} %get-tuple-element.31), channel_id=1, source_target_pairs={{0,2},{1,5},{2,0},{3,7},{4,6},{5,1},{6,4},{7,3},{8,10},{9,13},{10,... | collective-permute-start | bytes 1572872 | tf_op jit(solution)/shard_map/ppermute | solution.py:374
  68.1 30.8 %collective-permute-start.13 = (bf16[1024,256]{1,0:T(8,128)(2,1)}, bf16[1024,256]{1,0:T(8,128)(2,1)}, u32[]{:S(2)}, u32[]{:S(2)}) collective-permute-start(bf16[1024,256]{1,0:T(8,128)(2,1)} %collective-permute-done.12), channel_id=1, source_target_pairs={{0,2},{1,5},{2,0},{3,7},{4,6},{5,1},{6,4},{7,3},{8,10},{9,13},{10,... | collective-permute-start | bytes 1572872 | tf_op jit(solution)/shard_map/ppermute | solution.py:374
  78.9 3.6 %collective-permute-start.3 = (f32[48,128]{1,0:T(8,128)}, f32[48,128]{1,0:T(8,128)S(1)}, u32[]{:S(2)}, u32[]{:S(2)}) collective-permute-start(f32[48,128]{1,0:T(8,128)} %totals.1), channel_id=1, source_target_pairs={{0,4},{1,3},{2,6},{3,1},{4,0},{5,7},{6,2},{7,5},{8,12},{9,11},{10,... | collective-permute-start | bytes 73736 | tf_op jit(solution)/shard_map/ppermute | solution.py:374
  83.3 4.1 %collective-permute-start.4 = (f32[48,128]{1,0:T(8,128)S(1)}, f32[48,128]{1,0:T(8,128)S(1)}, u32[]{:S(2)}, u32[]{:S(2)}) collective-permute-start(f32[48,128]{1,0:T(8,128)S(1)} %add.52), channel_id=1, source_target_pairs={{0,8},{1,9},{2,10},{3,11},{4,12},{5,13},{6,14},{7,15},{8,0},{9,1},... | collective-permute-start | bytes 73736 | tf_op jit(solution)/shard_map/ppermute | solution.py:374
  95.7 49.2 %copy-start.10 = (f32[3,48,128]{2,1,0:T(8,128)S(1)}, f32[3,48,128]{2,1,0:T(8,128)}, u32[]{:S(2)}) copy-start(f32[3,48,128]{2,1,0:T(8,128)} %get-tuple-element.22.refs_6_.stats_ref) | copy-start | bytes 221188
  95.7 49.2 %copy-start.13 = (s32[48,1]{1,0:T(8,128)S(1)}, s32[48,1]{1,0:T(8,128)}, u32[]{:S(2)}) copy-start(s32[48,1]{1,0:T(8,128)} %copy.7.pick_ref) | copy-start | bytes 580
  104.6 7.7 %collective-permute-start.14 = (f32[4,112,256]{2,1,0:T(8,128)S(1)}, f32[4,112,256]{2,1,0:T(8,128)S(1)}, u32[]{:S(2)}, u32[]{:S(2)}) collective-permute-start(f32[4,112,256]{2,1,0:T(8,128)S(1)} %get-tuple-element.34), channel_id=1, source_target_pairs={{0,4},{1,3},{2,6},{3,1},{4,0},{5,7},{6,2},{7,5},{8,12},{9,11},{10,... | collective-permute-start | bytes 1376264 | tf_op jit(solution)/shard_map/ppermute | solution.py:374
  105.9 13.8 %collective-permute-start.6 = (f32[4,112,384]{2,1,0:T(8,128)S(1)}, f32[4,112,384]{2,1,0:T(8,128)S(1)}, u32[]{:S(2)}, u32[]{:S(2)}) collective-permute-start(f32[4,112,384]{2,1,0:T(8,128)S(1)} %get-tuple-element.28), channel_id=1, source_target_pairs={{0,4},{1,3},{2,6},{3,1},{4,0},{5,7},{6,2},{7,5},{8,12},{9,11},{10,... | collective-permute-start | bytes 2064392 | tf_op jit(solution)/shard_map/ppermute | solution.py:374
  112.3 17.8 %collective-permute-start.17 = (f32[112,256]{1,0:T(8,128)S(1)}, f32[112,256]{1,0:T(8,128)S(1)}, u32[]{:S(2)}, u32[]{:S(2)}) collective-permute-start(f32[112,256]{1,0:T(8,128)S(1)} %get-tuple-element.37), channel_id=1, source_target_pairs={{0,9},{1,8},{2,11},{3,10},{4,13},{5,12},{6,15},{7,14},{8,1},{9,0},... | collective-permute-start | bytes 344072 | tf_op jit(solution)/shard_map/ppermute | solution.py:374
  117.9 12.8 %collective-permute-start.16 = (f32[112,256]{1,0:T(8,128)S(1)}, f32[112,256]{1,0:T(8,128)S(1)}, u32[]{:S(2)}, u32[]{:S(2)}) collective-permute-start(f32[112,256]{1,0:T(8,128)S(1)} %get-tuple-element.38), channel_id=1, source_target_pairs={{0,8},{1,9},{2,10},{3,11},{4,12},{5,13},{6,14},{7,15},{8,0},{9,1},... | collective-permute-start | bytes 344072 | tf_op jit(solution)/shard_map/ppermute | solution.py:374
  119.7 21.5 %collective-permute-start.9 = (f32[112,384]{1,0:T(8,128)S(1)}, f32[112,384]{1,0:T(8,128)S(1)}, u32[]{:S(2)}, u32[]{:S(2)}) collective-permute-start(f32[112,384]{1,0:T(8,128)S(1)} %get-tuple-element.35), channel_id=1, source_target_pairs={{0,9},{1,8},{2,11},{3,10},{4,13},{5,12},{6,15},{7,14},{8,1},{9,0},... | collective-permute-start | bytes 516104 | tf_op jit(solution)/shard_map/ppermute | solution.py:374
  129.1 15.8 %collective-permute-start.8 = (f32[112,384]{1,0:T(8,128)S(1)}, f32[112,384]{1,0:T(8,128)S(1)}, u32[]{:S(2)}, u32[]{:S(2)}) collective-permute-start(f32[112,384]{1,0:T(8,128)S(1)} %get-tuple-element.36), channel_id=1, source_target_pairs={{0,8},{1,9},{2,10},{3,11},{4,12},{5,13},{6,14},{7,15},{8,0},{9,1},... | collective-permute-start | bytes 516104 | tf_op jit(solution)/shard_map/ppermute | solution.py:374
  130.0 14.9 %collective-permute-start.7 = (f32[112,384]{1,0:T(8,128)S(1)}, f32[112,384]{1,0:T(8,128)S(1)}, u32[]{:S(2)}, u32[]{:S(2)}) collective-permute-start(f32[112,384]{1,0:T(8,128)S(1)} %get-tuple-element.39), channel_id=1, source_target_pairs={{0,1},{1,0},{2,3},{3,2},{4,5},{5,4},{6,7},{7,6},{8,9},{9,8},{10,11... | collective-permute-start | bytes 516104 | tf_op jit(solution)/shard_map/ppermute | solution.py:374
  130.1 1.5 %collective-permute-start.15 = (f32[112,256]{1,0:T(8,128)S(1)}, f32[112,256]{1,0:T(8,128)S(1)}, u32[]{:S(2)}, u32[]{:S(2)}) collective-permute-start(f32[112,256]{1,0:T(8,128)S(1)} %get-tuple-element.41), channel_id=1, source_target_pairs={{0,1},{1,0},{2,3},{3,2},{4,5},{5,4},{6,7},{7,6},{8,9},{9,8},{10,11... | collective-permute-start | bytes 344072 | tf_op jit(solution)/shard_map/ppermute | solution.py:374
  (13 other events, 39.7 us)

commit v3 on v2

v3 whole, which is shorter than its diff:
```python
import functools

import jax
import jax.numpy as jnp
from jax import lax
from jax.experimental import pallas as pl
from jax.experimental.pallas import tpu as pltpu
from jax.sharding import PartitionSpec as P

LANES = 128


def round_up(value, multiple):
    return -(-value // multiple) * multiple


def pick_bits(value, bits):
    result = 0
    for place, bit in enumerate(bits):
        result = result + ((value >> bit) & 1) * (1 << place)
    return result


def spread_bits(value, bits):
    result = 0
    for place, bit in enumerate(bits):
        result += ((value >> place) & 1) << bit
    return result


class Plan:
    def __init__(self, n, block):
        self.n = n
        self.block = block
        self.tiles = round_up(block, LANES) // LANES
        self.share = (self.tiles + 1) // 2
        self.high_bits = list(range(3, n.bit_length() - 1))
        first = (3 * self.share + 4) // 5
        self.chunks = [(0, first)]
        if self.share > first:
            self.chunks.append((first, self.share - first))

    def width(self, chunk):
        return self.chunks[chunk][1] * LANES

    def ring(self, side, chunk):
        start, count = self.chunks[chunk]
        low = side * self.share + start
        return range(low, min(low + count, self.tiles if side else self.share))

    def folded(self, owner):
        first = owner * self.block // LANES
        return (owner * self.block + self.block - 1) // LANES - first == self.tiles

    def place_bits(self, side):
        return [2 - side] + self.high_bits + [0]

    def by_rows(self):
        return [(d, d ^ (2 + 2 * (d & 1))) for d in range(self.n)]

    def by_sums(self):
        return [(d, d ^ (4 - 2 * (d & 1))) for d in range(self.n)]

    def by_mask(self, mask):
        return [(d, d ^ mask) for d in range(self.n)]


def pack_kernel(plan, group, x_ref, *refs):
    count = len(plan.chunks)
    outs, buffers, sems = refs[:4 * count], refs[4 * count:5 * count], refs[-1]
    step = pl.program_id(0)
    me = lax.axis_index("pat")
    rows = x_ref.shape[0]
    for i in range(group):
        first = i * plan.block // LANES
        edge = i * plan.block % LANES
        owner = step * group + i
        for chunk, buffer in enumerate(buffers):
            for side in range(2):
                places = plan.ring(side, chunk)
                for slot, place in enumerate(places):
                    here = slice(slot * LANES, (slot + 1) * LANES)
                    tile = slice((first + place) * LANES, (first + place + 1) * LANES)
                    if place == 0 and plan.folded(i):
                        last = slice((first + plan.tiles) * LANES, (first + plan.tiles + 1) * LANES)
                        lane = lax.broadcasted_iota(jnp.int32, (rows, LANES), 1)
                        head = x_ref[:, tile].astype(jnp.float32)
                        tail = x_ref[:, last].astype(jnp.float32)
                        buffer[side, owner, :, here] = jnp.where(lane >= edge, head, tail).astype(
                            buffer.dtype
                        )
                    else:
                        buffer[side, owner, :, here] = x_ref[:, tile]
                for slot in range(len(places), plan.chunks[chunk][1]):
                    here = slice(slot * LANES, (slot + 1) * LANES)
                    buffer[side, owner, :, here] = jnp.zeros((rows, LANES), buffer.dtype)
                away = (me & 1) ^ side
                relative = owner ^ me ^ away
                target = 2 * away + ((relative >> (1 + side)) & 1)
                place = pick_bits(relative, plan.place_bits(side))
                for t in range(4):

                    @pl.when(target == t)
                    def _():
                        pltpu.make_async_copy(
                            buffer.at[side, owner],
                            outs[4 * chunk + t].at[pl.ds(pl.multiple_of(place * rows, rows), rows)],
                            sems.at[chunk, side, owner],
                        ).start()

    @pl.when(step == pl.num_programs(0) - 1)
    def _():
        for chunk, buffer in enumerate(buffers):
            for side in range(2):
                for owner in range(plan.n):
                    pltpu.make_async_copy(
                        buffer.at[side, owner],
                        outs[4 * chunk].at[pl.ds(0, rows)],
                        sems.at[chunk, side, owner],
                    ).wait()


def pack(covariates, plan):
    rows = covariates.shape[0]
    group = 4
    while group < plan.n and (group * plan.block) % LANES:
        group *= 2
    chunks = range(len(plan.chunks))
    outs = pl.pallas_call(
        functools.partial(pack_kernel, plan, group),
        grid=(plan.n // group,),
        in_specs=[pl.BlockSpec((rows, group * plan.block), lambda s: (0, s))],
        out_specs=[pl.BlockSpec(memory_space=pl.ANY)] * (4 * len(plan.chunks)),
        out_shape=[
            jax.ShapeDtypeStruct((plan.n // 2 * rows, plan.width(chunk)), covariates.dtype)
            for chunk in chunks
            for _ in range(4)
        ],
        scratch_shapes=[
            pltpu.VMEM((2, plan.n, rows, plan.width(chunk)), covariates.dtype) for chunk in chunks
        ]
        + [pltpu.SemaphoreType.DMA((len(plan.chunks), 2, plan.n))],
        compiler_params=pltpu.CompilerParams(vmem_limit_bytes=12 << 20),
        cost_estimate=pl.CostEstimate(
            flops=0, bytes_accessed=4 * covariates.size, transcendentals=0
        ),
        name="pack",
    )(covariates)
    return [outs[4 * chunk:4 * chunk + 4] for chunk in chunks]


def onehot_of(pick_ref, weightings, dtype):
    index = lax.broadcasted_iota(jnp.int32, (pick_ref.shape[0], weightings), 1)
    return jnp.where(index == pick_ref[...], 1.0, 0.0).astype(dtype)


def arm_columns(panel_ref, onehot):
    comps, weightings = onehot.shape
    weights = panel_ref[0:weightings, :]
    arms = panel_ref[weightings:weightings + comps, :].astype(jnp.float32)
    picked = jnp.dot(onehot, weights, preferred_element_type=jnp.float32)
    return weights, picked * arms, picked * (1.0 - arms)


def small_call(kernel, shapes, operands, after, name):
    vmem = pl.BlockSpec(memory_space=pltpu.VMEM)
    return pl.pallas_call(
        kernel,
        in_specs=[vmem] * len(operands) + [pl.BlockSpec(memory_space=pl.ANY)] * len(after),
        out_specs=[vmem] * len(shapes),
        out_shape=[jax.ShapeDtypeStruct(shape, dtype) for shape, dtype in shapes],
        compiler_params=pltpu.CompilerParams(vmem_limit_bytes=4 << 20),
        cost_estimate=pl.CostEstimate(flops=0, bytes_accessed=1 << 18, transcendentals=0),
        name=name,
    )(*operands, *after)


def totals_kernel(weightings, count, pick_ref, *refs):
    out_ref = refs[-1]
    onehot = onehot_of(pick_ref, weightings, jnp.bfloat16)
    target_sum, other_sum = 0.0, 0.0
    for ref in refs[:count]:
        _, target, other = arm_columns(ref, onehot)
        target_sum += target
        other_sum += other
    lane = lax.broadcasted_iota(jnp.int32, out_ref.shape, 1)
    out_ref[...] = jnp.where(
        lane == 0,
        jnp.sum(target_sum, axis=1, keepdims=True),
        jnp.sum(other_sum, axis=1, keepdims=True),
    )


def group_totals(members, pick_column, weightings, after):
    return small_call(
        functools.partial(totals_kernel, weightings, len(members)),
        [((pick_column.shape[0], LANES), jnp.float32)],
        [pick_column, *members],
        after,
        "totals",
    )[0]


def panel_kernel(weightings, pick_ref, near_ref, far_ref, *refs):
    member_refs, (first_ref, second_ref, stats_ref) = refs[:-3], refs[-3:]
    comps = pick_ref.shape[0]
    onehot = onehot_of(pick_ref, weightings, jnp.bfloat16)
    totals = near_ref[...] + far_ref[...]
    total_target, total_other = totals[:, 0:1], totals[:, 1:2]
    light = jnp.where(total_target <= total_other, 1.0, 0.0)
    stats_ref[0] = jnp.broadcast_to(1.0 / total_target, (comps, LANES))
    stats_ref[1] = jnp.broadcast_to(1.0 / total_other, (comps, LANES))
    stats_ref[2] = jnp.broadcast_to(light, (comps, LANES))
    for place, ref in enumerate(member_refs):
        weights, target, other = arm_columns(ref, onehot)
        lighter = light * target + (1.0 - light) * other
        here = slice(place * LANES, (place + 1) * LANES)
        first_ref[0:comps, here] = lighter.astype(jnp.bfloat16)
        first_ref[comps:comps + weightings, here] = weights
        second_ref[0:comps, here] = target.astype(jnp.bfloat16)
        second_ref[comps:2 * comps, here] = other.astype(jnp.bfloat16)


def make_panels(members, near, far, pick_column, weightings):
    comps = pick_column.shape[0]
    return small_call(
        functools.partial(panel_kernel, weightings),
        [
            ((comps + weightings, len(members) * LANES), jnp.bfloat16),
            ((2 * comps, len(members) * LANES), jnp.bfloat16),
            ((3, comps, LANES), jnp.float32),
        ],
        [pick_column, near, far, *members],
        [],
        "panels",
    )


def whole_spec(shape):
    return pl.BlockSpec(shape, lambda s: (0,) * len(shape))


def moments_kernel(rows, x_count, *refs):
    xs = refs[:x_count]
    first_ref, second_ref, stats_ref = refs[x_count:x_count + 3]
    outs = refs[-2:]
    first_rows = first_ref.shape[0]
    comps = second_ref.shape[0] // 2
    inverse_target = stats_ref[0][:, 0:1]
    inverse_other = stats_ref[1][:, 0:1]
    for place, out_ref in enumerate(outs):
        x = jnp.concatenate([ref[place * rows:(place + 1) * rows, :] for ref in xs], axis=0)
        first = jnp.dot(first_ref[...], x, preferred_element_type=jnp.float32)
        squares = (x.astype(jnp.float32) * x.astype(jnp.float32)).astype(jnp.bfloat16)
        second = jnp.dot(second_ref[...], squares, preferred_element_type=jnp.float32)
        out_ref[0, 0:first_rows, :] = first
        out_ref[0, first_rows:first_rows + comps, :] = (
            second[0:comps] * inverse_target + second[comps:2 * comps] * inverse_other
        )


def moments(xs, first, second, stats, places, after):
    rows = first.shape[1] // len(xs)
    width = xs[0].shape[1]
    comps = second.shape[0] // 2
    out_rows = first.shape[0] + comps
    return pl.pallas_call(
        functools.partial(moments_kernel, rows, len(xs)),
        grid=(places // 2,),
        in_specs=[pl.BlockSpec((2 * rows, width), lambda s: (s, 0))] * len(xs)
        + [whole_spec(array.shape) for array in (first, second, stats)]
        + [pl.BlockSpec(memory_space=pl.ANY)] * len(after),
        out_specs=[pl.BlockSpec((1, out_rows, width), lambda s: (s, 0, 0))] * 2,
        out_shape=[jax.ShapeDtypeStruct((places // 2, out_rows, width), jnp.float32)] * 2,
        compiler_params=pltpu.CompilerParams(vmem_limit_bytes=12 << 20),
        cost_estimate=pl.CostEstimate(
            flops=2 * places * len(xs) * rows * width * (first.shape[0] + second.shape[0]),
            bytes_accessed=places * width * (2 * len(xs) * rows + 4 * out_rows),
            transcendentals=0,
        ),
        name="moments",
    )(*xs, first, second, stats, *after)


def finish_kernel(plan, weightings, pick_ref, stats_ref, *refs):
    out_ref, ring_ref = refs[-2:]
    per_chunk = (len(refs) - 2) // len(plan.chunks)
    comps = pick_ref.shape[0]
    onehot = onehot_of(pick_ref, weightings, jnp.float32)
    inverse_target = stats_ref[0][:, 0:1]
    inverse_other = stats_ref[1][:, 0:1]
    light = stats_ref[2][:, 0:1] > 0.5
    me = lax.axis_index("pat")
    my_side = me & 1
    for chunk in range(len(plan.chunks)):
        arrays = refs[chunk * per_chunk:(chunk + 1) * per_chunk]
        for away in range(2):
            sums = arrays[away][...]
            for more in arrays[2 + away::2]:
                sums += more[...]
            lighter = sums[0:comps]
            both = jnp.dot(
                onehot,
                sums[comps:comps + weightings],
                precision=lax.Precision.HIGHEST,
                preferred_element_type=jnp.float32,
            )
            spread = sums[comps + weightings:2 * comps + weightings]
            heavier = both - lighter
            mean_target = jnp.where(light, lighter, heavier) * inverse_target
            mean_other = jnp.where(light, heavier, lighter) * inverse_other
            variance = spread - mean_target * mean_target - mean_other * mean_other
            pooled = jnp.maximum(variance / 2.0, 0.01)
            balance = (mean_target - mean_other) / jnp.sqrt(pooled)
            for side in range(2):
                places = plan.ring(side, chunk)
                if places:
                    lanes = slice(places[0] * LANES, places[-1] * LANES + LANES)

                    @pl.when(my_side ^ away == side)
                    def _():
                        ring_ref[:, lanes] = balance[:, 0:len(places) * LANES]
    width = plan.tiles * LANES
    shift = width - lax.rem(me * plan.block, LANES)
    out_ref[:, 0, :] = pltpu.roll(ring_ref[...], shift, 1)[:, 0:plan.block]


def finish(plan, parts, pick_column, stats, weightings):
    comps = pick_column.shape[0]
    operands = [array for part in parts for array in part]
    return pl.pallas_call(
        functools.partial(finish_kernel, plan, weightings),
        in_specs=[pl.BlockSpec(memory_space=pltpu.VMEM)] * (2 + len(operands)),
        out_specs=pl.BlockSpec(memory_space=pltpu.VMEM),
        out_shape=jax.ShapeDtypeStruct((comps, 1, plan.block), jnp.float32),
        scratch_shapes=[pltpu.VMEM((comps, plan.tiles * LANES), jnp.float32)],
        compiler_params=pltpu.CompilerParams(vmem_limit_bytes=12 << 20),
        cost_estimate=pl.CostEstimate(
            flops=20 * comps * plan.block,
            bytes_accessed=4 * sum(operand.size for operand in operands),
            transcendentals=comps * plan.block,
        ),
        name="finish",
    )(pick_column, stats, *operands)


def swap(array, pairs):
    return lax.ppermute(array, "pat", pairs)


def on_device(n, covs, covariates, weights, arms, pick):
    weightings = weights.shape[1]
    pick_column = pick.reshape(pick.shape[0], 1)
    plan = Plan(n, covariates.shape[1] // n)
    to_other_side = plan.by_mask(1)

    arm_rows = arms.T.astype(weights.dtype)
    if covs > 1:
        arm_rows = lax.all_gather(arm_rows, "cov", axis=0, tiled=True)
    mine = jnp.concatenate([weights.T, arm_rows], axis=0)
    across = [(pair ^ 1, d) for d, pair in plan.by_rows()]
    members = [mine] + [swap(mine, pairs) for pairs in (to_other_side, plan.by_rows(), across)]

    rows = []
    for kept, sent, other_kept, other_sent in pack(covariates, plan):
        passed = swap(other_sent, to_other_side)
        arrived = swap(sent, plan.by_rows())
        rows.append([kept, swap(other_kept, to_other_side), arrived, swap(passed, plan.by_rows())])

    near = group_totals(members, pick_column, weightings, [rows[0][2]])
    far = swap(near, plan.by_sums())
    for bit in plan.high_bits:
        near = near + far
        far = swap(near, plan.by_mask(1 << bit))
    first, second, stats = make_panels(members, near, far, pick_column, weightings)

    parts, after = [], []
    for chunk in range(len(plan.chunks)):
        kept, sent = moments(rows[chunk], first, second, stats, n // 2, after)
        after = [kept]
        arrived = swap(sent, plan.by_sums())
        for bit in plan.high_bits[:-1]:
            sent = kept[1::2] + arrived[1::2]
            kept = kept[0::2] + arrived[0::2]
            arrived = swap(sent, plan.by_mask(1 << bit))
        part = []
        for bit in plan.high_bits[-1:]:
            last = plan.by_mask(1 << bit)
            last_other = plan.by_mask((1 << bit) | 1)
            part = [
                swap(kept[1] + arrived[1], last),
                swap(kept[3] + arrived[3], last_other),
            ]
            kept, arrived = kept[0::2], arrived[0::2]
        part = [kept[0] + arrived[0], swap(kept[1] + arrived[1], to_other_side)] + part
        parts.append(part)
    return finish(plan, parts, pick_column, stats, weightings)


def solution(mesh):
    placed = (
        P(("groups", "pat"), "cov"),
        P(("groups", "pat"), None),
        P(("groups", "pat"), "cov"),
        P(),
    )
    body = functools.partial(on_device, mesh.shape["pat"], mesh.shape["cov"])
    return jax.shard_map(
        body, mesh=mesh, in_specs=placed, out_specs=P("groups", "cov", "pat"), check_vma=False
    )
```

time: 148 us -> 97.7 us (0.66)
  Pallas kernels: 66.4 us -> 12.5 us
  waiting for transfers between devices: 33.2 us -> 50.7 us
  local copies, waits for them, and re-layouts: 11.1 us -> 6.05 us
  starting transfers between devices: 33 us -> 28.1 us
  other arithmetic: 2.93 us -> 0.17 us
    pallas_call x4 -> x3, Pallas kernels: 58.3 us -> 7.58 us  [the longest x1 7.06 us: pack(): pl.pallas_call(functools.partial(pack_kernel, plan, group), grid=(plan.n...]
    ppermute x18 -> x21, waiting for transfers between devices: 33.2 us -> 50.7 us  [swap(): return lax.ppermute(array, 'pat', pairs)]
    ppermute x18 -> x21, starting transfers between devices: 33 us -> 28.1 us  [swap(): return lax.ppermute(array, 'pat', pairs)]
    unnamed x38 -> x16, local copies, waits for them, and re-layouts: 10.3 us -> 5.88 us
    pallas_call x2, Pallas kernels: 6.19 us -> 2.92 us  [moments(): pl.pallas_call(functools.partial(moments_kernel, rows, len(xs)), grid=(pl...]
  transfers between devices with their start and end apart: 18 -> 21, of which waited for: 8 -> 11; matrix products, arithmetic and copies ran while one was open for 2% -> 0% of each run, Pallas kernels for 27% -> 2%
where the time goes in v3:
time: 97.7 us; the launch traced here: 97.5 us
  waiting for transfers between devices  50.7 us (52%)
  starting transfers between devices  28.1 us (29%)
  Pallas kernels  12.5 us (13%)
  local copies, waits for them, and re-layouts  6.05 us (6%)
    ppermute x21, waiting for transfers between devices, swap(): return lax.ppermute(array, 'pat', pairs)  50.7 us
    ppermute x21, starting transfers between devices, swap(): return lax.ppermute(array, 'pat', pairs)  28.1 us
    pallas_call x1, Pallas kernels, pack(): pl.pallas_call(functools.partial(pack_kernel, plan, group), grid=(plan.n...  7.06 us
    unnamed x16, local copies, waits for them, and re-layouts  5.88 us
    pallas_call x2, Pallas kernels, moments(): pl.pallas_call(functools.partial(moments_kernel, rows, len(xs)), grid=(pl...  2.92 us
    pallas_call x1, Pallas kernels, finish(): pl.pallas_call(functools.partial(finish_kernel, plan, weightings), in_spe...  1.96 us
  transfers between devices with their start and end apart: 21, of which 11 were waited for; matrix products, arithmetic and copies ran while one was open for 0% of the time, Pallas kernels for 2%

profile of v3, /device:TPU:1, one launch (start us, length us, event | category | flops | bytes accessed | tf_op | source)
XLA Modules:
  0.0 97.5 jit_solution(12300819931438625439)
XLA Ops:
  0.0 2.4 %copy-done = bf16[128,19968]{1,0:T(8,128)(2,1)S(1)} copy-done((bf16[128,19968]{1,0:T(8,128)(2,1)S(1)}, bf16[128,19968]{1,0:T(8,128)(2,1)}, u32[]{:S(2)}) %copy-start) | copy-done | bytes 5111832
  2.5 7.1 %pack.1 = (bf16[1024,384]{1,0:T(8,128)(2,1)S(1)}, bf16[1024,384]{1,0:T(8,128)(2,1)}, bf16[1024,384]{1,0:T(8,128)(2,1)}, bf16[1024,384]{1,0:T(8,128)(2,1)S(1)}, b...) custom-call(bf16[128,19968]{1,0:T(8,128)(2,1)S(1)} %copy-done), custom_call_target="tpu_custom_call" | custom-call | bytes 10223616 | tf_op jit(solution)/shard_map/pack/pallas_call | solution.py:129
  12.0 2.6 %collective-permute-start.3 = (bf16[1024,384]{1,0:T(8,128)(2,1)}, bf16[1024,384]{1,0:T(8,128)(2,1)S(1)}, u32[]{:S(2)}, u32[]{:S(2)}) collective-permute-start(bf16[1024,384]{1,0:T(8,128)(2,1)} %get-tuple-element.20), channel_id=1, source_target_pairs={{0,2},{1,5},{2,0},{3,7},{4,6},{5,1},{6,4},{7,3},{8,10},{9,13},{10,... | collective-permute-start | bytes 2359304 | tf_op jit(solution)/shard_map/ppermute | solution.py:348
  15.2 1.5 %collective-permute-start.8 = (bf16[1024,384]{1,0:T(8,128)(2,1)}, bf16[1024,384]{1,0:T(8,128)(2,1)S(1)}, u32[]{:S(2)}, u32[]{:S(2)}) collective-permute-start(bf16[1024,384]{1,0:T(8,128)(2,1)} %collective-permute-done.7), channel_id=1, source_target_pairs={{0,2},{1,5},{2,0},{3,7},{4,6},{5,1},{6,4},{7,3},{8,10},{9,13},{10,... | collective-permute-start | bytes 2359304 | tf_op jit(solution)/shard_map/ppermute | solution.py:348
  17.2 3.3 %collective-permute-done.2.refs_3_ = bf16[64,128]{1,0:T(8,128)(2,1)S(1)} collective-permute-done((bf16[64,128]{1,0:T(8,128)(2,1)S(1)}, bf16[64,128]{1,0:T(8,128)(2,1)S(1)}, u32[]{:S(2)}, u32[]{:S(2)}) %collective-permute-start.2) | collective-permute-done | bytes 16416 | tf_op jit(solution)/shard_map/ppermute | solution.py:348
  20.8 12.5 %collective-permute-done.1.refs_2_ = bf16[64,128]{1,0:T(8,128)(2,1)S(1)} collective-permute-done((bf16[64,128]{1,0:T(8,128)(2,1)S(1)}, bf16[64,128]{1,0:T(8,128)(2,1)S(1)}, u32[]{:S(2)}, u32[]{:S(2)}) %collective-permute-start.1) | collective-permute-done | bytes 16416 | tf_op jit(solution)/shard_map/ppermute | solution.py:348
  35.1 1.8 %collective-permute-start.4 = (f32[48,128]{1,0:T(8,128)S(1)}, f32[48,128]{1,0:T(8,128)S(1)}, u32[]{:S(2)}, u32[]{:S(2)}) collective-permute-start(f32[48,128]{1,0:T(8,128)S(1)} %totals.1), channel_id=1, source_target_pairs={{0,4},{1,3},{2,6},{3,1},{4,0},{5,7},{6,2},{7,5},{8,12},{9,11},{10,... | collective-permute-start | bytes 73736 | tf_op jit(solution)/shard_map/ppermute | solution.py:348
  36.9 1.2 %collective-permute-done.4 = f32[48,128]{1,0:T(8,128)S(1)} collective-permute-done((f32[48,128]{1,0:T(8,128)S(1)}, f32[48,128]{1,0:T(8,128)S(1)}, u32[]{:S(2)}, u32[]{:S(2)}) %collective-permute-start.4) | collective-permute-done | bytes 24608 | tf_op jit(solution)/shard_map/ppermute | solution.py:348
  38.1 2.5 %collective-permute-start.5 = (f32[48,128]{1,0:T(8,128)S(1)}, f32[48,128]{1,0:T(8,128)S(1)}, u32[]{:S(2)}, u32[]{:S(2)}) collective-permute-start(f32[48,128]{1,0:T(8,128)S(1)} %add.49.near_ref), channel_id=1, source_target_pairs={{0,8},{1,9},{2,10},{3,11},{4,12},{5,13},{6,14},{7,15},{8,0},{9,1},... | collective-permute-start | bytes 73736 | tf_op jit(solution)/shard_map/ppermute | solution.py:348
  40.7 1.8 %collective-permute-start.13 = (bf16[1024,256]{1,0:T(8,128)(2,1)}, bf16[1024,256]{1,0:T(8,128)(2,1)S(1)}, u32[]{:S(2)}, u32[]{:S(2)}) collective-permute-start(bf16[1024,256]{1,0:T(8,128)(2,1)} %copy-done.4), channel_id=1, source_target_pairs={{0,1},{1,0},{2,3},{3,2},{4,5},{5,4},{6,7},{7,6},{8,9},{9,8},{10,11... | collective-permute-start | bytes 1572872 | tf_op jit(solution)/shard_map/ppermute | solution.py:348
  44.2 1.7 %moments.2 = (f32[4,112,384]{2,1,0:T(8,128)S(1)}, f32[4,112,384]{2,1,0:T(8,128)S(1)}) custom-call(bf16[1024,384]{1,0:T(8,128)(2,1)S(1)} %get-tuple-element.22.refs_0_, bf16[1024,384]{1,0:T(8,128)(2,1)S(1)} %collective-permute-done.6.refs_1_, bf16[1024,384]{1,0:T(8,128)(2,1)S(1)} %collective-permute-done.3.refs_4_.refs_2_, ...), custom_call_target="tpu_custom_call" | custom-call | flops 503316480 | bytes 4521984 | tf_op jit(solution)/shard_map/moments/pallas_call | solution.py:267
  45.8 5.1 %collective-permute-done.14.refs_2_ = bf16[1024,256]{1,0:T(8,128)(2,1)S(1)} collective-permute-done((bf16[1024,256]{1,0:T(8,128)(2,1)}, bf16[1024,256]{1,0:T(8,128)(2,1)S(1)}, u32[]{:S(2)}, u32[]{:S(2)}) %collective-permute-start.14) | collective-permute-done | bytes 524320 | tf_op jit(solution)/shard_map/ppermute | solution.py:348
  51.0 5.6 %collective-permute-done.16.refs_3_ = bf16[1024,256]{1,0:T(8,128)(2,1)S(1)} collective-permute-done((bf16[1024,256]{1,0:T(8,128)(2,1)}, bf16[1024,256]{1,0:T(8,128)(2,1)S(1)}, u32[]{:S(2)}, u32[]{:S(2)}) %collective-permute-start.16) | collective-permute-done | bytes 524320 | tf_op jit(solution)/shard_map/ppermute | solution.py:348
  57.6 1.3 %moments.3 = (f32[4,112,256]{2,1,0:T(8,128)S(1)}, f32[4,112,256]{2,1,0:T(8,128)S(1)}) custom-call(bf16[1024,256]{1,0:T(8,128)(2,1)S(1)} %copy-done.2, bf16[1024,256]{1,0:T(8,128)(2,1)S(1)} %collective-permute-done.13.refs_1_, bf16[1024,256]{1,0:T(8,128)(2,1)S(1)} %collective-permute-done.14.refs_2_, bf16[1024,256]{1,0:T(8,128)(2,1)S(1)} %collective-permute-done.16.refs_3_, ...), custom_call_target="tpu_custom_call" | custom-call | flops 335544320 | bytes 3014656 | tf_op jit(solution)/shard_map/moments/pallas_call | solution.py:267
  58.9 1.3 %collective-permute-start.17 = (f32[4,112,256]{2,1,0:T(8,128)S(1)}, f32[4,112,256]{2,1,0:T(8,128)S(1)}, u32[]{:S(2)}, u32[]{:S(2)}) collective-permute-start(f32[4,112,256]{2,1,0:T(8,128)S(1)} %get-tuple-element.34), channel_id=1, source_target_pairs={{0,4},{1,3},{2,6},{3,1},{4,0},{5,7},{6,2},{7,5},{8,12},{9,11},{10,... | collective-permute-start | bytes 1376264 | tf_op jit(solution)/shard_map/ppermute | solution.py:348
  60.5 6.1 %collective-permute-done.17 = f32[4,112,256]{2,1,0:T(8,128)S(1)} collective-permute-done((f32[4,112,256]{2,1,0:T(8,128)S(1)}, f32[4,112,256]{2,1,0:T(8,128)S(1)}, u32[]{:S(2)}, u32[]{:S(2)}) %collective-permute-start.17) | collective-permute-done | bytes 458784 | tf_op jit(solution)/shard_map/ppermute | solution.py:348
  66.6 1.5 %collective-permute-start.20 = (f32[112,256]{1,0:T(8,128)S(1)}, f32[112,256]{1,0:T(8,128)S(1)}, u32[]{:S(2)}, u32[]{:S(2)}) collective-permute-start(f32[112,256]{1,0:T(8,128)S(1)} %get-tuple-element.37), channel_id=1, source_target_pairs={{0,9},{1,8},{2,11},{3,10},{4,13},{5,12},{6,15},{7,14},{8,1},{9,0},... | collective-permute-start | bytes 344072 | tf_op jit(solution)/shard_map/ppermute | solution.py:348
  68.2 2.5 %collective-permute-start.19 = (f32[112,256]{1,0:T(8,128)S(1)}, f32[112,256]{1,0:T(8,128)S(1)}, u32[]{:S(2)}, u32[]{:S(2)}) collective-permute-start(f32[112,256]{1,0:T(8,128)S(1)} %get-tuple-element.38), channel_id=1, source_target_pairs={{0,8},{1,9},{2,10},{3,11},{4,12},{5,13},{6,14},{7,15},{8,0},{9,1},... | collective-permute-start | bytes 344072 | tf_op jit(solution)/shard_map/ppermute | solution.py:348
  70.7 3.3 %collective-permute-done.9 = f32[4,112,384]{2,1,0:T(8,128)S(1)} collective-permute-done((f32[4,112,384]{2,1,0:T(8,128)S(1)}, f32[4,112,384]{2,1,0:T(8,128)S(1)}, u32[]{:S(2)}, u32[]{:S(2)}) %collective-permute-start.9) | collective-permute-done | bytes 688160 | tf_op jit(solution)/shard_map/ppermute | solution.py:348
  74.0 5.6 %collective-permute-start.12 = (f32[112,384]{1,0:T(8,128)S(1)}, f32[112,384]{1,0:T(8,128)S(1)}, u32[]{:S(2)}, u32[]{:S(2)}) collective-permute-start(f32[112,384]{1,0:T(8,128)S(1)} %get-tuple-element.35), channel_id=1, source_target_pairs={{0,9},{1,8},{2,11},{3,10},{4,13},{5,12},{6,15},{7,14},{8,1},{9,0},... | collective-permute-start | bytes 516104 | tf_op jit(solution)/shard_map/ppermute | solution.py:348
  79.6 2.5 %collective-permute-start.11 = (f32[112,384]{1,0:T(8,128)S(1)}, f32[112,384]{1,0:T(8,128)S(1)}, u32[]{:S(2)}, u32[]{:S(2)}) collective-permute-start(f32[112,384]{1,0:T(8,128)S(1)} %get-tuple-element.36), channel_id=1, source_target_pairs={{0,8},{1,9},{2,10},{3,11},{4,12},{5,13},{6,14},{7,15},{8,0},{9,1},... | collective-permute-start | bytes 516104 | tf_op jit(solution)/shard_map/ppermute | solution.py:348
  83.8 6.8 %collective-permute-done.12.refs_3_ = f32[112,384]{1,0:T(8,128)S(1)} collective-permute-done((f32[112,384]{1,0:T(8,128)S(1)}, f32[112,384]{1,0:T(8,128)S(1)}, u32[]{:S(2)}, u32[]{:S(2)}) %collective-permute-start.12) | collective-permute-done | bytes 172064 | tf_op jit(solution)/shard_map/ppermute | solution.py:348
  90.6 5.0 %collective-permute-done.11.refs_2_ = f32[112,384]{1,0:T(8,128)S(1)} collective-permute-done((f32[112,384]{1,0:T(8,128)S(1)}, f32[112,384]{1,0:T(8,128)S(1)}, u32[]{:S(2)}, u32[]{:S(2)}) %collective-permute-start.11) | collective-permute-done | bytes 172064 | tf_op jit(solution)/shard_map/ppermute | solution.py:348
  95.6 2.0 %finish.1 = f32[48,1,1248]{2,1,0:T(1,128)} custom-call(s32[48,1]{1,0:T(8,128)S(1)} %copy.7.pick_ref, f32[3,48,128]{2,1,0:T(8,128)S(1)} %get-tuple-element.21.refs_6_.stats_ref, f32[112,384]{1,0:T(8,128)S(1)} %get-tuple-element.40.refs_0_, f32[112,384]{1,0:T(8,128)S(1)} %collective-permute-done.10.refs_1_, f32[112,384]{1,0:T(8,128)S(1)} %collective-permute-done.11.refs_2_, ...), custom_call_target="tpu_custom_call" | custom-call | flops 1198080 | bytes 1146880 | tf_op jit(solution)/shard_map/finish/pallas_call | solution.py:331
  (52 shorter events, 10.4 us)
Async XLA Ops:
  2.5 14.2 %copy-start.5 = (s32[128,48]{0,1:T(8,128)S(1)}, s32[128,48]{0,1:T(8,128)}, u32[]{:S(2)}) copy-start(s32[128,48]{0,1:T(8,128)} %param.6) | copy-start | bytes 73732
  2.5 14.2 %copy-start.6 = (bf16[128,16]{0,1:T(8,128)(2,1)S(1)}, bf16[128,16]{0,1:T(8,128)(2,1)}, u32[]{:S(2)}) copy-start(bf16[128,16]{0,1:T(8,128)(2,1)} %param.5) | copy-start | bytes 12292
  2.5 31.5 %copy-start.7 = (s32[48]{0:T(128)S(1)}, s32[48]{0:T(128)}, u32[]{:S(2)}) copy-start(s32[48]{0:T(128)} %param.7) | copy-start | bytes 580
  11.9 3.2 %collective-permute-start.7 = (bf16[1024,384]{1,0:T(8,128)(2,1)S(1)}, bf16[1024,384]{1,0:T(8,128)(2,1)}, u32[]{:S(2)}, u32[]{:S(2)}) collective-permute-start(bf16[1024,384]{1,0:T(8,128)(2,1)S(1)} %get-tuple-element.24), channel_id=1, source_target_pairs={{0,1},{1,0},{2,3},{3,2},{4,5},{5,4},{6,7},{7,6},{8,9},{9,8},{10,11... | collective-permute-start | bytes 2359304 | tf_op jit(solution)/shard_map/ppermute | solution.py:348
  12.0 22.8 %collective-permute-start.3 = (bf16[1024,384]{1,0:T(8,128)(2,1)}, bf16[1024,384]{1,0:T(8,128)(2,1)S(1)}, u32[]{:S(2)}, u32[]{:S(2)}) collective-permute-start(bf16[1024,384]{1,0:T(8,128)(2,1)} %get-tuple-element.20), channel_id=1, source_target_pairs={{0,2},{1,5},{2,0},{3,7},{4,6},{5,1},{6,4},{7,3},{8,10},{9,13},{10,... | collective-permute-start | bytes 2359304 | tf_op jit(solution)/shard_map/ppermute | solution.py:348
  14.6 27.8 %collective-permute-start.15 = (bf16[1024,256]{1,0:T(8,128)(2,1)}, bf16[1024,256]{1,0:T(8,128)(2,1)}, u32[]{:S(2)}, u32[]{:S(2)}) collective-permute-start(bf16[1024,256]{1,0:T(8,128)(2,1)} %get-tuple-element.32), channel_id=1, source_target_pairs={{0,1},{1,0},{2,3},{3,2},{4,5},{5,4},{6,7},{7,6},{8,9},{9,8},{10,11... | collective-permute-start | bytes 1572872 | tf_op jit(solution)/shard_map/ppermute | solution.py:348
  15.0 29.2 %collective-permute-start.6 = (bf16[1024,384]{1,0:T(8,128)(2,1)}, bf16[1024,384]{1,0:T(8,128)(2,1)S(1)}, u32[]{:S(2)}, u32[]{:S(2)}) collective-permute-start(bf16[1024,384]{1,0:T(8,128)(2,1)} %get-tuple-element.23), channel_id=1, source_target_pairs={{0,1},{1,0},{2,3},{3,2},{4,5},{5,4},{6,7},{7,6},{8,9},{9,8},{10,11... | collective-permute-start | bytes 2359304 | tf_op jit(solution)/shard_map/ppermute | solution.py:348
  15.2 29.0 %collective-permute-start.8 = (bf16[1024,384]{1,0:T(8,128)(2,1)}, bf16[1024,384]{1,0:T(8,128)(2,1)S(1)}, u32[]{:S(2)}, u32[]{:S(2)}) collective-permute-start(bf16[1024,384]{1,0:T(8,128)(2,1)} %collective-permute-done.7), channel_id=1, source_target_pairs={{0,2},{1,5},{2,0},{3,7},{4,6},{5,1},{6,4},{7,3},{8,10},{9,13},{10,... | collective-permute-start | bytes 2359304 | tf_op jit(solution)/shard_map/ppermute | solution.py:348
  16.7 3.8 %collective-permute-start.2 = (bf16[64,128]{1,0:T(8,128)(2,1)S(1)}, bf16[64,128]{1,0:T(8,128)(2,1)S(1)}, u32[]{:S(2)}, u32[]{:S(2)}) collective-permute-start(bf16[64,128]{1,0:T(8,128)(2,1)S(1)} %pad_maximum_fusion.refs_0_), channel_id=1, source_target_pairs={{3,0},{4,1},{1,2},{6,3},{7,4},{0,5},{5,6},{2,7},{11,8},{12,9},{9,1... | collective-permute-start | bytes 49160 | tf_op jit(solution)/shard_map/ppermute | solution.py:348
  20.5 12.8 %collective-permute-start.1 = (bf16[64,128]{1,0:T(8,128)(2,1)S(1)}, bf16[64,128]{1,0:T(8,128)(2,1)S(1)}, u32[]{:S(2)}, u32[]{:S(2)}) collective-permute-start(bf16[64,128]{1,0:T(8,128)(2,1)S(1)} %pad_maximum_fusion.refs_0_), channel_id=1, source_target_pairs={{0,2},{1,5},{2,0},{3,7},{4,6},{5,1},{6,4},{7,3},{8,10},{9,13},{10,... | collective-permute-start | bytes 49160 | tf_op jit(solution)/shard_map/ppermute | solution.py:348
  33.3 1.5 %collective-permute-start = (bf16[64,128]{1,0:T(8,128)(2,1)S(1)}, bf16[64,128]{1,0:T(8,128)(2,1)S(1)}, u32[]{:S(2)}, u32[]{:S(2)}) collective-permute-start(bf16[64,128]{1,0:T(8,128)(2,1)S(1)} %pad_maximum_fusion.refs_0_), channel_id=1, source_target_pairs={{0,1},{1,0},{2,3},{3,2},{4,5},{5,4},{6,7},{7,6},{8,9},{9,8},{10,11... | collective-permute-start | bytes 49160 | tf_op jit(solution)/shard_map/ppermute | solution.py:348
  35.1 3.0 %collective-permute-start.4 = (f32[48,128]{1,0:T(8,128)S(1)}, f32[48,128]{1,0:T(8,128)S(1)}, u32[]{:S(2)}, u32[]{:S(2)}) collective-permute-start(f32[48,128]{1,0:T(8,128)S(1)} %totals.1), channel_id=1, source_target_pairs={{0,4},{1,3},{2,6},{3,1},{4,0},{5,7},{6,2},{7,5},{8,12},{9,11},{10,... | collective-permute-start | bytes 73736 | tf_op jit(solution)/shard_map/ppermute | solution.py:348
  38.1 5.5 %collective-permute-start.5 = (f32[48,128]{1,0:T(8,128)S(1)}, f32[48,128]{1,0:T(8,128)S(1)}, u32[]{:S(2)}, u32[]{:S(2)}) collective-permute-start(f32[48,128]{1,0:T(8,128)S(1)} %add.49.near_ref), channel_id=1, source_target_pairs={{0,8},{1,9},{2,10},{3,11},{4,12},{5,13},{6,14},{7,15},{8,0},{9,1},... | collective-permute-start | bytes 73736 | tf_op jit(solution)/shard_map/ppermute | solution.py:348
  40.7 5.2 %collective-permute-start.13 = (bf16[1024,256]{1,0:T(8,128)(2,1)}, bf16[1024,256]{1,0:T(8,128)(2,1)S(1)}, u32[]{:S(2)}, u32[]{:S(2)}) collective-permute-start(bf16[1024,256]{1,0:T(8,128)(2,1)} %copy-done.4), channel_id=1, source_target_pairs={{0,1},{1,0},{2,3},{3,2},{4,5},{5,4},{6,7},{7,6},{8,9},{9,8},{10,11... | collective-permute-start | bytes 1572872 | tf_op jit(solution)/shard_map/ppermute | solution.py:348
  42.4 8.5 %collective-permute-start.14 = (bf16[1024,256]{1,0:T(8,128)(2,1)}, bf16[1024,256]{1,0:T(8,128)(2,1)S(1)}, u32[]{:S(2)}, u32[]{:S(2)}) collective-permute-start(bf16[1024,256]{1,0:T(8,128)(2,1)} %copy-done.3), channel_id=1, source_target_pairs={{0,2},{1,5},{2,0},{3,7},{4,6},{5,1},{6,4},{7,3},{8,10},{9,13},{10,... | collective-permute-start | bytes 1572872 | tf_op jit(solution)/shard_map/ppermute | solution.py:348
  43.6 13.0 %collective-permute-start.16 = (bf16[1024,256]{1,0:T(8,128)(2,1)}, bf16[1024,256]{1,0:T(8,128)(2,1)S(1)}, u32[]{:S(2)}, u32[]{:S(2)}) collective-permute-start(bf16[1024,256]{1,0:T(8,128)(2,1)} %collective-permute-done.15), channel_id=1, source_target_pairs={{0,2},{1,5},{2,0},{3,7},{4,6},{5,1},{6,4},{7,3},{8,10},{9,13},{10,... | collective-permute-start | bytes 1572872 | tf_op jit(solution)/shard_map/ppermute | solution.py:348
  58.9 7.7 %collective-permute-start.17 = (f32[4,112,256]{2,1,0:T(8,128)S(1)}, f32[4,112,256]{2,1,0:T(8,128)S(1)}, u32[]{:S(2)}, u32[]{:S(2)}) collective-permute-start(f32[4,112,256]{2,1,0:T(8,128)S(1)} %get-tuple-element.34), channel_id=1, source_target_pairs={{0,4},{1,3},{2,6},{3,1},{4,0},{5,7},{6,2},{7,5},{8,12},{9,11},{10,... | collective-permute-start | bytes 1376264 | tf_op jit(solution)/shard_map/ppermute | solution.py:348
  60.2 13.8 %collective-permute-start.9 = (f32[4,112,384]{2,1,0:T(8,128)S(1)}, f32[4,112,384]{2,1,0:T(8,128)S(1)}, u32[]{:S(2)}, u32[]{:S(2)}) collective-permute-start(f32[4,112,384]{2,1,0:T(8,128)S(1)} %get-tuple-element.28), channel_id=1, source_target_pairs={{0,4},{1,3},{2,6},{3,1},{4,0},{5,7},{6,2},{7,5},{8,12},{9,11},{10,... | collective-permute-start | bytes 2064392 | tf_op jit(solution)/shard_map/ppermute | solution.py:348
  66.6 15.6 %collective-permute-start.20 = (f32[112,256]{1,0:T(8,128)S(1)}, f32[112,256]{1,0:T(8,128)S(1)}, u32[]{:S(2)}, u32[]{:S(2)}) collective-permute-start(f32[112,256]{1,0:T(8,128)S(1)} %get-tuple-element.37), channel_id=1, source_target_pairs={{0,9},{1,8},{2,11},{3,10},{4,13},{5,12},{6,15},{7,14},{8,1},{9,0},... | collective-permute-start | bytes 344072 | tf_op jit(solution)/shard_map/ppermute | solution.py:348
  68.2 14.7 %collective-permute-start.19 = (f32[112,256]{1,0:T(8,128)S(1)}, f32[112,256]{1,0:T(8,128)S(1)}, u32[]{:S(2)}, u32[]{:S(2)}) collective-permute-start(f32[112,256]{1,0:T(8,128)S(1)} %get-tuple-element.38), channel_id=1, source_target_pairs={{0,8},{1,9},{2,10},{3,11},{4,12},{5,13},{6,14},{7,15},{8,0},{9,1},... | collective-permute-start | bytes 344072 | tf_op jit(solution)/shard_map/ppermute | solution.py:348
  74.0 16.6 %collective-permute-start.12 = (f32[112,384]{1,0:T(8,128)S(1)}, f32[112,384]{1,0:T(8,128)S(1)}, u32[]{:S(2)}, u32[]{:S(2)}) collective-permute-start(f32[112,384]{1,0:T(8,128)S(1)} %get-tuple-element.35), channel_id=1, source_target_pairs={{0,9},{1,8},{2,11},{3,10},{4,13},{5,12},{6,15},{7,14},{8,1},{9,0},... | collective-permute-start | bytes 516104 | tf_op jit(solution)/shard_map/ppermute | solution.py:348
  79.6 16.0 %collective-permute-start.11 = (f32[112,384]{1,0:T(8,128)S(1)}, f32[112,384]{1,0:T(8,128)S(1)}, u32[]{:S(2)}, u32[]{:S(2)}) collective-permute-start(f32[112,384]{1,0:T(8,128)S(1)} %get-tuple-element.36), channel_id=1, source_target_pairs={{0,8},{1,9},{2,10},{3,11},{4,12},{5,13},{6,14},{7,15},{8,0},{9,1},... | collective-permute-start | bytes 516104 | tf_op jit(solution)/shard_map/ppermute | solution.py:348
  82.1 13.4 %collective-permute-start.10 = (f32[112,384]{1,0:T(8,128)S(1)}, f32[112,384]{1,0:T(8,128)S(1)}, u32[]{:S(2)}, u32[]{:S(2)}) collective-permute-start(f32[112,384]{1,0:T(8,128)S(1)} %get-tuple-element.39), channel_id=1, source_target_pairs={{0,1},{1,0},{2,3},{3,2},{4,5},{5,4},{6,7},{7,6},{8,9},{9,8},{10,11... | collective-permute-start | bytes 516104 | tf_op jit(solution)/shard_map/ppermute | solution.py:348
  82.3 1.5 %collective-permute-start.18 = (f32[112,256]{1,0:T(8,128)S(1)}, f32[112,256]{1,0:T(8,128)S(1)}, u32[]{:S(2)}, u32[]{:S(2)}) collective-permute-start(f32[112,256]{1,0:T(8,128)S(1)} %get-tuple-element.41), channel_id=1, source_target_pairs={{0,1},{1,0},{2,3},{3,2},{4,5},{5,4},{6,7},{7,6},{8,9},{9,8},{10,11... | collective-permute-start | bytes 344072 | tf_op jit(solution)/shard_map/ppermute | solution.py:348
  (5 other events, 5.9 us)

commit v4 on v0

v4 whole, which is shorter than its diff:
```python
import functools

import jax
import jax.numpy as jnp
from jax import lax
from jax.experimental import pallas as pl
from jax.experimental.pallas import tpu as pltpu
from jax.sharding import PartitionSpec as P

LANES = 128


def round_up(value, multiple):
    return -(-value // multiple) * multiple


class Plan:
    def __init__(self, n, block):
        self.n = n
        self.block = block
        self.tiles = round_up(block, LANES) // LANES
        self.share = (self.tiles + 1) // 2
        self.width = self.share * LANES
        self.places = n // 4
        self.high_bits = list(range(3, n.bit_length() - 1))

    def by_rows(self):
        return [(d, d ^ (2 + 2 * (d & 1))) for d in range(self.n)]

    def by_sums(self):
        return [(d, d ^ (4 - 2 * (d & 1))) for d in range(self.n)]

    def by_mask(self, mask):
        return [(d, d ^ mask) for d in range(self.n)]


def pack_kernel(plan, x_ref, *refs):
    step = pl.program_id(0)
    me = lax.axis_index("pat")
    rows, columns = x_ref.shape
    last_tile = columns // LANES - 1
    lane = lax.broadcasted_iota(jnp.int32, (rows, LANES), 1)

    def tile(index):
        return pl.ds(pl.multiple_of(jnp.minimum(index, last_tile) * LANES, LANES), LANES)

    for away in range(2):
        side = (me & 1) ^ away
        holder = me ^ away
        for sent in range(2):
            for chunk in range(2):
                relative = (
                    chunk
                    | (sent << (1 + side))
                    | ((step & 1) << (2 - side))
                    | ((step >> 1) << 3)
                )
                column = (holder ^ relative) * plan.block
                first = column // LANES
                edge = (column - first * LANES) * (1 - side)
                head = x_ref[:, tile(first + side * plan.share)]
                tail = x_ref[:, tile(first + plan.tiles)]
                folded = jnp.where(lane >= edge, head.astype(jnp.float32), tail.astype(jnp.float32))
                if sent:
                    target = refs[2 + 2 * away + chunk]
                else:
                    target = refs[away].at[chunk]
                target[:, 0:LANES] = folded.astype(x_ref.dtype)
                for slot in range(1, plan.share):
                    here = slice(slot * LANES, (slot + 1) * LANES)
                    target[:, here] = x_ref[:, tile(first + side * plan.share + slot)]


def pack(covariates, plan):
    rows = covariates.shape[0]
    dtype = covariates.dtype
    length = plan.places * rows
    kept = jax.ShapeDtypeStruct((2, length, plan.width), dtype)
    sent = jax.ShapeDtypeStruct((length, plan.width), dtype)
    kept_spec = pl.BlockSpec((2, rows, plan.width), lambda s: (0, s, 0))
    sent_spec = pl.BlockSpec((rows, plan.width), lambda s: (s, 0))
    return pl.pallas_call(
        functools.partial(pack_kernel, plan),
        grid=(plan.places,),
        in_specs=[pl.BlockSpec(memory_space=pltpu.VMEM)],
        out_specs=[kept_spec] * 2 + [sent_spec] * 4,
        out_shape=[kept] * 2 + [sent] * 4,
        compiler_params=pltpu.CompilerParams(vmem_limit_bytes=12 << 20),
        cost_estimate=pl.CostEstimate(flops=0, bytes_accessed=1 << 14, transcendentals=0),
        name="pack",
    )(covariates)


def onehot_of(pick_ref, weightings, dtype):
    index = lax.broadcasted_iota(jnp.int32, (pick_ref.shape[0], weightings), 1)
    return jnp.where(index == pick_ref[...], 1.0, 0.0).astype(dtype)


def arm_columns(panel_ref, onehot):
    comps, weightings = onehot.shape
    weights = panel_ref[0:weightings, :]
    arms = panel_ref[weightings:weightings + comps, :].astype(jnp.float32)
    picked = jnp.dot(onehot, weights, preferred_element_type=jnp.float32)
    return weights, picked * arms, picked * (1.0 - arms)


def small_call(kernel, shapes, operands, after, name):
    vmem = pl.BlockSpec(memory_space=pltpu.VMEM)
    return pl.pallas_call(
        kernel,
        in_specs=[vmem] * len(operands) + [pl.BlockSpec(memory_space=pl.ANY)] * len(after),
        out_specs=[vmem] * len(shapes),
        out_shape=[jax.ShapeDtypeStruct(shape, dtype) for shape, dtype in shapes],
        compiler_params=pltpu.CompilerParams(vmem_limit_bytes=4 << 20),
        cost_estimate=pl.CostEstimate(flops=0, bytes_accessed=1 << 14, transcendentals=0),
        name=name,
    )(*operands, *after)


def totals_kernel(weightings, pick_ref, near_ref, far_ref, *refs):
    out_ref = refs[-1]
    onehot = onehot_of(pick_ref, weightings, jnp.bfloat16)
    target_sum, other_sum = 0.0, 0.0
    for ref in (near_ref.at[0], near_ref.at[1], far_ref.at[0], far_ref.at[1]):
        _, target, other = arm_columns(ref, onehot)
        target_sum += target
        other_sum += other
    lane = lax.broadcasted_iota(jnp.int32, out_ref.shape, 1)
    out_ref[...] = jnp.where(
        lane == 0,
        jnp.sum(target_sum, axis=1, keepdims=True),
        jnp.sum(other_sum, axis=1, keepdims=True),
    )


def group_totals(near, far, pick_column, weightings, after):
    return small_call(
        functools.partial(totals_kernel, weightings),
        [((pick_column.shape[0], LANES), jnp.float32)],
        [pick_column, near, far],
        after,
        "totals",
    )[0]


def panel_kernel(weightings, pick_ref, near_ref, far_ref, here_ref, there_ref, *refs):
    first_ref, second_ref, stats_ref = refs
    comps = pick_ref.shape[0]
    onehot = onehot_of(pick_ref, weightings, jnp.bfloat16)
    totals = here_ref[...] + there_ref[...]
    total_target, total_other = totals[:, 0:1], totals[:, 1:2]
    light = jnp.where(total_target <= total_other, 1.0, 0.0)
    stats_ref[0] = jnp.broadcast_to(1.0 / total_target, (comps, LANES))
    stats_ref[1] = jnp.broadcast_to(1.0 / total_other, (comps, LANES))
    stats_ref[2] = jnp.broadcast_to(light, (comps, LANES))
    members = (near_ref.at[0], near_ref.at[1], far_ref.at[1], far_ref.at[0])
    for place, ref in enumerate(members):
        weights, target, other = arm_columns(ref, onehot)
        lighter = light * target + (1.0 - light) * other
        here = slice(place * LANES, (place + 1) * LANES)
        first_ref[0:comps, here] = lighter.astype(jnp.bfloat16)
        first_ref[comps:comps + weightings, here] = weights
        second_ref[0:comps, here] = target.astype(jnp.bfloat16)
        second_ref[comps:2 * comps, here] = other.astype(jnp.bfloat16)


def make_panels(near, far, totals, others, pick_column, weightings):
    comps = pick_column.shape[0]
    return small_call(
        functools.partial(panel_kernel, weightings),
        [
            ((comps + weightings, 4 * LANES), jnp.bfloat16),
            ((2 * comps, 4 * LANES), jnp.bfloat16),
            ((3, comps, LANES), jnp.float32),
        ],
        [pick_column, near, far, totals, others],
        [],
        "panels",
    )


def whole_spec(shape):
    return pl.BlockSpec(shape, lambda s: (0,) * len(shape))


def moments_kernel(rows, *refs):
    xs, (first_ref, second_ref, stats_ref), outs = refs[:4], refs[4:7], refs[-2:]
    first_rows = first_ref.shape[0]
    comps = second_ref.shape[0] // 2
    inverse_target = stats_ref[0][:, 0:1]
    inverse_other = stats_ref[1][:, 0:1]
    for place, out_ref in enumerate(outs):
        here = slice(place * rows, (place + 1) * rows)
        x = jnp.concatenate([ref[here, :] for ref in xs], axis=0)
        first = jnp.dot(first_ref[...], x, preferred_element_type=jnp.float32)
        squares = (x.astype(jnp.float32) * x.astype(jnp.float32)).astype(jnp.bfloat16)
        second = jnp.dot(second_ref[...], squares, preferred_element_type=jnp.float32)
        out_ref[0, 0:first_rows, :] = first
        out_ref[0, first_rows:first_rows + comps, :] = (
            second[0:comps] * inverse_target + second[comps:2 * comps] * inverse_other
        )


def moments(plan, chunk, kept, swapped, first, second, stats, after):
    rows = first.shape[1] // 4
    out_rows = first.shape[0] + second.shape[0] // 2
    out = (plan.places // 2, out_rows, plan.width)
    return pl.pallas_call(
        functools.partial(moments_kernel, rows),
        grid=(plan.places // 2,),
        in_specs=[pl.BlockSpec((None, 2 * rows, plan.width), lambda s: (chunk, s, 0))] * 2
        + [pl.BlockSpec((2 * rows, plan.width), lambda s: (s, 0))] * 2
        + [whole_spec(array.shape) for array in (first, second, stats)]
        + [pl.BlockSpec(memory_space=pl.ANY)] * len(after),
        out_specs=[pl.BlockSpec((1, out_rows, plan.width), lambda s: (s, 0, 0))] * 2,
        out_shape=[jax.ShapeDtypeStruct(out, jnp.float32)] * 2,
        compiler_params=pltpu.CompilerParams(vmem_limit_bytes=16 << 20),
        cost_estimate=pl.CostEstimate(flops=0, bytes_accessed=1 << 14, transcendentals=0),
        name="moments",
    )(*kept, *swapped, first, second, stats, *after)


def finish_kernel(plan, weightings, counts, pick_ref, stats_ref, *refs):
    out_ref, ring_ref = refs[-2:]
    comps = pick_ref.shape[0]
    onehot = onehot_of(pick_ref, weightings, jnp.float32)
    inverse_target = stats_ref[0][:, 0:1]
    inverse_other = stats_ref[1][:, 0:1]
    light = stats_ref[2][:, 0:1] > 0.5
    me = lax.axis_index("pat")
    for away, count in enumerate(counts):
        sums = refs[0][...]
        for more in refs[1:count]:
            sums += more[...]
        refs = refs[count:]
        lighter = sums[0:comps]
        both = jnp.dot(
            onehot,
            sums[comps:comps + weightings],
            precision=lax.Precision.HIGHEST,
            preferred_element_type=jnp.float32,
        )
        spread = sums[comps + weightings:2 * comps + weightings]
        heavier = both - lighter
        mean_target = jnp.where(light, lighter, heavier) * inverse_target
        mean_other = jnp.where(light, heavier, lighter) * inverse_other
        variance = spread - mean_target * mean_target - mean_other * mean_other
        pooled = jnp.maximum(variance / 2.0, 0.01)
        balance = (mean_target - mean_other) / jnp.sqrt(pooled)
        for side in range(2):
            count = plan.tiles - plan.share if side else plan.share
            if count:
                lanes = slice(side * plan.width, side * plan.width + count * LANES)

                @pl.when((me & 1) ^ away == side)
                def _():
                    ring_ref[:, lanes] = balance[:, 0:count * LANES]
    width = plan.tiles * LANES
    shift = width - lax.rem(me * plan.block, LANES)
    out_ref[:, 0, :] = pltpu.roll(ring_ref[...], shift, 1)[:, 0:plan.block]


def finish(plan, parts, pick_column, stats, weightings):
    comps = pick_column.shape[0]
    operands = [array for part in parts for array in part]
    return pl.pallas_call(
        functools.partial(finish_kernel, plan, weightings, [len(part) for part in parts]),
        in_specs=[pl.BlockSpec(memory_space=pltpu.VMEM)] * (2 + len(operands)),
        out_specs=pl.BlockSpec(memory_space=pltpu.VMEM),
        out_shape=jax.ShapeDtypeStruct((comps, 1, plan.block), jnp.float32),
        scratch_shapes=[pltpu.VMEM((comps, plan.tiles * LANES), jnp.float32)],
        compiler_params=pltpu.CompilerParams(vmem_limit_bytes=12 << 20),
        cost_estimate=pl.CostEstimate(flops=0, bytes_accessed=1 << 14, transcendentals=0),
        name="finish",
    )(pick_column, stats, *operands)


def swap(array, pairs):
    return lax.ppermute(array, "pat", pairs)


def on_device(n, covs, covariates, weights, arms, pick):
    weightings = weights.shape[1]
    pick_column = pick.reshape(pick.shape[0], 1)
    plan = Plan(n, covariates.shape[1] // n)
    to_other_side = plan.by_mask(1)

    arm_rows = arms.T.astype(weights.dtype)
    if covs > 1:
        arm_rows = lax.all_gather(arm_rows, "cov", axis=0, tiled=True)
    mine = jnp.concatenate([weights.T, arm_rows], axis=0)
    near = jnp.stack([mine, swap(mine, to_other_side)])
    far = swap(near, [(pair ^ 1, d) for d, pair in plan.by_rows()])

    kept, other_kept, sent0, sent1, other_sent0, other_sent1 = pack(covariates, plan)
    swapped = {}
    for chunk, sent, other_sent in ((1, sent1, other_sent1), (0, sent0, other_sent0)):
        passed = swap(other_sent, to_other_side)
        swapped[chunk] = [swap(sent, plan.by_rows()), swap(passed, plan.by_rows())]
    kept = [kept, swap(other_kept, to_other_side)]

    totals = group_totals(near, far, pick_column, weightings, [swapped[1][0]])
    others = swap(totals, plan.by_sums())
    for bit in plan.high_bits:
        totals = totals + others
        others = swap(totals, plan.by_mask(1 << bit))
    first, second, stats = make_panels(near, far, totals, others, pick_column, weightings)

    parts, after = [[], []], []
    for chunk in (1, 0):
        even, odd = moments(plan, chunk, kept, swapped[chunk], first, second, stats, after)
        arrived = swap(odd, plan.by_sums())
        after = [arrived]
        for bit in plan.high_bits[:-1]:
            odd = even[1::2] + arrived[1::2]
            even = even[0::2] + arrived[0::2]
            arrived = swap(odd, plan.by_mask(1 << bit))
        for bit in plan.high_bits[-1:]:
            parts[chunk].append(swap(even[1] + arrived[1], plan.by_mask((1 << bit) | chunk)))
        own = even[0] + arrived[0]
        parts[chunk].append(swap(own, to_other_side) if chunk else own)
    return finish(plan, parts, pick_column, stats, weightings)


def solution(mesh):
    placed = (
        P(("groups", "pat"), "cov"),
        P(("groups", "pat"), None),
        P(("groups", "pat"), "cov"),
        P(),
    )
    body = functools.partial(on_device, mesh.shape["pat"], mesh.shape["cov"])
    return jax.shard_map(
        body, mesh=mesh, in_specs=placed, out_specs=P("groups", "cov", "pat"), check_vma=False
    )
```

time: 352 us -> 90.3 us (0.26)
  waiting for transfers between devices: 178 us -> 55.6 us
  local copies, waits for them, and re-layouts: 102 us -> 2.55 us
  blocking collectives: 30.6 us -> 0 us
  starting transfers between devices: 0.01 us -> 21.2 us
  between operations: 13.5 us -> 0.09 us
  other arithmetic: 12.6 us -> 0.16 us
  matrix products: 12.1 us -> 0 us
  Pallas kernels: 0 us -> 9.65 us
    unnamed x2 -> x0, waiting for transfers between devices: 178 us -> none
    unnamed x15 -> x8, local copies, waits for them, and re-layouts: 98.3 us -> 2.46 us
    ppermute x0 -> x16, waiting for transfers between devices: none -> 55.6 us  [swap(): return lax.ppermute(array, 'pat', pairs)]
    psum x1 -> x0, blocking collectives: 30.6 us -> none  [on_device(): totals = lax.psum(placed, ('pat', 'cov'))]
    ppermute x0 -> x16, starting transfers between devices: none -> 21.2 us  [swap(): return lax.ppermute(array, 'pat', pairs)]
    another operation x3 -> x2, other arithmetic: 12.4 us -> 0.01 us  [on_device(): near = jnp.stack([mine, swap(mine, to_other_side)])]
    dot_general x3 -> x0, matrix products: 12.1 us -> none  [the longest x1 6.82 us: moment_pair(): lax.dot_general(columns, squares, dims, preferred_element_type=jnp.float32)]
    pallas_call x0 -> x6, Pallas kernels: none -> 9.65 us  [the longest x2 4.62 us: moments(): pl.pallas_call(functools.partial(moments_kernel, rows), grid=(plan.places...]
  transfers between devices with their start and end apart: 1 -> 16, of which waited for: 1 -> 8; matrix products, arithmetic and copies ran while one was open for 0% -> 0% of each run, Pallas kernels for 0% -> 3%
where the time goes in v4:
time: 90.3 us; the launch traced here: 89.2 us
  waiting for transfers between devices  55.6 us (62%)
  starting transfers between devices  21.2 us (23%)
  Pallas kernels  9.65 us (11%)
  local copies, waits for them, and re-layouts  2.55 us (3%)
    ppermute x16, waiting for transfers between devices, swap(): return lax.ppermute(array, 'pat', pairs)  55.6 us
    ppermute x16, starting transfers between devices, swap(): return lax.ppermute(array, 'pat', pairs)  21.2 us
    pallas_call x2, Pallas kernels, moments(): pl.pallas_call(functools.partial(moments_kernel, rows), grid=(plan.places...  4.62 us
    pallas_call x1, Pallas kernels, pack(): pl.pallas_call(functools.partial(pack_kernel, plan), grid=(plan.places,),...  2.9 us
    unnamed x8, local copies, waits for them, and re-layouts  2.46 us
  transfers between devices with their start and end apart: 16, of which 8 were waited for; matrix products, arithmetic and copies ran while one was open for 0% of the time, Pallas kernels for 3%

profile of v4, /device:TPU:1, one launch (start us, length us, event | category | flops | bytes accessed | tf_op | source)
XLA Modules:
  0.0 89.2 jit_solution(8748428043230259512)
XLA Ops:
  0.0 2.4 %copy-done = bf16[128,19968]{1,0:T(8,128)(2,1)S(1)} copy-done((bf16[128,19968]{1,0:T(8,128)(2,1)S(1)}, bf16[128,19968]{1,0:T(8,128)(2,1)}, u32[]{:S(2)}) %copy-start) | copy-done | bytes 5111832
  2.5 2.9 %pack.1 = (bf16[2,512,640]{2,1,0:T(8,128)(2,1)S(1)}, bf16[2,512,640]{2,1,0:T(8,128)(2,1)}, bf16[512,640]{1,0:T(8,128)(2,1)}, bf16[512,640]{1,0:T(8,128)(2,1)}, b...) custom-call(bf16[128,19968]{1,0:T(8,128)(2,1)S(1)} %copy-done), custom_call_target="tpu_custom_call" | custom-call | bytes 16384 | tf_op jit(solution)/shard_map/pack/pallas_call | solution.py:82
  5.9 2.7 %collective-permute-start.2 = (bf16[512,640]{1,0:T(8,128)(2,1)}, bf16[512,640]{1,0:T(8,128)(2,1)S(1)}, u32[]{:S(2)}, u32[]{:S(2)}) collective-permute-start(bf16[512,640]{1,0:T(8,128)(2,1)} %get-tuple-element.18), channel_id=1, source_target_pairs={{0,2},{1,5},{2,0},{3,7},{4,6},{5,1},{6,4},{7,3},{8,10},{9,13},{10,... | collective-permute-start | bytes 1966088 | tf_op jit(solution)/shard_map/ppermute | solution.py:279
  8.7 2.2 %collective-permute-start.10 = (bf16[512,640]{1,0:T(8,128)(2,1)}, bf16[512,640]{1,0:T(8,128)(2,1)}, u32[]{:S(2)}, u32[]{:S(2)}) collective-permute-start(bf16[512,640]{1,0:T(8,128)(2,1)} %collective-permute-done.9), channel_id=1, source_target_pairs={{0,2},{1,5},{2,0},{3,7},{4,6},{5,1},{6,4},{7,3},{8,10},{9,13},{10,... | collective-permute-start | bytes 1966088 | tf_op jit(solution)/shard_map/ppermute | solution.py:279
  10.9 0.7 collective-permute-start
  11.6 0.8 collective-permute-done
  12.5 1.0 %collective-permute-start.1 = (bf16[2,64,128]{2,1,0:T(8,128)(2,1)S(1)}, bf16[2,64,128]{2,1,0:T(8,128)(2,1)S(1)}, u32[]{:S(2)}, u32[]{:S(2)}) collective-permute-start(bf16[2,64,128]{2,1,0:T(8,128)(2,1)S(1)} %pad_maximum_fusion.near_ref), channel_id=1, source_target_pairs={{3,0},{4,1},{1,2},{6,3},{7,4},{0,5},{5,6},{2,7},{11,8},{12,9},{9,1... | collective-permute-start | bytes 98312 | tf_op jit(solution)/shard_map/ppermute | solution.py:279
  13.5 3.0 %collective-permute-done.1.far_ref = bf16[2,64,128]{2,1,0:T(8,128)(2,1)S(1)} collective-permute-done((bf16[2,64,128]{2,1,0:T(8,128)(2,1)S(1)}, bf16[2,64,128]{2,1,0:T(8,128)(2,1)S(1)}, u32[]{:S(2)}, u32[]{:S(2)}) %collective-permute-start.1) | collective-permute-done | bytes 32800 | tf_op jit(solution)/shard_map/ppermute | solution.py:279
  16.5 1.3 %collective-permute-start.6 = (bf16[512,640]{1,0:T(8,128)(2,1)}, bf16[512,640]{1,0:T(8,128)(2,1)}, u32[]{:S(2)}, u32[]{:S(2)}) collective-permute-start(bf16[512,640]{1,0:T(8,128)(2,1)} %get-tuple-element.22), channel_id=1, source_target_pairs={{0,2},{1,5},{2,0},{3,7},{4,6},{5,1},{6,4},{7,3},{8,10},{9,13},{10,... | collective-permute-start | bytes 1966088 | tf_op jit(solution)/shard_map/ppermute | solution.py:279
  18.4 1.1 %collective-permute-start.3 = (f32[48,128]{1,0:T(8,128)S(1)}, f32[48,128]{1,0:T(8,128)S(1)}, u32[]{:S(2)}, u32[]{:S(2)}) collective-permute-start(f32[48,128]{1,0:T(8,128)S(1)} %totals.1), channel_id=1, source_target_pairs={{0,4},{1,3},{2,6},{3,1},{4,0},{5,7},{6,2},{7,5},{8,12},{9,11},{10,... | collective-permute-start | bytes 73736 | tf_op jit(solution)/shard_map/ppermute | solution.py:279
  19.4 2.4 %collective-permute-done.3 = f32[48,128]{1,0:T(8,128)S(1)} collective-permute-done((f32[48,128]{1,0:T(8,128)S(1)}, f32[48,128]{1,0:T(8,128)S(1)}, u32[]{:S(2)}, u32[]{:S(2)}) %collective-permute-start.3) | collective-permute-done | bytes 24608 | tf_op jit(solution)/shard_map/ppermute | solution.py:279
  21.8 2.3 %collective-permute-start.4 = (f32[48,128]{1,0:T(8,128)S(1)}, f32[48,128]{1,0:T(8,128)S(1)}, u32[]{:S(2)}, u32[]{:S(2)}) collective-permute-start(f32[48,128]{1,0:T(8,128)S(1)} %add.26.here_ref), channel_id=1, source_target_pairs={{0,8},{1,9},{2,10},{3,11},{4,12},{5,13},{6,14},{7,15},{8,0},{9,1},... | collective-permute-start | bytes 73736 | tf_op jit(solution)/shard_map/ppermute | solution.py:279
  24.2 19.9 %collective-permute-done.4.there_ref = f32[48,128]{1,0:T(8,128)S(1)} collective-permute-done((f32[48,128]{1,0:T(8,128)S(1)}, f32[48,128]{1,0:T(8,128)S(1)}, u32[]{:S(2)}, u32[]{:S(2)}) %collective-permute-start.4) | collective-permute-done | bytes 24608 | tf_op jit(solution)/shard_map/ppermute | solution.py:279
  44.3 2.3 %moments.2 = (f32[2,112,640]{2,1,0:T(8,128)S(1)}, f32[2,112,640]{2,1,0:T(8,128)S(1)}) custom-call(bf16[2,512,640]{2,1,0:T(8,128)(2,1)S(1)} %get-tuple-element.20.refs_0_, bf16[2,512,640]{2,1,0:T(8,128)(2,1)S(1)} %collective-permute-done.5.refs_1_, bf16[512,640]{1,0:T(8,128)(2,1)S(1)} %collective-permute-done.2.refs_0_.refs_2_, ...), custom_call_target="tpu_custom_call" | custom-call | bytes 16384 | tf_op jit(solution)/shard_map/moments/pallas_call | solution.py:208
  46.6 1.5 %collective-permute-start.11 = (f32[2,112,640]{2,1,0:T(8,128)S(1)}, f32[2,112,640]{2,1,0:T(8,128)S(1)}, u32[]{:S(2)}, u32[]{:S(2)}) collective-permute-start(f32[2,112,640]{2,1,0:T(8,128)S(1)} %get-tuple-element.27), channel_id=1, source_target_pairs={{0,4},{1,3},{2,6},{3,1},{4,0},{5,7},{6,2},{7,5},{8,12},{9,11},{10,... | collective-permute-start | bytes 1720328 | tf_op jit(solution)/shard_map/ppermute | solution.py:279
  48.0 7.4 %collective-permute-done.11.refs_7_ = f32[2,112,640]{2,1,0:T(8,128)S(1)} collective-permute-done((f32[2,112,640]{2,1,0:T(8,128)S(1)}, f32[2,112,640]{2,1,0:T(8,128)S(1)}, u32[]{:S(2)}, u32[]{:S(2)}) %collective-permute-start.11) | collective-permute-done | bytes 573472 | tf_op jit(solution)/shard_map/ppermute | solution.py:279
  55.5 2.4 %moments.3 = (f32[2,112,640]{2,1,0:T(8,128)S(1)}, f32[2,112,640]{2,1,0:T(8,128)S(1)}) custom-call(bf16[2,512,640]{2,1,0:T(8,128)(2,1)S(1)} %get-tuple-element.20.refs_0_, bf16[2,512,640]{2,1,0:T(8,128)(2,1)S(1)} %collective-permute-done.5.refs_1_, bf16[512,640]{1,0:T(8,128)(2,1)} %collective-permute-done.6.refs_2_, ...), custom_call_target="tpu_custom_call" | custom-call | bytes 16384 | tf_op jit(solution)/shard_map/moments/pallas_call | solution.py:208
  57.9 1.5 %collective-permute-start.12 = (f32[2,112,640]{2,1,0:T(8,128)S(1)}, f32[2,112,640]{2,1,0:T(8,128)S(1)}, u32[]{:S(2)}, u32[]{:S(2)}) collective-permute-start(f32[2,112,640]{2,1,0:T(8,128)S(1)} %get-tuple-element.29), channel_id=1, source_target_pairs={{0,4},{1,3},{2,6},{3,1},{4,0},{5,7},{6,2},{7,5},{8,12},{9,11},{10,... | collective-permute-start | bytes 1720328 | tf_op jit(solution)/shard_map/ppermute | solution.py:279
  59.5 3.2 %collective-permute-start.14 = (f32[112,640]{1,0:T(8,128)S(1)}, f32[112,640]{1,0:T(8,128)S(1)}, u32[]{:S(2)}, u32[]{:S(2)}) collective-permute-start(f32[112,640]{1,0:T(8,128)S(1)} %get-tuple-element.32), channel_id=1, source_target_pairs={{0,9},{1,8},{2,11},{3,10},{4,13},{5,12},{6,15},{7,14},{8,1},{9,0},... | collective-permute-start | bytes 860168 | tf_op jit(solution)/shard_map/ppermute | solution.py:279
  62.7 4.1 %collective-permute-done.12 = f32[2,112,640]{2,1,0:T(8,128)S(1)} collective-permute-done((f32[2,112,640]{2,1,0:T(8,128)S(1)}, f32[2,112,640]{2,1,0:T(8,128)S(1)}, u32[]{:S(2)}, u32[]{:S(2)}) %collective-permute-start.12) | collective-permute-done | bytes 573472 | tf_op jit(solution)/shard_map/ppermute | solution.py:279
  66.9 2.9 %collective-permute-start.13 = (f32[112,640]{1,0:T(8,128)S(1)}, f32[112,640]{1,0:T(8,128)S(1)}, u32[]{:S(2)}, u32[]{:S(2)}) collective-permute-start(f32[112,640]{1,0:T(8,128)S(1)} %get-tuple-element.34), channel_id=1, source_target_pairs={{0,8},{1,9},{2,10},{3,11},{4,12},{5,13},{6,14},{7,15},{8,0},{9,1},... | collective-permute-start | bytes 860168 | tf_op jit(solution)/shard_map/ppermute | solution.py:279
  69.7 12.6 %collective-permute-done.14.refs_2_ = f32[112,640]{1,0:T(8,128)S(1)} collective-permute-done((f32[112,640]{1,0:T(8,128)S(1)}, f32[112,640]{1,0:T(8,128)S(1)}, u32[]{:S(2)}, u32[]{:S(2)}) %collective-permute-start.14) | collective-permute-done | bytes 286752 | tf_op jit(solution)/shard_map/ppermute | solution.py:279
  82.3 5.3 %collective-permute-done.13.refs_0_ = f32[112,640]{1,0:T(8,128)S(1)} collective-permute-done((f32[112,640]{1,0:T(8,128)S(1)}, f32[112,640]{1,0:T(8,128)S(1)}, u32[]{:S(2)}, u32[]{:S(2)}) %collective-permute-start.13) | collective-permute-done | bytes 286752 | tf_op jit(solution)/shard_map/ppermute | solution.py:279
  87.6 1.6 %finish.1 = f32[48,1,1248]{2,1,0:T(1,128)} custom-call(s32[48,1]{1,0:T(8,128)S(1)} %copy.7.pick_ref, f32[3,48,128]{2,1,0:T(8,128)S(1)} %get-tuple-element.19.refs_6_.stats_ref, f32[112,640]{1,0:T(8,128)S(1)} %collective-permute-done.13.refs_0_, f32[112,640]{1,0:T(8,128)S(1)} %get-tuple-element.33.refs_1_, f32[112,640]{1,0:T(8,128)S(1)} %collective-permute-done.14.refs_2_, ...), custom_call_target="tpu_custom_call" | custom-call | bytes 16384 | tf_op jit(solution)/shard_map/finish/pallas_call | solution.py:266
  (29 shorter events, 1.6 us)
Async XLA Ops:
  0.0 2.4 %copy-start = (bf16[128,19968]{1,0:T(8,128)(2,1)S(1)}, bf16[128,19968]{1,0:T(8,128)(2,1)}, u32[]{:S(2)}) copy-start(bf16[128,19968]{1,0:T(8,128)(2,1)} %x_ref.1) | copy-start | bytes 15335428
  2.5 8.5 %copy-start.1 = (s32[128,48]{0,1:T(8,128)S(1)}, s32[128,48]{0,1:T(8,128)}, u32[]{:S(2)}) copy-start(s32[128,48]{0,1:T(8,128)} %param.6) | copy-start | bytes 73732
  2.5 8.5 %copy-start.2 = (bf16[128,16]{0,1:T(8,128)(2,1)S(1)}, bf16[128,16]{0,1:T(8,128)(2,1)}, u32[]{:S(2)}) copy-start(bf16[128,16]{0,1:T(8,128)(2,1)} %param.5) | copy-start | bytes 12292
  2.5 15.5 %copy-start.3 = (s32[48]{0:T(128)S(1)}, s32[48]{0:T(128)}, u32[]{:S(2)}) copy-start(s32[48]{0:T(128)} %param.7) | copy-start | bytes 580
  5.4 3.3 %collective-permute-start.9 = (bf16[512,640]{1,0:T(8,128)(2,1)S(1)}, bf16[512,640]{1,0:T(8,128)(2,1)}, u32[]{:S(2)}, u32[]{:S(2)}) collective-permute-start(bf16[512,640]{1,0:T(8,128)(2,1)S(1)} %get-tuple-element.26), channel_id=1, source_target_pairs={{0,1},{1,0},{2,3},{3,2},{4,5},{5,4},{6,7},{7,6},{8,9},{9,8},{10,11... | collective-permute-start | bytes 1966088 | tf_op jit(solution)/shard_map/ppermute | solution.py:279
  5.4 38.9 %collective-permute-start.5 = (bf16[2,512,640]{2,1,0:T(8,128)(2,1)}, bf16[2,512,640]{2,1,0:T(8,128)(2,1)S(1)}, u32[]{:S(2)}, u32[]{:S(2)}) collective-permute-start(bf16[2,512,640]{2,1,0:T(8,128)(2,1)} %get-tuple-element.21), channel_id=1, source_target_pairs={{0,1},{1,0},{2,3},{3,2},{4,5},{5,4},{6,7},{7,6},{8,9},{9,8},{10,11... | collective-permute-start | bytes 3932168 | tf_op jit(solution)/shard_map/ppermute | solution.py:279
  5.9 11.9 %collective-permute-start.7 = (bf16[512,640]{1,0:T(8,128)(2,1)S(1)}, bf16[512,640]{1,0:T(8,128)(2,1)}, u32[]{:S(2)}, u32[]{:S(2)}) collective-permute-start(bf16[512,640]{1,0:T(8,128)(2,1)S(1)} %get-tuple-element.23), channel_id=1, source_target_pairs={{0,1},{1,0},{2,3},{3,2},{4,5},{5,4},{6,7},{7,6},{8,9},{9,8},{10,11... | collective-permute-start | bytes 1966088 | tf_op jit(solution)/shard_map/ppermute | solution.py:279
  5.9 12.1 %collective-permute-start.2 = (bf16[512,640]{1,0:T(8,128)(2,1)}, bf16[512,640]{1,0:T(8,128)(2,1)S(1)}, u32[]{:S(2)}, u32[]{:S(2)}) collective-permute-start(bf16[512,640]{1,0:T(8,128)(2,1)} %get-tuple-element.18), channel_id=1, source_target_pairs={{0,2},{1,5},{2,0},{3,7},{4,6},{5,1},{6,4},{7,3},{8,10},{9,13},{10,... | collective-permute-start | bytes 1966088 | tf_op jit(solution)/shard_map/ppermute | solution.py:279
  8.7 35.6 %collective-permute-start.10 = (bf16[512,640]{1,0:T(8,128)(2,1)}, bf16[512,640]{1,0:T(8,128)(2,1)}, u32[]{:S(2)}, u32[]{:S(2)}) collective-permute-start(bf16[512,640]{1,0:T(8,128)(2,1)} %collective-permute-done.9), channel_id=1, source_target_pairs={{0,2},{1,5},{2,0},{3,7},{4,6},{5,1},{6,4},{7,3},{8,10},{9,13},{10,... | collective-permute-start | bytes 1966088 | tf_op jit(solution)/shard_map/ppermute | solution.py:279
  10.9 1.5 %collective-permute-start = (bf16[64,128]{1,0:T(8,128)(2,1)S(1)}, bf16[64,128]{1,0:T(8,128)(2,1)S(1)}, u32[]{:S(2)}, u32[]{:S(2)}) collective-permute-start(bf16[64,128]{1,0:T(8,128)(2,1)S(1)} %get-tuple-element.36), channel_id=1, source_target_pairs={{0,1},{1,0},{2,3},{3,2},{4,5},{5,4},{6,7},{7,6},{8,9},{9,8},{10,11... | collective-permute-start | bytes 49160 | tf_op jit(solution)/shard_map/ppermute | solution.py:279
  12.5 4.0 %collective-permute-start.1 = (bf16[2,64,128]{2,1,0:T(8,128)(2,1)S(1)}, bf16[2,64,128]{2,1,0:T(8,128)(2,1)S(1)}, u32[]{:S(2)}, u32[]{:S(2)}) collective-permute-start(bf16[2,64,128]{2,1,0:T(8,128)(2,1)S(1)} %pad_maximum_fusion.near_ref), channel_id=1, source_target_pairs={{3,0},{4,1},{1,2},{6,3},{7,4},{0,5},{5,6},{2,7},{11,8},{12,9},{9,1... | collective-permute-start | bytes 98312 | tf_op jit(solution)/shard_map/ppermute | solution.py:279
  16.5 31.5 %collective-permute-start.6 = (bf16[512,640]{1,0:T(8,128)(2,1)}, bf16[512,640]{1,0:T(8,128)(2,1)}, u32[]{:S(2)}, u32[]{:S(2)}) collective-permute-start(bf16[512,640]{1,0:T(8,128)(2,1)} %get-tuple-element.22), channel_id=1, source_target_pairs={{0,2},{1,5},{2,0},{3,7},{4,6},{5,1},{6,4},{7,3},{8,10},{9,13},{10,... | collective-permute-start | bytes 1966088 | tf_op jit(solution)/shard_map/ppermute | solution.py:279
  17.8 30.2 %collective-permute-start.8 = (bf16[512,640]{1,0:T(8,128)(2,1)}, bf16[512,640]{1,0:T(8,128)(2,1)}, u32[]{:S(2)}, u32[]{:S(2)}) collective-permute-start(bf16[512,640]{1,0:T(8,128)(2,1)} %collective-permute-done.7), channel_id=1, source_target_pairs={{0,2},{1,5},{2,0},{3,7},{4,6},{5,1},{6,4},{7,3},{8,10},{9,13},{10,... | collective-permute-start | bytes 1966088 | tf_op jit(solution)/shard_map/ppermute | solution.py:279
  18.4 3.5 %collective-permute-start.3 = (f32[48,128]{1,0:T(8,128)S(1)}, f32[48,128]{1,0:T(8,128)S(1)}, u32[]{:S(2)}, u32[]{:S(2)}) collective-permute-start(f32[48,128]{1,0:T(8,128)S(1)} %totals.1), channel_id=1, source_target_pairs={{0,4},{1,3},{2,6},{3,1},{4,0},{5,7},{6,2},{7,5},{8,12},{9,11},{10,... | collective-permute-start | bytes 73736 | tf_op jit(solution)/shard_map/ppermute | solution.py:279
  21.8 22.2 %collective-permute-start.4 = (f32[48,128]{1,0:T(8,128)S(1)}, f32[48,128]{1,0:T(8,128)S(1)}, u32[]{:S(2)}, u32[]{:S(2)}) collective-permute-start(f32[48,128]{1,0:T(8,128)S(1)} %add.26.here_ref), channel_id=1, source_target_pairs={{0,8},{1,9},{2,10},{3,11},{4,12},{5,13},{6,14},{7,15},{8,0},{9,1},... | collective-permute-start | bytes 73736 | tf_op jit(solution)/shard_map/ppermute | solution.py:279
  46.6 8.9 %collective-permute-start.11 = (f32[2,112,640]{2,1,0:T(8,128)S(1)}, f32[2,112,640]{2,1,0:T(8,128)S(1)}, u32[]{:S(2)}, u32[]{:S(2)}) collective-permute-start(f32[2,112,640]{2,1,0:T(8,128)S(1)} %get-tuple-element.27), channel_id=1, source_target_pairs={{0,4},{1,3},{2,6},{3,1},{4,0},{5,7},{6,2},{7,5},{8,12},{9,11},{10,... | collective-permute-start | bytes 1720328 | tf_op jit(solution)/shard_map/ppermute | solution.py:279
  57.9 8.9 %collective-permute-start.12 = (f32[2,112,640]{2,1,0:T(8,128)S(1)}, f32[2,112,640]{2,1,0:T(8,128)S(1)}, u32[]{:S(2)}, u32[]{:S(2)}) collective-permute-start(f32[2,112,640]{2,1,0:T(8,128)S(1)} %get-tuple-element.29), channel_id=1, source_target_pairs={{0,4},{1,3},{2,6},{3,1},{4,0},{5,7},{6,2},{7,5},{8,12},{9,11},{10,... | collective-permute-start | bytes 1720328 | tf_op jit(solution)/shard_map/ppermute | solution.py:279
  59.4 10.3 %collective-permute-start.15 = (f32[112,640]{1,0:T(8,128)S(1)}, f32[112,640]{1,0:T(8,128)S(1)}, u32[]{:S(2)}, u32[]{:S(2)}) collective-permute-start(f32[112,640]{1,0:T(8,128)S(1)} %get-tuple-element.31), channel_id=1, source_target_pairs={{0,1},{1,0},{2,3},{3,2},{4,5},{5,4},{6,7},{7,6},{8,9},{9,8},{10,11... | collective-permute-start | bytes 860168 | tf_op jit(solution)/shard_map/ppermute | solution.py:279
  59.5 22.8 %collective-permute-start.14 = (f32[112,640]{1,0:T(8,128)S(1)}, f32[112,640]{1,0:T(8,128)S(1)}, u32[]{:S(2)}, u32[]{:S(2)}) collective-permute-start(f32[112,640]{1,0:T(8,128)S(1)} %get-tuple-element.32), channel_id=1, source_target_pairs={{0,9},{1,8},{2,11},{3,10},{4,13},{5,12},{6,15},{7,14},{8,1},{9,0},... | collective-permute-start | bytes 860168 | tf_op jit(solution)/shard_map/ppermute | solution.py:279
  66.9 20.8 %collective-permute-start.13 = (f32[112,640]{1,0:T(8,128)S(1)}, f32[112,640]{1,0:T(8,128)S(1)}, u32[]{:S(2)}, u32[]{:S(2)}) collective-permute-start(f32[112,640]{1,0:T(8,128)S(1)} %get-tuple-element.34), channel_id=1, source_target_pairs={{0,8},{1,9},{2,10},{3,11},{4,12},{5,13},{6,14},{7,15},{8,0},{9,1},... | collective-permute-start | bytes 860168 | tf_op jit(solution)/shard_map/ppermute | solution.py:279

commit v5 on v4

--- a/solution.py
+++ b/solution.py
@@ -143,11 +143,12 @@
     )[0]
 
 
-def panel_kernel(weightings, pick_ref, near_ref, far_ref, here_ref, there_ref, *refs):
+def panel_kernel(weightings, pick_ref, near_ref, far_ref, here_ref, told_ref, *refs):
     first_ref, second_ref, stats_ref = refs
     comps = pick_ref.shape[0]
     onehot = onehot_of(pick_ref, weightings, jnp.bfloat16)
-    totals = here_ref[...] + there_ref[...]
+    side = jnp.full(here_ref.shape, lax.axis_index("pat") & 1)
+    totals = jnp.where(side == 0, here_ref[...], told_ref[...])
     total_target, total_other = totals[:, 0:1], totals[:, 1:2]
     light = jnp.where(total_target <= total_other, 1.0, 0.0)
     stats_ref[0] = jnp.broadcast_to(1.0 / total_target, (comps, LANES))
@@ -164,7 +165,7 @@
         second_ref[comps:2 * comps, here] = other.astype(jnp.bfloat16)
 
 
-def make_panels(near, far, totals, others, pick_column, weightings):
+def make_panels(near, far, totals, told, pick_column, weightings):
     comps = pick_column.shape[0]
     return small_call(
         functools.partial(panel_kernel, weightings),
@@ -173,7 +174,7 @@
             ((2 * comps, 4 * LANES), jnp.bfloat16),
             ((3, comps, LANES), jnp.float32),
         ],
-        [pick_column, near, far, totals, others],
+        [pick_column, near, far, totals, told],
         [],
         "panels",
     )
@@ -300,11 +301,11 @@
     kept = [kept, swap(other_kept, to_other_side)]
 
     totals = group_totals(near, far, pick_column, weightings, [swapped[1][0]])
-    others = swap(totals, plan.by_sums())
+    totals = totals + swap(totals, plan.by_sums())
     for bit in plan.high_bits:
-        totals = totals + others
-        others = swap(totals, plan.by_mask(1 << bit))
-    first, second, stats = make_panels(near, far, totals, others, pick_column, weightings)
+        totals = totals + swap(totals, plan.by_mask(1 << bit)[0::2])
+    told = swap(totals, to_other_side[0::2])
+    first, second, stats = make_panels(near, far, totals, told, pick_column, weightings)
 
     parts, after = [[], []], []
     for chunk in (1, 0):

time: 90.3 us -> 80.2 us (0.89)
  waiting for transfers between devices: 55.6 us -> 46.5 us
  starting transfers between devices: 21.2 us -> 20.2 us
    ppermute x16 -> x17, waiting for transfers between devices: 55.6 us -> 46.5 us  [swap(): return lax.ppermute(array, 'pat', pairs)]
    ppermute x16 -> x17, starting transfers between devices: 21.2 us -> 20.2 us  [swap(): return lax.ppermute(array, 'pat', pairs)]
  transfers between devices with their start and end apart: 16 -> 17, of which waited for: 8 -> 9; matrix products, arithmetic and copies ran while one was open for 0% -> 0% of each run, Pallas kernels for 3% -> 4%
where the time goes in v5:
time: 80.2 us; the launch traced here: 79.1 us
  waiting for transfers between devices  46.5 us (58%)
  starting transfers between devices  20.2 us (25%)
  Pallas kernels  9.61 us (12%)
  local copies, waits for them, and re-layouts  2.55 us (3%)
    ppermute x17, waiting for transfers between devices, swap(): return lax.ppermute(array, 'pat', pairs)  46.5 us
    ppermute x17, starting transfers between devices, swap(): return lax.ppermute(array, 'pat', pairs)  20.2 us
    pallas_call x2, Pallas kernels, moments(): pl.pallas_call(functools.partial(moments_kernel, rows), grid=(plan.places...  4.61 us
    pallas_call x1, Pallas kernels, pack(): pl.pallas_call(functools.partial(pack_kernel, plan), grid=(plan.places,),...  2.87 us
    unnamed x8, local copies, waits for them, and re-layouts  2.46 us
    pallas_call x1, Pallas kernels, finish(): pl.pallas_call(functools.partial(finish_kernel, plan, weightings, [len(pa...  1.61 us
  transfers between devices with their start and end apart: 17, of which 9 were waited for; matrix products, arithmetic and copies ran while one was open for 0% of the time, Pallas kernels for 4%

profile of v5, /device:TPU:1, one launch (start us, length us, event | category | flops | bytes accessed | tf_op | source)
XLA Modules:
  0.0 79.1 jit_solution(17308049274001786470)
XLA Ops:
  0.0 2.4 %copy-done = bf16[128,19968]{1,0:T(8,128)(2,1)S(1)} copy-done((bf16[128,19968]{1,0:T(8,128)(2,1)S(1)}, bf16[128,19968]{1,0:T(8,128)(2,1)}, u32[]{:S(2)}) %copy-start) | copy-done | bytes 5111832
  2.5 2.9 %pack.1 = (bf16[2,512,640]{2,1,0:T(8,128)(2,1)S(1)}, bf16[2,512,640]{2,1,0:T(8,128)(2,1)}, bf16[512,640]{1,0:T(8,128)(2,1)}, bf16[512,640]{1,0:T(8,128)(2,1)}, b...) custom-call(bf16[128,19968]{1,0:T(8,128)(2,1)S(1)} %copy-done), custom_call_target="tpu_custom_call" | custom-call | bytes 16384 | tf_op jit(solution)/shard_map/pack/pallas_call | solution.py:82
  5.9 2.7 %collective-permute-start.2 = (bf16[512,640]{1,0:T(8,128)(2,1)}, bf16[512,640]{1,0:T(8,128)(2,1)S(1)}, u32[]{:S(2)}, u32[]{:S(2)}) collective-permute-start(bf16[512,640]{1,0:T(8,128)(2,1)} %get-tuple-element.18), channel_id=1, source_target_pairs={{0,2},{1,5},{2,0},{3,7},{4,6},{5,1},{6,4},{7,3},{8,10},{9,13},{10,... | collective-permute-start | bytes 1966088 | tf_op jit(solution)/shard_map/ppermute | solution.py:280
  8.6 2.2 %collective-permute-start.11 = (bf16[512,640]{1,0:T(8,128)(2,1)}, bf16[512,640]{1,0:T(8,128)(2,1)}, u32[]{:S(2)}, u32[]{:S(2)}) collective-permute-start(bf16[512,640]{1,0:T(8,128)(2,1)} %collective-permute-done.10), channel_id=1, source_target_pairs={{0,2},{1,5},{2,0},{3,7},{4,6},{5,1},{6,4},{7,3},{8,10},{9,13},{10,... | collective-permute-start | bytes 1966088 | tf_op jit(solution)/shard_map/ppermute | solution.py:280
  11.6 0.8 %collective-permute-done = bf16[64,128]{1,0:T(8,128)(2,1)S(1)} collective-permute-done((bf16[64,128]{1,0:T(8,128)(2,1)S(1)}, bf16[64,128]{1,0:T(8,128)(2,1)S(1)}, u32[]{:S(2)}, u32[]{:S(2)}) %collective-permute-start) | collective-permute-done | bytes 16416 | tf_op jit(solution)/shard_map/ppermute | solution.py:280
  12.4 1.0 %collective-permute-start.1 = (bf16[2,64,128]{2,1,0:T(8,128)(2,1)S(1)}, bf16[2,64,128]{2,1,0:T(8,128)(2,1)S(1)}, u32[]{:S(2)}, u32[]{:S(2)}) collective-permute-start(bf16[2,64,128]{2,1,0:T(8,128)(2,1)S(1)} %pad_maximum_fusion.near_ref), channel_id=1, source_target_pairs={{3,0},{4,1},{1,2},{6,3},{7,4},{0,5},{5,6},{2,7},{11,8},{12,9},{9,1... | collective-permute-start | bytes 98312 | tf_op jit(solution)/shard_map/ppermute | solution.py:280
  13.5 3.0 %collective-permute-done.1.far_ref = bf16[2,64,128]{2,1,0:T(8,128)(2,1)S(1)} collective-permute-done((bf16[2,64,128]{2,1,0:T(8,128)(2,1)S(1)}, bf16[2,64,128]{2,1,0:T(8,128)(2,1)S(1)}, u32[]{:S(2)}, u32[]{:S(2)}) %collective-permute-start.1) | collective-permute-done | bytes 32800 | tf_op jit(solution)/shard_map/ppermute | solution.py:280
  16.5 1.3 %collective-permute-start.7 = (bf16[512,640]{1,0:T(8,128)(2,1)}, bf16[512,640]{1,0:T(8,128)(2,1)}, u32[]{:S(2)}, u32[]{:S(2)}) collective-permute-start(bf16[512,640]{1,0:T(8,128)(2,1)} %get-tuple-element.22), channel_id=1, source_target_pairs={{0,2},{1,5},{2,0},{3,7},{4,6},{5,1},{6,4},{7,3},{8,10},{9,13},{10,... | collective-permute-start | bytes 1966088 | tf_op jit(solution)/shard_map/ppermute | solution.py:280
  18.3 1.1 %collective-permute-start.3 = (f32[48,128]{1,0:T(8,128)S(1)}, f32[48,128]{1,0:T(8,128)S(1)}, u32[]{:S(2)}, u32[]{:S(2)}) collective-permute-start(f32[48,128]{1,0:T(8,128)S(1)} %totals.1), channel_id=1, source_target_pairs={{0,4},{1,3},{2,6},{3,1},{4,0},{5,7},{6,2},{7,5},{8,12},{9,11},{10,... | collective-permute-start | bytes 73736 | tf_op jit(solution)/shard_map/ppermute | solution.py:280
  19.4 2.4 %collective-permute-done.3 = f32[48,128]{1,0:T(8,128)S(1)} collective-permute-done((f32[48,128]{1,0:T(8,128)S(1)}, f32[48,128]{1,0:T(8,128)S(1)}, u32[]{:S(2)}, u32[]{:S(2)}) %collective-permute-start.3) | collective-permute-done | bytes 24608 | tf_op jit(solution)/shard_map/ppermute | solution.py:280
  22.5 1.3 %collective-permute-start.5 = (f32[48,128]{1,0:T(8,128)S(1)}, f32[48,128]{1,0:T(8,128)S(1)}, u32[]{:S(2)}, u32[]{:S(2)}) collective-permute-start(f32[48,128]{1,0:T(8,128)S(1)} %add.30.here_ref), channel_id=1, source_target_pairs={{0,1},{2,3},{4,5},{6,7},{8,9},{10,11},{12,13},{14,15},{16,17},{18,... | collective-permute-start | bytes 73736 | tf_op jit(solution)/shard_map/ppermute | solution.py:280
  23.8 8.1 %collective-permute-done.5.told_ref = f32[48,128]{1,0:T(8,128)S(1)} collective-permute-done((f32[48,128]{1,0:T(8,128)S(1)}, f32[48,128]{1,0:T(8,128)S(1)}, u32[]{:S(2)}, u32[]{:S(2)}) %collective-permute-start.5) | collective-permute-done | bytes 24608 | tf_op jit(solution)/shard_map/ppermute | solution.py:280
  32.1 2.3 %moments.2 = (f32[2,112,640]{2,1,0:T(8,128)S(1)}, f32[2,112,640]{2,1,0:T(8,128)S(1)}) custom-call(bf16[2,512,640]{2,1,0:T(8,128)(2,1)S(1)} %get-tuple-element.20.refs_0_, bf16[2,512,640]{2,1,0:T(8,128)(2,1)S(1)} %collective-permute-done.6.refs_1_, bf16[512,640]{1,0:T(8,128)(2,1)S(1)} %collective-permute-done.2.refs_0_.refs_2_, ...), custom_call_target="tpu_custom_call" | custom-call | bytes 16384 | tf_op jit(solution)/shard_map/moments/pallas_call | solution.py:209
  34.4 1.1 %collective-permute-start.12 = (f32[2,112,640]{2,1,0:T(8,128)S(1)}, f32[2,112,640]{2,1,0:T(8,128)S(1)}, u32[]{:S(2)}, u32[]{:S(2)}) collective-permute-start(f32[2,112,640]{2,1,0:T(8,128)S(1)} %get-tuple-element.27), channel_id=1, source_target_pairs={{0,4},{1,3},{2,6},{3,1},{4,0},{5,7},{6,2},{7,5},{8,12},{9,11},{10,... | collective-permute-start | bytes 1720328 | tf_op jit(solution)/shard_map/ppermute | solution.py:280
  35.5 4.9 %collective-permute-done.9.refs_3_ = bf16[512,640]{1,0:T(8,128)(2,1)} collective-permute-done((bf16[512,640]{1,0:T(8,128)(2,1)}, bf16[512,640]{1,0:T(8,128)(2,1)}, u32[]{:S(2)}, u32[]{:S(2)}) %collective-permute-start.9) | collective-permute-done | bytes 655392 | tf_op jit(solution)/shard_map/ppermute | solution.py:280
  40.4 4.7 %collective-permute-done.12.refs_7_ = f32[2,112,640]{2,1,0:T(8,128)S(1)} collective-permute-done((f32[2,112,640]{2,1,0:T(8,128)S(1)}, f32[2,112,640]{2,1,0:T(8,128)S(1)}, u32[]{:S(2)}, u32[]{:S(2)}) %collective-permute-start.12) | collective-permute-done | bytes 573472 | tf_op jit(solution)/shard_map/ppermute | solution.py:280
  45.1 2.4 %moments.3 = (f32[2,112,640]{2,1,0:T(8,128)S(1)}, f32[2,112,640]{2,1,0:T(8,128)S(1)}) custom-call(bf16[2,512,640]{2,1,0:T(8,128)(2,1)S(1)} %get-tuple-element.20.refs_0_, bf16[2,512,640]{2,1,0:T(8,128)(2,1)S(1)} %collective-permute-done.6.refs_1_, bf16[512,640]{1,0:T(8,128)(2,1)} %collective-permute-done.7.refs_2_, ...), custom_call_target="tpu_custom_call" | custom-call | bytes 16384 | tf_op jit(solution)/shard_map/moments/pallas_call | solution.py:209
  47.4 1.6 %collective-permute-start.13 = (f32[2,112,640]{2,1,0:T(8,128)S(1)}, f32[2,112,640]{2,1,0:T(8,128)S(1)}, u32[]{:S(2)}, u32[]{:S(2)}) collective-permute-start(f32[2,112,640]{2,1,0:T(8,128)S(1)} %get-tuple-element.29), channel_id=1, source_target_pairs={{0,4},{1,3},{2,6},{3,1},{4,0},{5,7},{6,2},{7,5},{8,12},{9,11},{10,... | collective-permute-start | bytes 1720328 | tf_op jit(solution)/shard_map/ppermute | solution.py:280
  49.9 2.3 %collective-permute-start.15 = (f32[112,640]{1,0:T(8,128)S(1)}, f32[112,640]{1,0:T(8,128)S(1)}, u32[]{:S(2)}, u32[]{:S(2)}) collective-permute-start(f32[112,640]{1,0:T(8,128)S(1)} %get-tuple-element.32), channel_id=1, source_target_pairs={{0,9},{1,8},{2,11},{3,10},{4,13},{5,12},{6,15},{7,14},{8,1},{9,0},... | collective-permute-start | bytes 860168 | tf_op jit(solution)/shard_map/ppermute | solution.py:280
  52.2 4.2 %collective-permute-done.13 = f32[2,112,640]{2,1,0:T(8,128)S(1)} collective-permute-done((f32[2,112,640]{2,1,0:T(8,128)S(1)}, f32[2,112,640]{2,1,0:T(8,128)S(1)}, u32[]{:S(2)}, u32[]{:S(2)}) %collective-permute-start.13) | collective-permute-done | bytes 573472 | tf_op jit(solution)/shard_map/ppermute | solution.py:280
  56.5 2.6 %collective-permute-start.14 = (f32[112,640]{1,0:T(8,128)S(1)}, f32[112,640]{1,0:T(8,128)S(1)}, u32[]{:S(2)}, u32[]{:S(2)}) collective-permute-start(f32[112,640]{1,0:T(8,128)S(1)} %get-tuple-element.34), channel_id=1, source_target_pairs={{0,8},{1,9},{2,10},{3,11},{4,12},{5,13},{6,14},{7,15},{8,0},{9,1},... | collective-permute-start | bytes 860168 | tf_op jit(solution)/shard_map/ppermute | solution.py:280
  59.1 13.1 %collective-permute-done.15.refs_2_ = f32[112,640]{1,0:T(8,128)S(1)} collective-permute-done((f32[112,640]{1,0:T(8,128)S(1)}, f32[112,640]{1,0:T(8,128)S(1)}, u32[]{:S(2)}, u32[]{:S(2)}) %collective-permute-start.15) | collective-permute-done | bytes 286752 | tf_op jit(solution)/shard_map/ppermute | solution.py:280
  72.2 5.3 %collective-permute-done.14.refs_0_ = f32[112,640]{1,0:T(8,128)S(1)} collective-permute-done((f32[112,640]{1,0:T(8,128)S(1)}, f32[112,640]{1,0:T(8,128)S(1)}, u32[]{:S(2)}, u32[]{:S(2)}) %collective-permute-start.14) | collective-permute-done | bytes 286752 | tf_op jit(solution)/shard_map/ppermute | solution.py:280
  77.5 1.6 %finish.1 = f32[48,1,1248]{2,1,0:T(1,128)} custom-call(s32[48,1]{1,0:T(8,128)S(1)} %copy.7.pick_ref, f32[3,48,128]{2,1,0:T(8,128)S(1)} %get-tuple-element.19.refs_6_.stats_ref, f32[112,640]{1,0:T(8,128)S(1)} %collective-permute-done.14.refs_0_, f32[112,640]{1,0:T(8,128)S(1)} %get-tuple-element.33.refs_1_, f32[112,640]{1,0:T(8,128)S(1)} %collective-permute-done.15.refs_2_, ...), custom_call_target="tpu_custom_call" | custom-call | bytes 16384 | tf_op jit(solution)/shard_map/finish/pallas_call | solution.py:267
  (32 shorter events, 3.7 us)
Async XLA Ops:
  0.0 2.4 %copy-start = (bf16[128,19968]{1,0:T(8,128)(2,1)S(1)}, bf16[128,19968]{1,0:T(8,128)(2,1)}, u32[]{:S(2)}) copy-start(bf16[128,19968]{1,0:T(8,128)(2,1)} %x_ref.1) | copy-start | bytes 15335428
  2.5 8.4 %copy-start.1 = (s32[128,48]{0,1:T(8,128)S(1)}, s32[128,48]{0,1:T(8,128)}, u32[]{:S(2)}) copy-start(s32[128,48]{0,1:T(8,128)} %param.6) | copy-start | bytes 73732
  2.5 8.5 %copy-start.2 = (bf16[128,16]{0,1:T(8,128)(2,1)S(1)}, bf16[128,16]{0,1:T(8,128)(2,1)}, u32[]{:S(2)}) copy-start(bf16[128,16]{0,1:T(8,128)(2,1)} %param.5) | copy-start | bytes 12292
  2.5 15.5 %copy-start.3 = (s32[48]{0:T(128)S(1)}, s32[48]{0:T(128)}, u32[]{:S(2)}) copy-start(s32[48]{0:T(128)} %param.7) | copy-start | bytes 580
  5.3 3.3 %collective-permute-start.10 = (bf16[512,640]{1,0:T(8,128)(2,1)S(1)}, bf16[512,640]{1,0:T(8,128)(2,1)}, u32[]{:S(2)}, u32[]{:S(2)}) collective-permute-start(bf16[512,640]{1,0:T(8,128)(2,1)S(1)} %get-tuple-element.26), channel_id=1, source_target_pairs={{0,1},{1,0},{2,3},{3,2},{4,5},{5,4},{6,7},{7,6},{8,9},{9,8},{10,11... | collective-permute-start | bytes 1966088 | tf_op jit(solution)/shard_map/ppermute | solution.py:280
  5.4 26.7 %collective-permute-start.6 = (bf16[2,512,640]{2,1,0:T(8,128)(2,1)}, bf16[2,512,640]{2,1,0:T(8,128)(2,1)S(1)}, u32[]{:S(2)}, u32[]{:S(2)}) collective-permute-start(bf16[2,512,640]{2,1,0:T(8,128)(2,1)} %get-tuple-element.21), channel_id=1, source_target_pairs={{0,1},{1,0},{2,3},{3,2},{4,5},{5,4},{6,7},{7,6},{8,9},{9,8},{10,11... | collective-permute-start | bytes 3932168 | tf_op jit(solution)/shard_map/ppermute | solution.py:280
  5.8 11.9 %collective-permute-start.8 = (bf16[512,640]{1,0:T(8,128)(2,1)S(1)}, bf16[512,640]{1,0:T(8,128)(2,1)}, u32[]{:S(2)}, u32[]{:S(2)}) collective-permute-start(bf16[512,640]{1,0:T(8,128)(2,1)S(1)} %get-tuple-element.23), channel_id=1, source_target_pairs={{0,1},{1,0},{2,3},{3,2},{4,5},{5,4},{6,7},{7,6},{8,9},{9,8},{10,11... | collective-permute-start | bytes 1966088 | tf_op jit(solution)/shard_map/ppermute | solution.py:280
  5.9 12.1 %collective-permute-start.2 = (bf16[512,640]{1,0:T(8,128)(2,1)}, bf16[512,640]{1,0:T(8,128)(2,1)S(1)}, u32[]{:S(2)}, u32[]{:S(2)}) collective-permute-start(bf16[512,640]{1,0:T(8,128)(2,1)} %get-tuple-element.18), channel_id=1, source_target_pairs={{0,2},{1,5},{2,0},{3,7},{4,6},{5,1},{6,4},{7,3},{8,10},{9,13},{10,... | collective-permute-start | bytes 1966088 | tf_op jit(solution)/shard_map/ppermute | solution.py:280
  8.6 23.4 %collective-permute-start.11 = (bf16[512,640]{1,0:T(8,128)(2,1)}, bf16[512,640]{1,0:T(8,128)(2,1)}, u32[]{:S(2)}, u32[]{:S(2)}) collective-permute-start(bf16[512,640]{1,0:T(8,128)(2,1)} %collective-permute-done.10), channel_id=1, source_target_pairs={{0,2},{1,5},{2,0},{3,7},{4,6},{5,1},{6,4},{7,3},{8,10},{9,13},{10,... | collective-permute-start | bytes 1966088 | tf_op jit(solution)/shard_map/ppermute | solution.py:280
  10.9 1.5 %collective-permute-start = (bf16[64,128]{1,0:T(8,128)(2,1)S(1)}, bf16[64,128]{1,0:T(8,128)(2,1)S(1)}, u32[]{:S(2)}, u32[]{:S(2)}) collective-permute-start(bf16[64,128]{1,0:T(8,128)(2,1)S(1)} %get-tuple-element.36), channel_id=1, source_target_pairs={{0,1},{1,0},{2,3},{3,2},{4,5},{5,4},{6,7},{7,6},{8,9},{9,8},{10,11... | collective-permute-start | bytes 49160 | tf_op jit(solution)/shard_map/ppermute | solution.py:280
  12.4 4.0 %collective-permute-start.1 = (bf16[2,64,128]{2,1,0:T(8,128)(2,1)S(1)}, bf16[2,64,128]{2,1,0:T(8,128)(2,1)S(1)}, u32[]{:S(2)}, u32[]{:S(2)}) collective-permute-start(bf16[2,64,128]{2,1,0:T(8,128)(2,1)S(1)} %pad_maximum_fusion.near_ref), channel_id=1, source_target_pairs={{3,0},{4,1},{1,2},{6,3},{7,4},{0,5},{5,6},{2,7},{11,8},{12,9},{9,1... | collective-permute-start | bytes 98312 | tf_op jit(solution)/shard_map/ppermute | solution.py:280
  16.5 19.0 %collective-permute-start.7 = (bf16[512,640]{1,0:T(8,128)(2,1)}, bf16[512,640]{1,0:T(8,128)(2,1)}, u32[]{:S(2)}, u32[]{:S(2)}) collective-permute-start(bf16[512,640]{1,0:T(8,128)(2,1)} %get-tuple-element.22), channel_id=1, source_target_pairs={{0,2},{1,5},{2,0},{3,7},{4,6},{5,1},{6,4},{7,3},{8,10},{9,13},{10,... | collective-permute-start | bytes 1966088 | tf_op jit(solution)/shard_map/ppermute | solution.py:280
  17.8 22.6 %collective-permute-start.9 = (bf16[512,640]{1,0:T(8,128)(2,1)}, bf16[512,640]{1,0:T(8,128)(2,1)}, u32[]{:S(2)}, u32[]{:S(2)}) collective-permute-start(bf16[512,640]{1,0:T(8,128)(2,1)} %collective-permute-done.8), channel_id=1, source_target_pairs={{0,2},{1,5},{2,0},{3,7},{4,6},{5,1},{6,4},{7,3},{8,10},{9,13},{10,... | collective-permute-start | bytes 1966088 | tf_op jit(solution)/shard_map/ppermute | solution.py:280
  18.3 3.5 %collective-permute-start.3 = (f32[48,128]{1,0:T(8,128)S(1)}, f32[48,128]{1,0:T(8,128)S(1)}, u32[]{:S(2)}, u32[]{:S(2)}) collective-permute-start(f32[48,128]{1,0:T(8,128)S(1)} %totals.1), channel_id=1, source_target_pairs={{0,4},{1,3},{2,6},{3,1},{4,0},{5,7},{6,2},{7,5},{8,12},{9,11},{10,... | collective-permute-start | bytes 73736 | tf_op jit(solution)/shard_map/ppermute | solution.py:280
  21.8 0.7 collective-permute-start.4
  22.5 9.4 %collective-permute-start.5 = (f32[48,128]{1,0:T(8,128)S(1)}, f32[48,128]{1,0:T(8,128)S(1)}, u32[]{:S(2)}, u32[]{:S(2)}) collective-permute-start(f32[48,128]{1,0:T(8,128)S(1)} %add.30.here_ref), channel_id=1, source_target_pairs={{0,1},{2,3},{4,5},{6,7},{8,9},{10,11},{12,13},{14,15},{16,17},{18,... | collective-permute-start | bytes 73736 | tf_op jit(solution)/shard_map/ppermute | solution.py:280
  34.4 10.7 %collective-permute-start.12 = (f32[2,112,640]{2,1,0:T(8,128)S(1)}, f32[2,112,640]{2,1,0:T(8,128)S(1)}, u32[]{:S(2)}, u32[]{:S(2)}) collective-permute-start(f32[2,112,640]{2,1,0:T(8,128)S(1)} %get-tuple-element.27), channel_id=1, source_target_pairs={{0,4},{1,3},{2,6},{3,1},{4,0},{5,7},{6,2},{7,5},{8,12},{9,11},{10,... | collective-permute-start | bytes 1720328 | tf_op jit(solution)/shard_map/ppermute | solution.py:280
  47.4 9.0 %collective-permute-start.13 = (f32[2,112,640]{2,1,0:T(8,128)S(1)}, f32[2,112,640]{2,1,0:T(8,128)S(1)}, u32[]{:S(2)}, u32[]{:S(2)}) collective-permute-start(f32[2,112,640]{2,1,0:T(8,128)S(1)} %get-tuple-element.29), channel_id=1, source_target_pairs={{0,4},{1,3},{2,6},{3,1},{4,0},{5,7},{6,2},{7,5},{8,12},{9,11},{10,... | collective-permute-start | bytes 1720328 | tf_op jit(solution)/shard_map/ppermute | solution.py:280
  49.1 10.0 %collective-permute-start.16 = (f32[112,640]{1,0:T(8,128)S(1)}, f32[112,640]{1,0:T(8,128)S(1)}, u32[]{:S(2)}, u32[]{:S(2)}) collective-permute-start(f32[112,640]{1,0:T(8,128)S(1)} %get-tuple-element.31), channel_id=1, source_target_pairs={{0,1},{1,0},{2,3},{3,2},{4,5},{5,4},{6,7},{7,6},{8,9},{9,8},{10,11... | collective-permute-start | bytes 860168 | tf_op jit(solution)/shard_map/ppermute | solution.py:280
  49.9 22.3 %collective-permute-start.15 = (f32[112,640]{1,0:T(8,128)S(1)}, f32[112,640]{1,0:T(8,128)S(1)}, u32[]{:S(2)}, u32[]{:S(2)}) collective-permute-start(f32[112,640]{1,0:T(8,128)S(1)} %get-tuple-element.32), channel_id=1, source_target_pairs={{0,9},{1,8},{2,11},{3,10},{4,13},{5,12},{6,15},{7,14},{8,1},{9,0},... | collective-permute-start | bytes 860168 | tf_op jit(solution)/shard_map/ppermute | solution.py:280
  56.5 21.0 %collective-permute-start.14 = (f32[112,640]{1,0:T(8,128)S(1)}, f32[112,640]{1,0:T(8,128)S(1)}, u32[]{:S(2)}, u32[]{:S(2)}) collective-permute-start(f32[112,640]{1,0:T(8,128)S(1)} %get-tuple-element.34), channel_id=1, source_target_pairs={{0,8},{1,9},{2,10},{3,11},{4,12},{5,13},{6,14},{7,15},{8,0},{9,1},... | collective-permute-start | bytes 860168 | tf_op jit(solution)/shard_map/ppermute | solution.py:280

commit v6 on v5

--- a/solution.py
+++ b/solution.py
@@ -22,7 +22,7 @@
         self.share = (self.tiles + 1) // 2
         self.width = self.share * LANES
         self.places = n // 4
-        self.high_bits = list(range(3, n.bit_length() - 1))
+        *self.middle_bits, self.top_bit = range(3, n.bit_length() - 1)
 
     def by_rows(self):
         return [(d, d ^ (2 + 2 * (d & 1))) for d in range(self.n)]
@@ -34,61 +34,84 @@
         return [(d, d ^ mask) for d in range(self.n)]
 
 
-def pack_kernel(plan, x_ref, *refs):
+def pack_kernel(plan, chunk, x_hbm, *refs):
+    kept_ref, sent_ref, other_ref, x_ref, sems = refs[-5:]
     step = pl.program_id(0)
     me = lax.axis_index("pat")
     rows, columns = x_ref.shape
     last_tile = columns // LANES - 1
+    start = ((me >> plan.top_bit) ^ chunk) * columns
     lane = lax.broadcasted_iota(jnp.int32, (rows, LANES), 1)
+
+    @pl.when(step == 0)
+    def _():
+        count = sems.shape[0]
+        edges = [columns // LANES * piece // count * LANES for piece in range(count + 1)]
+        copies = []
+        for number in range(count):
+            width = edges[number + 1] - edges[number]
+            there = pl.ds(pl.multiple_of(start + edges[number], LANES), width)
+            copies.append(
+                pltpu.make_async_copy(
+                    x_hbm.at[:, there], x_ref.at[:, pl.ds(edges[number], width)], sems.at[number]
+                )
+            )
+        for copy in copies:
+            copy.start()
+        for copy in copies:
+            copy.wait()
 
     def tile(index):
         return pl.ds(pl.multiple_of(jnp.minimum(index, last_tile) * LANES, LANES), LANES)
 
+    middle = len(plan.middle_bits)
     for away in range(2):
         side = (me & 1) ^ away
         holder = me ^ away
         for sent in range(2):
-            for chunk in range(2):
-                relative = (
-                    chunk
-                    | (sent << (1 + side))
-                    | ((step & 1) << (2 - side))
-                    | ((step >> 1) << 3)
-                )
-                column = (holder ^ relative) * plan.block
-                first = column // LANES
-                edge = (column - first * LANES) * (1 - side)
-                head = x_ref[:, tile(first + side * plan.share)]
-                tail = x_ref[:, tile(first + plan.tiles)]
-                folded = jnp.where(lane >= edge, head.astype(jnp.float32), tail.astype(jnp.float32))
-                if sent:
-                    target = refs[2 + 2 * away + chunk]
-                else:
-                    target = refs[away].at[chunk]
-                target[:, 0:LANES] = folded.astype(x_ref.dtype)
-                for slot in range(1, plan.share):
-                    here = slice(slot * LANES, (slot + 1) * LANES)
-                    target[:, here] = x_ref[:, tile(first + side * plan.share + slot)]
-
-
-def pack(covariates, plan):
-    rows = covariates.shape[0]
+            relative = (
+                (step >> (1 + middle))
+                | (sent << (1 + side))
+                | ((step & 1) << (2 - side))
+                | (((step >> 1) & ((1 << middle) - 1)) << 3)
+                | (chunk << plan.top_bit)
+            )
+            column = (holder ^ relative) * plan.block - start
+            first = column // LANES
+            edge = (column - first * LANES) * (1 - side)
+            head = x_ref[:, tile(first + side * plan.share)]
+            tail = x_ref[:, tile(first + plan.tiles)]
+            folded = jnp.where(lane >= edge, head.astype(jnp.float32), tail.astype(jnp.float32))
+            target = other_ref.at[sent] if away else (kept_ref, sent_ref)[sent]
+            target[:, 0:LANES] = folded.astype(x_ref.dtype)
+            for slot in range(1, plan.share):
+                here = slice(slot * LANES, (slot + 1) * LANES)
+                target[:, here] = x_ref[:, tile(first + side * plan.share + slot)]
+
+
+def pack(covariates, plan, chunk, after):
+    rows, columns = covariates.shape
     dtype = covariates.dtype
     length = plan.places * rows
-    kept = jax.ShapeDtypeStruct((2, length, plan.width), dtype)
-    sent = jax.ShapeDtypeStruct((length, plan.width), dtype)
-    kept_spec = pl.BlockSpec((2, rows, plan.width), lambda s: (0, s, 0))
-    sent_spec = pl.BlockSpec((rows, plan.width), lambda s: (s, 0))
+    mine = jax.ShapeDtypeStruct((length, plan.width), dtype)
+    other = jax.ShapeDtypeStruct((2, length, plan.width), dtype)
+    mine_spec = pl.BlockSpec((rows, plan.width), lambda s: (s, 0))
+    other_spec = pl.BlockSpec((2, rows, plan.width), lambda s: (0, s, 0))
     return pl.pallas_call(
-        functools.partial(pack_kernel, plan),
+        functools.partial(pack_kernel, plan, chunk),
         grid=(plan.places,),
-        in_specs=[pl.BlockSpec(memory_space=pltpu.VMEM)],
-        out_specs=[kept_spec] * 2 + [sent_spec] * 4,
-        out_shape=[kept] * 2 + [sent] * 4,
-        compiler_params=pltpu.CompilerParams(vmem_limit_bytes=12 << 20),
-        cost_estimate=pl.CostEstimate(flops=0, bytes_accessed=1 << 14, transcendentals=0),
+        in_specs=[pl.BlockSpec(memory_space=pl.ANY)] * (1 + len(after)),
+        out_specs=[mine_spec] * 2 + [other_spec],
+        out_shape=[mine] * 2 + [other],
+        scratch_shapes=[
+            pltpu.VMEM((rows, columns // 2), dtype), pltpu.SemaphoreType.DMA((3,))
+        ],
+        compiler_params=pltpu.CompilerParams(vmem_limit_bytes=(58 if chunk else 10) << 20),
+        cost_estimate=pl.CostEstimate(
+            flops=0, bytes_accessed=4 * covariates.size, transcendentals=0
+        ),
         name="pack",
-    )(covariates)
+    )(covariates, *after)
 
 
 def onehot_of(pick_ref, weightings, dtype):
@@ -184,41 +207,47 @@
     return pl.BlockSpec(shape, lambda s: (0,) * len(shape))
 
 
-def moments_kernel(rows, *refs):
-    xs, (first_ref, second_ref, stats_ref), outs = refs[:4], refs[4:7], refs[-2:]
+def moments_kernel(rows, split, *refs):
+    kept_ref, passed_ref, *swapped_refs, first_ref, second_ref, stats_ref = refs[:7]
+    outs = refs[-(2 if split is None else split):]
     first_rows = first_ref.shape[0]
     comps = second_ref.shape[0] // 2
     inverse_target = stats_ref[0][:, 0:1]
     inverse_other = stats_ref[1][:, 0:1]
-    for place, out_ref in enumerate(outs):
+    for place in range(swapped_refs[0].shape[0] // rows):
         here = slice(place * rows, (place + 1) * rows)
-        x = jnp.concatenate([ref[here, :] for ref in xs], axis=0)
+        x = jnp.concatenate(
+            [kept_ref[here, :], passed_ref[0, here, :]]
+            + [ref[here, :] for ref in swapped_refs],
+            axis=0,
+        )
         first = jnp.dot(first_ref[...], x, preferred_element_type=jnp.float32)
         squares = (x.astype(jnp.float32) * x.astype(jnp.float32)).astype(jnp.bfloat16)
         second = jnp.dot(second_ref[...], squares, preferred_element_type=jnp.float32)
-        out_ref[0, 0:first_rows, :] = first
-        out_ref[0, first_rows:first_rows + comps, :] = (
+        out = outs[place % 2].at[place // 2] if split is None else outs[place]
+        out[0:first_rows, :] = first
+        out[first_rows:first_rows + comps, :] = (
             second[0:comps] * inverse_target + second[comps:2 * comps] * inverse_other
         )
 
 
-def moments(plan, chunk, kept, swapped, first, second, stats, after):
+def moments(plan, rows_here, first, second, stats, split, after):
     rows = first.shape[1] // 4
-    out_rows = first.shape[0] + second.shape[0] // 2
-    out = (plan.places // 2, out_rows, plan.width)
+    sums = (first.shape[0] + second.shape[0] // 2, plan.width)
+    if split:
+        out_shape = [jax.ShapeDtypeStruct(sums, jnp.float32)] * plan.places
+    else:
+        out_shape = [jax.ShapeDtypeStruct((plan.places // 2,) + sums, jnp.float32)] * 2
     return pl.pallas_call(
-        functools.partial(moments_kernel, rows),
-        grid=(plan.places // 2,),
-        in_specs=[pl.BlockSpec((None, 2 * rows, plan.width), lambda s: (chunk, s, 0))] * 2
-        + [pl.BlockSpec((2 * rows, plan.width), lambda s: (s, 0))] * 2
-        + [whole_spec(array.shape) for array in (first, second, stats)]
+        functools.partial(moments_kernel, rows, plan.places if split else None),
+        in_specs=[pl.BlockSpec(memory_space=pltpu.VMEM)] * 7
         + [pl.BlockSpec(memory_space=pl.ANY)] * len(after),
-        out_specs=[pl.BlockSpec((1, out_rows, plan.width), lambda s: (s, 0, 0))] * 2,
-        out_shape=[jax.ShapeDtypeStruct(out, jnp.float32)] * 2,
-        compiler_params=pltpu.CompilerParams(vmem_limit_bytes=16 << 20),
-        cost_estimate=pl.CostEstimate(flops=0, bytes_accessed=1 << 14, transcendentals=0),
+        out_specs=[pl.BlockSpec(memory_space=pltpu.VMEM)] * len(out_shape),
+        out_shape=out_shape,
+        compiler_params=pltpu.CompilerParams(vmem_limit_bytes=20 << 20),
+        cost_estimate=pl.CostEstimate(flops=0, bytes_accessed=6 << 20, transcendentals=0),
         name="moments",
-    )(*kept, *swapped, first, second, stats, *after)
+    )(*rows_here, first, second, stats, *after)
 
 
 def finish_kernel(plan, weightings, counts, pick_ref, stats_ref, *refs):
@@ -276,6 +305,14 @@
     )(pick_column, stats, *operands)
 
 
+def add_kernel(left_ref, right_ref, *refs):
+    refs[-1][...] = left_ref[...] + right_ref[...]
+
+
+def add(left, right, after):
+    return small_call(add_kernel, [(left.shape, left.dtype)], [left, right], after, "add")[0]
+
+
 def swap(array, pairs):
     return lax.ppermute(array, "pat", pairs)
 
@@ -293,33 +330,49 @@
     near = jnp.stack([mine, swap(mine, to_other_side)])
     far = swap(near, [(pair ^ 1, d) for d, pair in plan.by_rows()])
 
-    kept, other_kept, sent0, sent1, other_sent0, other_sent1 = pack(covariates, plan)
-    swapped = {}
-    for chunk, sent, other_sent in ((1, sent1, other_sent1), (0, sent0, other_sent0)):
-        passed = swap(other_sent, to_other_side)
-        swapped[chunk] = [swap(sent, plan.by_rows()), swap(passed, plan.by_rows())]
-    kept = [kept, swap(other_kept, to_other_side)]
-
-    totals = group_totals(near, far, pick_column, weightings, [swapped[1][0]])
+    rows_here, after = {}, []
+    for chunk in (1, 0):
+        kept, sent, other = pack(covariates, plan, chunk, after)
+        passed = swap(other, to_other_side)
+        rows_here[chunk] = [
+            kept, passed, swap(sent, plan.by_rows()), swap(passed[1], plan.by_rows())
+        ]
+        after = [near]
+
+    totals = group_totals(near, far, pick_column, weightings, [passed, rows_here[1][2]])
     totals = totals + swap(totals, plan.by_sums())
-    for bit in plan.high_bits:
+    for bit in plan.middle_bits + [plan.top_bit]:
         totals = totals + swap(totals, plan.by_mask(1 << bit)[0::2])
     told = swap(totals, to_other_side[0::2])
     first, second, stats = make_panels(near, far, totals, told, pick_column, weightings)
 
-    parts, after = [[], []], []
-    for chunk in (1, 0):
-        even, odd = moments(plan, chunk, kept, swapped[chunk], first, second, stats, after)
+    even, odd = moments(plan, rows_here[1], first, second, stats, False, [])
+    arrived = swap(odd, plan.by_sums())
+    for bit in plan.middle_bits:
+        odd = even[1::2] + arrived[1::2]
+        even = even[0::2] + arrived[0::2]
+        arrived = swap(odd, plan.by_mask(1 << bit))
+    across = add(even, arrived, [rows_here[0][2]])
+    top = swap(across, plan.by_mask(1 << plan.top_bit))
+
+    last = not plan.middle_bits
+    sums = moments(plan, rows_here[0], first, second, stats, last, [across])
+    if last:
+        even, odd = sums[0::2], sums[1::2]
+        other_owner = [(d, pair ^ 1) for d, pair in plan.by_sums()]
+        parts = [
+            [even[0], top[0], swap(odd[0], plan.by_sums())],
+            [swap(even[1] + top[1], to_other_side), swap(odd[1], other_owner)],
+        ]
+    else:
+        even, odd = sums
         arrived = swap(odd, plan.by_sums())
-        after = [arrived]
-        for bit in plan.high_bits[:-1]:
+        for bit in plan.middle_bits:
             odd = even[1::2] + arrived[1::2]
             even = even[0::2] + arrived[0::2]
             arrived = swap(odd, plan.by_mask(1 << bit))
-        for bit in plan.high_bits[-1:]:
-            parts[chunk].append(swap(even[1] + arrived[1], plan.by_mask((1 << bit) | chunk)))
-        own = even[0] + arrived[0]
-        parts[chunk].append(swap(own, to_other_side) if chunk else own)
+        total = even + arrived + top
+        parts = [[total[0]], [swap(total[1], to_other_side)]]
     return finish(plan, parts, pick_column, stats, weightings)
 
 

time: 80.2 us -> 83.2 us (1.037)
  starting transfers between devices: 20.2 us -> 26 us
  waiting for transfers between devices: 46.5 us -> 42.3 us
  Pallas kernels: 9.61 us -> 12.1 us
    ppermute x17 -> x16, starting transfers between devices: 20.2 us -> 26 us  [swap(): return lax.ppermute(array, 'pat', pairs)]
    ppermute x17 -> x16, waiting for transfers between devices: 46.5 us -> 42.3 us  [swap(): return lax.ppermute(array, 'pat', pairs)]
    pallas_call x3 -> x4, Pallas kernels: 7.48 us -> 9.85 us  [the longest x2 6.35 us: pack(): pl.pallas_call(functools.partial(pack_kernel, plan, chunk), grid=(plan.pl...]
    unnamed x8 -> x18, local copies, waits for them, and re-layouts: 2.46 us -> 1.1 us
    squeeze x0 -> x3, local copies, waits for them, and re-layouts: none -> 0.97 us  [the longest x2 0.95 us: on_device(): passed[1]]
  transfers between devices with their start and end apart: 17 -> 16, of which waited for: 9 -> 9; matrix products, arithmetic and copies ran while one was open for 0% -> 1% of each run, Pallas kernels for 4% -> 8%
where the time goes in v6:
time: 83.2 us; the launch traced here: 82.7 us
  waiting for transfers between devices  42.3 us (51%)
  starting transfers between devices  26 us (31%)
  Pallas kernels  12.1 us (15%)
  local copies, waits for them, and re-layouts  2.16 us (3%)
    ppermute x16, waiting for transfers between devices, swap(): return lax.ppermute(array, 'pat', pairs)  42.3 us
    ppermute x16, starting transfers between devices, swap(): return lax.ppermute(array, 'pat', pairs)  26 us
    pallas_call x2, Pallas kernels, pack(): pl.pallas_call(functools.partial(pack_kernel, plan, chunk), grid=(plan.pl...  6.35 us
    pallas_call x2, Pallas kernels, moments(): pl.pallas_call(functools.partial(moments_kernel, rows, plan.places if spl...  3.5 us
  transfers between devices with their start and end apart: 16, of which 9 were waited for; matrix products, arithmetic and copies ran while one was open for 1% of the time, Pallas kernels for 8%

profile of v6, /device:TPU:1, one launch (start us, length us, event | category | flops | bytes accessed | tf_op | source)
XLA Modules:
  0.0 82.7 jit_solution(4526967949893938446)
XLA Ops:
  0.0 4.1 %pack.3 = (bf16[512,640]{1,0:T(8,128)(2,1)}, bf16[512,640]{1,0:T(8,128)(2,1)}, bf16[2,512,640]{2,1,0:T(8,128)(2,1)}) custom-call(bf16[128,19968]{1,0:T(8,128)(2,1)} %x_hbm.3), custom_call_target="tpu_custom_call" | custom-call | bytes 10223616 | tf_op jit(solution)/shard_map/pack/pallas_call | solution.py:100
  4.8 2.1 %collective-permute-done = bf16[64,128]{1,0:T(8,128)(2,1)S(1)} collective-permute-done((bf16[64,128]{1,0:T(8,128)(2,1)S(1)}, bf16[64,128]{1,0:T(8,128)(2,1)S(1)}, u32[]{:S(2)}, u32[]{:S(2)}) %collective-permute-start) | collective-permute-done | bytes 16416 | tf_op jit(solution)/shard_map/ppermute | solution.py:317
  6.9 2.3 %pack.2 = (bf16[512,640]{1,0:T(8,128)(2,1)S(1)}, bf16[512,640]{1,0:T(8,128)(2,1)}, bf16[2,512,640]{2,1,0:T(8,128)(2,1)}) custom-call(bf16[128,19968]{1,0:T(8,128)(2,1)S(1)} %copy-done, bf16[2,64,128]{2,1,0:T(8,128)(2,1)S(1)} %pad_maximum_fusion.refs_0_.near_ref), custom_call_target="tpu_custom_call" | custom-call | bytes 10223616 | tf_op jit(solution)/shard_map/pack/pallas_call | solution.py:100
  9.7 2.4 %collective-permute-start.3 = (bf16[512,640]{1,0:T(8,128)(2,1)}, bf16[512,640]{1,0:T(8,128)(2,1)}, u32[]{:S(2)}, u32[]{:S(2)}) collective-permute-start(bf16[512,640]{1,0:T(8,128)(2,1)} %get-tuple-element.21), channel_id=1, source_target_pairs={{0,2},{1,5},{2,0},{3,7},{4,6},{5,1},{6,4},{7,3},{8,10},{9,13},{10,... | collective-permute-start | bytes 1966088 | tf_op jit(solution)/shard_map/ppermute | solution.py:317
  14.0 2.2 %collective-permute-start.1 = (bf16[2,64,128]{2,1,0:T(8,128)(2,1)S(1)}, bf16[2,64,128]{2,1,0:T(8,128)(2,1)S(1)}, u32[]{:S(2)}, u32[]{:S(2)}) collective-permute-start(bf16[2,64,128]{2,1,0:T(8,128)(2,1)S(1)} %pad_maximum_fusion.refs_0_.near_ref), channel_id=1, source_target_pairs={{3,0},{4,1},{1,2},{6,3},{7,4},{0,5},{5,6},{2,7},{11,8},{12,9},{9,1... | collective-permute-start | bytes 98312 | tf_op jit(solution)/shard_map/ppermute | solution.py:317
  16.2 1.3 %collective-permute-start.7 = (bf16[512,640]{1,0:T(8,128)(2,1)}, bf16[512,640]{1,0:T(8,128)(2,1)S(1)}, u32[]{:S(2)}, u32[]{:S(2)}) collective-permute-start(bf16[512,640]{1,0:T(8,128)(2,1)} %get-tuple-element.24), channel_id=1, source_target_pairs={{0,2},{1,5},{2,0},{3,7},{4,6},{5,1},{6,4},{7,3},{8,10},{9,13},{10,... | collective-permute-start | bytes 1966088 | tf_op jit(solution)/shard_map/ppermute | solution.py:317
  17.6 1.1 %collective-permute-done.1.far_ref = bf16[2,64,128]{2,1,0:T(8,128)(2,1)S(1)} collective-permute-done((bf16[2,64,128]{2,1,0:T(8,128)(2,1)S(1)}, bf16[2,64,128]{2,1,0:T(8,128)(2,1)S(1)}, u32[]{:S(2)}, u32[]{:S(2)}) %collective-permute-start.1) | collective-permute-done | bytes 32800 | tf_op jit(solution)/shard_map/ppermute | solution.py:317
  18.7 2.3 %collective-permute-done.3.refs_1_.refs_2_ = bf16[512,640]{1,0:T(8,128)(2,1)} collective-permute-done((bf16[512,640]{1,0:T(8,128)(2,1)}, bf16[512,640]{1,0:T(8,128)(2,1)}, u32[]{:S(2)}, u32[]{:S(2)}) %collective-permute-start.3) | collective-permute-done | bytes 655392 | tf_op jit(solution)/shard_map/ppermute | solution.py:317
  21.3 1.5 %collective-permute-start.4 = (f32[48,128]{1,0:T(8,128)S(1)}, f32[48,128]{1,0:T(8,128)S(1)}, u32[]{:S(2)}, u32[]{:S(2)}) collective-permute-start(f32[48,128]{1,0:T(8,128)S(1)} %totals.1), channel_id=1, source_target_pairs={{0,4},{1,3},{2,6},{3,1},{4,0},{5,7},{6,2},{7,5},{8,12},{9,11},{10,... | collective-permute-start | bytes 73736 | tf_op jit(solution)/shard_map/ppermute | solution.py:317
  22.7 2.0 %collective-permute-done.4 = f32[48,128]{1,0:T(8,128)S(1)} collective-permute-done((f32[48,128]{1,0:T(8,128)S(1)}, f32[48,128]{1,0:T(8,128)S(1)}, u32[]{:S(2)}, u32[]{:S(2)}) %collective-permute-start.4) | collective-permute-done | bytes 24608 | tf_op jit(solution)/shard_map/ppermute | solution.py:317
  25.4 1.3 %collective-permute-start.6 = (f32[48,128]{1,0:T(8,128)S(1)}, f32[48,128]{1,0:T(8,128)S(1)}, u32[]{:S(2)}, u32[]{:S(2)}) collective-permute-start(f32[48,128]{1,0:T(8,128)S(1)} %add.11.here_ref), channel_id=1, source_target_pairs={{0,1},{2,3},{4,5},{6,7},{8,9},{10,11},{12,13},{14,15},{16,17},{18,... | collective-permute-start | bytes 73736 | tf_op jit(solution)/shard_map/ppermute | solution.py:317
  26.7 8.5 %collective-permute-done.6.told_ref = f32[48,128]{1,0:T(8,128)S(1)} collective-permute-done((f32[48,128]{1,0:T(8,128)S(1)}, f32[48,128]{1,0:T(8,128)S(1)}, u32[]{:S(2)}, u32[]{:S(2)}) %collective-permute-start.6) | collective-permute-done | bytes 24608 | tf_op jit(solution)/shard_map/ppermute | solution.py:317
  35.5 2.4 %moments.2 = (f32[2,112,640]{2,1,0:T(8,128)S(1)}, f32[2,112,640]{2,1,0:T(8,128)S(1)}) custom-call(bf16[512,640]{1,0:T(8,128)(2,1)S(1)} %copy-done.5, bf16[2,512,640]{2,1,0:T(8,128)(2,1)S(1)} %copy-done.2, bf16[512,640]{1,0:T(8,128)(2,1)} %collective-permute-done.3.refs_1_.refs_2_, bf16[512,640]{1,0:T(8,128)(2,1)} %collective-permute-done.10.refs_3_, ...), custom_call_target="tpu_custom_call" | custom-call | bytes 6291456 | tf_op jit(solution)/shard_map/moments/pallas_call | solution.py:241
  37.9 1.6 %collective-permute-start.11 = (f32[2,112,640]{2,1,0:T(8,128)S(1)}, f32[2,112,640]{2,1,0:T(8,128)S(1)}, u32[]{:S(2)}, u32[]{:S(2)}) collective-permute-start(f32[2,112,640]{2,1,0:T(8,128)S(1)} %get-tuple-element.30), channel_id=1, source_target_pairs={{0,4},{1,3},{2,6},{3,1},{4,0},{5,7},{6,2},{7,5},{8,12},{9,11},{10,... | collective-permute-start | bytes 1720328 | tf_op jit(solution)/shard_map/ppermute | solution.py:317
  39.6 1.6 %collective-permute-start.8 = (bf16[512,640]{1,0:T(8,128)(2,1)S(1)}, bf16[512,640]{1,0:T(8,128)(2,1)S(1)}, u32[]{:S(2)}, u32[]{:S(2)}) collective-permute-start(bf16[512,640]{1,0:T(8,128)(2,1)S(1)} %slice_bitcast_fusion.1), channel_id=1, source_target_pairs={{0,2},{1,5},{2,0},{3,7},{4,6},{5,1},{6,4},{7,3},{8,10},{9,13},{10,... | collective-permute-start | bytes 1966088 | tf_op jit(solution)/shard_map/ppermute | solution.py:317
  41.2 9.0 %collective-permute-done.11.right_ref = f32[2,112,640]{2,1,0:T(8,128)S(1)} collective-permute-done((f32[2,112,640]{2,1,0:T(8,128)S(1)}, f32[2,112,640]{2,1,0:T(8,128)S(1)}, u32[]{:S(2)}, u32[]{:S(2)}) %collective-permute-start.11) | collective-permute-done | bytes 573472 | tf_op jit(solution)/shard_map/ppermute | solution.py:317
  50.3 3.2 %collective-permute-start.12 = (f32[2,112,640]{2,1,0:T(8,128)S(1)}, f32[2,112,640]{2,1,0:T(8,128)S(1)}, u32[]{:S(2)}, u32[]{:S(2)}) collective-permute-start(f32[2,112,640]{2,1,0:T(8,128)S(1)} %add.14.refs_7_), channel_id=1, source_target_pairs={{0,8},{1,9},{2,10},{3,11},{4,12},{5,13},{6,14},{7,15},{8,0},{9,1},... | collective-permute-start | bytes 1720328 | tf_op jit(solution)/shard_map/ppermute | solution.py:317
  54.3 1.1 %moments.3 = (f32[112,640]{1,0:T(8,128)S(1)}, f32[112,640]{1,0:T(8,128)S(1)}, f32[112,640]{1,0:T(8,128)S(1)}, f32[112,640]{1,0:T(8,128)S(1)}) custom-call(bf16[512,640]{1,0:T(8,128)(2,1)S(1)} %copy-done.4, bf16[2,512,640]{2,1,0:T(8,128)(2,1)S(1)} %collective-permute-done.2.refs_0_.refs_1_, bf16[512,640]{1,0:T(8,128)(2,1)S(1)} %collective-permute-done.7.refs_0_.refs_2_, ...), custom_call_target="tpu_custom_call" | custom-call | bytes 6291456 | tf_op jit(solution)/shard_map/moments/pallas_call | solution.py:241
  55.4 1.3 %collective-permute-start.13 = (f32[112,640]{1,0:T(8,128)S(1)}, f32[112,640]{1,0:T(8,128)S(1)}, u32[]{:S(2)}, u32[]{:S(2)}) collective-permute-start(f32[112,640]{1,0:T(8,128)S(1)} %get-tuple-element.32), channel_id=1, source_target_pairs={{0,4},{1,3},{2,6},{3,1},{4,0},{5,7},{6,2},{7,5},{8,12},{9,11},{10,... | collective-permute-start | bytes 860168 | tf_op jit(solution)/shard_map/ppermute | solution.py:317
  56.7 4.5 %collective-permute-start.15 = (f32[112,640]{1,0:T(8,128)S(1)}, f32[112,640]{1,0:T(8,128)S(1)}, u32[]{:S(2)}, u32[]{:S(2)}) collective-permute-start(f32[112,640]{1,0:T(8,128)S(1)} %get-tuple-element.34), channel_id=1, source_target_pairs={{0,5},{1,2},{2,7},{3,0},{4,1},{5,6},{6,3},{7,4},{8,13},{9,10},{10,... | collective-permute-start | bytes 860168 | tf_op jit(solution)/shard_map/ppermute | solution.py:317
  61.2 15.3 %collective-permute-done.12 = f32[2,112,640]{2,1,0:T(8,128)S(1)} collective-permute-done((f32[2,112,640]{2,1,0:T(8,128)S(1)}, f32[2,112,640]{2,1,0:T(8,128)S(1)}, u32[]{:S(2)}, u32[]{:S(2)}) %collective-permute-start.12) | collective-permute-done | bytes 573472 | tf_op jit(solution)/shard_map/ppermute | solution.py:317
  76.5 3.3 %collective-permute-start.14 = (f32[112,640]{1,0:T(8,128)S(1)}, f32[112,640]{1,0:T(8,128)S(1)}, u32[]{:S(2)}, u32[]{:S(2)}) collective-permute-start(f32[112,640]{1,0:T(8,128)S(1)} %fusion), channel_id=1, source_target_pairs={{0,1},{1,0},{2,3},{3,2},{4,5},{5,4},{6,7},{7,6},{8,9},{9,8},{10,11... | collective-permute-start | bytes 860168 | tf_op jit(solution)/shard_map/ppermute | solution.py:317
  79.9 1.2 %collective-permute-done.14.refs_3_ = f32[112,640]{1,0:T(8,128)S(1)} collective-permute-done((f32[112,640]{1,0:T(8,128)S(1)}, f32[112,640]{1,0:T(8,128)S(1)}, u32[]{:S(2)}, u32[]{:S(2)}) %collective-permute-start.14) | collective-permute-done | bytes 286752 | tf_op jit(solution)/shard_map/ppermute | solution.py:317
  81.1 1.6 %finish.1 = f32[48,1,1248]{2,1,0:T(1,128)} custom-call(s32[48,1]{1,0:T(8,128)S(1)} %copy.7.pick_ref, f32[3,48,128]{2,1,0:T(8,128)S(1)} %get-tuple-element.22.refs_6_.stats_ref, f32[112,640]{1,0:T(8,128)S(1)} %get-tuple-element.31.refs_0_, f32[112,640]{1,0:T(8,128)S(1)} %slice_bitcast_fusion.3.refs_1_, f32[112,640]{1,0:T(8,128)S(1)} %collective-permute-done.13.refs_2_, ...), custom_call_target="tpu_custom_call" | custom-call | bytes 16384 | tf_op jit(solution)/shard_map/finish/pallas_call | solution.py:296
  (44 shorter events, 5.3 us)
Async XLA Ops:
  0.0 4.2 %copy-start.6 = (s32[128,48]{0,1:T(8,128)S(1)}, s32[128,48]{0,1:T(8,128)}, u32[]{:S(2)}) copy-start(s32[128,48]{0,1:T(8,128)} %param.6) | copy-start | bytes 73732
  0.0 4.2 %copy-start.7 = (bf16[128,16]{0,1:T(8,128)(2,1)S(1)}, bf16[128,16]{0,1:T(8,128)(2,1)}, u32[]{:S(2)}) copy-start(bf16[128,16]{0,1:T(8,128)(2,1)} %param.5) | copy-start | bytes 12292
  0.0 6.9 %copy-start = (bf16[128,19968]{1,0:T(8,128)(2,1)S(1)}, bf16[128,19968]{1,0:T(8,128)(2,1)}, u32[]{:S(2)}) copy-start(bf16[128,19968]{1,0:T(8,128)(2,1)} %x_hbm.3) | copy-start | bytes 15335428
  4.1 7.9 %collective-permute-start.9 = (bf16[2,512,640]{2,1,0:T(8,128)(2,1)}, bf16[2,512,640]{2,1,0:T(8,128)(2,1)S(1)}, u32[]{:S(2)}, u32[]{:S(2)}) collective-permute-start(bf16[2,512,640]{2,1,0:T(8,128)(2,1)} %get-tuple-element.28), channel_id=1, source_target_pairs={{0,1},{1,0},{2,3},{3,2},{4,5},{5,4},{6,7},{7,6},{8,9},{9,8},{10,11... | collective-permute-start | bytes 3932168 | tf_op jit(solution)/shard_map/ppermute | solution.py:317
  4.3 2.7 %collective-permute-start = (bf16[64,128]{1,0:T(8,128)(2,1)S(1)}, bf16[64,128]{1,0:T(8,128)(2,1)S(1)}, u32[]{:S(2)}, u32[]{:S(2)}) collective-permute-start(bf16[64,128]{1,0:T(8,128)(2,1)S(1)} %get-tuple-element.36), channel_id=1, source_target_pairs={{0,1},{1,0},{2,3},{3,2},{4,5},{5,4},{6,7},{7,6},{8,9},{9,8},{10,11... | collective-permute-start | bytes 49160 | tf_op jit(solution)/shard_map/ppermute | solution.py:317
  9.2 7.1 %copy-start.3 = (bf16[512,640]{1,0:T(8,128)(2,1)}, bf16[512,640]{1,0:T(8,128)(2,1)S(1)}, u32[]{:S(2)}) copy-start(bf16[512,640]{1,0:T(8,128)(2,1)S(1)} %get-tuple-element.23.refs_0_) | copy-start | bytes 1966084
  9.2 8.3 %copy-start.8 = (s32[48]{0:T(128)S(1)}, s32[48]{0:T(128)}, u32[]{:S(2)}) copy-start(s32[48]{0:T(128)} %param.7) | copy-start | bytes 580
  9.2 11.8 %collective-permute-start.2 = (bf16[2,512,640]{2,1,0:T(8,128)(2,1)}, bf16[2,512,640]{2,1,0:T(8,128)(2,1)S(1)}, u32[]{:S(2)}, u32[]{:S(2)}) collective-permute-start(bf16[2,512,640]{2,1,0:T(8,128)(2,1)} %get-tuple-element.20), channel_id=1, source_target_pairs={{0,1},{1,0},{2,3},{3,2},{4,5},{5,4},{6,7},{7,6},{8,9},{9,8},{10,11... | collective-permute-start | bytes 3932168 | tf_op jit(solution)/shard_map/ppermute | solution.py:317
  9.7 11.3 %collective-permute-start.3 = (bf16[512,640]{1,0:T(8,128)(2,1)}, bf16[512,640]{1,0:T(8,128)(2,1)}, u32[]{:S(2)}, u32[]{:S(2)}) collective-permute-start(bf16[512,640]{1,0:T(8,128)(2,1)} %get-tuple-element.21), channel_id=1, source_target_pairs={{0,2},{1,5},{2,0},{3,7},{4,6},{5,1},{6,4},{7,3},{8,10},{9,13},{10,... | collective-permute-start | bytes 1966088 | tf_op jit(solution)/shard_map/ppermute | solution.py:317
  14.0 21.5 %collective-permute-start.10 = (bf16[512,640]{1,0:T(8,128)(2,1)}, bf16[512,640]{1,0:T(8,128)(2,1)}, u32[]{:S(2)}, u32[]{:S(2)}) collective-permute-start(bf16[512,640]{1,0:T(8,128)(2,1)} %slice_bitcast_fusion), channel_id=1, source_target_pairs={{0,2},{1,5},{2,0},{3,7},{4,6},{5,1},{6,4},{7,3},{8,10},{9,13},{10,... | collective-permute-start | bytes 1966088 | tf_op jit(solution)/shard_map/ppermute | solution.py:317
  14.0 21.5 %copy-start.2 = (bf16[2,512,640]{2,1,0:T(8,128)(2,1)S(1)}, bf16[2,512,640]{2,1,0:T(8,128)(2,1)}, u32[]{:S(2)}) copy-start(bf16[2,512,640]{2,1,0:T(8,128)(2,1)} %copy-done.1) | copy-start | bytes 3932164
  14.0 4.7 %collective-permute-start.1 = (bf16[2,64,128]{2,1,0:T(8,128)(2,1)S(1)}, bf16[2,64,128]{2,1,0:T(8,128)(2,1)S(1)}, u32[]{:S(2)}, u32[]{:S(2)}) collective-permute-start(bf16[2,64,128]{2,1,0:T(8,128)(2,1)S(1)} %pad_maximum_fusion.refs_0_.near_ref), channel_id=1, source_target_pairs={{3,0},{4,1},{1,2},{6,3},{7,4},{0,5},{5,6},{2,7},{11,8},{12,9},{9,1... | collective-permute-start | bytes 98312 | tf_op jit(solution)/shard_map/ppermute | solution.py:317
  16.2 24.9 %collective-permute-start.7 = (bf16[512,640]{1,0:T(8,128)(2,1)}, bf16[512,640]{1,0:T(8,128)(2,1)S(1)}, u32[]{:S(2)}, u32[]{:S(2)}) collective-permute-start(bf16[512,640]{1,0:T(8,128)(2,1)} %get-tuple-element.24), channel_id=1, source_target_pairs={{0,2},{1,5},{2,0},{3,7},{4,6},{5,1},{6,4},{7,3},{8,10},{9,13},{10,... | collective-permute-start | bytes 1966088 | tf_op jit(solution)/shard_map/ppermute | solution.py:317
  17.6 17.9 %copy-start.5 = (bf16[512,640]{1,0:T(8,128)(2,1)S(1)}, bf16[512,640]{1,0:T(8,128)(2,1)}, u32[]{:S(2)}) copy-start(bf16[512,640]{1,0:T(8,128)(2,1)} %get-tuple-element.27.refs_0_) | copy-start | bytes 1966084
  21.3 3.5 %collective-permute-start.4 = (f32[48,128]{1,0:T(8,128)S(1)}, f32[48,128]{1,0:T(8,128)S(1)}, u32[]{:S(2)}, u32[]{:S(2)}) collective-permute-start(f32[48,128]{1,0:T(8,128)S(1)} %totals.1), channel_id=1, source_target_pairs={{0,4},{1,3},{2,6},{3,1},{4,0},{5,7},{6,2},{7,5},{8,12},{9,11},{10,... | collective-permute-start | bytes 73736 | tf_op jit(solution)/shard_map/ppermute | solution.py:317
  24.7 0.7 collective-permute-start.5
  25.4 9.8 %collective-permute-start.6 = (f32[48,128]{1,0:T(8,128)S(1)}, f32[48,128]{1,0:T(8,128)S(1)}, u32[]{:S(2)}, u32[]{:S(2)}) collective-permute-start(f32[48,128]{1,0:T(8,128)S(1)} %add.11.here_ref), channel_id=1, source_target_pairs={{0,1},{2,3},{4,5},{6,7},{8,9},{10,11},{12,13},{14,15},{16,17},{18,... | collective-permute-start | bytes 73736 | tf_op jit(solution)/shard_map/ppermute | solution.py:317
  37.9 12.3 %collective-permute-start.11 = (f32[2,112,640]{2,1,0:T(8,128)S(1)}, f32[2,112,640]{2,1,0:T(8,128)S(1)}, u32[]{:S(2)}, u32[]{:S(2)}) collective-permute-start(f32[2,112,640]{2,1,0:T(8,128)S(1)} %get-tuple-element.30), channel_id=1, source_target_pairs={{0,4},{1,3},{2,6},{3,1},{4,0},{5,7},{6,2},{7,5},{8,12},{9,11},{10,... | collective-permute-start | bytes 1720328 | tf_op jit(solution)/shard_map/ppermute | solution.py:317
  39.6 14.7 %copy-start.4 = (bf16[512,640]{1,0:T(8,128)(2,1)S(1)}, bf16[512,640]{1,0:T(8,128)(2,1)}, u32[]{:S(2)}) copy-start(bf16[512,640]{1,0:T(8,128)(2,1)} %copy-done.3) | copy-start | bytes 1966084
  39.6 14.7 %collective-permute-start.8 = (bf16[512,640]{1,0:T(8,128)(2,1)S(1)}, bf16[512,640]{1,0:T(8,128)(2,1)S(1)}, u32[]{:S(2)}, u32[]{:S(2)}) collective-permute-start(bf16[512,640]{1,0:T(8,128)(2,1)S(1)} %slice_bitcast_fusion.1), channel_id=1, source_target_pairs={{0,2},{1,5},{2,0},{3,7},{4,6},{5,1},{6,4},{7,3},{8,10},{9,13},{10,... | collective-permute-start | bytes 1966088 | tf_op jit(solution)/shard_map/ppermute | solution.py:317
  50.3 26.2 %collective-permute-start.12 = (f32[2,112,640]{2,1,0:T(8,128)S(1)}, f32[2,112,640]{2,1,0:T(8,128)S(1)}, u32[]{:S(2)}, u32[]{:S(2)}) collective-permute-start(f32[2,112,640]{2,1,0:T(8,128)S(1)} %add.14.refs_7_), channel_id=1, source_target_pairs={{0,8},{1,9},{2,10},{3,11},{4,12},{5,13},{6,14},{7,15},{8,0},{9,1},... | collective-permute-start | bytes 1720328 | tf_op jit(solution)/shard_map/ppermute | solution.py:317
  55.4 24.5 %collective-permute-start.13 = (f32[112,640]{1,0:T(8,128)S(1)}, f32[112,640]{1,0:T(8,128)S(1)}, u32[]{:S(2)}, u32[]{:S(2)}) collective-permute-start(f32[112,640]{1,0:T(8,128)S(1)} %get-tuple-element.32), channel_id=1, source_target_pairs={{0,4},{1,3},{2,6},{3,1},{4,0},{5,7},{6,2},{7,5},{8,12},{9,11},{10,... | collective-permute-start | bytes 860168 | tf_op jit(solution)/shard_map/ppermute | solution.py:317
  56.7 23.2 %collective-permute-start.15 = (f32[112,640]{1,0:T(8,128)S(1)}, f32[112,640]{1,0:T(8,128)S(1)}, u32[]{:S(2)}, u32[]{:S(2)}) collective-permute-start(f32[112,640]{1,0:T(8,128)S(1)} %get-tuple-element.34), channel_id=1, source_target_pairs={{0,5},{1,2},{2,7},{3,0},{4,1},{5,6},{6,3},{7,4},{8,13},{9,10},{10,... | collective-permute-start | bytes 860168 | tf_op jit(solution)/shard_map/ppermute | solution.py:317
  76.5 4.5 %collective-permute-start.14 = (f32[112,640]{1,0:T(8,128)S(1)}, f32[112,640]{1,0:T(8,128)S(1)}, u32[]{:S(2)}, u32[]{:S(2)}) collective-permute-start(f32[112,640]{1,0:T(8,128)S(1)} %fusion), channel_id=1, source_target_pairs={{0,1},{1,0},{2,3},{3,2},{4,5},{5,4},{6,7},{7,6},{8,9},{9,8},{10,11... | collective-permute-start | bytes 860168 | tf_op jit(solution)/shard_map/ppermute | solution.py:317
  (1 other events, 1.1 us)

commit v7 on v6

--- a/solution.py
+++ b/solution.py
@@ -34,63 +34,51 @@
         return [(d, d ^ mask) for d in range(self.n)]
 
 
-def pack_kernel(plan, chunk, x_hbm, *refs):
-    kept_ref, sent_ref, other_ref, x_ref, sems = refs[-5:]
+def pack_kernel(
+    plan, x_ref, kept0_ref, kept1_ref, sent0_ref, sent1_ref, other0_ref, other1_ref
+):
     step = pl.program_id(0)
     me = lax.axis_index("pat")
     rows, columns = x_ref.shape
     last_tile = columns // LANES - 1
-    start = ((me >> plan.top_bit) ^ chunk) * columns
     lane = lax.broadcasted_iota(jnp.int32, (rows, LANES), 1)
-
-    @pl.when(step == 0)
-    def _():
-        count = sems.shape[0]
-        edges = [columns // LANES * piece // count * LANES for piece in range(count + 1)]
-        copies = []
-        for number in range(count):
-            width = edges[number + 1] - edges[number]
-            there = pl.ds(pl.multiple_of(start + edges[number], LANES), width)
-            copies.append(
-                pltpu.make_async_copy(
-                    x_hbm.at[:, there], x_ref.at[:, pl.ds(edges[number], width)], sems.at[number]
-                )
-            )
-        for copy in copies:
-            copy.start()
-        for copy in copies:
-            copy.wait()
 
     def tile(index):
         return pl.ds(pl.multiple_of(jnp.minimum(index, last_tile) * LANES, LANES), LANES)
 
-    middle = len(plan.middle_bits)
     for away in range(2):
         side = (me & 1) ^ away
         holder = me ^ away
         for sent in range(2):
-            relative = (
-                (step >> (1 + middle))
-                | (sent << (1 + side))
-                | ((step & 1) << (2 - side))
-                | (((step >> 1) & ((1 << middle) - 1)) << 3)
-                | (chunk << plan.top_bit)
-            )
-            column = (holder ^ relative) * plan.block - start
-            first = column // LANES
-            edge = (column - first * LANES) * (1 - side)
-            head = x_ref[:, tile(first + side * plan.share)]
-            tail = x_ref[:, tile(first + plan.tiles)]
-            folded = jnp.where(lane >= edge, head.astype(jnp.float32), tail.astype(jnp.float32))
-            target = other_ref.at[sent] if away else (kept_ref, sent_ref)[sent]
-            target[:, 0:LANES] = folded.astype(x_ref.dtype)
-            for slot in range(1, plan.share):
-                here = slice(slot * LANES, (slot + 1) * LANES)
-                target[:, here] = x_ref[:, tile(first + side * plan.share + slot)]
-
-
-def pack(covariates, plan, chunk, after):
-    rows, columns = covariates.shape
+            for chunk in range(2):
+                middle = len(plan.middle_bits)
+                relative = (
+                    (step >> (1 + middle))
+                    | (sent << (1 + side))
+                    | ((step & 1) << (2 - side))
+                    | (((step >> 1) & ((1 << middle) - 1)) << 3)
+                    | (chunk << plan.top_bit)
+                )
+                column = (holder ^ relative) * plan.block
+                first = column // LANES
+                edge = (column - first * LANES) * (1 - side)
+                head = x_ref[:, tile(first + side * plan.share)]
+                tail = x_ref[:, tile(first + plan.tiles)]
+                folded = jnp.where(lane >= edge, head.astype(jnp.float32), tail.astype(jnp.float32))
+                if away:
+                    target = (other0_ref, other1_ref)[chunk].at[sent]
+                elif sent:
+                    target = (sent0_ref, sent1_ref)[chunk]
+                else:
+                    target = (kept0_ref, kept1_ref)[chunk]
+                target[:, 0:LANES] = folded.astype(x_ref.dtype)
+                for slot in range(1, plan.share):
+                    here = slice(slot * LANES, (slot + 1) * LANES)
+                    target[:, here] = x_ref[:, tile(first + side * plan.share + slot)]
+
+
+def pack(covariates, plan):
+    rows = covariates.shape[0]
     dtype = covariates.dtype
     length = plan.places * rows
     mine = jax.ShapeDtypeStruct((length, plan.width), dtype)
@@ -98,20 +86,17 @@
     mine_spec = pl.BlockSpec((rows, plan.width), lambda s: (s, 0))
     other_spec = pl.BlockSpec((2, rows, plan.width), lambda s: (0, s, 0))
     return pl.pallas_call(
-        functools.partial(pack_kernel, plan, chunk),
+        functools.partial(pack_kernel, plan),
         grid=(plan.places,),
-        in_specs=[pl.BlockSpec(memory_space=pl.ANY)] * (1 + len(after)),
-        out_specs=[mine_spec] * 2 + [other_spec],
-        out_shape=[mine] * 2 + [other],
-        scratch_shapes=[
-            pltpu.VMEM((rows, columns // 2), dtype), pltpu.SemaphoreType.DMA((3,))
-        ],
-        compiler_params=pltpu.CompilerParams(vmem_limit_bytes=(58 if chunk else 10) << 20),
+        in_specs=[pl.BlockSpec(memory_space=pltpu.VMEM)],
+        out_specs=[mine_spec] * 4 + [other_spec] * 2,
+        out_shape=[mine] * 4 + [other] * 2,
+        compiler_params=pltpu.CompilerParams(vmem_limit_bytes=12 << 20),
         cost_estimate=pl.CostEstimate(
             flops=0, bytes_accessed=4 * covariates.size, transcendentals=0
         ),
         name="pack",
-    )(covariates, *after)
+    )(covariates)
 
 
 def onehot_of(pick_ref, weightings, dtype):
@@ -134,36 +119,59 @@
         in_specs=[vmem] * len(operands) + [pl.BlockSpec(memory_space=pl.ANY)] * len(after),
         out_specs=[vmem] * len(shapes),
         out_shape=[jax.ShapeDtypeStruct(shape, dtype) for shape, dtype in shapes],
-        compiler_params=pltpu.CompilerParams(vmem_limit_bytes=4 << 20),
+        compiler_params=pltpu.CompilerParams(vmem_limit_bytes=8 << 20),
         cost_estimate=pl.CostEstimate(flops=0, bytes_accessed=1 << 14, transcendentals=0),
         name=name,
     )(*operands, *after)
 
 
-def totals_kernel(weightings, pick_ref, near_ref, far_ref, *refs):
-    out_ref = refs[-1]
+def lighter_of(totals):
+    return jnp.where(totals[:, 0:1] <= totals[:, 1:2], 1.0, 0.0)
+
+
+def lighter_panel(ref, members, onehot, light):
+    comps, weightings = onehot.shape
+    columns = []
+    for place, member in enumerate(members):
+        weights, target, other = arm_columns(member, onehot)
+        here = slice(place * LANES, (place + 1) * LANES)
+        lighter = light * target + (1.0 - light) * other
+        ref[0:comps, here] = lighter.astype(jnp.bfloat16)
+        ref[comps:comps + weightings, here] = weights
+        columns.append((target, other))
+    return columns
+
+
+def members_of(near_ref, far_ref):
+    return (near_ref.at[0], near_ref.at[1], far_ref.at[1], far_ref.at[0])
+
+
+def group_kernel(weightings, pick_ref, near_ref, far_ref, totals_ref, panel_ref):
     onehot = onehot_of(pick_ref, weightings, jnp.bfloat16)
     target_sum, other_sum = 0.0, 0.0
-    for ref in (near_ref.at[0], near_ref.at[1], far_ref.at[0], far_ref.at[1]):
-        _, target, other = arm_columns(ref, onehot)
+    for member in members_of(near_ref, far_ref):
+        _, target, other = arm_columns(member, onehot)
         target_sum += target
         other_sum += other
-    lane = lax.broadcasted_iota(jnp.int32, out_ref.shape, 1)
-    out_ref[...] = jnp.where(
+    lane = lax.broadcasted_iota(jnp.int32, totals_ref.shape, 1)
+    totals = jnp.where(
         lane == 0,
         jnp.sum(target_sum, axis=1, keepdims=True),
         jnp.sum(other_sum, axis=1, keepdims=True),
     )
-
-
-def group_totals(near, far, pick_column, weightings, after):
+    totals_ref[...] = totals
+    lighter_panel(panel_ref, members_of(near_ref, far_ref), onehot, lighter_of(totals))
+
+
+def make_group(near, far, pick_column, weightings):
+    comps = pick_column.shape[0]
     return small_call(
-        functools.partial(totals_kernel, weightings),
-        [((pick_column.shape[0], LANES), jnp.float32)],
+        functools.partial(group_kernel, weightings),
+        [((comps, LANES), jnp.float32), ((comps + weightings, 4 * LANES), jnp.bfloat16)],
         [pick_column, near, far],
-        after,
-        "totals",
-    )[0]
+        [],
+        "group",
+    )
 
 
 def panel_kernel(weightings, pick_ref, near_ref, far_ref, here_ref, told_ref, *refs):
@@ -172,18 +180,13 @@
     onehot = onehot_of(pick_ref, weightings, jnp.bfloat16)
     side = jnp.full(here_ref.shape, lax.axis_index("pat") & 1)
     totals = jnp.where(side == 0, here_ref[...], told_ref[...])
-    total_target, total_other = totals[:, 0:1], totals[:, 1:2]
-    light = jnp.where(total_target <= total_other, 1.0, 0.0)
-    stats_ref[0] = jnp.broadcast_to(1.0 / total_target, (comps, LANES))
-    stats_ref[1] = jnp.broadcast_to(1.0 / total_other, (comps, LANES))
+    light = lighter_of(totals)
+    stats_ref[0] = jnp.broadcast_to(1.0 / totals[:, 0:1], (comps, LANES))
+    stats_ref[1] = jnp.broadcast_to(1.0 / totals[:, 1:2], (comps, LANES))
     stats_ref[2] = jnp.broadcast_to(light, (comps, LANES))
-    members = (near_ref.at[0], near_ref.at[1], far_ref.at[1], far_ref.at[0])
-    for place, ref in enumerate(members):
-        weights, target, other = arm_columns(ref, onehot)
-        lighter = light * target + (1.0 - light) * other
+    columns = lighter_panel(first_ref, members_of(near_ref, far_ref), onehot, light)
+    for place, (target, other) in enumerate(columns):
         here = slice(place * LANES, (place + 1) * LANES)
-        first_ref[0:comps, here] = lighter.astype(jnp.bfloat16)
-        first_ref[comps:comps + weightings, here] = weights
         second_ref[0:comps, here] = target.astype(jnp.bfloat16)
         second_ref[comps:2 * comps, here] = other.astype(jnp.bfloat16)
 
@@ -201,6 +204,55 @@
         [],
         "panels",
     )
+
+
+def both_arms(sums, onehot, light):
+    comps, weightings = onehot.shape
+    lighter = sums[0:comps]
+    both = jnp.dot(
+        onehot,
+        sums[comps:comps + weightings],
+        precision=lax.Precision.HIGHEST,
+        preferred_element_type=jnp.float32,
+    )
+    target = jnp.where(light, lighter, both - lighter)
+    return target, jnp.where(light, both - lighter, lighter)
+
+
+def meet_kernel(pick_ref, near_ref, far_ref, stats_ref, left_ref, right_ref, *refs):
+    out_ref = refs[-1]
+    comps = pick_ref.shape[0]
+    rows = left_ref.shape[1] // 2
+    onehot = onehot_of(pick_ref, rows - comps, jnp.float32)
+    light = stats_ref[2][:, 0:1] > 0.5
+    for block in range(left_ref.shape[0]):
+        arms = []
+        for moment in range(2):
+            here = slice(moment * rows, (moment + 1) * rows)
+            target, other = 0.0, 0.0
+            for ref, totals_ref in ((left_ref, near_ref), (right_ref, far_ref)):
+                more = both_arms(ref[block, here, :], onehot, lighter_of(totals_ref[...]) > 0.5)
+                target, other = target + more[0], other + more[1]
+            arms.append((target, other))
+        out_ref[block, 0:comps, :] = jnp.where(light, arms[0][0], arms[0][1])
+        out_ref[block, comps:rows, :] = (
+            left_ref[block, comps:rows, :] + right_ref[block, comps:rows, :]
+        )
+        out_ref[block, rows:rows + comps, :] = (
+            arms[1][0] * stats_ref[0][:, 0:1] + arms[1][1] * stats_ref[1][:, 0:1]
+        )
+
+
+def meet(pick_column, near_totals, far_totals, stats, left, right, after):
+    blocks, rows, width = left.shape
+    out = (blocks, rows // 2 + pick_column.shape[0], width)
+    return small_call(
+        meet_kernel,
+        [(out, jnp.float32)],
+        [pick_column, near_totals, far_totals, stats, left, right],
+        after,
+        "meet",
+    )[0]
 
 
 def whole_spec(shape):
@@ -229,6 +281,42 @@
         out[first_rows:first_rows + comps, :] = (
             second[0:comps] * inverse_target + second[comps:2 * comps] * inverse_other
         )
+
+
+def group_moments_kernel(rows, *refs):
+    kept_ref, passed_ref, *swapped_refs, panel_ref = refs[:5]
+    outs = refs[-2:]
+    height = panel_ref.shape[0]
+    for place in range(kept_ref.shape[0] // rows):
+        here = slice(place * rows, (place + 1) * rows)
+        x = jnp.concatenate(
+            [kept_ref[here, :], passed_ref[0, here, :]]
+            + [ref[here, :] for ref in swapped_refs],
+            axis=0,
+        )
+        squares = (x.astype(jnp.float32) * x.astype(jnp.float32)).astype(jnp.bfloat16)
+        out = outs[place % 2].at[place // 2]
+        out[0:height, :] = jnp.dot(panel_ref[...], x, preferred_element_type=jnp.float32)
+        out[height:2 * height, :] = jnp.dot(
+            panel_ref[...], squares, preferred_element_type=jnp.float32
+        )
+
+
+def group_moments(plan, rows_here, panel, after):
+    rows = panel.shape[1] // 4
+    out = jax.ShapeDtypeStruct(
+        (plan.places // 2, 2 * panel.shape[0], plan.width), jnp.float32
+    )
+    return pl.pallas_call(
+        functools.partial(group_moments_kernel, rows),
+        in_specs=[pl.BlockSpec(memory_space=pltpu.VMEM)] * 5
+        + [pl.BlockSpec(memory_space=pl.ANY)] * len(after),
+        out_specs=[pl.BlockSpec(memory_space=pltpu.VMEM)] * 2,
+        out_shape=[out] * 2,
+        compiler_params=pltpu.CompilerParams(vmem_limit_bytes=20 << 20),
+        cost_estimate=pl.CostEstimate(flops=0, bytes_accessed=6 << 20, transcendentals=0),
+        name="group_moments",
+    )(*rows_here, panel, *after)
 
 
 def moments(plan, rows_here, first, second, stats, split, after):
@@ -263,17 +351,10 @@
         for more in refs[1:count]:
             sums += more[...]
         refs = refs[count:]
-        lighter = sums[0:comps]
-        both = jnp.dot(
-            onehot,
-            sums[comps:comps + weightings],
-            precision=lax.Precision.HIGHEST,
-            preferred_element_type=jnp.float32,
-        )
+        target, other = both_arms(sums, onehot, light)
         spread = sums[comps + weightings:2 * comps + weightings]
-        heavier = both - lighter
-        mean_target = jnp.where(light, lighter, heavier) * inverse_target
-        mean_other = jnp.where(light, heavier, lighter) * inverse_other
+        mean_target = target * inverse_target
+        mean_other = other * inverse_other
         variance = spread - mean_target * mean_target - mean_other * mean_other
         pooled = jnp.maximum(variance / 2.0, 0.01)
         balance = (mean_target - mean_other) / jnp.sqrt(pooled)
@@ -305,14 +386,6 @@
     )(pick_column, stats, *operands)
 
 
-def add_kernel(left_ref, right_ref, *refs):
-    refs[-1][...] = left_ref[...] + right_ref[...]
-
-
-def add(left, right, after):
-    return small_call(add_kernel, [(left.shape, left.dtype)], [left, right], after, "add")[0]
-
-
 def swap(array, pairs):
     return lax.ppermute(array, "pat", pairs)
 
@@ -330,29 +403,29 @@
     near = jnp.stack([mine, swap(mine, to_other_side)])
     far = swap(near, [(pair ^ 1, d) for d, pair in plan.by_rows()])
 
-    rows_here, after = {}, []
-    for chunk in (1, 0):
-        kept, sent, other = pack(covariates, plan, chunk, after)
+    kept0, kept1, sent0, sent1, other0, other1 = pack(covariates, plan)
+    rows_here = {}
+    for chunk, kept, sent, other in ((1, kept1, sent1, other1), (0, kept0, sent0, other0)):
         passed = swap(other, to_other_side)
         rows_here[chunk] = [
             kept, passed, swap(sent, plan.by_rows()), swap(passed[1], plan.by_rows())
         ]
-        after = [near]
-
-    totals = group_totals(near, far, pick_column, weightings, [passed, rows_here[1][2]])
-    totals = totals + swap(totals, plan.by_sums())
+
+    near_totals, panel = make_group(near, far, pick_column, weightings)
+    far_totals = swap(near_totals, plan.by_sums())
+    totals = near_totals + far_totals
     for bit in plan.middle_bits + [plan.top_bit]:
         totals = totals + swap(totals, plan.by_mask(1 << bit)[0::2])
     told = swap(totals, to_other_side[0::2])
     first, second, stats = make_panels(near, far, totals, told, pick_column, weightings)
 
-    even, odd = moments(plan, rows_here[1], first, second, stats, False, [])
+    even, odd = group_moments(plan, rows_here[1], panel, [totals])
     arrived = swap(odd, plan.by_sums())
+    across = meet(
+        pick_column, near_totals, far_totals, stats, even, arrived, [rows_here[0][2]]
+    )
     for bit in plan.middle_bits:
-        odd = even[1::2] + arrived[1::2]
-        even = even[0::2] + arrived[0::2]
-        arrived = swap(odd, plan.by_mask(1 << bit))
-    across = add(even, arrived, [rows_here[0][2]])
+        across = across[0::2] + swap(across[1::2], plan.by_mask(1 << bit))
     top = swap(across, plan.by_mask(1 << plan.top_bit))
 
     last = not plan.middle_bits

time: 83.2 us -> 78.8 us (0.947)
  waiting for transfers between devices: 42.3 us -> 38.4 us
  local copies, waits for them, and re-layouts: 2.16 us -> 5.46 us
  Pallas kernels: 12.1 us -> 9.44 us
  starting transfers between devices: 26 us -> 24.7 us
    ppermute x16, waiting for transfers between devices: 42.3 us -> 38.4 us  [swap(): return lax.ppermute(array, 'pat', pairs)]
    unnamed x18 -> x14, local copies, waits for them, and re-layouts: 1.1 us -> 4.39 us
    pallas_call x2 -> x1, Pallas kernels: 3.5 us -> 1.1 us  [moments(): pl.pallas_call(functools.partial(moments_kernel, rows, plan.places if spl...]
    pallas_call x2, Pallas kernels: 6.35 us -> 4.99 us  [the longest x1 2.61 us: pack(): pl.pallas_call(functools.partial(pack_kernel, plan), grid=(plan.places,),...]
    ppermute x16, starting transfers between devices: 26 us -> 24.7 us  [swap(): return lax.ppermute(array, 'pat', pairs)]
    pallas_call x3, Pallas kernels: 0.59 us -> 1.74 us  [small_call(): pl.pallas_call(kernel, in_specs=[vmem] * len(operands) + [pl.BlockSpec(me...]
  transfers between devices with their start and end apart: 16 -> 16, of which waited for: 9 -> 8; matrix products, arithmetic and copies ran while one was open for 1% -> 1% of each run, Pallas kernels for 8% -> 7%
where the time goes in v7:
time: 78.8 us; the launch traced here: 78.2 us
  waiting for transfers between devices  38.4 us (49%)
  starting transfers between devices  24.7 us (31%)
  Pallas kernels  9.44 us (12%)
  local copies, waits for them, and re-layouts  5.46 us (7%)
    ppermute x16, waiting for transfers between devices, swap(): return lax.ppermute(array, 'pat', pairs)  38.4 us
    ppermute x16, starting transfers between devices, swap(): return lax.ppermute(array, 'pat', pairs)  24.7 us
    unnamed x14, local copies, waits for them, and re-layouts  4.39 us
    pallas_call x1, Pallas kernels, pack(): pl.pallas_call(functools.partial(pack_kernel, plan), grid=(plan.places,),...  2.61 us
    pallas_call x1, Pallas kernels, group_moments(): pl.pallas_call(functools.partial(group_moments_kernel, rows), in_specs=[p...  2.38 us
    pallas_call x3, Pallas kernels, small_call(): pl.pallas_call(kernel, in_specs=[vmem] * len(operands) + [pl.BlockSpec(me...  1.74 us
    pallas_call x1, Pallas kernels, finish(): pl.pallas_call(functools.partial(finish_kernel, plan, weightings, [len(pa...  1.61 us
  transfers between devices with their start and end apart: 16, of which 8 were waited for; matrix products, arithmetic and copies ran while one was open for 1% of the time, Pallas kernels for 7%

profile of v7, /device:TPU:1, one launch (start us, length us, event | category | flops | bytes accessed | tf_op | source)
XLA Modules:
  0.0 78.2 jit_solution(2441184039796815862)
XLA Ops:
  0.0 2.4 %copy-done = bf16[128,19968]{1,0:T(8,128)(2,1)S(1)} copy-done((bf16[128,19968]{1,0:T(8,128)(2,1)S(1)}, bf16[128,19968]{1,0:T(8,128)(2,1)}, u32[]{:S(2)}) %copy-start) | copy-done | bytes 5111832
  2.5 2.6 %pack.1 = (bf16[512,640]{1,0:T(8,128)(2,1)S(1)}, bf16[512,640]{1,0:T(8,128)(2,1)S(1)}, bf16[512,640]{1,0:T(8,128)(2,1)S(1)}, bf16[512,640]{1,0:T(8,128)(2,1)}, b...) custom-call(bf16[128,19968]{1,0:T(8,128)(2,1)S(1)} %copy-done), custom_call_target="tpu_custom_call" | custom-call | bytes 10223616 | tf_op jit(solution)/shard_map/pack/pallas_call | solution.py:88
  6.5 2.4 %collective-permute-start.9 = (bf16[512,640]{1,0:T(8,128)(2,1)}, bf16[512,640]{1,0:T(8,128)(2,1)}, u32[]{:S(2)}, u32[]{:S(2)}) collective-permute-start(bf16[512,640]{1,0:T(8,128)(2,1)} %get-tuple-element.31), channel_id=1, source_target_pairs={{0,2},{1,5},{2,0},{3,7},{4,6},{5,1},{6,4},{7,3},{8,10},{9,13},{10,... | collective-permute-start | bytes 1966088 | tf_op jit(solution)/shard_map/ppermute | solution.py:390
  8.9 1.2 %collective-permute-done.8.refs_1_ = bf16[2,512,640]{2,1,0:T(8,128)(2,1)S(1)} collective-permute-done((bf16[2,512,640]{2,1,0:T(8,128)(2,1)S(1)}, bf16[2,512,640]{2,1,0:T(8,128)(2,1)S(1)}, u32[]{:S(2)}, u32[]{:S(2)}) %collective-permute-start.8) | collective-permute-done | bytes 1310752 | tf_op jit(solution)/shard_map/ppermute | solution.py:390
  11.0 2.4 %collective-permute-start.10 = (bf16[512,640]{1,0:T(8,128)(2,1)}, bf16[512,640]{1,0:T(8,128)(2,1)}, u32[]{:S(2)}, u32[]{:S(2)}) collective-permute-start(bf16[512,640]{1,0:T(8,128)(2,1)} %slice_bitcast_fusion), channel_id=1, source_target_pairs={{0,2},{1,5},{2,0},{3,7},{4,6},{5,1},{6,4},{7,3},{8,10},{9,13},{10,... | collective-permute-start | bytes 1966088 | tf_op jit(solution)/shard_map/ppermute | solution.py:390
  16.1 3.0 %collective-permute-done.1.far_ref = bf16[2,64,128]{2,1,0:T(8,128)(2,1)S(1)} collective-permute-done((bf16[2,64,128]{2,1,0:T(8,128)(2,1)S(1)}, bf16[2,64,128]{2,1,0:T(8,128)(2,1)S(1)}, u32[]{:S(2)}, u32[]{:S(2)}) %collective-permute-start.1) | collective-permute-done | bytes 32800 | tf_op jit(solution)/shard_map/ppermute | solution.py:390
  20.6 2.4 %collective-permute-done.2.far_ref = f32[48,128]{1,0:T(8,128)S(1)} collective-permute-done((f32[48,128]{1,0:T(8,128)S(1)}, f32[48,128]{1,0:T(8,128)S(1)}, u32[]{:S(2)}, u32[]{:S(2)}) %collective-permute-start.2) | collective-permute-done | bytes 24608 | tf_op jit(solution)/shard_map/ppermute | solution.py:390
  23.7 1.4 %collective-permute-start.6 = (bf16[512,640]{1,0:T(8,128)(2,1)}, bf16[512,640]{1,0:T(8,128)(2,1)S(1)}, u32[]{:S(2)}, u32[]{:S(2)}) collective-permute-start(bf16[512,640]{1,0:T(8,128)(2,1)} %copy-done.3), channel_id=1, source_target_pairs={{0,2},{1,5},{2,0},{3,7},{4,6},{5,1},{6,4},{7,3},{8,10},{9,13},{10,... | collective-permute-start | bytes 1966088 | tf_op jit(solution)/shard_map/ppermute | solution.py:390
  25.1 1.1 %copy-done.2 = bf16[512,640]{1,0:T(8,128)(2,1)S(1)} copy-done((bf16[512,640]{1,0:T(8,128)(2,1)S(1)}, bf16[512,640]{1,0:T(8,128)(2,1)}, u32[]{:S(2)}) %copy-start.2) | copy-done | bytes 655384
  26.2 2.4 %group_moments.1 = (f32[2,128,640]{2,1,0:T(8,128)S(1)}, f32[2,128,640]{2,1,0:T(8,128)S(1)}) custom-call(bf16[512,640]{1,0:T(8,128)(2,1)S(1)} %copy-done.2, bf16[2,512,640]{2,1,0:T(8,128)(2,1)S(1)} %collective-permute-done.8.refs_1_, bf16[512,640]{1,0:T(8,128)(2,1)} %collective-permute-done.9.refs_2_, bf16[512,640]{1,0:T(8,128)(2,1)} %collective-permute-done.10.refs_3_, ...), custom_call_target="tpu_custom_call" | custom-call | bytes 6291456 | tf_op jit(solution)/shard_map/group_moments/pallas_call | solution.py:310
  28.6 1.4 %collective-permute-start.11 = (f32[2,128,640]{2,1,0:T(8,128)S(1)}, f32[2,128,640]{2,1,0:T(8,128)S(1)}, u32[]{:S(2)}, u32[]{:S(2)}) collective-permute-start(f32[2,128,640]{2,1,0:T(8,128)S(1)} %get-tuple-element.34), channel_id=1, source_target_pairs={{0,4},{1,3},{2,6},{3,1},{4,0},{5,7},{6,2},{7,5},{8,12},{9,11},{10,... | collective-permute-start | bytes 1966088 | tf_op jit(solution)/shard_map/ppermute | solution.py:390
  30.1 1.4 %collective-permute-start.7 = (bf16[512,640]{1,0:T(8,128)(2,1)S(1)}, bf16[512,640]{1,0:T(8,128)(2,1)S(1)}, u32[]{:S(2)}, u32[]{:S(2)}) collective-permute-start(bf16[512,640]{1,0:T(8,128)(2,1)S(1)} %slice_bitcast_fusion.1), channel_id=1, source_target_pairs={{0,2},{1,5},{2,0},{3,7},{4,6},{5,1},{6,4},{7,3},{8,10},{9,13},{10,... | collective-permute-start | bytes 1966088 | tf_op jit(solution)/shard_map/ppermute | solution.py:390
  31.5 1.3 %collective-permute-start.4 = (f32[48,128]{1,0:T(8,128)S(1)}, f32[48,128]{1,0:T(8,128)S(1)}, u32[]{:S(2)}, u32[]{:S(2)}) collective-permute-start(f32[48,128]{1,0:T(8,128)S(1)} %add.10.here_ref.refs_5_), channel_id=1, source_target_pairs={{0,1},{2,3},{4,5},{6,7},{8,9},{10,11},{12,13},{14,15},{16,17},{18,... | collective-permute-start | bytes 73736 | tf_op jit(solution)/shard_map/ppermute | solution.py:390
  32.7 5.6 %collective-permute-done.4.told_ref = f32[48,128]{1,0:T(8,128)S(1)} collective-permute-done((f32[48,128]{1,0:T(8,128)S(1)}, f32[48,128]{1,0:T(8,128)S(1)}, u32[]{:S(2)}, u32[]{:S(2)}) %collective-permute-start.4) | collective-permute-done | bytes 24608 | tf_op jit(solution)/shard_map/ppermute | solution.py:390
  38.6 6.4 %collective-permute-done.11.right_ref = f32[2,128,640]{2,1,0:T(8,128)S(1)} collective-permute-done((f32[2,128,640]{2,1,0:T(8,128)S(1)}, f32[2,128,640]{2,1,0:T(8,128)S(1)}, u32[]{:S(2)}, u32[]{:S(2)}) %collective-permute-start.11) | collective-permute-done | bytes 655392 | tf_op jit(solution)/shard_map/ppermute | solution.py:390
  45.1 1.1 %meet.1.refs_7_ = f32[2,112,640]{2,1,0:T(8,128)S(1)} custom-call(s32[48,1]{1,0:T(8,128)S(1)} %copy.8.pick_ref, f32[48,128]{1,0:T(8,128)S(1)} %get-tuple-element.22.near_ref, f32[48,128]{1,0:T(8,128)S(1)} %collective-permute-done.2.far_ref, f32[3,48,128]{2,1,0:T(8,128)S(1)} %get-tuple-element.23.stats_ref.refs_6_, ...), custom_call_target="tpu_custom_call" | custom-call | bytes 16384 | tf_op jit(solution)/shard_map/meet/pallas_call | solution.py:117
  46.1 2.9 %collective-permute-start.12 = (f32[2,112,640]{2,1,0:T(8,128)S(1)}, f32[2,112,640]{2,1,0:T(8,128)S(1)}, u32[]{:S(2)}, u32[]{:S(2)}) collective-permute-start(f32[2,112,640]{2,1,0:T(8,128)S(1)} %meet.1.refs_7_), channel_id=1, source_target_pairs={{0,8},{1,9},{2,10},{3,11},{4,12},{5,13},{6,14},{7,15},{8,0},{9,1},... | collective-permute-start | bytes 1720328 | tf_op jit(solution)/shard_map/ppermute | solution.py:390
  49.0 1.1 %moments.1 = (f32[112,640]{1,0:T(8,128)S(1)}, f32[112,640]{1,0:T(8,128)S(1)}, f32[112,640]{1,0:T(8,128)S(1)}, f32[112,640]{1,0:T(8,128)S(1)}) custom-call(bf16[512,640]{1,0:T(8,128)(2,1)S(1)} %get-tuple-element.24.refs_0_, bf16[2,512,640]{2,1,0:T(8,128)(2,1)S(1)} %collective-permute-done.5.refs_1_, ...), custom_call_target="tpu_custom_call" | custom-call | bytes 6291456 | tf_op jit(solution)/shard_map/moments/pallas_call | solution.py:329
  50.2 1.3 %collective-permute-start.13 = (f32[112,640]{1,0:T(8,128)S(1)}, f32[112,640]{1,0:T(8,128)S(1)}, u32[]{:S(2)}, u32[]{:S(2)}) collective-permute-start(f32[112,640]{1,0:T(8,128)S(1)} %get-tuple-element.36), channel_id=1, source_target_pairs={{0,4},{1,3},{2,6},{3,1},{4,0},{5,7},{6,2},{7,5},{8,12},{9,11},{10,... | collective-permute-start | bytes 860168 | tf_op jit(solution)/shard_map/ppermute | solution.py:390
  51.5 4.5 %collective-permute-start.15 = (f32[112,640]{1,0:T(8,128)S(1)}, f32[112,640]{1,0:T(8,128)S(1)}, u32[]{:S(2)}, u32[]{:S(2)}) collective-permute-start(f32[112,640]{1,0:T(8,128)S(1)} %get-tuple-element.38), channel_id=1, source_target_pairs={{0,5},{1,2},{2,7},{3,0},{4,1},{5,6},{6,3},{7,4},{8,13},{9,10},{10,... | collective-permute-start | bytes 860168 | tf_op jit(solution)/shard_map/ppermute | solution.py:390
  56.0 17.7 %collective-permute-done.12 = f32[2,112,640]{2,1,0:T(8,128)S(1)} collective-permute-done((f32[2,112,640]{2,1,0:T(8,128)S(1)}, f32[2,112,640]{2,1,0:T(8,128)S(1)}, u32[]{:S(2)}, u32[]{:S(2)}) %collective-permute-start.12) | collective-permute-done | bytes 573472 | tf_op jit(solution)/shard_map/ppermute | solution.py:390
  73.7 1.7 %collective-permute-start.14 = (f32[112,640]{1,0:T(8,128)S(1)}, f32[112,640]{1,0:T(8,128)S(1)}, u32[]{:S(2)}, u32[]{:S(2)}) collective-permute-start(f32[112,640]{1,0:T(8,128)S(1)} %fusion), channel_id=1, source_target_pairs={{0,1},{1,0},{2,3},{3,2},{4,5},{5,4},{6,7},{7,6},{8,9},{9,8},{10,11... | collective-permute-start | bytes 860168 | tf_op jit(solution)/shard_map/ppermute | solution.py:390
  75.4 1.2 %collective-permute-done.14.refs_3_ = f32[112,640]{1,0:T(8,128)S(1)} collective-permute-done((f32[112,640]{1,0:T(8,128)S(1)}, f32[112,640]{1,0:T(8,128)S(1)}, u32[]{:S(2)}, u32[]{:S(2)}) %collective-permute-start.14) | collective-permute-done | bytes 286752 | tf_op jit(solution)/shard_map/ppermute | solution.py:390
  76.6 1.6 %finish.1 = f32[48,1,1248]{2,1,0:T(1,128)} custom-call(s32[48,1]{1,0:T(8,128)S(1)} %copy.8.pick_ref, f32[3,48,128]{2,1,0:T(8,128)S(1)} %get-tuple-element.23.stats_ref.refs_6_, f32[112,640]{1,0:T(8,128)S(1)} %get-tuple-element.35.refs_0_, f32[112,640]{1,0:T(8,128)S(1)} %slice_bitcast_fusion.3.refs_1_, f32[112,640]{1,0:T(8,128)S(1)} %collective-permute-done.13.refs_2_, ...), custom_call_target="tpu_custom_call" | custom-call | bytes 16384 | tf_op jit(solution)/shard_map/finish/pallas_call | solution.py:377
  (39 shorter events, 7.5 us)
Async XLA Ops:
  0.0 2.4 %copy-start = (bf16[128,19968]{1,0:T(8,128)(2,1)S(1)}, bf16[128,19968]{1,0:T(8,128)(2,1)}, u32[]{:S(2)}) copy-start(bf16[128,19968]{1,0:T(8,128)(2,1)} %x_ref.1) | copy-start | bytes 15335428
  5.1 0.8 %copy-start.1 = (bf16[512,640]{1,0:T(8,128)(2,1)}, bf16[512,640]{1,0:T(8,128)(2,1)S(1)}, u32[]{:S(2)}) copy-start(bf16[512,640]{1,0:T(8,128)(2,1)S(1)} %get-tuple-element.29.refs_0_) | copy-start | bytes 1966084
  5.9 10.1 %copy-start.3 = (bf16[512,640]{1,0:T(8,128)(2,1)}, bf16[512,640]{1,0:T(8,128)(2,1)S(1)}, u32[]{:S(2)}) copy-start(bf16[512,640]{1,0:T(8,128)(2,1)S(1)} %get-tuple-element.26) | copy-start | bytes 1966084
  5.9 7.5 %copy-start.4 = (s32[128,48]{0,1:T(8,128)S(1)}, s32[128,48]{0,1:T(8,128)}, u32[]{:S(2)}) copy-start(s32[128,48]{0,1:T(8,128)} %param.6) | copy-start | bytes 73732
  5.9 7.5 %copy-start.5 = (bf16[128,16]{0,1:T(8,128)(2,1)S(1)}, bf16[128,16]{0,1:T(8,128)(2,1)}, u32[]{:S(2)}) copy-start(bf16[128,16]{0,1:T(8,128)(2,1)} %param.5) | copy-start | bytes 12292
  5.9 10.1 %copy-start.6 = (s32[48]{0:T(128)S(1)}, s32[48]{0:T(128)}, u32[]{:S(2)}) copy-start(s32[48]{0:T(128)} %param.7) | copy-start | bytes 580
  5.9 4.2 %collective-permute-start.8 = (bf16[2,512,640]{2,1,0:T(8,128)(2,1)S(1)}, bf16[2,512,640]{2,1,0:T(8,128)(2,1)S(1)}, u32[]{:S(2)}, u32[]{:S(2)}) collective-permute-start(bf16[2,512,640]{2,1,0:T(8,128)(2,1)S(1)} %get-tuple-element.30), channel_id=1, source_target_pairs={{0,1},{1,0},{2,3},{3,2},{4,5},{5,4},{6,7},{7,6},{8,9},{9,8},{10,11... | collective-permute-start | bytes 3932168 | tf_op jit(solution)/shard_map/ppermute | solution.py:390
  6.0 24.0 %collective-permute-start.5 = (bf16[2,512,640]{2,1,0:T(8,128)(2,1)}, bf16[2,512,640]{2,1,0:T(8,128)(2,1)S(1)}, u32[]{:S(2)}, u32[]{:S(2)}) collective-permute-start(bf16[2,512,640]{2,1,0:T(8,128)(2,1)} %get-tuple-element.25), channel_id=1, source_target_pairs={{0,1},{1,0},{2,3},{3,2},{4,5},{5,4},{6,7},{7,6},{8,9},{9,8},{10,11... | collective-permute-start | bytes 3932168 | tf_op jit(solution)/shard_map/ppermute | solution.py:390
  6.5 18.6 %collective-permute-start.9 = (bf16[512,640]{1,0:T(8,128)(2,1)}, bf16[512,640]{1,0:T(8,128)(2,1)}, u32[]{:S(2)}, u32[]{:S(2)}) collective-permute-start(bf16[512,640]{1,0:T(8,128)(2,1)} %get-tuple-element.31), channel_id=1, source_target_pairs={{0,2},{1,5},{2,0},{3,7},{4,6},{5,1},{6,4},{7,3},{8,10},{9,13},{10,... | collective-permute-start | bytes 1966088 | tf_op jit(solution)/shard_map/ppermute | solution.py:390
  11.0 14.1 %collective-permute-start.10 = (bf16[512,640]{1,0:T(8,128)(2,1)}, bf16[512,640]{1,0:T(8,128)(2,1)}, u32[]{:S(2)}, u32[]{:S(2)}) collective-permute-start(bf16[512,640]{1,0:T(8,128)(2,1)} %slice_bitcast_fusion), channel_id=1, source_target_pairs={{0,2},{1,5},{2,0},{3,7},{4,6},{5,1},{6,4},{7,3},{8,10},{9,13},{10,... | collective-permute-start | bytes 1966088 | tf_op jit(solution)/shard_map/ppermute | solution.py:390
  13.5 1.5 %collective-permute-start = (bf16[64,128]{1,0:T(8,128)(2,1)S(1)}, bf16[64,128]{1,0:T(8,128)(2,1)S(1)}, u32[]{:S(2)}, u32[]{:S(2)}) collective-permute-start(bf16[64,128]{1,0:T(8,128)(2,1)S(1)} %get-tuple-element.40), channel_id=1, source_target_pairs={{0,1},{1,0},{2,3},{3,2},{4,5},{5,4},{6,7},{7,6},{8,9},{9,8},{10,11... | collective-permute-start | bytes 49160 | tf_op jit(solution)/shard_map/ppermute | solution.py:390
  15.0 4.2 %collective-permute-start.1 = (bf16[2,64,128]{2,1,0:T(8,128)(2,1)S(1)}, bf16[2,64,128]{2,1,0:T(8,128)(2,1)S(1)}, u32[]{:S(2)}, u32[]{:S(2)}) collective-permute-start(bf16[2,64,128]{2,1,0:T(8,128)(2,1)S(1)} %pad_maximum_fusion.near_ref), channel_id=1, source_target_pairs={{3,0},{4,1},{1,2},{6,3},{7,4},{0,5},{5,6},{2,7},{11,8},{12,9},{9,1... | collective-permute-start | bytes 98312 | tf_op jit(solution)/shard_map/ppermute | solution.py:390
  19.6 3.5 %collective-permute-start.2 = (f32[48,128]{1,0:T(8,128)S(1)}, f32[48,128]{1,0:T(8,128)S(1)}, u32[]{:S(2)}, u32[]{:S(2)}) collective-permute-start(f32[48,128]{1,0:T(8,128)S(1)} %get-tuple-element.22.near_ref), channel_id=1, source_target_pairs={{0,4},{1,3},{2,6},{3,1},{4,0},{5,7},{6,2},{7,5},{8,12},{9,11},{10,... | collective-permute-start | bytes 73736 | tf_op jit(solution)/shard_map/ppermute | solution.py:390
  23.1 2.0 %collective-permute-start.3 = (f32[48,128]{1,0:T(8,128)S(1)}, f32[48,128]{1,0:T(8,128)S(1)}, u32[]{:S(2)}, u32[]{:S(2)}) collective-permute-start(f32[48,128]{1,0:T(8,128)S(1)} %add.9), channel_id=1, source_target_pairs={{0,8},{2,10},{4,12},{6,14},{8,0},{10,2},{12,4},{14,6},{16,24},{18,... | collective-permute-start | bytes 73736 | tf_op jit(solution)/shard_map/ppermute | solution.py:390
  23.7 14.9 %collective-permute-start.6 = (bf16[512,640]{1,0:T(8,128)(2,1)}, bf16[512,640]{1,0:T(8,128)(2,1)S(1)}, u32[]{:S(2)}, u32[]{:S(2)}) collective-permute-start(bf16[512,640]{1,0:T(8,128)(2,1)} %copy-done.3), channel_id=1, source_target_pairs={{0,2},{1,5},{2,0},{3,7},{4,6},{5,1},{6,4},{7,3},{8,10},{9,13},{10,... | collective-permute-start | bytes 1966088 | tf_op jit(solution)/shard_map/ppermute | solution.py:390
  25.1 1.1 %copy-start.2 = (bf16[512,640]{1,0:T(8,128)(2,1)S(1)}, bf16[512,640]{1,0:T(8,128)(2,1)}, u32[]{:S(2)}) copy-start(bf16[512,640]{1,0:T(8,128)(2,1)} %copy-done.1) | copy-start | bytes 1966084
  28.6 16.5 %collective-permute-start.11 = (f32[2,128,640]{2,1,0:T(8,128)S(1)}, f32[2,128,640]{2,1,0:T(8,128)S(1)}, u32[]{:S(2)}, u32[]{:S(2)}) collective-permute-start(f32[2,128,640]{2,1,0:T(8,128)S(1)} %get-tuple-element.34), channel_id=1, source_target_pairs={{0,4},{1,3},{2,6},{3,1},{4,0},{5,7},{6,2},{7,5},{8,12},{9,11},{10,... | collective-permute-start | bytes 1966088 | tf_op jit(solution)/shard_map/ppermute | solution.py:390
  30.1 19.0 %collective-permute-start.7 = (bf16[512,640]{1,0:T(8,128)(2,1)S(1)}, bf16[512,640]{1,0:T(8,128)(2,1)S(1)}, u32[]{:S(2)}, u32[]{:S(2)}) collective-permute-start(bf16[512,640]{1,0:T(8,128)(2,1)S(1)} %slice_bitcast_fusion.1), channel_id=1, source_target_pairs={{0,2},{1,5},{2,0},{3,7},{4,6},{5,1},{6,4},{7,3},{8,10},{9,13},{10,... | collective-permute-start | bytes 1966088 | tf_op jit(solution)/shard_map/ppermute | solution.py:390
  31.5 6.9 %collective-permute-start.4 = (f32[48,128]{1,0:T(8,128)S(1)}, f32[48,128]{1,0:T(8,128)S(1)}, u32[]{:S(2)}, u32[]{:S(2)}) collective-permute-start(f32[48,128]{1,0:T(8,128)S(1)} %add.10.here_ref.refs_5_), channel_id=1, source_target_pairs={{0,1},{2,3},{4,5},{6,7},{8,9},{10,11},{12,13},{14,15},{16,17},{18,... | collective-permute-start | bytes 73736 | tf_op jit(solution)/shard_map/ppermute | solution.py:390
  46.1 27.5 %collective-permute-start.12 = (f32[2,112,640]{2,1,0:T(8,128)S(1)}, f32[2,112,640]{2,1,0:T(8,128)S(1)}, u32[]{:S(2)}, u32[]{:S(2)}) collective-permute-start(f32[2,112,640]{2,1,0:T(8,128)S(1)} %meet.1.refs_7_), channel_id=1, source_target_pairs={{0,8},{1,9},{2,10},{3,11},{4,12},{5,13},{6,14},{7,15},{8,0},{9,1},... | collective-permute-start | bytes 1720328 | tf_op jit(solution)/shard_map/ppermute | solution.py:390
  50.2 25.3 %collective-permute-start.13 = (f32[112,640]{1,0:T(8,128)S(1)}, f32[112,640]{1,0:T(8,128)S(1)}, u32[]{:S(2)}, u32[]{:S(2)}) collective-permute-start(f32[112,640]{1,0:T(8,128)S(1)} %get-tuple-element.36), channel_id=1, source_target_pairs={{0,4},{1,3},{2,6},{3,1},{4,0},{5,7},{6,2},{7,5},{8,12},{9,11},{10,... | collective-permute-start | bytes 860168 | tf_op jit(solution)/shard_map/ppermute | solution.py:390
  51.5 23.9 %collective-permute-start.15 = (f32[112,640]{1,0:T(8,128)S(1)}, f32[112,640]{1,0:T(8,128)S(1)}, u32[]{:S(2)}, u32[]{:S(2)}) collective-permute-start(f32[112,640]{1,0:T(8,128)S(1)} %get-tuple-element.38), channel_id=1, source_target_pairs={{0,5},{1,2},{2,7},{3,0},{4,1},{5,6},{6,3},{7,4},{8,13},{9,10},{10,... | collective-permute-start | bytes 860168 | tf_op jit(solution)/shard_map/ppermute | solution.py:390
  73.7 2.9 %collective-permute-start.14 = (f32[112,640]{1,0:T(8,128)S(1)}, f32[112,640]{1,0:T(8,128)S(1)}, u32[]{:S(2)}, u32[]{:S(2)}) collective-permute-start(f32[112,640]{1,0:T(8,128)S(1)} %fusion), channel_id=1, source_target_pairs={{0,1},{1,0},{2,3},{3,2},{4,5},{5,4},{6,7},{7,6},{8,9},{9,8},{10,11... | collective-permute-start | bytes 860168 | tf_op jit(solution)/shard_map/ppermute | solution.py:390

commit v8 on v7

--- a/solution.py
+++ b/solution.py
@@ -283,11 +283,12 @@
         )
 
 
-def group_moments_kernel(rows, *refs):
+def group_moments_kernel(rows, count, *refs):
     kept_ref, passed_ref, *swapped_refs, panel_ref = refs[:5]
-    outs = refs[-2:]
+    outs = refs[-2 * count:]
     height = panel_ref.shape[0]
-    for place in range(kept_ref.shape[0] // rows):
+    places = kept_ref.shape[0] // rows
+    for place in range(places):
         here = slice(place * rows, (place + 1) * rows)
         x = jnp.concatenate(
             [kept_ref[here, :], passed_ref[0, here, :]]
@@ -295,7 +296,8 @@
             axis=0,
         )
         squares = (x.astype(jnp.float32) * x.astype(jnp.float32)).astype(jnp.bfloat16)
-        out = outs[place % 2].at[place // 2]
+        owner_side, middle = divmod(place // 2, places // 2 // count)
+        out = outs[2 * owner_side + place % 2].at[middle]
         out[0:height, :] = jnp.dot(panel_ref[...], x, preferred_element_type=jnp.float32)
         out[height:2 * height, :] = jnp.dot(
             panel_ref[...], squares, preferred_element_type=jnp.float32
@@ -305,18 +307,19 @@
 def group_moments(plan, rows_here, panel, after):
     rows = panel.shape[1] // 4
     out = jax.ShapeDtypeStruct(
-        (plan.places // 2, 2 * panel.shape[0], plan.width), jnp.float32
-    )
-    return pl.pallas_call(
-        functools.partial(group_moments_kernel, rows),
+        (plan.places // 4, 2 * panel.shape[0], plan.width), jnp.float32
+    )
+    outs = pl.pallas_call(
+        functools.partial(group_moments_kernel, rows, 2),
         in_specs=[pl.BlockSpec(memory_space=pltpu.VMEM)] * 5
         + [pl.BlockSpec(memory_space=pl.ANY)] * len(after),
-        out_specs=[pl.BlockSpec(memory_space=pltpu.VMEM)] * 2,
-        out_shape=[out] * 2,
+        out_specs=[pl.BlockSpec(memory_space=pltpu.VMEM)] * 4,
+        out_shape=[out] * 4,
         compiler_params=pltpu.CompilerParams(vmem_limit_bytes=20 << 20),
         cost_estimate=pl.CostEstimate(flops=0, bytes_accessed=6 << 20, transcendentals=0),
         name="group_moments",
     )(*rows_here, panel, *after)
+    return outs[0:2], outs[2:4]
 
 
 def moments(plan, rows_here, first, second, stats, split, after):
@@ -414,22 +417,24 @@
     near_totals, panel = make_group(near, far, pick_column, weightings)
     far_totals = swap(near_totals, plan.by_sums())
     totals = near_totals + far_totals
-    for bit in plan.middle_bits + [plan.top_bit]:
-        totals = totals + swap(totals, plan.by_mask(1 << bit)[0::2])
+    for mask in range(8, n, 8):
+        for more in (mask, mask | 4):
+            totals = totals + swap(near_totals, plan.by_mask(more)[0::2])
     told = swap(totals, to_other_side[0::2])
     first, second, stats = make_panels(near, far, totals, told, pick_column, weightings)
 
-    even, odd = group_moments(plan, rows_here[1], panel, [totals])
-    arrived = swap(odd, plan.by_sums())
-    across = meet(
-        pick_column, near_totals, far_totals, stats, even, arrived, [rows_here[0][2]]
-    )
-    for bit in plan.middle_bits:
-        across = across[0::2] + swap(across[1::2], plan.by_mask(1 << bit))
-    top = swap(across, plan.by_mask(1 << plan.top_bit))
+    across, top, after = [], [], [rows_here[0][2]]
+    for even, odd in group_moments(plan, rows_here[1], panel, [totals]):
+        arrived = swap(odd, plan.by_sums())
+        met = meet(pick_column, near_totals, far_totals, stats, even, arrived, after)
+        for bit in plan.middle_bits:
+            met = met[0::2] + swap(met[1::2], plan.by_mask(1 << bit))
+        across.append(met)
+        top.append(swap(met, plan.by_mask(1 << plan.top_bit))[0])
+        after = []
 
     last = not plan.middle_bits
-    sums = moments(plan, rows_here[0], first, second, stats, last, [across])
+    sums = moments(plan, rows_here[0], first, second, stats, last, across)
     if last:
         even, odd = sums[0::2], sums[1::2]
         other_owner = [(d, pair ^ 1) for d, pair in plan.by_sums()]
@@ -444,7 +449,7 @@
             odd = even[1::2] + arrived[1::2]
             even = even[0::2] + arrived[0::2]
             arrived = swap(odd, plan.by_mask(1 << bit))
-        total = even + arrived + top
+        total = [even[side] + arrived[side] + top[side] for side in range(2)]
         parts = [[total[0]], [swap(total[1], to_other_side)]]
     return finish(plan, parts, pick_column, stats, weightings)
 

time: 78.8 us -> 74.4 us (0.944)
  waiting for transfers between devices: 38.4 us -> 25.5 us
  starting transfers between devices: 24.7 us -> 35.2 us
  local copies, waits for them, and re-layouts: 5.46 us -> 3.53 us
    ppermute x16 -> x19, waiting for transfers between devices: 38.4 us -> 25.5 us  [swap(): return lax.ppermute(array, 'pat', pairs)]
    ppermute x16 -> x19, starting transfers between devices: 24.7 us -> 35.2 us  [swap(): return lax.ppermute(array, 'pat', pairs)]
    unnamed x14 -> x16, local copies, waits for them, and re-layouts: 4.39 us -> 2.47 us
    pallas_call x3 -> x4, Pallas kernels: 1.74 us -> 1.96 us  [small_call(): pl.pallas_call(kernel, in_specs=[vmem] * len(operands) + [pl.BlockSpec(me...]
  transfers between devices with their start and end apart: 16 -> 19, of which waited for: 8 -> 8; matrix products, arithmetic and copies ran while one was open for 1% -> 1% of each run, Pallas kernels for 7% -> 7%
where the time goes in v8:
time: 74.4 us; the launch traced here: 74.2 us
  starting transfers between devices  35.2 us (47%)
  waiting for transfers between devices  25.5 us (34%)
  Pallas kernels  9.73 us (13%)
  local copies, waits for them, and re-layouts  3.53 us (5%)
    ppermute x19, starting transfers between devices, swap(): return lax.ppermute(array, 'pat', pairs)  35.2 us
    ppermute x19, waiting for transfers between devices, swap(): return lax.ppermute(array, 'pat', pairs)  25.5 us
    pallas_call x1, Pallas kernels, pack(): pl.pallas_call(functools.partial(pack_kernel, plan), grid=(plan.places,),...  2.66 us
    unnamed x16, local copies, waits for them, and re-layouts  2.47 us
    pallas_call x1, Pallas kernels, group_moments(): pl.pallas_call(functools.partial(group_moments_kernel, rows, 2), in_specs...  2.35 us
    pallas_call x4, Pallas kernels, small_call(): pl.pallas_call(kernel, in_specs=[vmem] * len(operands) + [pl.BlockSpec(me...  1.96 us
    pallas_call x1, Pallas kernels, finish(): pl.pallas_call(functools.partial(finish_kernel, plan, weightings, [len(pa...  1.62 us
  transfers between devices with their start and end apart: 19, of which 8 were waited for; matrix products, arithmetic and copies ran while one was open for 1% of the time, Pallas kernels for 7%

profile of v8, /device:TPU:1, one launch (start us, length us, event | category | flops | bytes accessed | tf_op | source)
XLA Modules:
  0.0 74.2 jit_solution(9189100825750263890)
XLA Ops:
  0.0 2.4 %copy-done = bf16[128,19968]{1,0:T(8,128)(2,1)S(1)} copy-done((bf16[128,19968]{1,0:T(8,128)(2,1)S(1)}, bf16[128,19968]{1,0:T(8,128)(2,1)}, u32[]{:S(2)}) %copy-start) | copy-done | bytes 5111832
  2.5 2.7 %pack.1 = (bf16[512,640]{1,0:T(8,128)(2,1)S(1)}, bf16[512,640]{1,0:T(8,128)(2,1)S(1)}, bf16[512,640]{1,0:T(8,128)(2,1)S(1)}, bf16[512,640]{1,0:T(8,128)(2,1)}, b...) custom-call(bf16[128,19968]{1,0:T(8,128)(2,1)S(1)} %copy-done), custom_call_target="tpu_custom_call" | custom-call | bytes 10223616 | tf_op jit(solution)/shard_map/pack/pallas_call | solution.py:88
  5.7 2.4 %collective-permute-start.10 = (bf16[512,640]{1,0:T(8,128)(2,1)}, bf16[512,640]{1,0:T(8,128)(2,1)}, u32[]{:S(2)}, u32[]{:S(2)}) collective-permute-start(bf16[512,640]{1,0:T(8,128)(2,1)} %get-tuple-element.33), channel_id=1, source_target_pairs={{0,2},{1,5},{2,0},{3,7},{4,6},{5,1},{6,4},{7,3},{8,10},{9,13},{10,... | collective-permute-start | bytes 1966088 | tf_op jit(solution)/shard_map/ppermute | solution.py:393
  8.1 1.2 %collective-permute-done.9.refs_1_ = bf16[2,512,640]{2,1,0:T(8,128)(2,1)S(1)} collective-permute-done((bf16[2,512,640]{2,1,0:T(8,128)(2,1)S(1)}, bf16[2,512,640]{2,1,0:T(8,128)(2,1)S(1)}, u32[]{:S(2)}, u32[]{:S(2)}) %collective-permute-start.9) | collective-permute-done | bytes 1310752 | tf_op jit(solution)/shard_map/ppermute | solution.py:393
  9.3 0.9 %slice_bitcast_fusion = bf16[512,640]{1,0:T(8,128)(2,1)} fusion(bf16[2,512,640]{2,1,0:T(8,128)(2,1)S(1)} %collective-permute-done.9.refs_1_), kind=kLoop, calls=%fused_computation | loop fusion | bytes 1310720 | tf_op jit(solution)/shard_map/squeeze | solution.py:414
  10.2 2.4 %collective-permute-start.11 = (bf16[512,640]{1,0:T(8,128)(2,1)}, bf16[512,640]{1,0:T(8,128)(2,1)}, u32[]{:S(2)}, u32[]{:S(2)}) collective-permute-start(bf16[512,640]{1,0:T(8,128)(2,1)} %slice_bitcast_fusion), channel_id=1, source_target_pairs={{0,2},{1,5},{2,0},{3,7},{4,6},{5,1},{6,4},{7,3},{8,10},{9,13},{10,... | collective-permute-start | bytes 1966088 | tf_op jit(solution)/shard_map/ppermute | solution.py:393
  13.2 0.8 %collective-permute-done = bf16[64,128]{1,0:T(8,128)(2,1)S(1)} collective-permute-done((bf16[64,128]{1,0:T(8,128)(2,1)S(1)}, bf16[64,128]{1,0:T(8,128)(2,1)S(1)}, u32[]{:S(2)}, u32[]{:S(2)}) %collective-permute-start) | collective-permute-done | bytes 16416 | tf_op jit(solution)/shard_map/ppermute | solution.py:393
  14.1 1.0 %collective-permute-start.1 = (bf16[2,64,128]{2,1,0:T(8,128)(2,1)S(1)}, bf16[2,64,128]{2,1,0:T(8,128)(2,1)S(1)}, u32[]{:S(2)}, u32[]{:S(2)}) collective-permute-start(bf16[2,64,128]{2,1,0:T(8,128)(2,1)S(1)} %pad_maximum_fusion.near_ref), channel_id=1, source_target_pairs={{3,0},{4,1},{1,2},{6,3},{7,4},{0,5},{5,6},{2,7},{11,8},{12,9},{9,1... | collective-permute-start | bytes 98312 | tf_op jit(solution)/shard_map/ppermute | solution.py:393
  15.2 3.0 %collective-permute-done.1.far_ref = bf16[2,64,128]{2,1,0:T(8,128)(2,1)S(1)} collective-permute-done((bf16[2,64,128]{2,1,0:T(8,128)(2,1)S(1)}, bf16[2,64,128]{2,1,0:T(8,128)(2,1)S(1)}, u32[]{:S(2)}, u32[]{:S(2)}) %collective-permute-start.1) | collective-permute-done | bytes 32800 | tf_op jit(solution)/shard_map/ppermute | solution.py:393
  18.7 1.0 %collective-permute-start.2 = (f32[48,128]{1,0:T(8,128)S(1)}, f32[48,128]{1,0:T(8,128)S(1)}, u32[]{:S(2)}, u32[]{:S(2)}) collective-permute-start(f32[48,128]{1,0:T(8,128)S(1)} %get-tuple-element.24.near_ref), channel_id=1, source_target_pairs={{0,4},{1,3},{2,6},{3,1},{4,0},{5,7},{6,2},{7,5},{8,12},{9,11},{10,... | collective-permute-start | bytes 73736 | tf_op jit(solution)/shard_map/ppermute | solution.py:393
  21.2 1.0 %collective-permute-done.2.far_ref = f32[48,128]{1,0:T(8,128)S(1)} collective-permute-done((f32[48,128]{1,0:T(8,128)S(1)}, f32[48,128]{1,0:T(8,128)S(1)}, u32[]{:S(2)}, u32[]{:S(2)}) %collective-permute-start.2) | collective-permute-done | bytes 24608 | tf_op jit(solution)/shard_map/ppermute | solution.py:393
  22.2 1.3 %collective-permute-start.7 = (bf16[512,640]{1,0:T(8,128)(2,1)S(1)}, bf16[512,640]{1,0:T(8,128)(2,1)S(1)}, u32[]{:S(2)}, u32[]{:S(2)}) collective-permute-start(bf16[512,640]{1,0:T(8,128)(2,1)S(1)} %copy-done.4), channel_id=1, source_target_pairs={{0,2},{1,5},{2,0},{3,7},{4,6},{5,1},{6,4},{7,3},{8,10},{9,13},{10,... | collective-permute-start | bytes 1966088 | tf_op jit(solution)/shard_map/ppermute | solution.py:393
  24.3 2.4 %group_moments.1 = (f32[1,128,640]{2,1,0:T(8,128)S(1)}, f32[1,128,640]{2,1,0:T(8,128)S(1)}, f32[1,128,640]{2,1,0:T(8,128)S(1)}, f32[1,128,640]{2,1,0:T(8,128)S(1)}) custom-call(bf16[512,640]{1,0:T(8,128)(2,1)S(1)} %copy-done.2, bf16[2,512,640]{2,1,0:T(8,128)(2,1)S(1)} %collective-permute-done.9.refs_1_, bf16[512,640]{1,0:T(8,128)(2,1)} %collective-permute-done.10.refs_2_, ...), custom_call_target="tpu_custom_call" | custom-call | bytes 6291456 | tf_op jit(solution)/shard_map/group_moments/pallas_call | solution.py:312
  26.7 1.5 %collective-permute-start.13 = (f32[1,128,640]{2,1,0:T(8,128)S(1)}, f32[1,128,640]{2,1,0:T(8,128)S(1)}, u32[]{:S(2)}, u32[]{:S(2)}) collective-permute-start(f32[1,128,640]{2,1,0:T(8,128)S(1)} %get-tuple-element.38), channel_id=1, source_target_pairs={{0,4},{1,3},{2,6},{3,1},{4,0},{5,7},{6,2},{7,5},{8,12},{9,11},{10,... | collective-permute-start | bytes 983048 | tf_op jit(solution)/shard_map/ppermute | solution.py:393
  28.2 1.3 %collective-permute-start.5 = (f32[48,128]{1,0:T(8,128)S(1)}, f32[48,128]{1,0:T(8,128)S(1)}, u32[]{:S(2)}, u32[]{:S(2)}) collective-permute-start(f32[48,128]{1,0:T(8,128)S(1)} %add_add_fusion.here_ref.refs_5_), channel_id=1, source_target_pairs={{0,1},{2,3},{4,5},{6,7},{8,9},{10,11},{12,13},{14,15},{16,17},{18,... | collective-permute-start | bytes 73736 | tf_op jit(solution)/shard_map/ppermute | solution.py:393
  29.5 9.6 %collective-permute-done.5.told_ref = f32[48,128]{1,0:T(8,128)S(1)} collective-permute-done((f32[48,128]{1,0:T(8,128)S(1)}, f32[48,128]{1,0:T(8,128)S(1)}, u32[]{:S(2)}, u32[]{:S(2)}) %collective-permute-start.5) | collective-permute-done | bytes 24608 | tf_op jit(solution)/shard_map/ppermute | solution.py:393
  40.1 2.6 %collective-permute-done.12.right_ref = f32[1,128,640]{2,1,0:T(8,128)S(1)} collective-permute-done((f32[1,128,640]{2,1,0:T(8,128)S(1)}, f32[1,128,640]{2,1,0:T(8,128)S(1)}, u32[]{:S(2)}, u32[]{:S(2)}) %collective-permute-start.12) | collective-permute-done | bytes 327712 | tf_op jit(solution)/shard_map/ppermute | solution.py:393
  43.3 3.4 %collective-permute-start.14 = (f32[1,112,640]{2,1,0:T(8,128)S(1)}, f32[1,112,640]{2,1,0:T(8,128)S(1)}, u32[]{:S(2)}, u32[]{:S(2)}) collective-permute-start(f32[1,112,640]{2,1,0:T(8,128)S(1)} %meet.2.refs_7_), channel_id=1, source_target_pairs={{0,8},{1,9},{2,10},{3,11},{4,12},{5,13},{6,14},{7,15},{8,0},{9,1},... | collective-permute-start | bytes 860168 | tf_op jit(solution)/shard_map/ppermute | solution.py:393
  46.8 1.1 %moments.1 = (f32[112,640]{1,0:T(8,128)S(1)}, f32[112,640]{1,0:T(8,128)S(1)}, f32[112,640]{1,0:T(8,128)S(1)}, f32[112,640]{1,0:T(8,128)S(1)}) custom-call(bf16[512,640]{1,0:T(8,128)(2,1)S(1)} %get-tuple-element.26.refs_0_, bf16[2,512,640]{2,1,0:T(8,128)(2,1)S(1)} %collective-permute-done.6.refs_1_, ...), custom_call_target="tpu_custom_call" | custom-call | bytes 6291456 | tf_op jit(solution)/shard_map/moments/pallas_call | solution.py:332
  47.9 1.4 %collective-permute-start.15 = (f32[112,640]{1,0:T(8,128)S(1)}, f32[112,640]{1,0:T(8,128)S(1)}, u32[]{:S(2)}, u32[]{:S(2)}) collective-permute-start(f32[112,640]{1,0:T(8,128)S(1)} %get-tuple-element.40), channel_id=1, source_target_pairs={{0,4},{1,3},{2,6},{3,1},{4,0},{5,7},{6,2},{7,5},{8,12},{9,11},{10,... | collective-permute-start | bytes 860168 | tf_op jit(solution)/shard_map/ppermute | solution.py:393
  49.4 8.1 %collective-permute-start.18 = (f32[112,640]{1,0:T(8,128)S(1)}, f32[112,640]{1,0:T(8,128)S(1)}, u32[]{:S(2)}, u32[]{:S(2)}) collective-permute-start(f32[112,640]{1,0:T(8,128)S(1)} %get-tuple-element.42), channel_id=1, source_target_pairs={{0,5},{1,2},{2,7},{3,0},{4,1},{5,6},{6,3},{7,4},{8,13},{9,10},{10,... | collective-permute-start | bytes 860168 | tf_op jit(solution)/shard_map/ppermute | solution.py:393
  57.5 8.5 %collective-permute-start.17 = (f32[112,640]{1,0:T(8,128)S(1)}, f32[112,640]{1,0:T(8,128)S(1)}, u32[]{:S(2)}, u32[]{:S(2)}) collective-permute-start(f32[112,640]{1,0:T(8,128)S(1)} %bitcast_add_fusion), channel_id=1, source_target_pairs={{0,1},{1,0},{2,3},{3,2},{4,5},{5,4},{6,7},{7,6},{8,9},{9,8},{10,11... | collective-permute-start | bytes 860168 | tf_op jit(solution)/shard_map/ppermute | solution.py:393
  66.0 6.6 %collective-permute-done.18.refs_4_ = f32[112,640]{1,0:T(8,128)S(1)} collective-permute-done((f32[112,640]{1,0:T(8,128)S(1)}, f32[112,640]{1,0:T(8,128)S(1)}, u32[]{:S(2)}, u32[]{:S(2)}) %collective-permute-start.18) | collective-permute-done | bytes 286752 | tf_op jit(solution)/shard_map/ppermute | solution.py:393
  72.6 1.6 %finish.1 = f32[48,1,1248]{2,1,0:T(1,128)} custom-call(s32[48,1]{1,0:T(8,128)S(1)} %copy.9.pick_ref, f32[3,48,128]{2,1,0:T(8,128)S(1)} %get-tuple-element.25.stats_ref.refs_6_, f32[112,640]{1,0:T(8,128)S(1)} %get-tuple-element.39.refs_0_, f32[112,640]{1,0:T(8,128)S(1)} %bitcast.14, f32[112,640]{1,0:T(8,128)S(1)} %collective-permute-done.15.refs_2_, ...), custom_call_target="tpu_custom_call" | custom-call | bytes 16384 | tf_op jit(solution)/shard_map/finish/pallas_call | solution.py:380
  (46 shorter events, 5.6 us)
Async XLA Ops:
  5.1 10.0 %copy-start.1 = (bf16[512,640]{1,0:T(8,128)(2,1)}, bf16[512,640]{1,0:T(8,128)(2,1)S(1)}, u32[]{:S(2)}) copy-start(bf16[512,640]{1,0:T(8,128)(2,1)S(1)} %get-tuple-element.31.refs_0_) | copy-start | bytes 1966084
  5.1 10.0 %copy-start.3 = (bf16[512,640]{1,0:T(8,128)(2,1)}, bf16[512,640]{1,0:T(8,128)(2,1)S(1)}, u32[]{:S(2)}) copy-start(bf16[512,640]{1,0:T(8,128)(2,1)S(1)} %get-tuple-element.28) | copy-start | bytes 1966084
  5.1 7.5 %copy-start.6 = (bf16[128,16]{0,1:T(8,128)(2,1)S(1)}, bf16[128,16]{0,1:T(8,128)(2,1)}, u32[]{:S(2)}) copy-start(bf16[128,16]{0,1:T(8,128)(2,1)} %param.5) | copy-start | bytes 12292
  5.1 10.0 %copy-start.7 = (s32[48]{0:T(128)S(1)}, s32[48]{0:T(128)}, u32[]{:S(2)}) copy-start(s32[48]{0:T(128)} %param.7) | copy-start | bytes 580
  5.1 4.2 %collective-permute-start.9 = (bf16[2,512,640]{2,1,0:T(8,128)(2,1)S(1)}, bf16[2,512,640]{2,1,0:T(8,128)(2,1)S(1)}, u32[]{:S(2)}, u32[]{:S(2)}) collective-permute-start(bf16[2,512,640]{2,1,0:T(8,128)(2,1)S(1)} %get-tuple-element.32), channel_id=1, source_target_pairs={{0,1},{1,0},{2,3},{3,2},{4,5},{5,4},{6,7},{7,6},{8,9},{9,8},{10,11... | collective-permute-start | bytes 3932168 | tf_op jit(solution)/shard_map/ppermute | solution.py:393
  5.2 15.2 %collective-permute-start.6 = (bf16[2,512,640]{2,1,0:T(8,128)(2,1)}, bf16[2,512,640]{2,1,0:T(8,128)(2,1)S(1)}, u32[]{:S(2)}, u32[]{:S(2)}) collective-permute-start(bf16[2,512,640]{2,1,0:T(8,128)(2,1)} %get-tuple-element.27), channel_id=1, source_target_pairs={{0,1},{1,0},{2,3},{3,2},{4,5},{5,4},{6,7},{7,6},{8,9},{9,8},{10,11... | collective-permute-start | bytes 3932168 | tf_op jit(solution)/shard_map/ppermute | solution.py:393
  5.7 18.0 %collective-permute-start.10 = (bf16[512,640]{1,0:T(8,128)(2,1)}, bf16[512,640]{1,0:T(8,128)(2,1)}, u32[]{:S(2)}, u32[]{:S(2)}) collective-permute-start(bf16[512,640]{1,0:T(8,128)(2,1)} %get-tuple-element.33), channel_id=1, source_target_pairs={{0,2},{1,5},{2,0},{3,7},{4,6},{5,1},{6,4},{7,3},{8,10},{9,13},{10,... | collective-permute-start | bytes 1966088 | tf_op jit(solution)/shard_map/ppermute | solution.py:393
  10.2 14.1 %collective-permute-start.11 = (bf16[512,640]{1,0:T(8,128)(2,1)}, bf16[512,640]{1,0:T(8,128)(2,1)}, u32[]{:S(2)}, u32[]{:S(2)}) collective-permute-start(bf16[512,640]{1,0:T(8,128)(2,1)} %slice_bitcast_fusion), channel_id=1, source_target_pairs={{0,2},{1,5},{2,0},{3,7},{4,6},{5,1},{6,4},{7,3},{8,10},{9,13},{10,... | collective-permute-start | bytes 1966088 | tf_op jit(solution)/shard_map/ppermute | solution.py:393
  12.7 1.4 %collective-permute-start = (bf16[64,128]{1,0:T(8,128)(2,1)S(1)}, bf16[64,128]{1,0:T(8,128)(2,1)S(1)}, u32[]{:S(2)}, u32[]{:S(2)}) collective-permute-start(bf16[64,128]{1,0:T(8,128)(2,1)S(1)} %get-tuple-element.44), channel_id=1, source_target_pairs={{0,1},{1,0},{2,3},{3,2},{4,5},{5,4},{6,7},{7,6},{8,9},{9,8},{10,11... | collective-permute-start | bytes 49160 | tf_op jit(solution)/shard_map/ppermute | solution.py:393
  14.1 4.2 %collective-permute-start.1 = (bf16[2,64,128]{2,1,0:T(8,128)(2,1)S(1)}, bf16[2,64,128]{2,1,0:T(8,128)(2,1)S(1)}, u32[]{:S(2)}, u32[]{:S(2)}) collective-permute-start(bf16[2,64,128]{2,1,0:T(8,128)(2,1)S(1)} %pad_maximum_fusion.near_ref), channel_id=1, source_target_pairs={{3,0},{4,1},{1,2},{6,3},{7,4},{0,5},{5,6},{2,7},{11,8},{12,9},{9,1... | collective-permute-start | bytes 98312 | tf_op jit(solution)/shard_map/ppermute | solution.py:393
  15.2 9.1 %copy-start.2 = (bf16[512,640]{1,0:T(8,128)(2,1)S(1)}, bf16[512,640]{1,0:T(8,128)(2,1)}, u32[]{:S(2)}) copy-start(bf16[512,640]{1,0:T(8,128)(2,1)} %copy-done.1) | copy-start | bytes 1966084
  18.7 3.5 %collective-permute-start.2 = (f32[48,128]{1,0:T(8,128)S(1)}, f32[48,128]{1,0:T(8,128)S(1)}, u32[]{:S(2)}, u32[]{:S(2)}) collective-permute-start(f32[48,128]{1,0:T(8,128)S(1)} %get-tuple-element.24.near_ref), channel_id=1, source_target_pairs={{0,4},{1,3},{2,6},{3,1},{4,0},{5,7},{6,2},{7,5},{8,12},{9,11},{10,... | collective-permute-start | bytes 73736 | tf_op jit(solution)/shard_map/ppermute | solution.py:393
  19.8 3.7 %collective-permute-start.3 = (f32[48,128]{1,0:T(8,128)S(1)}, f32[48,128]{1,0:T(8,128)S(1)}, u32[]{:S(2)}, u32[]{:S(2)}) collective-permute-start(f32[48,128]{1,0:T(8,128)S(1)} %get-tuple-element.24.near_ref), channel_id=1, source_target_pairs={{0,8},{2,10},{4,12},{6,14},{8,0},{10,2},{12,4},{14,6},{16,24},{18,... | collective-permute-start | bytes 73736 | tf_op jit(solution)/shard_map/ppermute | solution.py:393
  20.4 3.2 %collective-permute-start.4 = (f32[48,128]{1,0:T(8,128)S(1)}, f32[48,128]{1,0:T(8,128)S(1)}, u32[]{:S(2)}, u32[]{:S(2)}) collective-permute-start(f32[48,128]{1,0:T(8,128)S(1)} %get-tuple-element.24.near_ref), channel_id=1, source_target_pairs={{0,12},{2,14},{4,8},{6,10},{8,4},{10,6},{12,0},{14,2},{16,28},{18,... | collective-permute-start | bytes 73736 | tf_op jit(solution)/shard_map/ppermute | solution.py:393
  22.2 17.9 %collective-permute-start.7 = (bf16[512,640]{1,0:T(8,128)(2,1)S(1)}, bf16[512,640]{1,0:T(8,128)(2,1)S(1)}, u32[]{:S(2)}, u32[]{:S(2)}) collective-permute-start(bf16[512,640]{1,0:T(8,128)(2,1)S(1)} %copy-done.4), channel_id=1, source_target_pairs={{0,2},{1,5},{2,0},{3,7},{4,6},{5,1},{6,4},{7,3},{8,10},{9,13},{10,... | collective-permute-start | bytes 1966088 | tf_op jit(solution)/shard_map/ppermute | solution.py:393
  23.5 23.3 %collective-permute-start.8 = (bf16[512,640]{1,0:T(8,128)(2,1)S(1)}, bf16[512,640]{1,0:T(8,128)(2,1)S(1)}, u32[]{:S(2)}, u32[]{:S(2)}) collective-permute-start(bf16[512,640]{1,0:T(8,128)(2,1)S(1)} %slice_bitcast_fusion.1), channel_id=1, source_target_pairs={{0,2},{1,5},{2,0},{3,7},{4,6},{5,1},{6,4},{7,3},{8,10},{9,13},{10,... | collective-permute-start | bytes 1966088 | tf_op jit(solution)/shard_map/ppermute | solution.py:393
  26.7 12.7 %collective-permute-start.13 = (f32[1,128,640]{2,1,0:T(8,128)S(1)}, f32[1,128,640]{2,1,0:T(8,128)S(1)}, u32[]{:S(2)}, u32[]{:S(2)}) collective-permute-start(f32[1,128,640]{2,1,0:T(8,128)S(1)} %get-tuple-element.38), channel_id=1, source_target_pairs={{0,4},{1,3},{2,6},{3,1},{4,0},{5,7},{6,2},{7,5},{8,12},{9,11},{10,... | collective-permute-start | bytes 983048 | tf_op jit(solution)/shard_map/ppermute | solution.py:393
  28.1 14.6 %collective-permute-start.12 = (f32[1,128,640]{2,1,0:T(8,128)S(1)}, f32[1,128,640]{2,1,0:T(8,128)S(1)}, u32[]{:S(2)}, u32[]{:S(2)}) collective-permute-start(f32[1,128,640]{2,1,0:T(8,128)S(1)} %get-tuple-element.36), channel_id=1, source_target_pairs={{0,4},{1,3},{2,6},{3,1},{4,0},{5,7},{6,2},{7,5},{8,12},{9,11},{10,... | collective-permute-start | bytes 983048 | tf_op jit(solution)/shard_map/ppermute | solution.py:393
  28.2 10.9 %collective-permute-start.5 = (f32[48,128]{1,0:T(8,128)S(1)}, f32[48,128]{1,0:T(8,128)S(1)}, u32[]{:S(2)}, u32[]{:S(2)}) collective-permute-start(f32[48,128]{1,0:T(8,128)S(1)} %add_add_fusion.here_ref.refs_5_), channel_id=1, source_target_pairs={{0,1},{2,3},{4,5},{6,7},{8,9},{10,11},{12,13},{14,15},{16,17},{18,... | collective-permute-start | bytes 73736 | tf_op jit(solution)/shard_map/ppermute | solution.py:393
  40.0 17.5 %collective-permute-start.16 = (f32[1,112,640]{2,1,0:T(8,128)S(1)}, f32[1,112,640]{2,1,0:T(8,128)S(1)}, u32[]{:S(2)}, u32[]{:S(2)}) collective-permute-start(f32[1,112,640]{2,1,0:T(8,128)S(1)} %meet.3.refs_8_), channel_id=1, source_target_pairs={{0,8},{1,9},{2,10},{3,11},{4,12},{5,13},{6,14},{7,15},{8,0},{9,1},... | collective-permute-start | bytes 860168 | tf_op jit(solution)/shard_map/ppermute | solution.py:393
  43.3 29.2 %collective-permute-start.14 = (f32[1,112,640]{2,1,0:T(8,128)S(1)}, f32[1,112,640]{2,1,0:T(8,128)S(1)}, u32[]{:S(2)}, u32[]{:S(2)}) collective-permute-start(f32[1,112,640]{2,1,0:T(8,128)S(1)} %meet.2.refs_7_), channel_id=1, source_target_pairs={{0,8},{1,9},{2,10},{3,11},{4,12},{5,13},{6,14},{7,15},{8,0},{9,1},... | collective-permute-start | bytes 860168 | tf_op jit(solution)/shard_map/ppermute | solution.py:393
  47.9 18.1 %collective-permute-start.15 = (f32[112,640]{1,0:T(8,128)S(1)}, f32[112,640]{1,0:T(8,128)S(1)}, u32[]{:S(2)}, u32[]{:S(2)}) collective-permute-start(f32[112,640]{1,0:T(8,128)S(1)} %get-tuple-element.40), channel_id=1, source_target_pairs={{0,4},{1,3},{2,6},{3,1},{4,0},{5,7},{6,2},{7,5},{8,12},{9,11},{10,... | collective-permute-start | bytes 860168 | tf_op jit(solution)/shard_map/ppermute | solution.py:393
  49.4 23.2 %collective-permute-start.18 = (f32[112,640]{1,0:T(8,128)S(1)}, f32[112,640]{1,0:T(8,128)S(1)}, u32[]{:S(2)}, u32[]{:S(2)}) collective-permute-start(f32[112,640]{1,0:T(8,128)S(1)} %get-tuple-element.42), channel_id=1, source_target_pairs={{0,5},{1,2},{2,7},{3,0},{4,1},{5,6},{6,3},{7,4},{8,13},{9,10},{10,... | collective-permute-start | bytes 860168 | tf_op jit(solution)/shard_map/ppermute | solution.py:393
  57.5 15.1 %collective-permute-start.17 = (f32[112,640]{1,0:T(8,128)S(1)}, f32[112,640]{1,0:T(8,128)S(1)}, u32[]{:S(2)}, u32[]{:S(2)}) collective-permute-start(f32[112,640]{1,0:T(8,128)S(1)} %bitcast_add_fusion), channel_id=1, source_target_pairs={{0,1},{1,0},{2,3},{3,2},{4,5},{5,4},{6,7},{7,6},{8,9},{9,8},{10,11... | collective-permute-start | bytes 860168 | tf_op jit(solution)/shard_map/ppermute | solution.py:393
  (3 other events, 15.0 us)

commit v9 on v8

--- a/solution.py
+++ b/solution.py
@@ -35,63 +35,96 @@
 
 
 def pack_kernel(
-    plan, x_ref, kept0_ref, kept1_ref, sent0_ref, sent1_ref, other0_ref, other1_ref
+    plan, x_ref, kept0_ref, kept1_ref, sent0_ref, sent1_ref, other0_ref, other1_ref, x0_ref, x1_ref,
+    sems,
 ):
     step = pl.program_id(0)
     me = lax.axis_index("pat")
-    rows, columns = x_ref.shape
-    last_tile = columns // LANES - 1
+    rows, half = x0_ref.shape
+    last_tile = half // LANES - 1
     lane = lax.broadcasted_iota(jnp.int32, (rows, LANES), 1)
+
+    def start_of(chunk):
+        return ((me >> plan.top_bit) ^ chunk) * half
+
+    def load(chunk, buffer):
+        here = pl.ds(pl.multiple_of(start_of(chunk), LANES), half)
+        return pltpu.make_async_copy(x_ref.at[:, here], buffer, sems.at[chunk])
+
+    @pl.when(step == 0)
+    def _():
+        load(1, x1_ref).start()
+        load(0, x0_ref).start()
+        load(1, x1_ref).wait()
+
+    @pl.when(step == plan.places)
+    def _():
+        load(0, x0_ref).wait()
 
     def tile(index):
         return pl.ds(pl.multiple_of(jnp.minimum(index, last_tile) * LANES, LANES), LANES)
 
-    for away in range(2):
-        side = (me & 1) ^ away
-        holder = me ^ away
-        for sent in range(2):
-            for chunk in range(2):
-                middle = len(plan.middle_bits)
+    middle = len(plan.middle_bits)
+
+    def fill(chunk, place, buffer, targets):
+        for away in range(2):
+            side = (me & 1) ^ away
+            holder = me ^ away
+            for sent in range(2):
                 relative = (
-                    (step >> (1 + middle))
+                    (place >> (1 + middle))
                     | (sent << (1 + side))
-                    | ((step & 1) << (2 - side))
-                    | (((step >> 1) & ((1 << middle) - 1)) << 3)
+                    | ((place & 1) << (2 - side))
+                    | (((place >> 1) & ((1 << middle) - 1)) << 3)
                     | (chunk << plan.top_bit)
                 )
-                column = (holder ^ relative) * plan.block
+                column = (holder ^ relative) * plan.block - start_of(chunk)
                 first = column // LANES
                 edge = (column - first * LANES) * (1 - side)
-                head = x_ref[:, tile(first + side * plan.share)]
-                tail = x_ref[:, tile(first + plan.tiles)]
+                head = buffer[:, tile(first + side * plan.share)]
+                tail = buffer[:, tile(first + plan.tiles)]
                 folded = jnp.where(lane >= edge, head.astype(jnp.float32), tail.astype(jnp.float32))
-                if away:
-                    target = (other0_ref, other1_ref)[chunk].at[sent]
-                elif sent:
-                    target = (sent0_ref, sent1_ref)[chunk]
-                else:
-                    target = (kept0_ref, kept1_ref)[chunk]
-                target[:, 0:LANES] = folded.astype(x_ref.dtype)
+                target = targets[2].at[sent] if away else targets[sent]
+                target[:, 0:LANES] = folded.astype(buffer.dtype)
                 for slot in range(1, plan.share):
                     here = slice(slot * LANES, (slot + 1) * LANES)
-                    target[:, here] = x_ref[:, tile(first + side * plan.share + slot)]
+                    target[:, here] = buffer[:, tile(first + side * plan.share + slot)]
+
+    @pl.when(step < plan.places)
+    def _():
+        fill(1, step, x1_ref, (kept1_ref, sent1_ref, other1_ref))
+
+    @pl.when(step >= plan.places)
+    def _():
+        fill(0, step - plan.places, x0_ref, (kept0_ref, sent0_ref, other0_ref))
 
 
 def pack(covariates, plan):
-    rows = covariates.shape[0]
+    rows, columns = covariates.shape
     dtype = covariates.dtype
     length = plan.places * rows
     mine = jax.ShapeDtypeStruct((length, plan.width), dtype)
     other = jax.ShapeDtypeStruct((2, length, plan.width), dtype)
-    mine_spec = pl.BlockSpec((rows, plan.width), lambda s: (s, 0))
-    other_spec = pl.BlockSpec((2, rows, plan.width), lambda s: (0, s, 0))
+    last = plan.places - 1
+    specs = []
+    for index in (lambda s: jnp.maximum(s - plan.places, 0), lambda s: jnp.minimum(s, last)):
+        specs.append((
+            pl.BlockSpec((rows, plan.width), lambda s, index=index: (index(s), 0)),
+            pl.BlockSpec((2, rows, plan.width), lambda s, index=index: (0, index(s), 0)),
+        ))
+    (mine0, other0), (mine1, other1) = specs
     return pl.pallas_call(
         functools.partial(pack_kernel, plan),
-        grid=(plan.places,),
-        in_specs=[pl.BlockSpec(memory_space=pltpu.VMEM)],
-        out_specs=[mine_spec] * 4 + [other_spec] * 2,
+        grid=(2 * plan.places,),
+        in_specs=[pl.BlockSpec(memory_space=pl.ANY)],
+        out_specs=[mine0, mine1, mine0, mine1, other0, other1],
         out_shape=[mine] * 4 + [other] * 2,
-        compiler_params=pltpu.CompilerParams(vmem_limit_bytes=12 << 20),
+        scratch_shapes=[
+            pltpu.VMEM((rows, columns // 2), dtype),
+            pltpu.VMEM((rows, columns // 2), dtype),
+            pltpu.SemaphoreType.DMA((2,)),
+        ],
+        compiler_params=pltpu.CompilerParams(vmem_limit_bytes=58 << 20),
         cost_estimate=pl.CostEstimate(
             flops=0, bytes_accessed=4 * covariates.size, transcendentals=0
         ),
@@ -179,7 +212,7 @@
     comps = pick_ref.shape[0]
     onehot = onehot_of(pick_ref, weightings, jnp.bfloat16)
     side = jnp.full(here_ref.shape, lax.axis_index("pat") & 1)
-    totals = jnp.where(side == 0, here_ref[...], told_ref[...])
+    totals = jnp.where(side == 1, here_ref[...], told_ref[...])
     light = lighter_of(totals)
     stats_ref[0] = jnp.broadcast_to(1.0 / totals[:, 0:1], (comps, LANES))
     stats_ref[1] = jnp.broadcast_to(1.0 / totals[:, 1:2], (comps, LANES))
@@ -389,6 +422,24 @@
     )(pick_column, stats, *operands)
 
 
+def hold_kernel(*refs):
+    del refs
+
+
+def hold(array, after):
+    any_space = pl.BlockSpec(memory_space=pl.ANY)
+    return pl.pallas_call(
+        hold_kernel,
+        in_specs=[any_space] * (1 + len(after)),
+        out_specs=any_space,
+        out_shape=jax.ShapeDtypeStruct(array.shape, array.dtype),
+        input_output_aliases={0: 0},
+        compiler_params=pltpu.CompilerParams(vmem_limit_bytes=1 << 20),
+        cost_estimate=pl.CostEstimate(flops=0, bytes_accessed=0, transcendentals=0),
+        name="hold",
+    )(array, *after)
+
+
 def swap(array, pairs):
     return lax.ppermute(array, "pat", pairs)
 
@@ -407,24 +458,29 @@
     far = swap(near, [(pair ^ 1, d) for d, pair in plan.by_rows()])
 
     kept0, kept1, sent0, sent1, other0, other1 = pack(covariates, plan)
-    rows_here = {}
-    for chunk, kept, sent, other in ((1, kept1, sent1, other1), (0, kept0, sent0, other0)):
-        passed = swap(other, to_other_side)
-        rows_here[chunk] = [
-            kept, passed, swap(sent, plan.by_rows()), swap(passed[1], plan.by_rows())
-        ]
-
     near_totals, panel = make_group(near, far, pick_column, weightings)
     far_totals = swap(near_totals, plan.by_sums())
     totals = near_totals + far_totals
     for mask in range(8, n, 8):
-        for more in (mask, mask | 4):
-            totals = totals + swap(near_totals, plan.by_mask(more)[0::2])
-    told = swap(totals, to_other_side[0::2])
+        for more in (mask, mask | 2):
+            totals = totals + swap(near_totals, plan.by_mask(more)[1::2])
+    told = swap(totals, to_other_side[1::2])
+
+    rows_here = {}
+    for chunk, kept, sent, other, after in (
+        (1, kept1, sent1, other1, []), (0, kept0, sent0, other0, [totals])
+    ):
+        passed = swap(other, to_other_side)
+        forward = passed[1]
+        if after:
+            sent, forward = hold(sent, after), hold(forward, after)
+        rows_here[chunk] = [
+            kept, passed, swap(sent, plan.by_rows()), swap(forward, plan.by_rows())
+        ]
     first, second, stats = make_panels(near, far, totals, told, pick_column, weightings)
 
     across, top, after = [], [], [rows_here[0][2]]
-    for even, odd in group_moments(plan, rows_here[1], panel, [totals]):
+    for even, odd in group_moments(plan, rows_here[1], panel, [far_totals]):
         arrived = swap(odd, plan.by_sums())
         met = meet(pick_column, near_totals, far_totals, stats, even, arrived, after)
         for bit in plan.middle_bits:

time: 74.4 us -> 80.7 us (1.085); the launches traced: 74.2 us -> 79.4 us
  waiting for transfers between devices: 25.5 us -> 40 us
  starting transfers between devices: 35.2 us -> 23 us
  Pallas kernels: 9.73 us -> 13.2 us
    ppermute x19, waiting for transfers between devices: 25.5 us -> 40 us  [swap(): return lax.ppermute(array, 'pat', pairs)]
    ppermute x19, starting transfers between devices: 35.2 us -> 23 us  [swap(): return lax.ppermute(array, 'pat', pairs)]
    pallas_call x1 -> x3, Pallas kernels: 2.66 us -> 6.3 us  [the longest x1 6.29 us: pack(): pl.pallas_call(functools.partial(pack_kernel, plan), grid=(2 * plan.place...]
    unnamed x16 -> x14, local copies, waits for them, and re-layouts: 2.47 us -> 1.93 us
where the time goes in v9:
time: 80.7 us; the launch traced here: 79.4 us
  waiting for transfers between devices  40 us (50%)
  starting transfers between devices  23 us (29%)
  Pallas kernels  13.2 us (16%)
  local copies, waits for them, and re-layouts  2.99 us (4%)
    ppermute x19, waiting for transfers between devices, swap(): return lax.ppermute(array, 'pat', pairs)  40 us
    ppermute x19, starting transfers between devices, swap(): return lax.ppermute(array, 'pat', pairs)  23 us
    pallas_call x1, Pallas kernels, pack(): pl.pallas_call(functools.partial(pack_kernel, plan), grid=(2 * plan.place...  6.29 us
    pallas_call x1, Pallas kernels, group_moments(): pl.pallas_call(functools.partial(group_moments_kernel, rows, 2), in_specs...  2.18 us
    pallas_call x4, Pallas kernels, small_call(): pl.pallas_call(kernel, in_specs=[vmem] * len(operands) + [pl.BlockSpec(me...  1.94 us
    unnamed x14, local copies, waits for them, and re-layouts  1.93 us
  transfers between devices with their start and end apart: 19, of which 8 were waited for; matrix products, arithmetic and copies ran while one was open for 1% of the time, Pallas kernels for 7%

profile of v9, /device:TPU:1, one launch (start us, length us, event | category | flops | bytes accessed | tf_op | source)
XLA Modules:
  0.0 79.4 jit_solution(10020558058456265123)
XLA Ops:
  0.0 6.3 %pack.1 = (bf16[512,640]{1,0:T(8,128)(2,1)}, bf16[512,640]{1,0:T(8,128)(2,1)}, bf16[512,640]{1,0:T(8,128)(2,1)}, bf16[512,640]{1,0:T(8,128)(2,1)}, bf16[2,512,64...) custom-call(bf16[128,19968]{1,0:T(8,128)(2,1)} %x_ref.1), custom_call_target="tpu_custom_call" | custom-call | bytes 10223616 | tf_op jit(solution)/shard_map/pack/pallas_call | solution.py:116
  7.1 2.7 %collective-permute-start.10 = (bf16[512,640]{1,0:T(8,128)(2,1)}, bf16[512,640]{1,0:T(8,128)(2,1)S(1)}, u32[]{:S(2)}, u32[]{:S(2)}) collective-permute-start(bf16[512,640]{1,0:T(8,128)(2,1)} %get-tuple-element.33), channel_id=1, source_target_pairs={{0,2},{1,5},{2,0},{3,7},{4,6},{5,1},{6,4},{7,3},{8,10},{9,13},{10,... | collective-permute-start | bytes 1966088 | tf_op jit(solution)/shard_map/ppermute | solution.py:444
  9.8 0.9 %slice_bitcast_fusion = bf16[512,640]{1,0:T(8,128)(2,1)} fusion(bf16[2,512,640]{2,1,0:T(8,128)(2,1)S(1)} %collective-permute-done.9.refs_1_), kind=kLoop, calls=%fused_computation | loop fusion | bytes 1310720 | tf_op jit(solution)/shard_map/squeeze | solution.py:474
  10.7 2.3 %collective-permute-start.11 = (bf16[512,640]{1,0:T(8,128)(2,1)}, bf16[512,640]{1,0:T(8,128)(2,1)}, u32[]{:S(2)}, u32[]{:S(2)}) collective-permute-start(bf16[512,640]{1,0:T(8,128)(2,1)} %slice_bitcast_fusion), channel_id=1, source_target_pairs={{0,2},{1,5},{2,0},{3,7},{4,6},{5,1},{6,4},{7,3},{8,10},{9,13},{10,... | collective-permute-start | bytes 1966088 | tf_op jit(solution)/shard_map/ppermute | solution.py:444
  13.3 3.8 %collective-permute-done.1.far_ref = bf16[2,64,128]{2,1,0:T(8,128)(2,1)S(1)} collective-permute-done((bf16[2,64,128]{2,1,0:T(8,128)(2,1)S(1)}, bf16[2,64,128]{2,1,0:T(8,128)(2,1)S(1)}, u32[]{:S(2)}, u32[]{:S(2)}) %collective-permute-start.1) | collective-permute-done | bytes 32800 | tf_op jit(solution)/shard_map/ppermute | solution.py:444
  17.6 1.3 %collective-permute-start.2 = (f32[48,128]{1,0:T(8,128)S(1)}, f32[48,128]{1,0:T(8,128)S(1)}, u32[]{:S(2)}, u32[]{:S(2)}) collective-permute-start(f32[48,128]{1,0:T(8,128)S(1)} %get-tuple-element.24.near_ref), channel_id=1, source_target_pairs={{0,4},{1,3},{2,6},{3,1},{4,0},{5,7},{6,2},{7,5},{8,12},{9,11},{10,... | collective-permute-start | bytes 73736 | tf_op jit(solution)/shard_map/ppermute | solution.py:444
  18.8 4.2 %collective-permute-start.3 = (f32[48,128]{1,0:T(8,128)S(1)}, f32[48,128]{1,0:T(8,128)S(1)}, u32[]{:S(2)}, u32[]{:S(2)}) collective-permute-start(f32[48,128]{1,0:T(8,128)S(1)} %get-tuple-element.24.near_ref), channel_id=1, source_target_pairs={{1,9},{3,11},{5,13},{7,15},{9,1},{11,3},{13,5},{15,7},{17,25},{19,... | collective-permute-start | bytes 73736 | tf_op jit(solution)/shard_map/ppermute | solution.py:444
  23.1 3.1 %collective-permute-start.4 = (f32[48,128]{1,0:T(8,128)S(1)}, f32[48,128]{1,0:T(8,128)S(1)}, u32[]{:S(2)}, u32[]{:S(2)}) collective-permute-start(f32[48,128]{1,0:T(8,128)S(1)} %get-tuple-element.24.near_ref), channel_id=1, source_target_pairs={{1,11},{3,9},{5,15},{7,13},{9,3},{11,1},{13,7},{15,5},{17,27},{19,... | collective-permute-start | bytes 73736 | tf_op jit(solution)/shard_map/ppermute | solution.py:444
  26.2 3.5 %collective-permute-done.4 = f32[48,128]{1,0:T(8,128)S(1)} collective-permute-done((f32[48,128]{1,0:T(8,128)S(1)}, f32[48,128]{1,0:T(8,128)S(1)}, u32[]{:S(2)}, u32[]{:S(2)}) %collective-permute-start.4) | collective-permute-done | bytes 24608 | tf_op jit(solution)/shard_map/ppermute | solution.py:444
  29.7 1.1 %copy-done.2 = bf16[512,640]{1,0:T(8,128)(2,1)S(1)} copy-done((bf16[512,640]{1,0:T(8,128)(2,1)S(1)}, bf16[512,640]{1,0:T(8,128)(2,1)}, u32[]{:S(2)}) %copy-start.2) | copy-done | bytes 655384
  30.8 0.8 %copy-done.3 = bf16[512,640]{1,0:T(8,128)(2,1)} copy-done((bf16[512,640]{1,0:T(8,128)(2,1)}, bf16[512,640]{1,0:T(8,128)(2,1)S(1)}, u32[]{:S(2)}) %copy-start.3) | copy-done | bytes 655384
  31.7 1.5 %collective-permute-start.8 = (bf16[512,640]{1,0:T(8,128)(2,1)S(1)}, bf16[512,640]{1,0:T(8,128)(2,1)S(1)}, u32[]{:S(2)}, u32[]{:S(2)}) collective-permute-start(bf16[512,640]{1,0:T(8,128)(2,1)S(1)} %hold.3), channel_id=1, source_target_pairs={{0,2},{1,5},{2,0},{3,7},{4,6},{5,1},{6,4},{7,3},{8,10},{9,13},{10,... | collective-permute-start | bytes 1966088 | tf_op jit(solution)/shard_map/ppermute | solution.py:444
  33.2 2.2 %group_moments.1 = (f32[1,128,640]{2,1,0:T(8,128)S(1)}, f32[1,128,640]{2,1,0:T(8,128)S(1)}, f32[1,128,640]{2,1,0:T(8,128)S(1)}, f32[1,128,640]{2,1,0:T(8,128)S(1)}) custom-call(bf16[512,640]{1,0:T(8,128)(2,1)S(1)} %copy-done.1, bf16[2,512,640]{2,1,0:T(8,128)(2,1)S(1)} %collective-permute-done.9.refs_1_, ...), custom_call_target="tpu_custom_call" | custom-call | bytes 6291456 | tf_op jit(solution)/shard_map/group_moments/pallas_call | solution.py:345
  35.8 1.2 %collective-permute-start.12 = (f32[1,128,640]{2,1,0:T(8,128)S(1)}, f32[1,128,640]{2,1,0:T(8,128)S(1)}, u32[]{:S(2)}, u32[]{:S(2)}) collective-permute-start(f32[1,128,640]{2,1,0:T(8,128)S(1)} %get-tuple-element.36), channel_id=1, source_target_pairs={{0,4},{1,3},{2,6},{3,1},{4,0},{5,7},{6,2},{7,5},{8,12},{9,11},{10,... | collective-permute-start | bytes 983048 | tf_op jit(solution)/shard_map/ppermute | solution.py:444
  37.0 1.3 %collective-permute-start.5 = (f32[48,128]{1,0:T(8,128)S(1)}, f32[48,128]{1,0:T(8,128)S(1)}, u32[]{:S(2)}, u32[]{:S(2)}) collective-permute-start(f32[48,128]{1,0:T(8,128)S(1)} %add_add_fusion.here_ref.refs_1_), channel_id=1, source_target_pairs={{1,0},{3,2},{5,4},{7,6},{9,8},{11,10},{13,12},{15,14},{17,16},{19,... | collective-permute-start | bytes 73736 | tf_op jit(solution)/shard_map/ppermute | solution.py:444
  39.3 6.0 %collective-permute-done.13.right_ref = f32[1,128,640]{2,1,0:T(8,128)S(1)} collective-permute-done((f32[1,128,640]{2,1,0:T(8,128)S(1)}, f32[1,128,640]{2,1,0:T(8,128)S(1)}, u32[]{:S(2)}, u32[]{:S(2)}) %collective-permute-start.13) | collective-permute-done | bytes 327712 | tf_op jit(solution)/shard_map/ppermute | solution.py:444
  46.0 3.1 %collective-permute-done.7.refs_0_.refs_2_ = bf16[512,640]{1,0:T(8,128)(2,1)S(1)} collective-permute-done((bf16[512,640]{1,0:T(8,128)(2,1)}, bf16[512,640]{1,0:T(8,128)(2,1)S(1)}, u32[]{:S(2)}, u32[]{:S(2)}) %collective-permute-start.7) | collective-permute-done | bytes 655392 | tf_op jit(solution)/shard_map/ppermute | solution.py:444
  49.8 2.4 %collective-permute-start.14 = (f32[1,112,640]{2,1,0:T(8,128)S(1)}, f32[1,112,640]{2,1,0:T(8,128)S(1)}, u32[]{:S(2)}, u32[]{:S(2)}) collective-permute-start(f32[1,112,640]{2,1,0:T(8,128)S(1)} %meet.2.refs_7_), channel_id=1, source_target_pairs={{0,8},{1,9},{2,10},{3,11},{4,12},{5,13},{6,14},{7,15},{8,0},{9,1},... | collective-permute-start | bytes 860168 | tf_op jit(solution)/shard_map/ppermute | solution.py:444
  52.2 16.3 %collective-permute-done.8.refs_3_ = bf16[512,640]{1,0:T(8,128)(2,1)S(1)} collective-permute-done((bf16[512,640]{1,0:T(8,128)(2,1)S(1)}, bf16[512,640]{1,0:T(8,128)(2,1)S(1)}, u32[]{:S(2)}, u32[]{:S(2)}) %collective-permute-start.8) | collective-permute-done | bytes 655392 | tf_op jit(solution)/shard_map/ppermute | solution.py:444
  68.5 1.1 %moments.1 = (f32[112,640]{1,0:T(8,128)S(1)}, f32[112,640]{1,0:T(8,128)S(1)}, f32[112,640]{1,0:T(8,128)S(1)}, f32[112,640]{1,0:T(8,128)S(1)}) custom-call(bf16[512,640]{1,0:T(8,128)(2,1)S(1)} %copy-done, bf16[2,512,640]{2,1,0:T(8,128)(2,1)S(1)} %collective-permute-done.6.refs_1_, bf16[512,640]{1,0:T(8,128)(2,1)S(1)} %collective-permute-done.7.refs_0_.refs_2_, ...), custom_call_target="tpu_custom_call" | custom-call | bytes 6291456 | tf_op jit(solution)/shard_map/moments/pallas_call | solution.py:365
  69.6 1.5 %collective-permute-start.15 = (f32[112,640]{1,0:T(8,128)S(1)}, f32[112,640]{1,0:T(8,128)S(1)}, u32[]{:S(2)}, u32[]{:S(2)}) collective-permute-start(f32[112,640]{1,0:T(8,128)S(1)} %get-tuple-element.40), channel_id=1, source_target_pairs={{0,4},{1,3},{2,6},{3,1},{4,0},{5,7},{6,2},{7,5},{8,12},{9,11},{10,... | collective-permute-start | bytes 860168 | tf_op jit(solution)/shard_map/ppermute | solution.py:444
  71.2 3.9 %collective-permute-done.15.refs_2_ = f32[112,640]{1,0:T(8,128)S(1)} collective-permute-done((f32[112,640]{1,0:T(8,128)S(1)}, f32[112,640]{1,0:T(8,128)S(1)}, u32[]{:S(2)}, u32[]{:S(2)}) %collective-permute-start.15) | collective-permute-done | bytes 286752 | tf_op jit(solution)/shard_map/ppermute | solution.py:444
  75.2 2.6 %collective-permute-done.18.refs_4_ = f32[112,640]{1,0:T(8,128)S(1)} collective-permute-done((f32[112,640]{1,0:T(8,128)S(1)}, f32[112,640]{1,0:T(8,128)S(1)}, u32[]{:S(2)}, u32[]{:S(2)}) %collective-permute-start.18) | collective-permute-done | bytes 286752 | tf_op jit(solution)/shard_map/ppermute | solution.py:444
  77.8 1.6 %finish.1 = f32[48,1,1248]{2,1,0:T(1,128)} custom-call(s32[48,1]{1,0:T(8,128)S(1)} %copy.11.pick_ref, f32[3,48,128]{2,1,0:T(8,128)S(1)} %get-tuple-element.25.stats_ref.refs_6_, f32[112,640]{1,0:T(8,128)S(1)} %get-tuple-element.39.refs_0_, f32[112,640]{1,0:T(8,128)S(1)} %bitcast.14, f32[112,640]{1,0:T(8,128)S(1)} %collective-permute-done.15.refs_2_, ...), custom_call_target="tpu_custom_call" | custom-call | bytes 16384 | tf_op jit(solution)/shard_map/finish/pallas_call | solution.py:413
  (46 shorter events, 4.5 us)
Async XLA Ops:
  0.0 6.9 %copy-start.4 = (s32[128,48]{0,1:T(8,128)S(1)}, s32[128,48]{0,1:T(8,128)}, u32[]{:S(2)}) copy-start(s32[128,48]{0,1:T(8,128)} %param.6) | copy-start | bytes 73732
  0.0 6.9 %copy-start.5 = (bf16[128,16]{0,1:T(8,128)(2,1)S(1)}, bf16[128,16]{0,1:T(8,128)(2,1)}, u32[]{:S(2)}) copy-start(bf16[128,16]{0,1:T(8,128)(2,1)} %param.5) | copy-start | bytes 12292
  6.3 6.9 %copy-start.6 = (s32[48]{0:T(128)S(1)}, s32[48]{0:T(128)}, u32[]{:S(2)}) copy-start(s32[48]{0:T(128)} %param.7) | copy-start | bytes 580
  6.3 3.5 %collective-permute-start.9 = (bf16[2,512,640]{2,1,0:T(8,128)(2,1)}, bf16[2,512,640]{2,1,0:T(8,128)(2,1)S(1)}, u32[]{:S(2)}, u32[]{:S(2)}) collective-permute-start(bf16[2,512,640]{2,1,0:T(8,128)(2,1)} %get-tuple-element.32), channel_id=1, source_target_pairs={{0,1},{1,0},{2,3},{3,2},{4,5},{5,4},{6,7},{7,6},{8,9},{9,8},{10,11... | collective-permute-start | bytes 3932168 | tf_op jit(solution)/shard_map/ppermute | solution.py:444
  6.4 25.2 %collective-permute-start.6 = (bf16[2,512,640]{2,1,0:T(8,128)(2,1)}, bf16[2,512,640]{2,1,0:T(8,128)(2,1)S(1)}, u32[]{:S(2)}, u32[]{:S(2)}) collective-permute-start(bf16[2,512,640]{2,1,0:T(8,128)(2,1)} %get-tuple-element.27), channel_id=1, source_target_pairs={{0,1},{1,0},{2,3},{3,2},{4,5},{5,4},{6,7},{7,6},{8,9},{9,8},{10,11... | collective-permute-start | bytes 3932168 | tf_op jit(solution)/shard_map/ppermute | solution.py:444
  6.9 6.1 %collective-permute-start = (bf16[64,128]{1,0:T(8,128)(2,1)S(1)}, bf16[64,128]{1,0:T(8,128)(2,1)S(1)}, u32[]{:S(2)}, u32[]{:S(2)}) collective-permute-start(bf16[64,128]{1,0:T(8,128)(2,1)S(1)} %get-tuple-element.44), channel_id=1, source_target_pairs={{0,1},{1,0},{2,3},{3,2},{4,5},{5,4},{6,7},{7,6},{8,9},{9,8},{10,11... | collective-permute-start | bytes 49160 | tf_op jit(solution)/shard_map/ppermute | solution.py:444
  7.1 26.2 %collective-permute-start.10 = (bf16[512,640]{1,0:T(8,128)(2,1)}, bf16[512,640]{1,0:T(8,128)(2,1)S(1)}, u32[]{:S(2)}, u32[]{:S(2)}) collective-permute-start(bf16[512,640]{1,0:T(8,128)(2,1)} %get-tuple-element.33), channel_id=1, source_target_pairs={{0,2},{1,5},{2,0},{3,7},{4,6},{5,1},{6,4},{7,3},{8,10},{9,13},{10,... | collective-permute-start | bytes 1966088 | tf_op jit(solution)/shard_map/ppermute | solution.py:444
  10.7 22.5 %collective-permute-start.11 = (bf16[512,640]{1,0:T(8,128)(2,1)}, bf16[512,640]{1,0:T(8,128)(2,1)}, u32[]{:S(2)}, u32[]{:S(2)}) collective-permute-start(bf16[512,640]{1,0:T(8,128)(2,1)} %slice_bitcast_fusion), channel_id=1, source_target_pairs={{0,2},{1,5},{2,0},{3,7},{4,6},{5,1},{6,4},{7,3},{8,10},{9,13},{10,... | collective-permute-start | bytes 1966088 | tf_op jit(solution)/shard_map/ppermute | solution.py:444
  13.0 4.1 %collective-permute-start.1 = (bf16[2,64,128]{2,1,0:T(8,128)(2,1)S(1)}, bf16[2,64,128]{2,1,0:T(8,128)(2,1)S(1)}, u32[]{:S(2)}, u32[]{:S(2)}) collective-permute-start(bf16[2,64,128]{2,1,0:T(8,128)(2,1)S(1)} %pad_maximum_fusion.near_ref), channel_id=1, source_target_pairs={{3,0},{4,1},{1,2},{6,3},{7,4},{0,5},{5,6},{2,7},{11,8},{12,9},{9,1... | collective-permute-start | bytes 98312 | tf_op jit(solution)/shard_map/ppermute | solution.py:444
  17.6 5.5 %collective-permute-start.2 = (f32[48,128]{1,0:T(8,128)S(1)}, f32[48,128]{1,0:T(8,128)S(1)}, u32[]{:S(2)}, u32[]{:S(2)}) collective-permute-start(f32[48,128]{1,0:T(8,128)S(1)} %get-tuple-element.24.near_ref), channel_id=1, source_target_pairs={{0,4},{1,3},{2,6},{3,1},{4,0},{5,7},{6,2},{7,5},{8,12},{9,11},{10,... | collective-permute-start | bytes 73736 | tf_op jit(solution)/shard_map/ppermute | solution.py:444
  18.8 7.3 %collective-permute-start.3 = (f32[48,128]{1,0:T(8,128)S(1)}, f32[48,128]{1,0:T(8,128)S(1)}, u32[]{:S(2)}, u32[]{:S(2)}) collective-permute-start(f32[48,128]{1,0:T(8,128)S(1)} %get-tuple-element.24.near_ref), channel_id=1, source_target_pairs={{1,9},{3,11},{5,13},{7,15},{9,1},{11,3},{13,5},{15,7},{17,25},{19,... | collective-permute-start | bytes 73736 | tf_op jit(solution)/shard_map/ppermute | solution.py:444
  23.1 6.6 %collective-permute-start.4 = (f32[48,128]{1,0:T(8,128)S(1)}, f32[48,128]{1,0:T(8,128)S(1)}, u32[]{:S(2)}, u32[]{:S(2)}) collective-permute-start(f32[48,128]{1,0:T(8,128)S(1)} %get-tuple-element.24.near_ref), channel_id=1, source_target_pairs={{1,11},{3,9},{5,15},{7,13},{9,3},{11,1},{13,7},{15,5},{17,27},{19,... | collective-permute-start | bytes 73736 | tf_op jit(solution)/shard_map/ppermute | solution.py:444
  31.6 1.6 %copy-start.1 = (bf16[512,640]{1,0:T(8,128)(2,1)S(1)}, bf16[512,640]{1,0:T(8,128)(2,1)}, u32[]{:S(2)}) copy-start(bf16[512,640]{1,0:T(8,128)(2,1)} %get-tuple-element.31.refs_0_) | copy-start | bytes 1966084
  31.6 17.5 %collective-permute-start.7 = (bf16[512,640]{1,0:T(8,128)(2,1)}, bf16[512,640]{1,0:T(8,128)(2,1)S(1)}, u32[]{:S(2)}, u32[]{:S(2)}) collective-permute-start(bf16[512,640]{1,0:T(8,128)(2,1)} %copy-done.3), channel_id=1, source_target_pairs={{0,2},{1,5},{2,0},{3,7},{4,6},{5,1},{6,4},{7,3},{8,10},{9,13},{10,... | collective-permute-start | bytes 1966088 | tf_op jit(solution)/shard_map/ppermute | solution.py:444
  31.7 36.7 %collective-permute-start.8 = (bf16[512,640]{1,0:T(8,128)(2,1)S(1)}, bf16[512,640]{1,0:T(8,128)(2,1)S(1)}, u32[]{:S(2)}, u32[]{:S(2)}) collective-permute-start(bf16[512,640]{1,0:T(8,128)(2,1)S(1)} %hold.3), channel_id=1, source_target_pairs={{0,2},{1,5},{2,0},{3,7},{4,6},{5,1},{6,4},{7,3},{8,10},{9,13},{10,... | collective-permute-start | bytes 1966088 | tf_op jit(solution)/shard_map/ppermute | solution.py:444
  35.4 9.9 %collective-permute-start.13 = (f32[1,128,640]{2,1,0:T(8,128)S(1)}, f32[1,128,640]{2,1,0:T(8,128)S(1)}, u32[]{:S(2)}, u32[]{:S(2)}) collective-permute-start(f32[1,128,640]{2,1,0:T(8,128)S(1)} %get-tuple-element.38), channel_id=1, source_target_pairs={{0,4},{1,3},{2,6},{3,1},{4,0},{5,7},{6,2},{7,5},{8,12},{9,11},{10,... | collective-permute-start | bytes 983048 | tf_op jit(solution)/shard_map/ppermute | solution.py:444
  35.8 13.3 %collective-permute-start.12 = (f32[1,128,640]{2,1,0:T(8,128)S(1)}, f32[1,128,640]{2,1,0:T(8,128)S(1)}, u32[]{:S(2)}, u32[]{:S(2)}) collective-permute-start(f32[1,128,640]{2,1,0:T(8,128)S(1)} %get-tuple-element.36), channel_id=1, source_target_pairs={{0,4},{1,3},{2,6},{3,1},{4,0},{5,7},{6,2},{7,5},{8,12},{9,11},{10,... | collective-permute-start | bytes 983048 | tf_op jit(solution)/shard_map/ppermute | solution.py:444
  37.0 2.1 %collective-permute-start.5 = (f32[48,128]{1,0:T(8,128)S(1)}, f32[48,128]{1,0:T(8,128)S(1)}, u32[]{:S(2)}, u32[]{:S(2)}) collective-permute-start(f32[48,128]{1,0:T(8,128)S(1)} %add_add_fusion.here_ref.refs_1_), channel_id=1, source_target_pairs={{1,0},{3,2},{5,4},{7,6},{9,8},{11,10},{13,12},{15,14},{17,16},{19,... | collective-permute-start | bytes 73736 | tf_op jit(solution)/shard_map/ppermute | solution.py:444
  45.3 23.2 %copy-start = (bf16[512,640]{1,0:T(8,128)(2,1)S(1)}, bf16[512,640]{1,0:T(8,128)(2,1)}, u32[]{:S(2)}) copy-start(bf16[512,640]{1,0:T(8,128)(2,1)} %get-tuple-element.26.refs_0_) | copy-start | bytes 1966084
  45.9 25.2 %collective-permute-start.16 = (f32[1,112,640]{2,1,0:T(8,128)S(1)}, f32[1,112,640]{2,1,0:T(8,128)S(1)}, u32[]{:S(2)}, u32[]{:S(2)}) collective-permute-start(f32[1,112,640]{2,1,0:T(8,128)S(1)} %meet.3.refs_8_), channel_id=1, source_target_pairs={{0,8},{1,9},{2,10},{3,11},{4,12},{5,13},{6,14},{7,15},{8,0},{9,1},... | collective-permute-start | bytes 860168 | tf_op jit(solution)/shard_map/ppermute | solution.py:444
  49.8 28.0 %collective-permute-start.14 = (f32[1,112,640]{2,1,0:T(8,128)S(1)}, f32[1,112,640]{2,1,0:T(8,128)S(1)}, u32[]{:S(2)}, u32[]{:S(2)}) collective-permute-start(f32[1,112,640]{2,1,0:T(8,128)S(1)} %meet.2.refs_7_), channel_id=1, source_target_pairs={{0,8},{1,9},{2,10},{3,11},{4,12},{5,13},{6,14},{7,15},{8,0},{9,1},... | collective-permute-start | bytes 860168 | tf_op jit(solution)/shard_map/ppermute | solution.py:444
  69.6 5.6 %collective-permute-start.15 = (f32[112,640]{1,0:T(8,128)S(1)}, f32[112,640]{1,0:T(8,128)S(1)}, u32[]{:S(2)}, u32[]{:S(2)}) collective-permute-start(f32[112,640]{1,0:T(8,128)S(1)} %get-tuple-element.40), channel_id=1, source_target_pairs={{0,4},{1,3},{2,6},{3,1},{4,0},{5,7},{6,2},{7,5},{8,12},{9,11},{10,... | collective-permute-start | bytes 860168 | tf_op jit(solution)/shard_map/ppermute | solution.py:444
  71.1 6.7 %collective-permute-start.18 = (f32[112,640]{1,0:T(8,128)S(1)}, f32[112,640]{1,0:T(8,128)S(1)}, u32[]{:S(2)}, u32[]{:S(2)}) collective-permute-start(f32[112,640]{1,0:T(8,128)S(1)} %get-tuple-element.42), channel_id=1, source_target_pairs={{0,5},{1,2},{2,7},{3,0},{4,1},{5,6},{6,3},{7,4},{8,13},{9,10},{10,... | collective-permute-start | bytes 860168 | tf_op jit(solution)/shard_map/ppermute | solution.py:444
  71.2 6.6 %collective-permute-start.17 = (f32[112,640]{1,0:T(8,128)S(1)}, f32[112,640]{1,0:T(8,128)S(1)}, u32[]{:S(2)}, u32[]{:S(2)}) collective-permute-start(f32[112,640]{1,0:T(8,128)S(1)} %bitcast_add_fusion), channel_id=1, source_target_pairs={{0,1},{1,0},{2,3},{3,2},{4,5},{5,4},{6,7},{7,6},{8,9},{9,8},{10,11... | collective-permute-start | bytes 860168 | tf_op jit(solution)/shard_map/ppermute | solution.py:444
  (2 other events, 1.9 us)

commit v10 on v8

--- a/solution.py
+++ b/solution.py
@@ -37,26 +37,25 @@
 def pack_kernel(
     plan, x_ref, kept0_ref, kept1_ref, sent0_ref, sent1_ref, other0_ref, other1_ref
 ):
-    step = pl.program_id(0)
     me = lax.axis_index("pat")
     rows, columns = x_ref.shape
     last_tile = columns // LANES - 1
     lane = lax.broadcasted_iota(jnp.int32, (rows, LANES), 1)
+    middle = len(plan.middle_bits)
 
     def tile(index):
         return pl.ds(pl.multiple_of(jnp.minimum(index, last_tile) * LANES, LANES), LANES)
 
-    for away in range(2):
-        side = (me & 1) ^ away
-        holder = me ^ away
-        for sent in range(2):
-            for chunk in range(2):
-                middle = len(plan.middle_bits)
+    def fill(place, chunk, targets):
+        for away in range(2):
+            side = (me & 1) ^ away
+            holder = me ^ away
+            for sent in range(2):
                 relative = (
-                    (step >> (1 + middle))
+                    (place >> (1 + middle))
                     | (sent << (1 + side))
-                    | ((step & 1) << (2 - side))
-                    | (((step >> 1) & ((1 << middle) - 1)) << 3)
+                    | ((place & 1) << (2 - side))
+                    | (((place >> 1) & ((1 << middle) - 1)) << 3)
                     | (chunk << plan.top_bit)
                 )
                 column = (holder ^ relative) * plan.block
@@ -65,38 +64,42 @@
                 head = x_ref[:, tile(first + side * plan.share)]
                 tail = x_ref[:, tile(first + plan.tiles)]
                 folded = jnp.where(lane >= edge, head.astype(jnp.float32), tail.astype(jnp.float32))
-                if away:
-                    target = (other0_ref, other1_ref)[chunk].at[sent]
-                elif sent:
-                    target = (sent0_ref, sent1_ref)[chunk]
-                else:
-                    target = (kept0_ref, kept1_ref)[chunk]
+                target = targets[2].at[sent, place] if away else targets[sent].at[place]
                 target[:, 0:LANES] = folded.astype(x_ref.dtype)
                 for slot in range(1, plan.share):
                     here = slice(slot * LANES, (slot + 1) * LANES)
                     target[:, here] = x_ref[:, tile(first + side * plan.share + slot)]
 
+    @pl.loop(0, plan.places)
+    def _(place):
+        fill(place, 1, (kept1_ref, sent1_ref, other1_ref))
+        fill(place, 0, (kept0_ref, sent0_ref, other0_ref))
+
 
 def pack(covariates, plan):
-    rows = covariates.shape[0]
+    rows, columns = covariates.shape
     dtype = covariates.dtype
-    length = plan.places * rows
-    mine = jax.ShapeDtypeStruct((length, plan.width), dtype)
-    other = jax.ShapeDtypeStruct((2, length, plan.width), dtype)
-    mine_spec = pl.BlockSpec((rows, plan.width), lambda s: (s, 0))
-    other_spec = pl.BlockSpec((2, rows, plan.width), lambda s: (0, s, 0))
-    return pl.pallas_call(
+    step = 32
+    mine = jax.ShapeDtypeStruct((plan.places, rows, plan.width), dtype)
+    other = jax.ShapeDtypeStruct((2, plan.places, rows, plan.width), dtype)
+    mine_spec = pl.BlockSpec((plan.places, step, plan.width), lambda s: (0, s, 0))
+    other_spec = pl.BlockSpec((2, plan.places, step, plan.width), lambda s: (0, 0, s, 0))
+    outs = pl.pallas_call(
         functools.partial(pack_kernel, plan),
-        grid=(plan.places,),
-        in_specs=[pl.BlockSpec(memory_space=pltpu.VMEM)],
+        grid=(rows // step,),
+        in_specs=[pl.BlockSpec((step, columns), lambda s: (s, 0))],
         out_specs=[mine_spec] * 4 + [other_spec] * 2,
         out_shape=[mine] * 4 + [other] * 2,
-        compiler_params=pltpu.CompilerParams(vmem_limit_bytes=12 << 20),
+        compiler_params=pltpu.CompilerParams(vmem_limit_bytes=58 << 20),
         cost_estimate=pl.CostEstimate(
             flops=0, bytes_accessed=4 * covariates.size, transcendentals=0
         ),
         name="pack",
     )(covariates)
+    length = plan.places * rows
+    return [out.reshape(length, plan.width) for out in outs[:4]] + [
+        out.reshape(2, length, plan.width) for out in outs[4:]
+    ]
 
 
 def onehot_of(pick_ref, weightings, dtype):

time: 74.4 us -> 75.3 us (1.012)
  Pallas kernels: 9.73 us -> 13.7 us
  local copies, waits for them, and re-layouts: 3.53 us -> 1.09 us
    pallas_call x1, Pallas kernels: 2.66 us -> 6.57 us  [pack(): pl.pallas_call(functools.partial(pack_kernel, plan), grid=(rows // step,)...]
    unnamed x16 -> x12, local copies, waits for them, and re-layouts: 2.47 us -> 0.02 us
where the time goes in v10:
time: 75.3 us; the launch traced here: 75 us
  starting transfers between devices  34.7 us (46%)
  waiting for transfers between devices  25.4 us (34%)
  Pallas kernels  13.7 us (18%)
  local copies, waits for them, and re-layouts  1.09 us (1%)
    ppermute x19, starting transfers between devices, swap(): return lax.ppermute(array, 'pat', pairs)  34.7 us
    ppermute x19, waiting for transfers between devices, swap(): return lax.ppermute(array, 'pat', pairs)  25.4 us
    pallas_call x1, Pallas kernels, pack(): pl.pallas_call(functools.partial(pack_kernel, plan), grid=(rows // step,)...  6.57 us
    pallas_call x1, Pallas kernels, group_moments(): pl.pallas_call(functools.partial(group_moments_kernel, rows, 2), in_specs...  2.36 us
    pallas_call x4, Pallas kernels, small_call(): pl.pallas_call(kernel, in_specs=[vmem] * len(operands) + [pl.BlockSpec(me...  1.96 us
    pallas_call x1, Pallas kernels, finish(): pl.pallas_call(functools.partial(finish_kernel, plan, weightings, [len(pa...  1.62 us
  transfers between devices with their start and end apart: 19, of which 8 were waited for; matrix products, arithmetic and copies ran while one was open for 1% of the time, Pallas kernels for 7%

profile of v10, /device:TPU:1, one launch (start us, length us, event | category | flops | bytes accessed | tf_op | source)
XLA Modules:
  0.0 75.0 jit_solution(16025547584004236888)
XLA Ops:
  0.0 6.6 %pack.1 = (bf16[4,128,640]{2,1,0:T(8,128)(2,1)}, bf16[4,128,640]{2,1,0:T(8,128)(2,1)}, bf16[4,128,640]{2,1,0:T(8,128)(2,1)}, bf16[4,128,640]{2,1,0:T(8,128)(2,1)...) custom-call(bf16[128,19968]{1,0:T(8,128)(2,1)} %x_ref.1), custom_call_target="tpu_custom_call" | custom-call | bytes 10223616 | tf_op jit(solution)/shard_map/pack/pallas_call | solution.py:87
  7.2 2.4 %collective-permute-start.10 = (bf16[512,640]{1,0:T(8,128)(2,1)}, bf16[512,640]{1,0:T(8,128)(2,1)}, u32[]{:S(2)}, u32[]{:S(2)}) collective-permute-start(bf16[512,640]{1,0:T(8,128)(2,1)} %bitcast.29), channel_id=1, source_target_pairs={{0,2},{1,5},{2,0},{3,7},{4,6},{5,1},{6,4},{7,3},{8,10},{9,13},{10,... | collective-permute-start | bytes 1966088 | tf_op jit(solution)/shard_map/ppermute | solution.py:396
  9.9 0.9 %slice_bitcast_fusion = bf16[512,640]{1,0:T(8,128)(2,1)} fusion(bf16[2,512,640]{2,1,0:T(8,128)(2,1)S(1)} %collective-permute-done.9.refs_1_), kind=kLoop, calls=%fused_computation | loop fusion | bytes 1310720 | tf_op jit(solution)/shard_map/squeeze | solution.py:417
  10.8 2.4 %collective-permute-start.11 = (bf16[512,640]{1,0:T(8,128)(2,1)}, bf16[512,640]{1,0:T(8,128)(2,1)}, u32[]{:S(2)}, u32[]{:S(2)}) collective-permute-start(bf16[512,640]{1,0:T(8,128)(2,1)} %slice_bitcast_fusion), channel_id=1, source_target_pairs={{0,2},{1,5},{2,0},{3,7},{4,6},{5,1},{6,4},{7,3},{8,10},{9,13},{10,... | collective-permute-start | bytes 1966088 | tf_op jit(solution)/shard_map/ppermute | solution.py:396
  13.8 0.8 %collective-permute-done = bf16[64,128]{1,0:T(8,128)(2,1)S(1)} collective-permute-done((bf16[64,128]{1,0:T(8,128)(2,1)S(1)}, bf16[64,128]{1,0:T(8,128)(2,1)S(1)}, u32[]{:S(2)}, u32[]{:S(2)}) %collective-permute-start) | collective-permute-done | bytes 16416 | tf_op jit(solution)/shard_map/ppermute | solution.py:396
  14.7 1.0 %collective-permute-start.1 = (bf16[2,64,128]{2,1,0:T(8,128)(2,1)S(1)}, bf16[2,64,128]{2,1,0:T(8,128)(2,1)S(1)}, u32[]{:S(2)}, u32[]{:S(2)}) collective-permute-start(bf16[2,64,128]{2,1,0:T(8,128)(2,1)S(1)} %pad_maximum_fusion.near_ref), channel_id=1, source_target_pairs={{3,0},{4,1},{1,2},{6,3},{7,4},{0,5},{5,6},{2,7},{11,8},{12,9},{9,1... | collective-permute-start | bytes 98312 | tf_op jit(solution)/shard_map/ppermute | solution.py:396
  15.8 3.0 %collective-permute-done.1.far_ref = bf16[2,64,128]{2,1,0:T(8,128)(2,1)S(1)} collective-permute-done((bf16[2,64,128]{2,1,0:T(8,128)(2,1)S(1)}, bf16[2,64,128]{2,1,0:T(8,128)(2,1)S(1)}, u32[]{:S(2)}, u32[]{:S(2)}) %collective-permute-start.1) | collective-permute-done | bytes 32800 | tf_op jit(solution)/shard_map/ppermute | solution.py:396
  19.3 1.1 %collective-permute-start.2 = (f32[48,128]{1,0:T(8,128)S(1)}, f32[48,128]{1,0:T(8,128)S(1)}, u32[]{:S(2)}, u32[]{:S(2)}) collective-permute-start(f32[48,128]{1,0:T(8,128)S(1)} %get-tuple-element.24.near_ref), channel_id=1, source_target_pairs={{0,4},{1,3},{2,6},{3,1},{4,0},{5,7},{6,2},{7,5},{8,12},{9,11},{10,... | collective-permute-start | bytes 73736 | tf_op jit(solution)/shard_map/ppermute | solution.py:396
  21.8 1.0 %collective-permute-done.2.far_ref = f32[48,128]{1,0:T(8,128)S(1)} collective-permute-done((f32[48,128]{1,0:T(8,128)S(1)}, f32[48,128]{1,0:T(8,128)S(1)}, u32[]{:S(2)}, u32[]{:S(2)}) %collective-permute-start.2) | collective-permute-done | bytes 24608 | tf_op jit(solution)/shard_map/ppermute | solution.py:396
  22.8 1.3 %collective-permute-start.7 = (bf16[512,640]{1,0:T(8,128)(2,1)S(1)}, bf16[512,640]{1,0:T(8,128)(2,1)S(1)}, u32[]{:S(2)}, u32[]{:S(2)}) collective-permute-start(bf16[512,640]{1,0:T(8,128)(2,1)S(1)} %bitcast.28), channel_id=1, source_target_pairs={{0,2},{1,5},{2,0},{3,7},{4,6},{5,1},{6,4},{7,3},{8,10},{9,13},{10,... | collective-permute-start | bytes 1966088 | tf_op jit(solution)/shard_map/ppermute | solution.py:396
  24.3 1.5 %collective-permute-done.11.refs_3_ = bf16[512,640]{1,0:T(8,128)(2,1)} collective-permute-done((bf16[512,640]{1,0:T(8,128)(2,1)}, bf16[512,640]{1,0:T(8,128)(2,1)}, u32[]{:S(2)}, u32[]{:S(2)}) %collective-permute-start.11) | collective-permute-done | bytes 655392 | tf_op jit(solution)/shard_map/ppermute | solution.py:396
  25.8 2.4 %group_moments.1 = (f32[1,128,640]{2,1,0:T(8,128)S(1)}, f32[1,128,640]{2,1,0:T(8,128)S(1)}, f32[1,128,640]{2,1,0:T(8,128)S(1)}, f32[1,128,640]{2,1,0:T(8,128)S(1)}) custom-call(bf16[512,640]{1,0:T(8,128)(2,1)S(1)} %bitcast.21, bf16[2,512,640]{2,1,0:T(8,128)(2,1)S(1)} %collective-permute-done.9.refs_1_, bf16[512,640]{1,0:T(8,128)(2,1)} %collective-permute-done.10.refs_2_, ...), custom_call_target="tpu_custom_call" | custom-call | bytes 6291456 | tf_op jit(solution)/shard_map/group_moments/pallas_call | solution.py:315
  28.1 1.5 %collective-permute-start.13 = (f32[1,128,640]{2,1,0:T(8,128)S(1)}, f32[1,128,640]{2,1,0:T(8,128)S(1)}, u32[]{:S(2)}, u32[]{:S(2)}) collective-permute-start(f32[1,128,640]{2,1,0:T(8,128)S(1)} %get-tuple-element.38), channel_id=1, source_target_pairs={{0,4},{1,3},{2,6},{3,1},{4,0},{5,7},{6,2},{7,5},{8,12},{9,11},{10,... | collective-permute-start | bytes 983048 | tf_op jit(solution)/shard_map/ppermute | solution.py:396
  29.7 1.3 %collective-permute-start.5 = (f32[48,128]{1,0:T(8,128)S(1)}, f32[48,128]{1,0:T(8,128)S(1)}, u32[]{:S(2)}, u32[]{:S(2)}) collective-permute-start(f32[48,128]{1,0:T(8,128)S(1)} %add_add_fusion.here_ref.refs_5_), channel_id=1, source_target_pairs={{0,1},{2,3},{4,5},{6,7},{8,9},{10,11},{12,13},{14,15},{16,17},{18,... | collective-permute-start | bytes 73736 | tf_op jit(solution)/shard_map/ppermute | solution.py:396
  31.0 8.7 %collective-permute-done.5.told_ref = f32[48,128]{1,0:T(8,128)S(1)} collective-permute-done((f32[48,128]{1,0:T(8,128)S(1)}, f32[48,128]{1,0:T(8,128)S(1)}, u32[]{:S(2)}, u32[]{:S(2)}) %collective-permute-start.5) | collective-permute-done | bytes 24608 | tf_op jit(solution)/shard_map/ppermute | solution.py:396
  40.6 0.8 %collective-permute-start.16 = (f32[1,112,640]{2,1,0:T(8,128)S(1)}, f32[1,112,640]{2,1,0:T(8,128)S(1)}, u32[]{:S(2)}, u32[]{:S(2)}) collective-permute-start(f32[1,112,640]{2,1,0:T(8,128)S(1)} %meet.3.refs_8_), channel_id=1, source_target_pairs={{0,8},{1,9},{2,10},{3,11},{4,12},{5,13},{6,14},{7,15},{8,0},{9,1},... | collective-permute-start | bytes 860168 | tf_op jit(solution)/shard_map/ppermute | solution.py:396
  41.4 3.5 %collective-permute-done.12.right_ref = f32[1,128,640]{2,1,0:T(8,128)S(1)} collective-permute-done((f32[1,128,640]{2,1,0:T(8,128)S(1)}, f32[1,128,640]{2,1,0:T(8,128)S(1)}, u32[]{:S(2)}, u32[]{:S(2)}) %collective-permute-start.12) | collective-permute-done | bytes 327712 | tf_op jit(solution)/shard_map/ppermute | solution.py:396
  45.6 2.8 %collective-permute-start.14 = (f32[1,112,640]{2,1,0:T(8,128)S(1)}, f32[1,112,640]{2,1,0:T(8,128)S(1)}, u32[]{:S(2)}, u32[]{:S(2)}) collective-permute-start(f32[1,112,640]{2,1,0:T(8,128)S(1)} %meet.2.refs_7_), channel_id=1, source_target_pairs={{0,8},{1,9},{2,10},{3,11},{4,12},{5,13},{6,14},{7,15},{8,0},{9,1},... | collective-permute-start | bytes 860168 | tf_op jit(solution)/shard_map/ppermute | solution.py:396
  48.4 1.1 %moments.1 = (f32[112,640]{1,0:T(8,128)S(1)}, f32[112,640]{1,0:T(8,128)S(1)}, f32[112,640]{1,0:T(8,128)S(1)}, f32[112,640]{1,0:T(8,128)S(1)}) custom-call(bf16[512,640]{1,0:T(8,128)(2,1)S(1)} %bitcast.20, bf16[2,512,640]{2,1,0:T(8,128)(2,1)S(1)} %collective-permute-done.6.refs_1_, bf16[512,640]{1,0:T(8,128)(2,1)S(1)} %collective-permute-done.7.refs_0_.refs_2_, ...), custom_call_target="tpu_custom_call" | custom-call | bytes 6291456 | tf_op jit(solution)/shard_map/moments/pallas_call | solution.py:335
  49.6 1.3 %collective-permute-start.15 = (f32[112,640]{1,0:T(8,128)S(1)}, f32[112,640]{1,0:T(8,128)S(1)}, u32[]{:S(2)}, u32[]{:S(2)}) collective-permute-start(f32[112,640]{1,0:T(8,128)S(1)} %get-tuple-element.40), channel_id=1, source_target_pairs={{0,4},{1,3},{2,6},{3,1},{4,0},{5,7},{6,2},{7,5},{8,12},{9,11},{10,... | collective-permute-start | bytes 860168 | tf_op jit(solution)/shard_map/ppermute | solution.py:396
  50.9 8.6 %collective-permute-start.18 = (f32[112,640]{1,0:T(8,128)S(1)}, f32[112,640]{1,0:T(8,128)S(1)}, u32[]{:S(2)}, u32[]{:S(2)}) collective-permute-start(f32[112,640]{1,0:T(8,128)S(1)} %get-tuple-element.42), channel_id=1, source_target_pairs={{0,5},{1,2},{2,7},{3,0},{4,1},{5,6},{6,3},{7,4},{8,13},{9,10},{10,... | collective-permute-start | bytes 860168 | tf_op jit(solution)/shard_map/ppermute | solution.py:396
  59.6 7.4 %collective-permute-start.17 = (f32[112,640]{1,0:T(8,128)S(1)}, f32[112,640]{1,0:T(8,128)S(1)}, u32[]{:S(2)}, u32[]{:S(2)}) collective-permute-start(f32[112,640]{1,0:T(8,128)S(1)} %bitcast_add_fusion), channel_id=1, source_target_pairs={{0,1},{1,0},{2,3},{3,2},{4,5},{5,4},{6,7},{7,6},{8,9},{9,8},{10,11... | collective-permute-start | bytes 860168 | tf_op jit(solution)/shard_map/ppermute | solution.py:396
  67.0 6.4 %collective-permute-done.18.refs_4_ = f32[112,640]{1,0:T(8,128)S(1)} collective-permute-done((f32[112,640]{1,0:T(8,128)S(1)}, f32[112,640]{1,0:T(8,128)S(1)}, u32[]{:S(2)}, u32[]{:S(2)}) %collective-permute-start.18) | collective-permute-done | bytes 286752 | tf_op jit(solution)/shard_map/ppermute | solution.py:396
  73.3 1.6 %finish.1 = f32[48,1,1248]{2,1,0:T(1,128)} custom-call(s32[48,1]{1,0:T(8,128)S(1)} %copy.9.pick_ref, f32[3,48,128]{2,1,0:T(8,128)S(1)} %get-tuple-element.25.stats_ref.refs_6_, f32[112,640]{1,0:T(8,128)S(1)} %get-tuple-element.39.refs_0_, f32[112,640]{1,0:T(8,128)S(1)} %bitcast.22, f32[112,640]{1,0:T(8,128)S(1)} %collective-permute-done.15.refs_2_, ...), custom_call_target="tpu_custom_call" | custom-call | bytes 16384 | tf_op jit(solution)/shard_map/finish/pallas_call | solution.py:383
  (42 shorter events, 5.3 us)
Async XLA Ops:
  0.0 9.5 %copy-start.2 = (s32[128,48]{0,1:T(8,128)S(1)}, s32[128,48]{0,1:T(8,128)}, u32[]{:S(2)}) copy-start(s32[128,48]{0,1:T(8,128)} %param.6) | copy-start | bytes 73732
  6.6 9.2 %copy-start.4 = (s32[48]{0:T(128)S(1)}, s32[48]{0:T(128)}, u32[]{:S(2)}) copy-start(s32[48]{0:T(128)} %param.7) | copy-start | bytes 580
  6.6 3.3 %collective-permute-start.9 = (bf16[2,512,640]{2,1,0:T(8,128)(2,1)}, bf16[2,512,640]{2,1,0:T(8,128)(2,1)S(1)}, u32[]{:S(2)}, u32[]{:S(2)}) collective-permute-start(bf16[2,512,640]{2,1,0:T(8,128)(2,1)} %bitcast.27), channel_id=1, source_target_pairs={{0,1},{1,0},{2,3},{3,2},{4,5},{5,4},{6,7},{7,6},{8,9},{9,8},{10,11... | collective-permute-start | bytes 3932168 | tf_op jit(solution)/shard_map/ppermute | solution.py:396
  6.7 14.3 %collective-permute-start.6 = (bf16[2,512,640]{2,1,0:T(8,128)(2,1)}, bf16[2,512,640]{2,1,0:T(8,128)(2,1)S(1)}, u32[]{:S(2)}, u32[]{:S(2)}) collective-permute-start(bf16[2,512,640]{2,1,0:T(8,128)(2,1)} %bitcast.26), channel_id=1, source_target_pairs={{0,1},{1,0},{2,3},{3,2},{4,5},{5,4},{6,7},{7,6},{8,9},{9,8},{10,11... | collective-permute-start | bytes 3932168 | tf_op jit(solution)/shard_map/ppermute | solution.py:396
  7.2 17.1 %collective-permute-start.10 = (bf16[512,640]{1,0:T(8,128)(2,1)}, bf16[512,640]{1,0:T(8,128)(2,1)}, u32[]{:S(2)}, u32[]{:S(2)}) collective-permute-start(bf16[512,640]{1,0:T(8,128)(2,1)} %bitcast.29), channel_id=1, source_target_pairs={{0,2},{1,5},{2,0},{3,7},{4,6},{5,1},{6,4},{7,3},{8,10},{9,13},{10,... | collective-permute-start | bytes 1966088 | tf_op jit(solution)/shard_map/ppermute | solution.py:396
  9.5 16.2 %copy-start.1 = (bf16[4,128,640]{2,1,0:T(8,128)(2,1)S(1)}, bf16[4,128,640]{2,1,0:T(8,128)(2,1)}, u32[]{:S(2)}) copy-start(bf16[4,128,640]{2,1,0:T(8,128)(2,1)} %get-tuple-element.31) | copy-start | bytes 1966084
  10.8 14.9 %collective-permute-start.11 = (bf16[512,640]{1,0:T(8,128)(2,1)}, bf16[512,640]{1,0:T(8,128)(2,1)}, u32[]{:S(2)}, u32[]{:S(2)}) collective-permute-start(bf16[512,640]{1,0:T(8,128)(2,1)} %slice_bitcast_fusion), channel_id=1, source_target_pairs={{0,2},{1,5},{2,0},{3,7},{4,6},{5,1},{6,4},{7,3},{8,10},{9,13},{10,... | collective-permute-start | bytes 1966088 | tf_op jit(solution)/shard_map/ppermute | solution.py:396
  13.2 1.4 %collective-permute-start = (bf16[64,128]{1,0:T(8,128)(2,1)S(1)}, bf16[64,128]{1,0:T(8,128)(2,1)S(1)}, u32[]{:S(2)}, u32[]{:S(2)}) collective-permute-start(bf16[64,128]{1,0:T(8,128)(2,1)S(1)} %get-tuple-element.44), channel_id=1, source_target_pairs={{0,1},{1,0},{2,3},{3,2},{4,5},{5,4},{6,7},{7,6},{8,9},{9,8},{10,11... | collective-permute-start | bytes 49160 | tf_op jit(solution)/shard_map/ppermute | solution.py:396
  14.7 4.2 %collective-permute-start.1 = (bf16[2,64,128]{2,1,0:T(8,128)(2,1)S(1)}, bf16[2,64,128]{2,1,0:T(8,128)(2,1)S(1)}, u32[]{:S(2)}, u32[]{:S(2)}) collective-permute-start(bf16[2,64,128]{2,1,0:T(8,128)(2,1)S(1)} %pad_maximum_fusion.near_ref), channel_id=1, source_target_pairs={{3,0},{4,1},{1,2},{6,3},{7,4},{0,5},{5,6},{2,7},{11,8},{12,9},{9,1... | collective-permute-start | bytes 98312 | tf_op jit(solution)/shard_map/ppermute | solution.py:396
  15.8 6.9 %copy-start.5 = (bf16[4,128,640]{2,1,0:T(8,128)(2,1)S(1)}, bf16[4,128,640]{2,1,0:T(8,128)(2,1)}, u32[]{:S(2)}) copy-start(bf16[4,128,640]{2,1,0:T(8,128)(2,1)} %get-tuple-element.28) | copy-start | bytes 1966084
  19.3 3.5 %collective-permute-start.2 = (f32[48,128]{1,0:T(8,128)S(1)}, f32[48,128]{1,0:T(8,128)S(1)}, u32[]{:S(2)}, u32[]{:S(2)}) collective-permute-start(f32[48,128]{1,0:T(8,128)S(1)} %get-tuple-element.24.near_ref), channel_id=1, source_target_pairs={{0,4},{1,3},{2,6},{3,1},{4,0},{5,7},{6,2},{7,5},{8,12},{9,11},{10,... | collective-permute-start | bytes 73736 | tf_op jit(solution)/shard_map/ppermute | solution.py:396
  20.3 3.7 %collective-permute-start.3 = (f32[48,128]{1,0:T(8,128)S(1)}, f32[48,128]{1,0:T(8,128)S(1)}, u32[]{:S(2)}, u32[]{:S(2)}) collective-permute-start(f32[48,128]{1,0:T(8,128)S(1)} %get-tuple-element.24.near_ref), channel_id=1, source_target_pairs={{0,8},{2,10},{4,12},{6,14},{8,0},{10,2},{12,4},{14,6},{16,24},{18,... | collective-permute-start | bytes 73736 | tf_op jit(solution)/shard_map/ppermute | solution.py:396
  21.0 3.2 %collective-permute-start.4 = (f32[48,128]{1,0:T(8,128)S(1)}, f32[48,128]{1,0:T(8,128)S(1)}, u32[]{:S(2)}, u32[]{:S(2)}) collective-permute-start(f32[48,128]{1,0:T(8,128)S(1)} %get-tuple-element.24.near_ref), channel_id=1, source_target_pairs={{0,12},{2,14},{4,8},{6,10},{8,4},{10,6},{12,0},{14,2},{16,28},{18,... | collective-permute-start | bytes 73736 | tf_op jit(solution)/shard_map/ppermute | solution.py:396
  22.8 18.6 %collective-permute-start.7 = (bf16[512,640]{1,0:T(8,128)(2,1)S(1)}, bf16[512,640]{1,0:T(8,128)(2,1)S(1)}, u32[]{:S(2)}, u32[]{:S(2)}) collective-permute-start(bf16[512,640]{1,0:T(8,128)(2,1)S(1)} %bitcast.28), channel_id=1, source_target_pairs={{0,2},{1,5},{2,0},{3,7},{4,6},{5,1},{6,4},{7,3},{8,10},{9,13},{10,... | collective-permute-start | bytes 1966088 | tf_op jit(solution)/shard_map/ppermute | solution.py:396
  24.1 24.4 %collective-permute-start.8 = (bf16[512,640]{1,0:T(8,128)(2,1)S(1)}, bf16[512,640]{1,0:T(8,128)(2,1)S(1)}, u32[]{:S(2)}, u32[]{:S(2)}) collective-permute-start(bf16[512,640]{1,0:T(8,128)(2,1)S(1)} %slice_bitcast_fusion.1), channel_id=1, source_target_pairs={{0,2},{1,5},{2,0},{3,7},{4,6},{5,1},{6,4},{7,3},{8,10},{9,13},{10,... | collective-permute-start | bytes 1966088 | tf_op jit(solution)/shard_map/ppermute | solution.py:396
  28.1 11.8 %collective-permute-start.13 = (f32[1,128,640]{2,1,0:T(8,128)S(1)}, f32[1,128,640]{2,1,0:T(8,128)S(1)}, u32[]{:S(2)}, u32[]{:S(2)}) collective-permute-start(f32[1,128,640]{2,1,0:T(8,128)S(1)} %get-tuple-element.38), channel_id=1, source_target_pairs={{0,4},{1,3},{2,6},{3,1},{4,0},{5,7},{6,2},{7,5},{8,12},{9,11},{10,... | collective-permute-start | bytes 983048 | tf_op jit(solution)/shard_map/ppermute | solution.py:396
  29.6 15.3 %collective-permute-start.12 = (f32[1,128,640]{2,1,0:T(8,128)S(1)}, f32[1,128,640]{2,1,0:T(8,128)S(1)}, u32[]{:S(2)}, u32[]{:S(2)}) collective-permute-start(f32[1,128,640]{2,1,0:T(8,128)S(1)} %get-tuple-element.36), channel_id=1, source_target_pairs={{0,4},{1,3},{2,6},{3,1},{4,0},{5,7},{6,2},{7,5},{8,12},{9,11},{10,... | collective-permute-start | bytes 983048 | tf_op jit(solution)/shard_map/ppermute | solution.py:396
  29.7 10.0 %collective-permute-start.5 = (f32[48,128]{1,0:T(8,128)S(1)}, f32[48,128]{1,0:T(8,128)S(1)}, u32[]{:S(2)}, u32[]{:S(2)}) collective-permute-start(f32[48,128]{1,0:T(8,128)S(1)} %add_add_fusion.here_ref.refs_5_), channel_id=1, source_target_pairs={{0,1},{2,3},{4,5},{6,7},{8,9},{10,11},{12,13},{14,15},{16,17},{18,... | collective-permute-start | bytes 73736 | tf_op jit(solution)/shard_map/ppermute | solution.py:396
  39.9 8.5 %copy-start = (bf16[4,128,640]{2,1,0:T(8,128)(2,1)S(1)}, bf16[4,128,640]{2,1,0:T(8,128)(2,1)}, u32[]{:S(2)}) copy-start(bf16[4,128,640]{2,1,0:T(8,128)(2,1)} %get-tuple-element.26) | copy-start | bytes 1966084
  40.6 18.9 %collective-permute-start.16 = (f32[1,112,640]{2,1,0:T(8,128)S(1)}, f32[1,112,640]{2,1,0:T(8,128)S(1)}, u32[]{:S(2)}, u32[]{:S(2)}) collective-permute-start(f32[1,112,640]{2,1,0:T(8,128)S(1)} %meet.3.refs_8_), channel_id=1, source_target_pairs={{0,8},{1,9},{2,10},{3,11},{4,12},{5,13},{6,14},{7,15},{8,0},{9,1},... | collective-permute-start | bytes 860168 | tf_op jit(solution)/shard_map/ppermute | solution.py:396
  45.6 27.8 %collective-permute-start.14 = (f32[1,112,640]{2,1,0:T(8,128)S(1)}, f32[1,112,640]{2,1,0:T(8,128)S(1)}, u32[]{:S(2)}, u32[]{:S(2)}) collective-permute-start(f32[1,112,640]{2,1,0:T(8,128)S(1)} %meet.2.refs_7_), channel_id=1, source_target_pairs={{0,8},{1,9},{2,10},{3,11},{4,12},{5,13},{6,14},{7,15},{8,0},{9,1},... | collective-permute-start | bytes 860168 | tf_op jit(solution)/shard_map/ppermute | solution.py:396
  49.6 17.4 %collective-permute-start.15 = (f32[112,640]{1,0:T(8,128)S(1)}, f32[112,640]{1,0:T(8,128)S(1)}, u32[]{:S(2)}, u32[]{:S(2)}) collective-permute-start(f32[112,640]{1,0:T(8,128)S(1)} %get-tuple-element.40), channel_id=1, source_target_pairs={{0,4},{1,3},{2,6},{3,1},{4,0},{5,7},{6,2},{7,5},{8,12},{9,11},{10,... | collective-permute-start | bytes 860168 | tf_op jit(solution)/shard_map/ppermute | solution.py:396
  50.9 22.4 %collective-permute-start.18 = (f32[112,640]{1,0:T(8,128)S(1)}, f32[112,640]{1,0:T(8,128)S(1)}, u32[]{:S(2)}, u32[]{:S(2)}) collective-permute-start(f32[112,640]{1,0:T(8,128)S(1)} %get-tuple-element.42), channel_id=1, source_target_pairs={{0,5},{1,2},{2,7},{3,0},{4,1},{5,6},{6,3},{7,4},{8,13},{9,10},{10,... | collective-permute-start | bytes 860168 | tf_op jit(solution)/shard_map/ppermute | solution.py:396
  59.6 13.8 %collective-permute-start.17 = (f32[112,640]{1,0:T(8,128)S(1)}, f32[112,640]{1,0:T(8,128)S(1)}, u32[]{:S(2)}, u32[]{:S(2)}) collective-permute-start(f32[112,640]{1,0:T(8,128)S(1)} %bitcast_add_fusion), channel_id=1, source_target_pairs={{0,1},{1,0},{2,3},{3,2},{4,5},{5,4},{6,7},{7,6},{8,9},{9,8},{10,11... | collective-permute-start | bytes 860168 | tf_op jit(solution)/shard_map/ppermute | solution.py:396
  (1 other events, 6.7 us)

commit v11 on v8

--- a/solution.py
+++ b/solution.py
@@ -35,7 +35,7 @@
 
 
 def pack_kernel(
-    plan, x_ref, kept0_ref, kept1_ref, sent0_ref, sent1_ref, other0_ref, other1_ref
+    plan, x_ref, kept0_ref, kept1_ref, sent0_ref, rest_ref, sent1_ref, other0_ref, other1_ref
 ):
     step = pl.program_id(0)
     me = lax.axis_index("pat")
@@ -52,10 +52,12 @@
         for sent in range(2):
             for chunk in range(2):
                 middle = len(plan.middle_bits)
+                far_owner = step >> (1 + middle)
+                way = side if chunk else side * (1 - far_owner)
                 relative = (
-                    (step >> (1 + middle))
-                    | (sent << (1 + side))
-                    | ((step & 1) << (2 - side))
+                    far_owner
+                    | (sent << (1 + way))
+                    | ((step & 1) << (2 - way))
                     | (((step >> 1) & ((1 << middle) - 1)) << 3)
                     | (chunk << plan.top_bit)
                 )
@@ -65,16 +67,25 @@
                 head = x_ref[:, tile(first + side * plan.share)]
                 tail = x_ref[:, tile(first + plan.tiles)]
                 folded = jnp.where(lane >= edge, head.astype(jnp.float32), tail.astype(jnp.float32))
+
+                def write(target):
+                    target[:, 0:LANES] = folded.astype(x_ref.dtype)
+                    for slot in range(1, plan.share):
+                        here = slice(slot * LANES, (slot + 1) * LANES)
+                        target[:, here] = x_ref[:, tile(first + side * plan.share + slot)]
+
                 if away:
-                    target = (other0_ref, other1_ref)[chunk].at[sent]
-                elif sent:
-                    target = (sent0_ref, sent1_ref)[chunk]
+                    write((other0_ref, other1_ref)[chunk].at[sent])
+                elif not sent:
+                    write((kept0_ref, kept1_ref)[chunk])
+                elif chunk:
+                    write(sent1_ref)
                 else:
-                    target = (kept0_ref, kept1_ref)[chunk]
-                target[:, 0:LANES] = folded.astype(x_ref.dtype)
-                for slot in range(1, plan.share):
-                    here = slice(slot * LANES, (slot + 1) * LANES)
-                    target[:, here] = x_ref[:, tile(first + side * plan.share + slot)]
+                    for half, ref in enumerate((sent0_ref, rest_ref)):
+
+                        @pl.when(far_owner == half)
+                        def _():
+                            write(ref)
 
 
 def pack(covariates, plan):
@@ -84,13 +95,19 @@
     mine = jax.ShapeDtypeStruct((length, plan.width), dtype)
     other = jax.ShapeDtypeStruct((2, length, plan.width), dtype)
     mine_spec = pl.BlockSpec((rows, plan.width), lambda s: (s, 0))
+    half = plan.places // 2
+    part = jax.ShapeDtypeStruct((half * rows, plan.width), dtype)
+    part_specs = [
+        pl.BlockSpec((rows, plan.width), lambda s: (jnp.minimum(s, half - 1), 0)),
+        pl.BlockSpec((rows, plan.width), lambda s: (jnp.maximum(s - half, 0), 0)),
+    ]
     other_spec = pl.BlockSpec((2, rows, plan.width), lambda s: (0, s, 0))
     return pl.pallas_call(
         functools.partial(pack_kernel, plan),
         grid=(plan.places,),
         in_specs=[pl.BlockSpec(memory_space=pltpu.VMEM)],
-        out_specs=[mine_spec] * 4 + [other_spec] * 2,
-        out_shape=[mine] * 4 + [other] * 2,
+        out_specs=[mine_spec] * 2 + part_specs + [mine_spec] + [other_spec] * 2,
+        out_shape=[mine] * 2 + [part] * 2 + [mine] + [other] * 2,
         compiler_params=pltpu.CompilerParams(vmem_limit_bytes=12 << 20),
         cost_estimate=pl.CostEstimate(
             flops=0, bytes_accessed=4 * covariates.size, transcendentals=0
@@ -146,7 +163,8 @@
     return (near_ref.at[0], near_ref.at[1], far_ref.at[1], far_ref.at[0])
 
 
-def group_kernel(weightings, pick_ref, near_ref, far_ref, totals_ref, panel_ref):
+def group_kernel(weightings, pick_ref, near_ref, far_ref, *refs):
+    totals_ref, panel_ref = refs[-2:]
     onehot = onehot_of(pick_ref, weightings, jnp.bfloat16)
     target_sum, other_sum = 0.0, 0.0
     for member in members_of(near_ref, far_ref):
@@ -163,13 +181,13 @@
     lighter_panel(panel_ref, members_of(near_ref, far_ref), onehot, lighter_of(totals))
 
 
-def make_group(near, far, pick_column, weightings):
+def make_group(near, far, pick_column, weightings, after):
     comps = pick_column.shape[0]
     return small_call(
         functools.partial(group_kernel, weightings),
         [((comps, LANES), jnp.float32), ((comps + weightings, 4 * LANES), jnp.bfloat16)],
         [pick_column, near, far],
-        [],
+        after,
         "group",
     )
 
@@ -203,6 +221,31 @@
         [pick_column, near, far, totals, told],
         [],
         "panels",
+    )
+
+
+def rest_kernel(weightings, pick_ref, near_ref, far_ref, stats_ref, first_ref, second_ref):
+    comps = pick_ref.shape[0]
+    onehot = onehot_of(pick_ref, weightings, jnp.bfloat16)
+    light = stats_ref[2][:, 0:1]
+    columns = lighter_panel(first_ref, members_of(near_ref, far_ref), onehot, light)
+    for place, (target, other) in enumerate(columns):
+        here = slice(place * LANES, (place + 1) * LANES)
+        second_ref[0:comps, here] = target.astype(jnp.bfloat16)
+        second_ref[comps:2 * comps, here] = other.astype(jnp.bfloat16)
+
+
+def rest_panels(near, far, stats, pick_column, weightings):
+    comps = pick_column.shape[0]
+    return small_call(
+        functools.partial(rest_kernel, weightings),
+        [
+            ((comps + weightings, 4 * LANES), jnp.bfloat16),
+            ((2 * comps, 4 * LANES), jnp.bfloat16),
+        ],
+        [pick_column, near, far, stats],
+        [],
+        "rest_panels",
     )
 
 
@@ -259,30 +302,6 @@
     return pl.BlockSpec(shape, lambda s: (0,) * len(shape))
 
 
-def moments_kernel(rows, split, *refs):
-    kept_ref, passed_ref, *swapped_refs, first_ref, second_ref, stats_ref = refs[:7]
-    outs = refs[-(2 if split is None else split):]
-    first_rows = first_ref.shape[0]
-    comps = second_ref.shape[0] // 2
-    inverse_target = stats_ref[0][:, 0:1]
-    inverse_other = stats_ref[1][:, 0:1]
-    for place in range(swapped_refs[0].shape[0] // rows):
-        here = slice(place * rows, (place + 1) * rows)
-        x = jnp.concatenate(
-            [kept_ref[here, :], passed_ref[0, here, :]]
-            + [ref[here, :] for ref in swapped_refs],
-            axis=0,
-        )
-        first = jnp.dot(first_ref[...], x, preferred_element_type=jnp.float32)
-        squares = (x.astype(jnp.float32) * x.astype(jnp.float32)).astype(jnp.bfloat16)
-        second = jnp.dot(second_ref[...], squares, preferred_element_type=jnp.float32)
-        out = outs[place % 2].at[place // 2] if split is None else outs[place]
-        out[0:first_rows, :] = first
-        out[first_rows:first_rows + comps, :] = (
-            second[0:comps] * inverse_target + second[comps:2 * comps] * inverse_other
-        )
-
-
 def group_moments_kernel(rows, count, *refs):
     kept_ref, passed_ref, *swapped_refs, panel_ref = refs[:5]
     outs = refs[-2 * count:]
@@ -322,23 +341,50 @@
     return outs[0:2], outs[2:4]
 
 
-def moments(plan, rows_here, first, second, stats, split, after):
+def moments_kernel(rows, half, kept_ref, passed_ref, swapped_ref, *refs):
+    first_ref, second_ref, stats_ref = refs[:3]
+    outs = refs[-2:]
+    first_rows = first_ref.shape[0]
+    comps = second_ref.shape[0] // 2
+    inverse_target = stats_ref[0][:, 0:1]
+    inverse_other = stats_ref[1][:, 0:1]
+    places = swapped_ref.shape[1] // rows
+    for place in range(places):
+        here = slice(place * rows, (place + 1) * rows)
+        there = slice((half * places + place) * rows, (half * places + place + 1) * rows)
+        x = jnp.concatenate(
+            [
+                kept_ref[there, :],
+                passed_ref[0, there, :],
+                swapped_ref[0, here, :],
+                swapped_ref[1, here, :],
+            ],
+            axis=0,
+        )
+        first = jnp.dot(first_ref[...], x, preferred_element_type=jnp.float32)
+        squares = (x.astype(jnp.float32) * x.astype(jnp.float32)).astype(jnp.bfloat16)
+        second = jnp.dot(second_ref[...], squares, preferred_element_type=jnp.float32)
+        out = outs[place % 2].at[place // 2]
+        out[0:first_rows, :] = first
+        out[first_rows:first_rows + comps, :] = (
+            second[0:comps] * inverse_target + second[comps:2 * comps] * inverse_other
+        )
+
+
+def moments(plan, half, kept, passed, swapped, first, second, stats, after):
     rows = first.shape[1] // 4
-    sums = (first.shape[0] + second.shape[0] // 2, plan.width)
-    if split:
-        out_shape = [jax.ShapeDtypeStruct(sums, jnp.float32)] * plan.places
-    else:
-        out_shape = [jax.ShapeDtypeStruct((plan.places // 2,) + sums, jnp.float32)] * 2
+    out_rows = first.shape[0] + second.shape[0] // 2
+    out = jax.ShapeDtypeStruct((plan.places // 4, out_rows, plan.width), jnp.float32)
     return pl.pallas_call(
-        functools.partial(moments_kernel, rows, plan.places if split else None),
-        in_specs=[pl.BlockSpec(memory_space=pltpu.VMEM)] * 7
+        functools.partial(moments_kernel, rows, half),
+        in_specs=[pl.BlockSpec(memory_space=pltpu.VMEM)] * 6
         + [pl.BlockSpec(memory_space=pl.ANY)] * len(after),
-        out_specs=[pl.BlockSpec(memory_space=pltpu.VMEM)] * len(out_shape),
-        out_shape=out_shape,
+        out_specs=[pl.BlockSpec(memory_space=pltpu.VMEM)] * 2,
+        out_shape=[out] * 2,
         compiler_params=pltpu.CompilerParams(vmem_limit_bytes=20 << 20),
-        cost_estimate=pl.CostEstimate(flops=0, bytes_accessed=6 << 20, transcendentals=0),
+        cost_estimate=pl.CostEstimate(flops=0, bytes_accessed=3 << 20, transcendentals=0),
         name="moments",
-    )(*rows_here, first, second, stats, *after)
+    )(kept, passed, swapped, first, second, stats, *after)
 
 
 def finish_kernel(plan, weightings, counts, pick_ref, stats_ref, *refs):
@@ -389,6 +435,24 @@
     )(pick_column, stats, *operands)
 
 
+def hold_kernel(*refs):
+    del refs
+
+
+def hold(array, after):
+    any_space = pl.BlockSpec(memory_space=pl.ANY)
+    return pl.pallas_call(
+        hold_kernel,
+        in_specs=[any_space] * (1 + len(after)),
+        out_specs=any_space,
+        out_shape=jax.ShapeDtypeStruct(array.shape, array.dtype),
+        input_output_aliases={0: 0},
+        compiler_params=pltpu.CompilerParams(vmem_limit_bytes=1 << 20),
+        cost_estimate=pl.CostEstimate(flops=0, bytes_accessed=0, transcendentals=0),
+        name="hold",
+    )(array, *after)
+
+
 def swap(array, pairs):
     return lax.ppermute(array, "pat", pairs)
 
@@ -403,18 +467,19 @@
     if covs > 1:
         arm_rows = lax.all_gather(arm_rows, "cov", axis=0, tiled=True)
     mine = jnp.concatenate([weights.T, arm_rows], axis=0)
-    near = jnp.stack([mine, swap(mine, to_other_side)])
+    kept0, kept1, sent0, rest, sent1, other0, other1 = pack(covariates, plan)
+    passed1 = swap(other1, to_other_side)
+    rows1 = [kept1, passed1, swap(sent1, plan.by_rows()), swap(passed1[1], plan.by_rows())]
+    passed0 = swap(other0, to_other_side)
+    length = rest.shape[0]
+    swapped0 = swap(jnp.stack([sent0, passed0[1, :length]]), plan.by_rows())
+
+    near = jnp.stack([mine, swap(hold(mine, [passed1]), to_other_side)])
     far = swap(near, [(pair ^ 1, d) for d, pair in plan.by_rows()])
 
-    kept0, kept1, sent0, sent1, other0, other1 = pack(covariates, plan)
-    rows_here = {}
-    for chunk, kept, sent, other in ((1, kept1, sent1, other1), (0, kept0, sent0, other0)):
-        passed = swap(other, to_other_side)
-        rows_here[chunk] = [
-            kept, passed, swap(sent, plan.by_rows()), swap(passed[1], plan.by_rows())
-        ]
-
-    near_totals, panel = make_group(near, far, pick_column, weightings)
+    far_rest = swap(near, plan.by_mask(3))
+
+    near_totals, panel = make_group(near, far, pick_column, weightings, [far_rest, rows1[2]])
     far_totals = swap(near_totals, plan.by_sums())
     totals = near_totals + far_totals
     for mask in range(8, n, 8):
@@ -423,8 +488,9 @@
     told = swap(totals, to_other_side[0::2])
     first, second, stats = make_panels(near, far, totals, told, pick_column, weightings)
 
-    across, top, after = [], [], [rows_here[0][2]]
-    for even, odd in group_moments(plan, rows_here[1], panel, [totals]):
+    across, top, after = [], [], [swapped0]
+    sums = group_moments(plan, rows1, panel, [totals])
+    for even, odd in sums:
         arrived = swap(odd, plan.by_sums())
         met = meet(pick_column, near_totals, far_totals, stats, even, arrived, after)
         for bit in plan.middle_bits:
@@ -433,24 +499,29 @@
         top.append(swap(met, plan.by_mask(1 << plan.top_bit))[0])
         after = []
 
-    last = not plan.middle_bits
-    sums = moments(plan, rows_here[0], first, second, stats, last, across)
-    if last:
-        even, odd = sums[0::2], sums[1::2]
-        other_owner = [(d, pair ^ 1) for d, pair in plan.by_sums()]
+    rest = hold(jnp.stack([rest, passed0[1, length:]]), [sums[0][0]])
+    swapped_rest = swap(rest, plan.by_mask(2))
+    first_rest, second_rest = rest_panels(near, far_rest, stats, pick_column, weightings)
+
+    even, odd = moments(
+        plan, 0, kept0, passed0, swapped0, first, second, stats, across
+    )
+    even_rest, odd_rest = moments(
+        plan, 1, kept0, passed0, swapped_rest, first_rest, second_rest, stats, [even]
+    )
+    if plan.middle_bits:
+        for half, pairs in ((0, plan.by_sums()), (1, plan.by_mask(4))):
+            here, there = ((even, odd), (even_rest, odd_rest))[half]
+            met = here + swap(there, pairs)
+            for bit in plan.middle_bits:
+                met = met[0::2] + swap(met[1::2], plan.by_mask(1 << bit))
+            top[half] = top[half] + met[0]
+        parts = [[top[0]], [swap(top[1], to_other_side)]]
+    else:
         parts = [
-            [even[0], top[0], swap(odd[0], plan.by_sums())],
-            [swap(even[1] + top[1], to_other_side), swap(odd[1], other_owner)],
+            [even[0], top[0], swap(odd, plan.by_sums())[0]],
+            [swap(even_rest[0] + top[1], to_other_side), swap(odd_rest, plan.by_mask(5))[0]],
         ]
-    else:
-        even, odd = sums
-        arrived = swap(odd, plan.by_sums())
-        for bit in plan.middle_bits:
-            odd = even[1::2] + arrived[1::2]
-            even = even[0::2] + arrived[0::2]
-            arrived = swap(odd, plan.by_mask(1 << bit))
-        total = [even[side] + arrived[side] + top[side] for side in range(2)]
-        parts = [[total[0]], [swap(total[1], to_other_side)]]
     return finish(plan, parts, pick_column, stats, weightings)
 
 

time: 74.4 us -> 87.3 us (1.17)
  waiting for transfers between devices: 25.5 us -> 47.1 us
  starting transfers between devices: 35.2 us -> 24.4 us
  local copies, waits for them, and re-layouts: 3.53 us -> 5.83 us
    ppermute x19 -> x20, waiting for transfers between devices: 25.5 us -> 47.1 us  [swap(): return lax.ppermute(array, 'pat', pairs)]
    ppermute x19 -> x20, starting transfers between devices: 35.2 us -> 24.4 us  [swap(): return lax.ppermute(array, 'pat', pairs)]
    unnamed x16 -> x24, local copies, waits for them, and re-layouts: 2.47 us -> 5.62 us
    pallas_call x1, Pallas kernels: 2.35 us -> 1.07 us  [group_moments(): pl.pallas_call(functools.partial(group_moments_kernel, rows, 2), in_specs...]
    squeeze x2 -> x1, local copies, waits for them, and re-layouts: 0.96 us -> 0.06 us  [on_device(): passed1[1]]
    pallas_call x4 -> x5, Pallas kernels: 1.96 us -> 2.17 us  [small_call(): pl.pallas_call(kernel, in_specs=[vmem] * len(operands) + [pl.BlockSpec(me...]
  transfers between devices with their start and end apart: 19 -> 20, of which waited for: 8 -> 10; matrix products, arithmetic and copies ran while one was open for 1% -> 0% of each run, Pallas kernels for 7% -> 5%
where the time goes in v11:
time: 87.3 us; the launch traced here: 86.7 us
  waiting for transfers between devices  47.1 us (54%)
  starting transfers between devices  24.4 us (28%)
  Pallas kernels  8.96 us (10%)
  local copies, waits for them, and re-layouts  5.83 us (7%)
    ppermute x20, waiting for transfers between devices, swap(): return lax.ppermute(array, 'pat', pairs)  47.1 us
    ppermute x20, starting transfers between devices, swap(): return lax.ppermute(array, 'pat', pairs)  24.4 us
    unnamed x24, local copies, waits for them, and re-layouts  5.62 us
    pallas_call x1, Pallas kernels, pack(): pl.pallas_call(functools.partial(pack_kernel, plan), grid=(plan.places,),...  2.86 us
    pallas_call x5, Pallas kernels, small_call(): pl.pallas_call(kernel, in_specs=[vmem] * len(operands) + [pl.BlockSpec(me...  2.17 us
  transfers between devices with their start and end apart: 20, of which 10 were waited for; matrix products, arithmetic and copies ran while one was open for 0% of the time, Pallas kernels for 5%

profile of v11, /device:TPU:1, one launch (start us, length us, event | category | flops | bytes accessed | tf_op | source)
XLA Modules:
  0.0 86.7 jit_solution(3068353063467106756)
XLA Ops:
  0.0 2.4 %copy-done = bf16[128,19968]{1,0:T(8,128)(2,1)S(1)} copy-done((bf16[128,19968]{1,0:T(8,128)(2,1)S(1)}, bf16[128,19968]{1,0:T(8,128)(2,1)}, u32[]{:S(2)}) %copy-start) | copy-done | bytes 5111832
  2.5 2.9 %pack.1 = (bf16[512,640]{1,0:T(8,128)(2,1)S(1)}, bf16[512,640]{1,0:T(8,128)(2,1)S(1)}, bf16[256,640]{1,0:T(8,128)(2,1)S(1)}, bf16[256,640]{1,0:T(8,128)(2,1)S(1)...) custom-call(bf16[128,19968]{1,0:T(8,128)(2,1)S(1)} %copy-done), custom_call_target="tpu_custom_call" | custom-call | bytes 10223616 | tf_op jit(solution)/shard_map/pack/pallas_call | solution.py:105
  9.0 2.3 %collective-permute-start.4 = (bf16[512,640]{1,0:T(8,128)(2,1)}, bf16[512,640]{1,0:T(8,128)(2,1)S(1)}, u32[]{:S(2)}, u32[]{:S(2)}) collective-permute-start(bf16[512,640]{1,0:T(8,128)(2,1)} %get-tuple-element.28), channel_id=1, source_target_pairs={{0,2},{1,5},{2,0},{3,7},{4,6},{5,1},{6,4},{7,3},{8,10},{9,13},{10,... | collective-permute-start | bytes 1966088 | tf_op jit(solution)/shard_map/ppermute | solution.py:457
  12.3 2.4 %collective-permute-start.11 = (bf16[512,640]{1,0:T(8,128)(2,1)S(1)}, bf16[512,640]{1,0:T(8,128)(2,1)S(1)}, u32[]{:S(2)}, u32[]{:S(2)}) collective-permute-start(bf16[512,640]{1,0:T(8,128)(2,1)S(1)} %slice_bitcast_fusion), channel_id=1, source_target_pairs={{0,2},{1,5},{2,0},{3,7},{4,6},{5,1},{6,4},{7,3},{8,10},{9,13},{10,... | collective-permute-start | bytes 1966088 | tf_op jit(solution)/shard_map/ppermute | solution.py:457
  14.7 1.6 %collective-permute-start.3 = (bf16[2,64,128]{2,1,0:T(8,128)(2,1)S(1)}, bf16[2,64,128]{2,1,0:T(8,128)(2,1)S(1)}, u32[]{:S(2)}, u32[]{:S(2)}) collective-permute-start(bf16[2,64,128]{2,1,0:T(8,128)(2,1)S(1)} %pad_maximum_fusion.2.near_ref), channel_id=1, source_target_pairs={{0,3},{1,2},{2,1},{3,0},{4,7},{5,6},{6,5},{7,4},{8,11},{9,10},{10,... | collective-permute-start | bytes 98312 | tf_op jit(solution)/shard_map/ppermute | solution.py:457
  16.6 1.4 %collective-permute-start.10 = (bf16[2,256,640]{2,1,0:T(8,128)(2,1)S(1)}, bf16[2,256,640]{2,1,0:T(8,128)(2,1)S(1)}, u32[]{:S(2)}, u32[]{:S(2)}) collective-permute-start(bf16[2,256,640]{2,1,0:T(8,128)(2,1)S(1)} %pad_maximum_fusion), channel_id=1, source_target_pairs={{0,2},{1,5},{2,0},{3,7},{4,6},{5,1},{6,4},{7,3},{8,10},{9,13},{10,... | collective-permute-start | bytes 1966088 | tf_op jit(solution)/shard_map/ppermute | solution.py:457
  18.1 1.7 %collective-permute-done.4.refs_1_.refs_2_ = bf16[512,640]{1,0:T(8,128)(2,1)S(1)} collective-permute-done((bf16[512,640]{1,0:T(8,128)(2,1)}, bf16[512,640]{1,0:T(8,128)(2,1)S(1)}, u32[]{:S(2)}, u32[]{:S(2)}) %collective-permute-start.4) | collective-permute-done | bytes 655392 | tf_op jit(solution)/shard_map/ppermute | solution.py:457
  19.8 8.4 %collective-permute-done.3.refs_0_.far_ref = bf16[2,64,128]{2,1,0:T(8,128)(2,1)S(1)} collective-permute-done((bf16[2,64,128]{2,1,0:T(8,128)(2,1)S(1)}, bf16[2,64,128]{2,1,0:T(8,128)(2,1)S(1)}, u32[]{:S(2)}, u32[]{:S(2)}) %collective-permute-start.3) | collective-permute-done | bytes 32800 | tf_op jit(solution)/shard_map/ppermute | solution.py:457
  30.0 1.8 %collective-permute-start.5 = (f32[48,128]{1,0:T(8,128)S(1)}, f32[48,128]{1,0:T(8,128)S(1)}, u32[]{:S(2)}, u32[]{:S(2)}) collective-permute-start(f32[48,128]{1,0:T(8,128)S(1)} %get-tuple-element.29.near_ref), channel_id=1, source_target_pairs={{0,4},{1,3},{2,6},{3,1},{4,0},{5,7},{6,2},{7,5},{8,12},{9,11},{10,... | collective-permute-start | bytes 73736 | tf_op jit(solution)/shard_map/ppermute | solution.py:457
  31.9 1.7 %collective-permute-done.5.far_ref = f32[48,128]{1,0:T(8,128)S(1)} collective-permute-done((f32[48,128]{1,0:T(8,128)S(1)}, f32[48,128]{1,0:T(8,128)S(1)}, u32[]{:S(2)}, u32[]{:S(2)}) %collective-permute-start.5) | collective-permute-done | bytes 24608 | tf_op jit(solution)/shard_map/ppermute | solution.py:457
  33.6 1.1 %group_moments.1 = (f32[1,128,640]{2,1,0:T(8,128)S(1)}, f32[1,128,640]{2,1,0:T(8,128)S(1)}, f32[1,128,640]{2,1,0:T(8,128)S(1)}, f32[1,128,640]{2,1,0:T(8,128)S(1)}) custom-call(bf16[512,640]{1,0:T(8,128)(2,1)S(1)} %copy-done.4, bf16[2,512,640]{2,1,0:T(8,128)(2,1)S(1)} %collective-permute-done.refs_1_, ...), custom_call_target="tpu_custom_call" | custom-call | bytes 6291456 | tf_op jit(solution)/shard_map/group_moments/pallas_call | solution.py:331
  34.7 1.5 %collective-permute-start.16 = (bf16[2,256,640]{2,1,0:T(8,128)(2,1)S(1)}, bf16[2,256,640]{2,1,0:T(8,128)(2,1)S(1)}, u32[]{:S(2)}, u32[]{:S(2)}) collective-permute-start(bf16[2,256,640]{2,1,0:T(8,128)(2,1)S(1)} %hold.3), channel_id=1, source_target_pairs={{0,2},{1,3},{2,0},{3,1},{4,6},{5,7},{6,4},{7,5},{8,10},{9,11},{10,... | collective-permute-start | bytes 1966088 | tf_op jit(solution)/shard_map/ppermute | solution.py:457
  36.3 1.4 %collective-permute-start.12 = (f32[1,128,640]{2,1,0:T(8,128)S(1)}, f32[1,128,640]{2,1,0:T(8,128)S(1)}, u32[]{:S(2)}, u32[]{:S(2)}) collective-permute-start(f32[1,128,640]{2,1,0:T(8,128)S(1)} %get-tuple-element.39), channel_id=1, source_target_pairs={{0,4},{1,3},{2,6},{3,1},{4,0},{5,7},{6,2},{7,5},{8,12},{9,11},{10,... | collective-permute-start | bytes 983048 | tf_op jit(solution)/shard_map/ppermute | solution.py:457
  37.7 1.3 %collective-permute-start.8 = (f32[48,128]{1,0:T(8,128)S(1)}, f32[48,128]{1,0:T(8,128)S(1)}, u32[]{:S(2)}, u32[]{:S(2)}) collective-permute-start(f32[48,128]{1,0:T(8,128)S(1)} %add_add_fusion.here_ref.refs_5_), channel_id=1, source_target_pairs={{0,1},{2,3},{4,5},{6,7},{8,9},{10,11},{12,13},{14,15},{16,17},{18,... | collective-permute-start | bytes 73736 | tf_op jit(solution)/shard_map/ppermute | solution.py:457
  39.0 7.7 %collective-permute-done.8.told_ref = f32[48,128]{1,0:T(8,128)S(1)} collective-permute-done((f32[48,128]{1,0:T(8,128)S(1)}, f32[48,128]{1,0:T(8,128)S(1)}, u32[]{:S(2)}, u32[]{:S(2)}) %collective-permute-start.8) | collective-permute-done | bytes 24608 | tf_op jit(solution)/shard_map/ppermute | solution.py:457
  46.9 4.2 %collective-permute-done.13.right_ref = f32[1,128,640]{2,1,0:T(8,128)S(1)} collective-permute-done((f32[1,128,640]{2,1,0:T(8,128)S(1)}, f32[1,128,640]{2,1,0:T(8,128)S(1)}, u32[]{:S(2)}, u32[]{:S(2)}) %collective-permute-start.13) | collective-permute-done | bytes 327712 | tf_op jit(solution)/shard_map/ppermute | solution.py:457
  51.8 2.9 %collective-permute-start.17 = (f32[1,112,640]{2,1,0:T(8,128)S(1)}, f32[1,112,640]{2,1,0:T(8,128)S(1)}, u32[]{:S(2)}, u32[]{:S(2)}) collective-permute-start(f32[1,112,640]{2,1,0:T(8,128)S(1)} %meet.3.refs_4_), channel_id=1, source_target_pairs={{0,8},{1,9},{2,10},{3,11},{4,12},{5,13},{6,14},{7,15},{8,0},{9,1},... | collective-permute-start | bytes 860168 | tf_op jit(solution)/shard_map/ppermute | solution.py:457
  54.9 2.9 %collective-permute-done.12.right_ref = f32[1,128,640]{2,1,0:T(8,128)S(1)} collective-permute-done((f32[1,128,640]{2,1,0:T(8,128)S(1)}, f32[1,128,640]{2,1,0:T(8,128)S(1)}, u32[]{:S(2)}, u32[]{:S(2)}) %collective-permute-start.12) | collective-permute-done | bytes 327712 | tf_op jit(solution)/shard_map/ppermute | solution.py:457
  58.5 3.1 %collective-permute-start.14 = (f32[1,112,640]{2,1,0:T(8,128)S(1)}, f32[1,112,640]{2,1,0:T(8,128)S(1)}, u32[]{:S(2)}, u32[]{:S(2)}) collective-permute-start(f32[1,112,640]{2,1,0:T(8,128)S(1)} %meet.2.refs_3_), channel_id=1, source_target_pairs={{0,8},{1,9},{2,10},{3,11},{4,12},{5,13},{6,14},{7,15},{8,0},{9,1},... | collective-permute-start | bytes 860168 | tf_op jit(solution)/shard_map/ppermute | solution.py:457
  62.3 1.5 %collective-permute-start.15 = (f32[1,112,640]{2,1,0:T(8,128)S(1)}, f32[1,112,640]{2,1,0:T(8,128)S(1)}, u32[]{:S(2)}, u32[]{:S(2)}) collective-permute-start(f32[1,112,640]{2,1,0:T(8,128)S(1)} %get-tuple-element.43), channel_id=1, source_target_pairs={{0,4},{1,3},{2,6},{3,1},{4,0},{5,7},{6,2},{7,5},{8,12},{9,11},{10,... | collective-permute-start | bytes 860168 | tf_op jit(solution)/shard_map/ppermute | solution.py:457
  64.4 8.6 %collective-permute-done.17 = f32[1,112,640]{2,1,0:T(8,128)S(1)} collective-permute-done((f32[1,112,640]{2,1,0:T(8,128)S(1)}, f32[1,112,640]{2,1,0:T(8,128)S(1)}, u32[]{:S(2)}, u32[]{:S(2)}) %collective-permute-start.17) | collective-permute-done | bytes 286752 | tf_op jit(solution)/shard_map/ppermute | solution.py:457
  73.6 5.4 %collective-permute-done.14 = f32[1,112,640]{2,1,0:T(8,128)S(1)} collective-permute-done((f32[1,112,640]{2,1,0:T(8,128)S(1)}, f32[1,112,640]{2,1,0:T(8,128)S(1)}, u32[]{:S(2)}, u32[]{:S(2)}) %collective-permute-start.14) | collective-permute-done | bytes 286752 | tf_op jit(solution)/shard_map/ppermute | solution.py:457
  79.0 6.2 %collective-permute-done.19 = f32[1,112,640]{2,1,0:T(8,128)S(1)} collective-permute-done((f32[1,112,640]{2,1,0:T(8,128)S(1)}, f32[1,112,640]{2,1,0:T(8,128)S(1)}, u32[]{:S(2)}, u32[]{:S(2)}) %collective-permute-start.19) | collective-permute-done | bytes 286752 | tf_op jit(solution)/shard_map/ppermute | solution.py:457
  85.1 1.6 %finish.1 = f32[48,1,1248]{2,1,0:T(1,128)} custom-call(s32[48,1]{1,0:T(8,128)S(1)} %copy.12.pick_ref, f32[3,48,128]{2,1,0:T(8,128)S(1)} %get-tuple-element.30.stats_ref.refs_2_, f32[112,640]{1,0:T(8,128)S(1)} %bitcast.17, f32[112,640]{1,0:T(8,128)S(1)} %bitcast.20, f32[112,640]{1,0:T(8,128)S(1)} %bitcast.21, f32[112,640]{1,0:T(8,128)S(1)} %collective-permute-done.18.refs_3_, ...), custom_call_target="tpu_custom_call" | custom-call | bytes 16384 | tf_op jit(solution)/shard_map/finish/pallas_call | solution.py:426
  (62 shorter events, 10.5 us)
Async XLA Ops:
  2.5 8.9 %copy-start.10 = (bf16[128,16]{0,1:T(8,128)(2,1)S(1)}, bf16[128,16]{0,1:T(8,128)(2,1)}, u32[]{:S(2)}) copy-start(bf16[128,16]{0,1:T(8,128)(2,1)} %param.5) | copy-start | bytes 12292
  8.5 3.2 %collective-permute-start = (bf16[2,512,640]{2,1,0:T(8,128)(2,1)}, bf16[2,512,640]{2,1,0:T(8,128)(2,1)S(1)}, u32[]{:S(2)}, u32[]{:S(2)}) collective-permute-start(bf16[2,512,640]{2,1,0:T(8,128)(2,1)} %get-tuple-element.27), channel_id=1, source_target_pairs={{0,1},{1,0},{2,3},{3,2},{4,5},{5,4},{6,7},{7,6},{8,9},{9,8},{10,11... | collective-permute-start | bytes 3932168 | tf_op jit(solution)/shard_map/ppermute | solution.py:457
  8.5 6.1 %collective-permute-start.9 = (bf16[2,512,640]{2,1,0:T(8,128)(2,1)}, bf16[2,512,640]{2,1,0:T(8,128)(2,1)S(1)}, u32[]{:S(2)}, u32[]{:S(2)}) collective-permute-start(bf16[2,512,640]{2,1,0:T(8,128)(2,1)} %get-tuple-element.32), channel_id=1, source_target_pairs={{0,1},{1,0},{2,3},{3,2},{4,5},{5,4},{6,7},{7,6},{8,9},{9,8},{10,11... | collective-permute-start | bytes 3932168 | tf_op jit(solution)/shard_map/ppermute | solution.py:457
  9.0 10.8 %collective-permute-start.4 = (bf16[512,640]{1,0:T(8,128)(2,1)}, bf16[512,640]{1,0:T(8,128)(2,1)S(1)}, u32[]{:S(2)}, u32[]{:S(2)}) collective-permute-start(bf16[512,640]{1,0:T(8,128)(2,1)} %get-tuple-element.28), channel_id=1, source_target_pairs={{0,2},{1,5},{2,0},{3,7},{4,6},{5,1},{6,4},{7,3},{8,10},{9,13},{10,... | collective-permute-start | bytes 1966088 | tf_op jit(solution)/shard_map/ppermute | solution.py:457
  11.7 3.0 %collective-permute-start.1 = (bf16[64,128]{1,0:T(8,128)(2,1)S(1)}, bf16[64,128]{1,0:T(8,128)(2,1)S(1)}, u32[]{:S(2)}, u32[]{:S(2)}) collective-permute-start(bf16[64,128]{1,0:T(8,128)(2,1)S(1)} %hold.2), channel_id=1, source_target_pairs={{0,1},{1,0},{2,3},{3,2},{4,5},{5,4},{6,7},{7,6},{8,9},{9,8},{10,11... | collective-permute-start | bytes 49160 | tf_op jit(solution)/shard_map/ppermute | solution.py:457
  12.3 21.3 %collective-permute-start.11 = (bf16[512,640]{1,0:T(8,128)(2,1)S(1)}, bf16[512,640]{1,0:T(8,128)(2,1)S(1)}, u32[]{:S(2)}, u32[]{:S(2)}) collective-permute-start(bf16[512,640]{1,0:T(8,128)(2,1)S(1)} %slice_bitcast_fusion), channel_id=1, source_target_pairs={{0,2},{1,5},{2,0},{3,7},{4,6},{5,1},{6,4},{7,3},{8,10},{9,13},{10,... | collective-permute-start | bytes 1966088 | tf_op jit(solution)/shard_map/ppermute | solution.py:457
  14.7 17.1 %copy-start.6 = (bf16[256,640]{1,0:T(8,128)(2,1)S(1)}, bf16[256,640]{1,0:T(8,128)(2,1)}, u32[]{:S(2)}) copy-start(bf16[256,640]{1,0:T(8,128)(2,1)} %copy-done.5) | copy-start | bytes 983044
  14.7 13.4 %collective-permute-start.3 = (bf16[2,64,128]{2,1,0:T(8,128)(2,1)S(1)}, bf16[2,64,128]{2,1,0:T(8,128)(2,1)S(1)}, u32[]{:S(2)}, u32[]{:S(2)}) collective-permute-start(bf16[2,64,128]{2,1,0:T(8,128)(2,1)S(1)} %pad_maximum_fusion.2.near_ref), channel_id=1, source_target_pairs={{0,3},{1,2},{2,1},{3,0},{4,7},{5,6},{6,5},{7,4},{8,11},{9,10},{10,... | collective-permute-start | bytes 98312 | tf_op jit(solution)/shard_map/ppermute | solution.py:457
  16.4 11.8 %collective-permute-start.2 = (bf16[2,64,128]{2,1,0:T(8,128)(2,1)S(1)}, bf16[2,64,128]{2,1,0:T(8,128)(2,1)S(1)}, u32[]{:S(2)}, u32[]{:S(2)}) collective-permute-start(bf16[2,64,128]{2,1,0:T(8,128)(2,1)S(1)} %pad_maximum_fusion.2.near_ref), channel_id=1, source_target_pairs={{3,0},{4,1},{1,2},{6,3},{7,4},{0,5},{5,6},{2,7},{11,8},{12,9},{9,1... | collective-permute-start | bytes 98312 | tf_op jit(solution)/shard_map/ppermute | solution.py:457
  16.6 17.0 %copy-start.4 = (bf16[512,640]{1,0:T(8,128)(2,1)S(1)}, bf16[512,640]{1,0:T(8,128)(2,1)}, u32[]{:S(2)}) copy-start(bf16[512,640]{1,0:T(8,128)(2,1)} %copy-done.3) | copy-start | bytes 1966084
  16.6 38.2 %collective-permute-start.10 = (bf16[2,256,640]{2,1,0:T(8,128)(2,1)S(1)}, bf16[2,256,640]{2,1,0:T(8,128)(2,1)S(1)}, u32[]{:S(2)}, u32[]{:S(2)}) collective-permute-start(bf16[2,256,640]{2,1,0:T(8,128)(2,1)S(1)} %pad_maximum_fusion), channel_id=1, source_target_pairs={{0,2},{1,5},{2,0},{3,7},{4,6},{5,1},{6,4},{7,3},{8,10},{9,13},{10,... | collective-permute-start | bytes 1966088 | tf_op jit(solution)/shard_map/ppermute | solution.py:457
  28.6 3.2 %collective-permute-start.7 = (f32[48,128]{1,0:T(8,128)S(1)}, f32[48,128]{1,0:T(8,128)S(1)}, u32[]{:S(2)}, u32[]{:S(2)}) collective-permute-start(f32[48,128]{1,0:T(8,128)S(1)} %get-tuple-element.29.near_ref), channel_id=1, source_target_pairs={{0,12},{2,14},{4,8},{6,10},{8,4},{10,6},{12,0},{14,2},{16,28},{18,... | collective-permute-start | bytes 73736 | tf_op jit(solution)/shard_map/ppermute | solution.py:457
  29.3 2.6 %collective-permute-start.6 = (f32[48,128]{1,0:T(8,128)S(1)}, f32[48,128]{1,0:T(8,128)S(1)}, u32[]{:S(2)}, u32[]{:S(2)}) collective-permute-start(f32[48,128]{1,0:T(8,128)S(1)} %get-tuple-element.29.near_ref), channel_id=1, source_target_pairs={{0,8},{2,10},{4,12},{6,14},{8,0},{10,2},{12,4},{14,6},{16,24},{18,... | collective-permute-start | bytes 73736 | tf_op jit(solution)/shard_map/ppermute | solution.py:457
  30.0 3.6 %collective-permute-start.5 = (f32[48,128]{1,0:T(8,128)S(1)}, f32[48,128]{1,0:T(8,128)S(1)}, u32[]{:S(2)}, u32[]{:S(2)}) collective-permute-start(f32[48,128]{1,0:T(8,128)S(1)} %get-tuple-element.29.near_ref), channel_id=1, source_target_pairs={{0,4},{1,3},{2,6},{3,1},{4,0},{5,7},{6,2},{7,5},{8,12},{9,11},{10,... | collective-permute-start | bytes 73736 | tf_op jit(solution)/shard_map/ppermute | solution.py:457
  34.7 29.0 %collective-permute-start.16 = (bf16[2,256,640]{2,1,0:T(8,128)(2,1)S(1)}, bf16[2,256,640]{2,1,0:T(8,128)(2,1)S(1)}, u32[]{:S(2)}, u32[]{:S(2)}) collective-permute-start(bf16[2,256,640]{2,1,0:T(8,128)(2,1)S(1)} %hold.3), channel_id=1, source_target_pairs={{0,2},{1,3},{2,0},{3,1},{4,6},{5,7},{6,4},{7,5},{8,10},{9,11},{10,... | collective-permute-start | bytes 1966088 | tf_op jit(solution)/shard_map/ppermute | solution.py:457
  36.3 14.9 %collective-permute-start.13 = (f32[1,128,640]{2,1,0:T(8,128)S(1)}, f32[1,128,640]{2,1,0:T(8,128)S(1)}, u32[]{:S(2)}, u32[]{:S(2)}) collective-permute-start(f32[1,128,640]{2,1,0:T(8,128)S(1)} %get-tuple-element.41), channel_id=1, source_target_pairs={{0,4},{1,3},{2,6},{3,1},{4,0},{5,7},{6,2},{7,5},{8,12},{9,11},{10,... | collective-permute-start | bytes 983048 | tf_op jit(solution)/shard_map/ppermute | solution.py:457
  36.3 21.5 %collective-permute-start.12 = (f32[1,128,640]{2,1,0:T(8,128)S(1)}, f32[1,128,640]{2,1,0:T(8,128)S(1)}, u32[]{:S(2)}, u32[]{:S(2)}) collective-permute-start(f32[1,128,640]{2,1,0:T(8,128)S(1)} %get-tuple-element.39), channel_id=1, source_target_pairs={{0,4},{1,3},{2,6},{3,1},{4,0},{5,7},{6,2},{7,5},{8,12},{9,11},{10,... | collective-permute-start | bytes 983048 | tf_op jit(solution)/shard_map/ppermute | solution.py:457
  37.7 8.9 %collective-permute-start.8 = (f32[48,128]{1,0:T(8,128)S(1)}, f32[48,128]{1,0:T(8,128)S(1)}, u32[]{:S(2)}, u32[]{:S(2)}) collective-permute-start(f32[48,128]{1,0:T(8,128)S(1)} %add_add_fusion.here_ref.refs_5_), channel_id=1, source_target_pairs={{0,1},{2,3},{4,5},{6,7},{8,9},{10,11},{12,13},{14,15},{16,17},{18,... | collective-permute-start | bytes 73736 | tf_op jit(solution)/shard_map/ppermute | solution.py:457
  51.1 10.5 %copy-start.2 = (bf16[512,640]{1,0:T(8,128)(2,1)S(1)}, bf16[512,640]{1,0:T(8,128)(2,1)}, u32[]{:S(2)}) copy-start(bf16[512,640]{1,0:T(8,128)(2,1)} %copy-done.1) | copy-start | bytes 1966084
  51.8 21.2 %collective-permute-start.17 = (f32[1,112,640]{2,1,0:T(8,128)S(1)}, f32[1,112,640]{2,1,0:T(8,128)S(1)}, u32[]{:S(2)}, u32[]{:S(2)}) collective-permute-start(f32[1,112,640]{2,1,0:T(8,128)S(1)} %meet.3.refs_4_), channel_id=1, source_target_pairs={{0,8},{1,9},{2,10},{3,11},{4,12},{5,13},{6,14},{7,15},{8,0},{9,1},... | collective-permute-start | bytes 860168 | tf_op jit(solution)/shard_map/ppermute | solution.py:457
  58.5 20.5 %collective-permute-start.14 = (f32[1,112,640]{2,1,0:T(8,128)S(1)}, f32[1,112,640]{2,1,0:T(8,128)S(1)}, u32[]{:S(2)}, u32[]{:S(2)}) collective-permute-start(f32[1,112,640]{2,1,0:T(8,128)S(1)} %meet.2.refs_3_), channel_id=1, source_target_pairs={{0,8},{1,9},{2,10},{3,11},{4,12},{5,13},{6,14},{7,15},{8,0},{9,1},... | collective-permute-start | bytes 860168 | tf_op jit(solution)/shard_map/ppermute | solution.py:457
  62.3 11.3 %collective-permute-start.15 = (f32[1,112,640]{2,1,0:T(8,128)S(1)}, f32[1,112,640]{2,1,0:T(8,128)S(1)}, u32[]{:S(2)}, u32[]{:S(2)}) collective-permute-start(f32[1,112,640]{2,1,0:T(8,128)S(1)} %get-tuple-element.43), channel_id=1, source_target_pairs={{0,4},{1,3},{2,6},{3,1},{4,0},{5,7},{6,2},{7,5},{8,12},{9,11},{10,... | collective-permute-start | bytes 860168 | tf_op jit(solution)/shard_map/ppermute | solution.py:457
  73.0 6.0 %collective-permute-start.18 = (f32[112,640]{1,0:T(8,128)S(1)}, f32[112,640]{1,0:T(8,128)S(1)}, u32[]{:S(2)}, u32[]{:S(2)}) collective-permute-start(f32[112,640]{1,0:T(8,128)S(1)} %add_bitcast_fusion), channel_id=1, source_target_pairs={{0,1},{1,0},{2,3},{3,2},{4,5},{5,4},{6,7},{7,6},{8,9},{9,8},{10,11... | collective-permute-start | bytes 860168 | tf_op jit(solution)/shard_map/ppermute | solution.py:457
  73.3 11.9 %collective-permute-start.19 = (f32[1,112,640]{2,1,0:T(8,128)S(1)}, f32[1,112,640]{2,1,0:T(8,128)S(1)}, u32[]{:S(2)}, u32[]{:S(2)}) collective-permute-start(f32[1,112,640]{2,1,0:T(8,128)S(1)} %get-tuple-element.48), channel_id=1, source_target_pairs={{0,5},{1,4},{2,7},{3,6},{4,1},{5,0},{6,3},{7,2},{8,13},{9,12},{10,... | collective-permute-start | bytes 860168 | tf_op jit(solution)/shard_map/ppermute | solution.py:457
  (8 other events, 28.2 us)

commit v12 on v8

--- a/solution.py
+++ b/solution.py
@@ -37,7 +37,6 @@
 def pack_kernel(
     plan, x_ref, kept0_ref, kept1_ref, sent0_ref, sent1_ref, other0_ref, other1_ref
 ):
-    step = pl.program_id(0)
     me = lax.axis_index("pat")
     rows, columns = x_ref.shape
     last_tile = columns // LANES - 1
@@ -46,35 +45,38 @@
     def tile(index):
         return pl.ds(pl.multiple_of(jnp.minimum(index, last_tile) * LANES, LANES), LANES)
 
-    for away in range(2):
-        side = (me & 1) ^ away
-        holder = me ^ away
-        for sent in range(2):
-            for chunk in range(2):
-                middle = len(plan.middle_bits)
-                relative = (
-                    (step >> (1 + middle))
-                    | (sent << (1 + side))
-                    | ((step & 1) << (2 - side))
-                    | (((step >> 1) & ((1 << middle) - 1)) << 3)
-                    | (chunk << plan.top_bit)
-                )
-                column = (holder ^ relative) * plan.block
-                first = column // LANES
-                edge = (column - first * LANES) * (1 - side)
-                head = x_ref[:, tile(first + side * plan.share)]
-                tail = x_ref[:, tile(first + plan.tiles)]
-                folded = jnp.where(lane >= edge, head.astype(jnp.float32), tail.astype(jnp.float32))
-                if away:
-                    target = (other0_ref, other1_ref)[chunk].at[sent]
-                elif sent:
-                    target = (sent0_ref, sent1_ref)[chunk]
-                else:
-                    target = (kept0_ref, kept1_ref)[chunk]
-                target[:, 0:LANES] = folded.astype(x_ref.dtype)
-                for slot in range(1, plan.share):
-                    here = slice(slot * LANES, (slot + 1) * LANES)
-                    target[:, here] = x_ref[:, tile(first + side * plan.share + slot)]
+    @pl.loop(0, plan.places)
+    def _(step):
+        here = pl.ds(pl.multiple_of(step * rows, rows), rows)
+        for away in range(2):
+            side = (me & 1) ^ away
+            holder = me ^ away
+            for sent in range(2):
+                for chunk in range(2):
+                    middle = len(plan.middle_bits)
+                    relative = (
+                        (step >> (1 + middle))
+                        | (sent << (1 + side))
+                        | ((step & 1) << (2 - side))
+                        | (((step >> 1) & ((1 << middle) - 1)) << 3)
+                        | (chunk << plan.top_bit)
+                    )
+                    column = (holder ^ relative) * plan.block
+                    first = column // LANES
+                    edge = (column - first * LANES) * (1 - side)
+                    head = x_ref[:, tile(first + side * plan.share)]
+                    tail = x_ref[:, tile(first + plan.tiles)]
+                    folded = jnp.where(lane >= edge, head.astype(jnp.float32), tail.astype(jnp.float32))
+                    if away:
+                        target = (other0_ref, other1_ref)[chunk].at[sent, here]
+                    elif sent:
+                        target = (sent0_ref, sent1_ref)[chunk].at[here]
+                    else:
+                        target = (kept0_ref, kept1_ref)[chunk].at[here]
+                    target[:, 0:LANES] = folded.astype(x_ref.dtype)
+                    for slot in range(1, plan.share):
+                        lanes = slice(slot * LANES, (slot + 1) * LANES)
+                        target[:, lanes] = x_ref[:, tile(first + side * plan.share + slot)]
 
 
 def pack(covariates, plan):
@@ -83,15 +85,12 @@
     length = plan.places * rows
     mine = jax.ShapeDtypeStruct((length, plan.width), dtype)
     other = jax.ShapeDtypeStruct((2, length, plan.width), dtype)
-    mine_spec = pl.BlockSpec((rows, plan.width), lambda s: (s, 0))
-    other_spec = pl.BlockSpec((2, rows, plan.width), lambda s: (0, s, 0))
     return pl.pallas_call(
         functools.partial(pack_kernel, plan),
-        grid=(plan.places,),
         in_specs=[pl.BlockSpec(memory_space=pltpu.VMEM)],
-        out_specs=[mine_spec] * 4 + [other_spec] * 2,
+        out_specs=[pl.BlockSpec(memory_space=pltpu.VMEM)] * 6,
         out_shape=[mine] * 4 + [other] * 2,
-        compiler_params=pltpu.CompilerParams(vmem_limit_bytes=12 << 20),
+        compiler_params=pltpu.CompilerParams(vmem_limit_bytes=8 << 20),
         cost_estimate=pl.CostEstimate(
             flops=0, bytes_accessed=4 * covariates.size, transcendentals=0
         ),
@@ -315,7 +314,7 @@
         + [pl.BlockSpec(memory_space=pl.ANY)] * len(after),
         out_specs=[pl.BlockSpec(memory_space=pltpu.VMEM)] * 4,
         out_shape=[out] * 4,
-        compiler_params=pltpu.CompilerParams(vmem_limit_bytes=20 << 20),
+        compiler_params=pltpu.CompilerParams(vmem_limit_bytes=10 << 20),
         cost_estimate=pl.CostEstimate(flops=0, bytes_accessed=6 << 20, transcendentals=0),
         name="group_moments",
     )(*rows_here, panel, *after)
@@ -335,7 +334,7 @@
         + [pl.BlockSpec(memory_space=pl.ANY)] * len(after),
         out_specs=[pl.BlockSpec(memory_space=pltpu.VMEM)] * len(out_shape),
         out_shape=out_shape,
-        compiler_params=pltpu.CompilerParams(vmem_limit_bytes=20 << 20),
+        compiler_params=pltpu.CompilerParams(vmem_limit_bytes=10 << 20),
         cost_estimate=pl.CostEstimate(flops=0, bytes_accessed=6 << 20, transcendentals=0),
         name="moments",
     )(*rows_here, first, second, stats, *after)
@@ -383,7 +382,7 @@
         out_specs=pl.BlockSpec(memory_space=pltpu.VMEM),
         out_shape=jax.ShapeDtypeStruct((comps, 1, plan.block), jnp.float32),
         scratch_shapes=[pltpu.VMEM((comps, plan.tiles * LANES), jnp.float32)],
-        compiler_params=pltpu.CompilerParams(vmem_limit_bytes=12 << 20),
+        compiler_params=pltpu.CompilerParams(vmem_limit_bytes=8 << 20),
         cost_estimate=pl.CostEstimate(flops=0, bytes_accessed=1 << 14, transcendentals=0),
         name="finish",
     )(pick_column, stats, *operands)

time: 74.4 us -> 77 us (1.035)
  local copies, waits for them, and re-layouts: 3.53 us -> 5.21 us
  starting transfers between devices: 35.2 us -> 36.7 us
    unnamed x16, local copies, waits for them, and re-layouts: 2.47 us -> 4.15 us
    ppermute x19, starting transfers between devices: 35.2 us -> 36.7 us  [swap(): return lax.ppermute(array, 'pat', pairs)]
  transfers between devices with their start and end apart: 19 -> 19, of which waited for: 8 -> 7; matrix products, arithmetic and copies ran while one was open for 1% -> 1% of each run, Pallas kernels for 7% -> 7%
where the time goes in v12:
time: 77 us; the launch traced here: 76.8 us
  starting transfers between devices  36.7 us (48%)
  waiting for transfers between devices  25 us (32%)
  Pallas kernels  9.71 us (13%)
  local copies, waits for them, and re-layouts  5.21 us (7%)
    ppermute x19, starting transfers between devices, swap(): return lax.ppermute(array, 'pat', pairs)  36.7 us
    ppermute x19, waiting for transfers between devices, swap(): return lax.ppermute(array, 'pat', pairs)  25 us
    unnamed x16, local copies, waits for them, and re-layouts  4.15 us
    pallas_call x1, Pallas kernels, pack(): pl.pallas_call(functools.partial(pack_kernel, plan), in_specs=[pl.BlockSp...  2.62 us
    pallas_call x1, Pallas kernels, group_moments(): pl.pallas_call(functools.partial(group_moments_kernel, rows, 2), in_specs...  2.36 us
    pallas_call x4, Pallas kernels, small_call(): pl.pallas_call(kernel, in_specs=[vmem] * len(operands) + [pl.BlockSpec(me...  1.96 us
    pallas_call x1, Pallas kernels, finish(): pl.pallas_call(functools.partial(finish_kernel, plan, weightings, [len(pa...  1.61 us
  transfers between devices with their start and end apart: 19, of which 7 were waited for; matrix products, arithmetic and copies ran while one was open for 1% of the time, Pallas kernels for 7%

profile of v12, /device:TPU:1, one launch (start us, length us, event | category | flops | bytes accessed | tf_op | source)
XLA Modules:
  0.0 76.8 jit_solution(14442143836188783896)
XLA Ops:
  0.0 2.4 %copy-done = bf16[128,19968]{1,0:T(8,128)(2,1)S(1)} copy-done((bf16[128,19968]{1,0:T(8,128)(2,1)S(1)}, bf16[128,19968]{1,0:T(8,128)(2,1)}, u32[]{:S(2)}) %copy-start) | copy-done | bytes 5111832
  2.5 2.6 %pack.1 = (bf16[512,640]{1,0:T(8,128)(2,1)S(1)}, bf16[512,640]{1,0:T(8,128)(2,1)S(1)}, bf16[512,640]{1,0:T(8,128)(2,1)S(1)}, bf16[512,640]{1,0:T(8,128)(2,1)}, b...) custom-call(bf16[128,19968]{1,0:T(8,128)(2,1)S(1)} %copy-done), custom_call_target="tpu_custom_call" | custom-call | bytes 10223616 | tf_op jit(solution)/shard_map/pack/pallas_call | solution.py:88
  5.9 0.8 %copy-done.3 = bf16[512,640]{1,0:T(8,128)(2,1)} copy-done((bf16[512,640]{1,0:T(8,128)(2,1)}, bf16[512,640]{1,0:T(8,128)(2,1)S(1)}, u32[]{:S(2)}) %copy-start.3) | copy-done | bytes 655384
  7.3 2.3 %collective-permute-start.10 = (bf16[512,640]{1,0:T(8,128)(2,1)}, bf16[512,640]{1,0:T(8,128)(2,1)}, u32[]{:S(2)}, u32[]{:S(2)}) collective-permute-start(bf16[512,640]{1,0:T(8,128)(2,1)} %get-tuple-element.33), channel_id=1, source_target_pairs={{0,2},{1,5},{2,0},{3,7},{4,6},{5,1},{6,4},{7,3},{8,10},{9,13},{10,... | collective-permute-start | bytes 1966088 | tf_op jit(solution)/shard_map/ppermute | solution.py:392
  9.6 1.5 %collective-permute-done.9.refs_1_ = bf16[2,512,640]{2,1,0:T(8,128)(2,1)S(1)} collective-permute-done((bf16[2,512,640]{2,1,0:T(8,128)(2,1)S(1)}, bf16[2,512,640]{2,1,0:T(8,128)(2,1)S(1)}, u32[]{:S(2)}, u32[]{:S(2)}) %collective-permute-start.9) | collective-permute-done | bytes 1310752 | tf_op jit(solution)/shard_map/ppermute | solution.py:392
  11.1 0.9 %slice_bitcast_fusion = bf16[512,640]{1,0:T(8,128)(2,1)} fusion(bf16[2,512,640]{2,1,0:T(8,128)(2,1)S(1)} %collective-permute-done.9.refs_1_), kind=kLoop, calls=%fused_computation | loop fusion | bytes 1310720 | tf_op jit(solution)/shard_map/squeeze | solution.py:413
  12.0 3.0 %collective-permute-start.11 = (bf16[512,640]{1,0:T(8,128)(2,1)}, bf16[512,640]{1,0:T(8,128)(2,1)}, u32[]{:S(2)}, u32[]{:S(2)}) collective-permute-start(bf16[512,640]{1,0:T(8,128)(2,1)} %slice_bitcast_fusion), channel_id=1, source_target_pairs={{0,2},{1,5},{2,0},{3,7},{4,6},{5,1},{6,4},{7,3},{8,10},{9,13},{10,... | collective-permute-start | bytes 1966088 | tf_op jit(solution)/shard_map/ppermute | solution.py:392
  16.4 1.0 %collective-permute-start.1 = (bf16[2,64,128]{2,1,0:T(8,128)(2,1)S(1)}, bf16[2,64,128]{2,1,0:T(8,128)(2,1)S(1)}, u32[]{:S(2)}, u32[]{:S(2)}) collective-permute-start(bf16[2,64,128]{2,1,0:T(8,128)(2,1)S(1)} %pad_maximum_fusion.near_ref), channel_id=1, source_target_pairs={{3,0},{4,1},{1,2},{6,3},{7,4},{0,5},{5,6},{2,7},{11,8},{12,9},{9,1... | collective-permute-start | bytes 98312 | tf_op jit(solution)/shard_map/ppermute | solution.py:392
  17.6 3.0 %collective-permute-done.1.far_ref = bf16[2,64,128]{2,1,0:T(8,128)(2,1)S(1)} collective-permute-done((bf16[2,64,128]{2,1,0:T(8,128)(2,1)S(1)}, bf16[2,64,128]{2,1,0:T(8,128)(2,1)S(1)}, u32[]{:S(2)}, u32[]{:S(2)}) %collective-permute-start.1) | collective-permute-done | bytes 32800 | tf_op jit(solution)/shard_map/ppermute | solution.py:392
  21.0 1.1 %collective-permute-start.2 = (f32[48,128]{1,0:T(8,128)S(1)}, f32[48,128]{1,0:T(8,128)S(1)}, u32[]{:S(2)}, u32[]{:S(2)}) collective-permute-start(f32[48,128]{1,0:T(8,128)S(1)} %get-tuple-element.24.near_ref), channel_id=1, source_target_pairs={{0,4},{1,3},{2,6},{3,1},{4,0},{5,7},{6,2},{7,5},{8,12},{9,11},{10,... | collective-permute-start | bytes 73736 | tf_op jit(solution)/shard_map/ppermute | solution.py:392
  23.5 1.0 %collective-permute-done.2.far_ref = f32[48,128]{1,0:T(8,128)S(1)} collective-permute-done((f32[48,128]{1,0:T(8,128)S(1)}, f32[48,128]{1,0:T(8,128)S(1)}, u32[]{:S(2)}, u32[]{:S(2)}) %collective-permute-start.2) | collective-permute-done | bytes 24608 | tf_op jit(solution)/shard_map/ppermute | solution.py:392
  24.5 1.3 %collective-permute-start.7 = (bf16[512,640]{1,0:T(8,128)(2,1)S(1)}, bf16[512,640]{1,0:T(8,128)(2,1)S(1)}, u32[]{:S(2)}, u32[]{:S(2)}) collective-permute-start(bf16[512,640]{1,0:T(8,128)(2,1)S(1)} %copy-done.4), channel_id=1, source_target_pairs={{0,2},{1,5},{2,0},{3,7},{4,6},{5,1},{6,4},{7,3},{8,10},{9,13},{10,... | collective-permute-start | bytes 1966088 | tf_op jit(solution)/shard_map/ppermute | solution.py:392
  26.0 2.4 %group_moments.1 = (f32[1,128,640]{2,1,0:T(8,128)S(1)}, f32[1,128,640]{2,1,0:T(8,128)S(1)}, f32[1,128,640]{2,1,0:T(8,128)S(1)}, f32[1,128,640]{2,1,0:T(8,128)S(1)}) custom-call(bf16[512,640]{1,0:T(8,128)(2,1)S(1)} %copy-done.2, bf16[2,512,640]{2,1,0:T(8,128)(2,1)S(1)} %collective-permute-done.9.refs_1_, bf16[512,640]{1,0:T(8,128)(2,1)} %collective-permute-done.10.refs_2_, ...), custom_call_target="tpu_custom_call" | custom-call | bytes 6291456 | tf_op jit(solution)/shard_map/group_moments/pallas_call | solution.py:311
  28.4 1.3 %collective-permute-start.13 = (f32[1,128,640]{2,1,0:T(8,128)S(1)}, f32[1,128,640]{2,1,0:T(8,128)S(1)}, u32[]{:S(2)}, u32[]{:S(2)}) collective-permute-start(f32[1,128,640]{2,1,0:T(8,128)S(1)} %get-tuple-element.38), channel_id=1, source_target_pairs={{0,4},{1,3},{2,6},{3,1},{4,0},{5,7},{6,2},{7,5},{8,12},{9,11},{10,... | collective-permute-start | bytes 983048 | tf_op jit(solution)/shard_map/ppermute | solution.py:392
  29.9 1.3 %collective-permute-start.5 = (f32[48,128]{1,0:T(8,128)S(1)}, f32[48,128]{1,0:T(8,128)S(1)}, u32[]{:S(2)}, u32[]{:S(2)}) collective-permute-start(f32[48,128]{1,0:T(8,128)S(1)} %add_add_fusion.here_ref.refs_5_), channel_id=1, source_target_pairs={{0,1},{2,3},{4,5},{6,7},{8,9},{10,11},{12,13},{14,15},{16,17},{18,... | collective-permute-start | bytes 73736 | tf_op jit(solution)/shard_map/ppermute | solution.py:392
  31.2 10.2 %collective-permute-done.5.told_ref = f32[48,128]{1,0:T(8,128)S(1)} collective-permute-done((f32[48,128]{1,0:T(8,128)S(1)}, f32[48,128]{1,0:T(8,128)S(1)}, u32[]{:S(2)}, u32[]{:S(2)}) %collective-permute-start.5) | collective-permute-done | bytes 24608 | tf_op jit(solution)/shard_map/ppermute | solution.py:392
  42.4 1.3 %collective-permute-done.12.right_ref = f32[1,128,640]{2,1,0:T(8,128)S(1)} collective-permute-done((f32[1,128,640]{2,1,0:T(8,128)S(1)}, f32[1,128,640]{2,1,0:T(8,128)S(1)}, u32[]{:S(2)}, u32[]{:S(2)}) %collective-permute-start.12) | collective-permute-done | bytes 327712 | tf_op jit(solution)/shard_map/ppermute | solution.py:392
  44.4 3.4 %collective-permute-start.14 = (f32[1,112,640]{2,1,0:T(8,128)S(1)}, f32[1,112,640]{2,1,0:T(8,128)S(1)}, u32[]{:S(2)}, u32[]{:S(2)}) collective-permute-start(f32[1,112,640]{2,1,0:T(8,128)S(1)} %meet.2.refs_7_), channel_id=1, source_target_pairs={{0,8},{1,9},{2,10},{3,11},{4,12},{5,13},{6,14},{7,15},{8,0},{9,1},... | collective-permute-start | bytes 860168 | tf_op jit(solution)/shard_map/ppermute | solution.py:392
  47.8 1.2 %moments.1 = (f32[112,640]{1,0:T(8,128)S(1)}, f32[112,640]{1,0:T(8,128)S(1)}, f32[112,640]{1,0:T(8,128)S(1)}, f32[112,640]{1,0:T(8,128)S(1)}) custom-call(bf16[512,640]{1,0:T(8,128)(2,1)S(1)} %get-tuple-element.26.refs_0_, bf16[2,512,640]{2,1,0:T(8,128)(2,1)S(1)} %collective-permute-done.6.refs_1_, ...), custom_call_target="tpu_custom_call" | custom-call | bytes 6291456 | tf_op jit(solution)/shard_map/moments/pallas_call | solution.py:331
  48.9 1.6 %collective-permute-start.15 = (f32[112,640]{1,0:T(8,128)S(1)}, f32[112,640]{1,0:T(8,128)S(1)}, u32[]{:S(2)}, u32[]{:S(2)}) collective-permute-start(f32[112,640]{1,0:T(8,128)S(1)} %get-tuple-element.40), channel_id=1, source_target_pairs={{0,4},{1,3},{2,6},{3,1},{4,0},{5,7},{6,2},{7,5},{8,12},{9,11},{10,... | collective-permute-start | bytes 860168 | tf_op jit(solution)/shard_map/ppermute | solution.py:392
  50.5 9.5 %collective-permute-start.18 = (f32[112,640]{1,0:T(8,128)S(1)}, f32[112,640]{1,0:T(8,128)S(1)}, u32[]{:S(2)}, u32[]{:S(2)}) collective-permute-start(f32[112,640]{1,0:T(8,128)S(1)} %get-tuple-element.42), channel_id=1, source_target_pairs={{0,5},{1,2},{2,7},{3,0},{4,1},{5,6},{6,3},{7,4},{8,13},{9,10},{10,... | collective-permute-start | bytes 860168 | tf_op jit(solution)/shard_map/ppermute | solution.py:392
  60.1 8.1 %collective-permute-start.17 = (f32[112,640]{1,0:T(8,128)S(1)}, f32[112,640]{1,0:T(8,128)S(1)}, u32[]{:S(2)}, u32[]{:S(2)}) collective-permute-start(f32[112,640]{1,0:T(8,128)S(1)} %bitcast_add_fusion), channel_id=1, source_target_pairs={{0,1},{1,0},{2,3},{3,2},{4,5},{5,4},{6,7},{7,6},{8,9},{9,8},{10,11... | collective-permute-start | bytes 860168 | tf_op jit(solution)/shard_map/ppermute | solution.py:392
  68.1 7.0 %collective-permute-done.18.refs_4_ = f32[112,640]{1,0:T(8,128)S(1)} collective-permute-done((f32[112,640]{1,0:T(8,128)S(1)}, f32[112,640]{1,0:T(8,128)S(1)}, u32[]{:S(2)}, u32[]{:S(2)}) %collective-permute-start.18) | collective-permute-done | bytes 286752 | tf_op jit(solution)/shard_map/ppermute | solution.py:392
  75.2 1.6 %finish.1 = f32[48,1,1248]{2,1,0:T(1,128)} custom-call(s32[48,1]{1,0:T(8,128)S(1)} %copy.9.pick_ref, f32[3,48,128]{2,1,0:T(8,128)S(1)} %get-tuple-element.25.stats_ref.refs_6_, f32[112,640]{1,0:T(8,128)S(1)} %get-tuple-element.39.refs_0_, f32[112,640]{1,0:T(8,128)S(1)} %bitcast.14, f32[112,640]{1,0:T(8,128)S(1)} %collective-permute-done.15.refs_2_, ...), custom_call_target="tpu_custom_call" | custom-call | bytes 16384 | tf_op jit(solution)/shard_map/finish/pallas_call | solution.py:379
  (46 shorter events, 6.8 us)
Async XLA Ops:
  2.5 7.1 %copy-start.5 = (s32[128,48]{0,1:T(8,128)S(1)}, s32[128,48]{0,1:T(8,128)}, u32[]{:S(2)}) copy-start(s32[128,48]{0,1:T(8,128)} %param.6) | copy-start | bytes 73732
  6.8 8.2 %copy-start.6 = (bf16[128,16]{0,1:T(8,128)(2,1)S(1)}, bf16[128,16]{0,1:T(8,128)(2,1)}, u32[]{:S(2)}) copy-start(bf16[128,16]{0,1:T(8,128)(2,1)} %param.5) | copy-start | bytes 12292
  6.8 10.7 %copy-start.7 = (s32[48]{0:T(128)S(1)}, s32[48]{0:T(128)}, u32[]{:S(2)}) copy-start(s32[48]{0:T(128)} %param.7) | copy-start | bytes 580
  6.8 4.3 %collective-permute-start.9 = (bf16[2,512,640]{2,1,0:T(8,128)(2,1)S(1)}, bf16[2,512,640]{2,1,0:T(8,128)(2,1)S(1)}, u32[]{:S(2)}, u32[]{:S(2)}) collective-permute-start(bf16[2,512,640]{2,1,0:T(8,128)(2,1)S(1)} %get-tuple-element.32), channel_id=1, source_target_pairs={{0,1},{1,0},{2,3},{3,2},{4,5},{5,4},{6,7},{7,6},{8,9},{9,8},{10,11... | collective-permute-start | bytes 3932168 | tf_op jit(solution)/shard_map/ppermute | solution.py:392
  6.8 15.9 %collective-permute-start.6 = (bf16[2,512,640]{2,1,0:T(8,128)(2,1)}, bf16[2,512,640]{2,1,0:T(8,128)(2,1)S(1)}, u32[]{:S(2)}, u32[]{:S(2)}) collective-permute-start(bf16[2,512,640]{2,1,0:T(8,128)(2,1)} %get-tuple-element.27), channel_id=1, source_target_pairs={{0,1},{1,0},{2,3},{3,2},{4,5},{5,4},{6,7},{7,6},{8,9},{9,8},{10,11... | collective-permute-start | bytes 3932168 | tf_op jit(solution)/shard_map/ppermute | solution.py:392
  7.3 18.7 %collective-permute-start.10 = (bf16[512,640]{1,0:T(8,128)(2,1)}, bf16[512,640]{1,0:T(8,128)(2,1)}, u32[]{:S(2)}, u32[]{:S(2)}) collective-permute-start(bf16[512,640]{1,0:T(8,128)(2,1)} %get-tuple-element.33), channel_id=1, source_target_pairs={{0,2},{1,5},{2,0},{3,7},{4,6},{5,1},{6,4},{7,3},{8,10},{9,13},{10,... | collective-permute-start | bytes 1966088 | tf_op jit(solution)/shard_map/ppermute | solution.py:392
  12.0 14.0 %collective-permute-start.11 = (bf16[512,640]{1,0:T(8,128)(2,1)}, bf16[512,640]{1,0:T(8,128)(2,1)}, u32[]{:S(2)}, u32[]{:S(2)}) collective-permute-start(bf16[512,640]{1,0:T(8,128)(2,1)} %slice_bitcast_fusion), channel_id=1, source_target_pairs={{0,2},{1,5},{2,0},{3,7},{4,6},{5,1},{6,4},{7,3},{8,10},{9,13},{10,... | collective-permute-start | bytes 1966088 | tf_op jit(solution)/shard_map/ppermute | solution.py:392
  15.0 1.4 %collective-permute-start = (bf16[64,128]{1,0:T(8,128)(2,1)S(1)}, bf16[64,128]{1,0:T(8,128)(2,1)S(1)}, u32[]{:S(2)}, u32[]{:S(2)}) collective-permute-start(bf16[64,128]{1,0:T(8,128)(2,1)S(1)} %get-tuple-element.44), channel_id=1, source_target_pairs={{0,1},{1,0},{2,3},{3,2},{4,5},{5,4},{6,7},{7,6},{8,9},{9,8},{10,11... | collective-permute-start | bytes 49160 | tf_op jit(solution)/shard_map/ppermute | solution.py:392
  16.4 4.2 %collective-permute-start.1 = (bf16[2,64,128]{2,1,0:T(8,128)(2,1)S(1)}, bf16[2,64,128]{2,1,0:T(8,128)(2,1)S(1)}, u32[]{:S(2)}, u32[]{:S(2)}) collective-permute-start(bf16[2,64,128]{2,1,0:T(8,128)(2,1)S(1)} %pad_maximum_fusion.near_ref), channel_id=1, source_target_pairs={{3,0},{4,1},{1,2},{6,3},{7,4},{0,5},{5,6},{2,7},{11,8},{12,9},{9,1... | collective-permute-start | bytes 98312 | tf_op jit(solution)/shard_map/ppermute | solution.py:392
  17.6 6.9 %copy-start.4 = (bf16[512,640]{1,0:T(8,128)(2,1)S(1)}, bf16[512,640]{1,0:T(8,128)(2,1)}, u32[]{:S(2)}) copy-start(bf16[512,640]{1,0:T(8,128)(2,1)} %copy-done.3) | copy-start | bytes 1966084
  17.6 8.4 %copy-start.2 = (bf16[512,640]{1,0:T(8,128)(2,1)S(1)}, bf16[512,640]{1,0:T(8,128)(2,1)}, u32[]{:S(2)}) copy-start(bf16[512,640]{1,0:T(8,128)(2,1)} %copy-done.1) | copy-start | bytes 1966084
  21.0 3.5 %collective-permute-start.2 = (f32[48,128]{1,0:T(8,128)S(1)}, f32[48,128]{1,0:T(8,128)S(1)}, u32[]{:S(2)}, u32[]{:S(2)}) collective-permute-start(f32[48,128]{1,0:T(8,128)S(1)} %get-tuple-element.24.near_ref), channel_id=1, source_target_pairs={{0,4},{1,3},{2,6},{3,1},{4,0},{5,7},{6,2},{7,5},{8,12},{9,11},{10,... | collective-permute-start | bytes 73736 | tf_op jit(solution)/shard_map/ppermute | solution.py:392
  22.1 3.7 %collective-permute-start.3 = (f32[48,128]{1,0:T(8,128)S(1)}, f32[48,128]{1,0:T(8,128)S(1)}, u32[]{:S(2)}, u32[]{:S(2)}) collective-permute-start(f32[48,128]{1,0:T(8,128)S(1)} %get-tuple-element.24.near_ref), channel_id=1, source_target_pairs={{0,8},{2,10},{4,12},{6,14},{8,0},{10,2},{12,4},{14,6},{16,24},{18,... | collective-permute-start | bytes 73736 | tf_op jit(solution)/shard_map/ppermute | solution.py:392
  22.7 3.2 %collective-permute-start.4 = (f32[48,128]{1,0:T(8,128)S(1)}, f32[48,128]{1,0:T(8,128)S(1)}, u32[]{:S(2)}, u32[]{:S(2)}) collective-permute-start(f32[48,128]{1,0:T(8,128)S(1)} %get-tuple-element.24.near_ref), channel_id=1, source_target_pairs={{0,12},{2,14},{4,8},{6,10},{8,4},{10,6},{12,0},{14,2},{16,28},{18,... | collective-permute-start | bytes 73736 | tf_op jit(solution)/shard_map/ppermute | solution.py:392
  24.5 17.9 %collective-permute-start.7 = (bf16[512,640]{1,0:T(8,128)(2,1)S(1)}, bf16[512,640]{1,0:T(8,128)(2,1)S(1)}, u32[]{:S(2)}, u32[]{:S(2)}) collective-permute-start(bf16[512,640]{1,0:T(8,128)(2,1)S(1)} %copy-done.4), channel_id=1, source_target_pairs={{0,2},{1,5},{2,0},{3,7},{4,6},{5,1},{6,4},{7,3},{8,10},{9,13},{10,... | collective-permute-start | bytes 1966088 | tf_op jit(solution)/shard_map/ppermute | solution.py:392
  25.8 22.0 %collective-permute-start.8 = (bf16[512,640]{1,0:T(8,128)(2,1)S(1)}, bf16[512,640]{1,0:T(8,128)(2,1)S(1)}, u32[]{:S(2)}, u32[]{:S(2)}) collective-permute-start(bf16[512,640]{1,0:T(8,128)(2,1)S(1)} %slice_bitcast_fusion.1), channel_id=1, source_target_pairs={{0,2},{1,5},{2,0},{3,7},{4,6},{5,1},{6,4},{7,3},{8,10},{9,13},{10,... | collective-permute-start | bytes 1966088 | tf_op jit(solution)/shard_map/ppermute | solution.py:392
  28.4 13.3 %collective-permute-start.13 = (f32[1,128,640]{2,1,0:T(8,128)S(1)}, f32[1,128,640]{2,1,0:T(8,128)S(1)}, u32[]{:S(2)}, u32[]{:S(2)}) collective-permute-start(f32[1,128,640]{2,1,0:T(8,128)S(1)} %get-tuple-element.38), channel_id=1, source_target_pairs={{0,4},{1,3},{2,6},{3,1},{4,0},{5,7},{6,2},{7,5},{8,12},{9,11},{10,... | collective-permute-start | bytes 983048 | tf_op jit(solution)/shard_map/ppermute | solution.py:392
  29.6 14.1 %collective-permute-start.12 = (f32[1,128,640]{2,1,0:T(8,128)S(1)}, f32[1,128,640]{2,1,0:T(8,128)S(1)}, u32[]{:S(2)}, u32[]{:S(2)}) collective-permute-start(f32[1,128,640]{2,1,0:T(8,128)S(1)} %get-tuple-element.36), channel_id=1, source_target_pairs={{0,4},{1,3},{2,6},{3,1},{4,0},{5,7},{6,2},{7,5},{8,12},{9,11},{10,... | collective-permute-start | bytes 983048 | tf_op jit(solution)/shard_map/ppermute | solution.py:392
  29.9 11.5 %collective-permute-start.5 = (f32[48,128]{1,0:T(8,128)S(1)}, f32[48,128]{1,0:T(8,128)S(1)}, u32[]{:S(2)}, u32[]{:S(2)}) collective-permute-start(f32[48,128]{1,0:T(8,128)S(1)} %add_add_fusion.here_ref.refs_5_), channel_id=1, source_target_pairs={{0,1},{2,3},{4,5},{6,7},{8,9},{10,11},{12,13},{14,15},{16,17},{18,... | collective-permute-start | bytes 73736 | tf_op jit(solution)/shard_map/ppermute | solution.py:392
  42.3 17.7 %collective-permute-start.16 = (f32[1,112,640]{2,1,0:T(8,128)S(1)}, f32[1,112,640]{2,1,0:T(8,128)S(1)}, u32[]{:S(2)}, u32[]{:S(2)}) collective-permute-start(f32[1,112,640]{2,1,0:T(8,128)S(1)} %meet.3.refs_8_), channel_id=1, source_target_pairs={{0,8},{1,9},{2,10},{3,11},{4,12},{5,13},{6,14},{7,15},{8,0},{9,1},... | collective-permute-start | bytes 860168 | tf_op jit(solution)/shard_map/ppermute | solution.py:392
  44.4 30.8 %collective-permute-start.14 = (f32[1,112,640]{2,1,0:T(8,128)S(1)}, f32[1,112,640]{2,1,0:T(8,128)S(1)}, u32[]{:S(2)}, u32[]{:S(2)}) collective-permute-start(f32[1,112,640]{2,1,0:T(8,128)S(1)} %meet.2.refs_7_), channel_id=1, source_target_pairs={{0,8},{1,9},{2,10},{3,11},{4,12},{5,13},{6,14},{7,15},{8,0},{9,1},... | collective-permute-start | bytes 860168 | tf_op jit(solution)/shard_map/ppermute | solution.py:392
  48.9 19.2 %collective-permute-start.15 = (f32[112,640]{1,0:T(8,128)S(1)}, f32[112,640]{1,0:T(8,128)S(1)}, u32[]{:S(2)}, u32[]{:S(2)}) collective-permute-start(f32[112,640]{1,0:T(8,128)S(1)} %get-tuple-element.40), channel_id=1, source_target_pairs={{0,4},{1,3},{2,6},{3,1},{4,0},{5,7},{6,2},{7,5},{8,12},{9,11},{10,... | collective-permute-start | bytes 860168 | tf_op jit(solution)/shard_map/ppermute | solution.py:392
  50.5 24.7 %collective-permute-start.18 = (f32[112,640]{1,0:T(8,128)S(1)}, f32[112,640]{1,0:T(8,128)S(1)}, u32[]{:S(2)}, u32[]{:S(2)}) collective-permute-start(f32[112,640]{1,0:T(8,128)S(1)} %get-tuple-element.42), channel_id=1, source_target_pairs={{0,5},{1,2},{2,7},{3,0},{4,1},{5,6},{6,3},{7,4},{8,13},{9,10},{10,... | collective-permute-start | bytes 860168 | tf_op jit(solution)/shard_map/ppermute | solution.py:392
  60.1 15.1 %collective-permute-start.17 = (f32[112,640]{1,0:T(8,128)S(1)}, f32[112,640]{1,0:T(8,128)S(1)}, u32[]{:S(2)}, u32[]{:S(2)}) collective-permute-start(f32[112,640]{1,0:T(8,128)S(1)} %bitcast_add_fusion), channel_id=1, source_target_pairs={{0,1},{1,0},{2,3},{3,2},{4,5},{5,4},{6,7},{7,6},{8,9},{9,8},{10,11... | collective-permute-start | bytes 860168 | tf_op jit(solution)/shard_map/ppermute | solution.py:392
  (3 other events, 4.1 us)

commit v13 on v8

--- a/solution.py
+++ b/solution.py
@@ -417,9 +417,8 @@
     near_totals, panel = make_group(near, far, pick_column, weightings)
     far_totals = swap(near_totals, plan.by_sums())
     totals = near_totals + far_totals
-    for mask in range(8, n, 8):
-        for more in (mask, mask | 4):
-            totals = totals + swap(near_totals, plan.by_mask(more)[0::2])
+    for bit in plan.middle_bits + [plan.top_bit]:
+        totals = totals + swap(totals, plan.by_mask(1 << bit)[0::2])
     told = swap(totals, to_other_side[0::2])
     first, second, stats = make_panels(near, far, totals, told, pick_column, weightings)
 

time: 74.4 us -> 72.7 us (0.977)
  waiting for transfers between devices: 25.5 us -> 24 us
    ppermute x19 -> x18, waiting for transfers between devices: 25.5 us -> 24 us  [swap(): return lax.ppermute(array, 'pat', pairs)]
    ppermute x19 -> x18, starting transfers between devices: 35.2 us -> 35 us  [swap(): return lax.ppermute(array, 'pat', pairs)]
  transfers between devices with their start and end apart: 19 -> 18, of which waited for: 8 -> 9; matrix products, arithmetic and copies ran while one was open for 1% -> 2% of each run, Pallas kernels for 7% -> 8%
where the time goes in v13:
time: 72.7 us; the launch traced here: 72.5 us
  starting transfers between devices  35 us (48%)
  waiting for transfers between devices  24 us (33%)
  Pallas kernels  9.77 us (13%)
  local copies, waits for them, and re-layouts  3.52 us (5%)
    ppermute x18, starting transfers between devices, swap(): return lax.ppermute(array, 'pat', pairs)  35 us
    ppermute x18, waiting for transfers between devices, swap(): return lax.ppermute(array, 'pat', pairs)  24 us
    pallas_call x1, Pallas kernels, pack(): pl.pallas_call(functools.partial(pack_kernel, plan), grid=(plan.places,),...  2.7 us
    unnamed x16, local copies, waits for them, and re-layouts  2.48 us
    pallas_call x1, Pallas kernels, group_moments(): pl.pallas_call(functools.partial(group_moments_kernel, rows, 2), in_specs...  2.36 us
    pallas_call x4, Pallas kernels, small_call(): pl.pallas_call(kernel, in_specs=[vmem] * len(operands) + [pl.BlockSpec(me...  1.96 us
    pallas_call x1, Pallas kernels, finish(): pl.pallas_call(functools.partial(finish_kernel, plan, weightings, [len(pa...  1.62 us
  transfers between devices with their start and end apart: 18, of which 9 were waited for; matrix products, arithmetic and copies ran while one was open for 2% of the time, Pallas kernels for 8%

profile of v13, /device:TPU:1, one launch (start us, length us, event | category | flops | bytes accessed | tf_op | source)
XLA Modules:
  0.0 72.5 jit_solution(3409486550306085706)
XLA Ops:
  0.0 2.4 %copy-done = bf16[128,19968]{1,0:T(8,128)(2,1)S(1)} copy-done((bf16[128,19968]{1,0:T(8,128)(2,1)S(1)}, bf16[128,19968]{1,0:T(8,128)(2,1)}, u32[]{:S(2)}) %copy-start) | copy-done | bytes 5111832
  2.5 2.7 %pack.1 = (bf16[512,640]{1,0:T(8,128)(2,1)S(1)}, bf16[512,640]{1,0:T(8,128)(2,1)S(1)}, bf16[512,640]{1,0:T(8,128)(2,1)}, bf16[512,640]{1,0:T(8,128)(2,1)}, bf16[...) custom-call(bf16[128,19968]{1,0:T(8,128)(2,1)S(1)} %copy-done), custom_call_target="tpu_custom_call" | custom-call | bytes 10223616 | tf_op jit(solution)/shard_map/pack/pallas_call | solution.py:88
  5.8 2.4 %collective-permute-start.9 = (bf16[512,640]{1,0:T(8,128)(2,1)}, bf16[512,640]{1,0:T(8,128)(2,1)}, u32[]{:S(2)}, u32[]{:S(2)}) collective-permute-start(bf16[512,640]{1,0:T(8,128)(2,1)} %get-tuple-element.33), channel_id=1, source_target_pairs={{0,2},{1,5},{2,0},{3,7},{4,6},{5,1},{6,4},{7,3},{8,10},{9,13},{10,... | collective-permute-start | bytes 1966088 | tf_op jit(solution)/shard_map/ppermute | solution.py:393
  8.1 1.2 %collective-permute-done.8.refs_1_ = bf16[2,512,640]{2,1,0:T(8,128)(2,1)S(1)} collective-permute-done((bf16[2,512,640]{2,1,0:T(8,128)(2,1)S(1)}, bf16[2,512,640]{2,1,0:T(8,128)(2,1)S(1)}, u32[]{:S(2)}, u32[]{:S(2)}) %collective-permute-start.8) | collective-permute-done | bytes 1310752 | tf_op jit(solution)/shard_map/ppermute | solution.py:393
  9.4 0.9 %slice_bitcast_fusion = bf16[512,640]{1,0:T(8,128)(2,1)} fusion(bf16[2,512,640]{2,1,0:T(8,128)(2,1)S(1)} %collective-permute-done.8.refs_1_), kind=kLoop, calls=%fused_computation | loop fusion | bytes 1310720 | tf_op jit(solution)/shard_map/squeeze | solution.py:414
  10.3 2.4 %collective-permute-start.10 = (bf16[512,640]{1,0:T(8,128)(2,1)}, bf16[512,640]{1,0:T(8,128)(2,1)}, u32[]{:S(2)}, u32[]{:S(2)}) collective-permute-start(bf16[512,640]{1,0:T(8,128)(2,1)} %slice_bitcast_fusion), channel_id=1, source_target_pairs={{0,2},{1,5},{2,0},{3,7},{4,6},{5,1},{6,4},{7,3},{8,10},{9,13},{10,... | collective-permute-start | bytes 1966088 | tf_op jit(solution)/shard_map/ppermute | solution.py:393
  14.2 1.0 %collective-permute-start.1 = (bf16[2,64,128]{2,1,0:T(8,128)(2,1)S(1)}, bf16[2,64,128]{2,1,0:T(8,128)(2,1)S(1)}, u32[]{:S(2)}, u32[]{:S(2)}) collective-permute-start(bf16[2,64,128]{2,1,0:T(8,128)(2,1)S(1)} %pad_maximum_fusion.near_ref), channel_id=1, source_target_pairs={{3,0},{4,1},{1,2},{6,3},{7,4},{0,5},{5,6},{2,7},{11,8},{12,9},{9,1... | collective-permute-start | bytes 98312 | tf_op jit(solution)/shard_map/ppermute | solution.py:393
  16.1 2.3 %collective-permute-done.1.far_ref = bf16[2,64,128]{2,1,0:T(8,128)(2,1)S(1)} collective-permute-done((bf16[2,64,128]{2,1,0:T(8,128)(2,1)S(1)}, bf16[2,64,128]{2,1,0:T(8,128)(2,1)S(1)}, u32[]{:S(2)}, u32[]{:S(2)}) %collective-permute-start.1) | collective-permute-done | bytes 32800 | tf_op jit(solution)/shard_map/ppermute | solution.py:393
  18.8 1.0 %collective-permute-start.2 = (f32[48,128]{1,0:T(8,128)S(1)}, f32[48,128]{1,0:T(8,128)S(1)}, u32[]{:S(2)}, u32[]{:S(2)}) collective-permute-start(f32[48,128]{1,0:T(8,128)S(1)} %get-tuple-element.24.near_ref), channel_id=1, source_target_pairs={{0,4},{1,3},{2,6},{3,1},{4,0},{5,7},{6,2},{7,5},{8,12},{9,11},{10,... | collective-permute-start | bytes 73736 | tf_op jit(solution)/shard_map/ppermute | solution.py:393
  20.5 1.8 %collective-permute-done.2.far_ref = f32[48,128]{1,0:T(8,128)S(1)} collective-permute-done((f32[48,128]{1,0:T(8,128)S(1)}, f32[48,128]{1,0:T(8,128)S(1)}, u32[]{:S(2)}, u32[]{:S(2)}) %collective-permute-start.2) | collective-permute-done | bytes 24608 | tf_op jit(solution)/shard_map/ppermute | solution.py:393
  23.0 1.3 %collective-permute-done.10.refs_3_ = bf16[512,640]{1,0:T(8,128)(2,1)} collective-permute-done((bf16[512,640]{1,0:T(8,128)(2,1)}, bf16[512,640]{1,0:T(8,128)(2,1)}, u32[]{:S(2)}, u32[]{:S(2)}) %collective-permute-start.10) | collective-permute-done | bytes 655392 | tf_op jit(solution)/shard_map/ppermute | solution.py:393
  24.3 2.4 %group_moments.1 = (f32[1,128,640]{2,1,0:T(8,128)S(1)}, f32[1,128,640]{2,1,0:T(8,128)S(1)}, f32[1,128,640]{2,1,0:T(8,128)S(1)}, f32[1,128,640]{2,1,0:T(8,128)S(1)}) custom-call(bf16[512,640]{1,0:T(8,128)(2,1)S(1)} %copy-done.4, bf16[2,512,640]{2,1,0:T(8,128)(2,1)S(1)} %collective-permute-done.8.refs_1_, bf16[512,640]{1,0:T(8,128)(2,1)} %collective-permute-done.9.refs_2_, ...), custom_call_target="tpu_custom_call" | custom-call | bytes 6291456 | tf_op jit(solution)/shard_map/group_moments/pallas_call | solution.py:312
  26.7 1.5 %collective-permute-start.12 = (f32[1,128,640]{2,1,0:T(8,128)S(1)}, f32[1,128,640]{2,1,0:T(8,128)S(1)}, u32[]{:S(2)}, u32[]{:S(2)}) collective-permute-start(f32[1,128,640]{2,1,0:T(8,128)S(1)} %get-tuple-element.38), channel_id=1, source_target_pairs={{0,4},{1,3},{2,6},{3,1},{4,0},{5,7},{6,2},{7,5},{8,12},{9,11},{10,... | collective-permute-start | bytes 983048 | tf_op jit(solution)/shard_map/ppermute | solution.py:393
  28.3 1.3 %collective-permute-start.4 = (f32[48,128]{1,0:T(8,128)S(1)}, f32[48,128]{1,0:T(8,128)S(1)}, u32[]{:S(2)}, u32[]{:S(2)}) collective-permute-start(f32[48,128]{1,0:T(8,128)S(1)} %add.10.here_ref.refs_5_), channel_id=1, source_target_pairs={{0,1},{2,3},{4,5},{6,7},{8,9},{10,11},{12,13},{14,15},{16,17},{18,... | collective-permute-start | bytes 73736 | tf_op jit(solution)/shard_map/ppermute | solution.py:393
  29.5 6.6 %collective-permute-done.4.told_ref = f32[48,128]{1,0:T(8,128)S(1)} collective-permute-done((f32[48,128]{1,0:T(8,128)S(1)}, f32[48,128]{1,0:T(8,128)S(1)}, u32[]{:S(2)}, u32[]{:S(2)}) %collective-permute-start.4) | collective-permute-done | bytes 24608 | tf_op jit(solution)/shard_map/ppermute | solution.py:393
  37.2 2.5 %collective-permute-start.15 = (f32[1,112,640]{2,1,0:T(8,128)S(1)}, f32[1,112,640]{2,1,0:T(8,128)S(1)}, u32[]{:S(2)}, u32[]{:S(2)}) collective-permute-start(f32[1,112,640]{2,1,0:T(8,128)S(1)} %meet.3.refs_8_), channel_id=1, source_target_pairs={{0,8},{1,9},{2,10},{3,11},{4,12},{5,13},{6,14},{7,15},{8,0},{9,1},... | collective-permute-start | bytes 860168 | tf_op jit(solution)/shard_map/ppermute | solution.py:393
  39.8 3.8 %collective-permute-done.11.right_ref = f32[1,128,640]{2,1,0:T(8,128)S(1)} collective-permute-done((f32[1,128,640]{2,1,0:T(8,128)S(1)}, f32[1,128,640]{2,1,0:T(8,128)S(1)}, u32[]{:S(2)}, u32[]{:S(2)}) %collective-permute-start.11) | collective-permute-done | bytes 327712 | tf_op jit(solution)/shard_map/ppermute | solution.py:393
  44.2 2.5 %collective-permute-start.13 = (f32[1,112,640]{2,1,0:T(8,128)S(1)}, f32[1,112,640]{2,1,0:T(8,128)S(1)}, u32[]{:S(2)}, u32[]{:S(2)}) collective-permute-start(f32[1,112,640]{2,1,0:T(8,128)S(1)} %meet.2.refs_7_), channel_id=1, source_target_pairs={{0,8},{1,9},{2,10},{3,11},{4,12},{5,13},{6,14},{7,15},{8,0},{9,1},... | collective-permute-start | bytes 860168 | tf_op jit(solution)/shard_map/ppermute | solution.py:393
  46.8 1.1 %moments.1 = (f32[112,640]{1,0:T(8,128)S(1)}, f32[112,640]{1,0:T(8,128)S(1)}, f32[112,640]{1,0:T(8,128)S(1)}, f32[112,640]{1,0:T(8,128)S(1)}) custom-call(bf16[512,640]{1,0:T(8,128)(2,1)S(1)} %copy-done.2, bf16[2,512,640]{2,1,0:T(8,128)(2,1)S(1)} %collective-permute-done.5.refs_1_, bf16[512,640]{1,0:T(8,128)(2,1)S(1)} %collective-permute-done.6.refs_0_.refs_2_, ...), custom_call_target="tpu_custom_call" | custom-call | bytes 6291456 | tf_op jit(solution)/shard_map/moments/pallas_call | solution.py:332
  47.9 1.3 %collective-permute-start.14 = (f32[112,640]{1,0:T(8,128)S(1)}, f32[112,640]{1,0:T(8,128)S(1)}, u32[]{:S(2)}, u32[]{:S(2)}) collective-permute-start(f32[112,640]{1,0:T(8,128)S(1)} %get-tuple-element.40), channel_id=1, source_target_pairs={{0,4},{1,3},{2,6},{3,1},{4,0},{5,7},{6,2},{7,5},{8,12},{9,11},{10,... | collective-permute-start | bytes 860168 | tf_op jit(solution)/shard_map/ppermute | solution.py:393
  49.2 7.5 %collective-permute-start.17 = (f32[112,640]{1,0:T(8,128)S(1)}, f32[112,640]{1,0:T(8,128)S(1)}, u32[]{:S(2)}, u32[]{:S(2)}) collective-permute-start(f32[112,640]{1,0:T(8,128)S(1)} %get-tuple-element.42), channel_id=1, source_target_pairs={{0,5},{1,2},{2,7},{3,0},{4,1},{5,6},{6,3},{7,4},{8,13},{9,10},{10,... | collective-permute-start | bytes 860168 | tf_op jit(solution)/shard_map/ppermute | solution.py:393
  56.7 8.2 %collective-permute-start.16 = (f32[112,640]{1,0:T(8,128)S(1)}, f32[112,640]{1,0:T(8,128)S(1)}, u32[]{:S(2)}, u32[]{:S(2)}) collective-permute-start(f32[112,640]{1,0:T(8,128)S(1)} %bitcast_add_fusion), channel_id=1, source_target_pairs={{0,1},{1,0},{2,3},{3,2},{4,5},{5,4},{6,7},{7,6},{8,9},{9,8},{10,11... | collective-permute-start | bytes 860168 | tf_op jit(solution)/shard_map/ppermute | solution.py:393
  65.0 5.9 %collective-permute-done.17.refs_4_ = f32[112,640]{1,0:T(8,128)S(1)} collective-permute-done((f32[112,640]{1,0:T(8,128)S(1)}, f32[112,640]{1,0:T(8,128)S(1)}, u32[]{:S(2)}, u32[]{:S(2)}) %collective-permute-start.17) | collective-permute-done | bytes 286752 | tf_op jit(solution)/shard_map/ppermute | solution.py:393
  70.9 1.6 %finish.1 = f32[48,1,1248]{2,1,0:T(1,128)} custom-call(s32[48,1]{1,0:T(8,128)S(1)} %copy.9.pick_ref, f32[3,48,128]{2,1,0:T(8,128)S(1)} %get-tuple-element.25.stats_ref.refs_6_, f32[112,640]{1,0:T(8,128)S(1)} %get-tuple-element.39.refs_0_, f32[112,640]{1,0:T(8,128)S(1)} %bitcast.14, f32[112,640]{1,0:T(8,128)S(1)} %collective-permute-done.14.refs_2_, ...), custom_call_target="tpu_custom_call" | custom-call | bytes 16384 | tf_op jit(solution)/shard_map/finish/pallas_call | solution.py:380
  (45 shorter events, 6.5 us)
Async XLA Ops:
  5.1 10.8 %copy-start.1 = (bf16[512,640]{1,0:T(8,128)(2,1)}, bf16[512,640]{1,0:T(8,128)(2,1)S(1)}, u32[]{:S(2)}) copy-start(bf16[512,640]{1,0:T(8,128)(2,1)S(1)} %get-tuple-element.26.refs_0_) | copy-start | bytes 1966084
  5.2 10.8 %copy-start.3 = (bf16[512,640]{1,0:T(8,128)(2,1)}, bf16[512,640]{1,0:T(8,128)(2,1)S(1)}, u32[]{:S(2)}) copy-start(bf16[512,640]{1,0:T(8,128)(2,1)S(1)} %get-tuple-element.31.refs_0_) | copy-start | bytes 1966084
  5.2 7.5 %copy-start.6 = (bf16[128,16]{0,1:T(8,128)(2,1)S(1)}, bf16[128,16]{0,1:T(8,128)(2,1)}, u32[]{:S(2)}) copy-start(bf16[128,16]{0,1:T(8,128)(2,1)} %param.5) | copy-start | bytes 12292
  5.2 10.8 %copy-start.7 = (s32[48]{0:T(128)S(1)}, s32[48]{0:T(128)}, u32[]{:S(2)}) copy-start(s32[48]{0:T(128)} %param.7) | copy-start | bytes 580
  5.2 4.2 %collective-permute-start.8 = (bf16[2,512,640]{2,1,0:T(8,128)(2,1)S(1)}, bf16[2,512,640]{2,1,0:T(8,128)(2,1)S(1)}, u32[]{:S(2)}, u32[]{:S(2)}) collective-permute-start(bf16[2,512,640]{2,1,0:T(8,128)(2,1)S(1)} %get-tuple-element.32), channel_id=1, source_target_pairs={{0,1},{1,0},{2,3},{3,2},{4,5},{5,4},{6,7},{7,6},{8,9},{9,8},{10,11... | collective-permute-start | bytes 3932168 | tf_op jit(solution)/shard_map/ppermute | solution.py:393
  5.3 14.6 %collective-permute-start.5 = (bf16[2,512,640]{2,1,0:T(8,128)(2,1)}, bf16[2,512,640]{2,1,0:T(8,128)(2,1)S(1)}, u32[]{:S(2)}, u32[]{:S(2)}) collective-permute-start(bf16[2,512,640]{2,1,0:T(8,128)(2,1)} %get-tuple-element.27), channel_id=1, source_target_pairs={{0,1},{1,0},{2,3},{3,2},{4,5},{5,4},{6,7},{7,6},{8,9},{9,8},{10,11... | collective-permute-start | bytes 3932168 | tf_op jit(solution)/shard_map/ppermute | solution.py:393
  5.8 17.2 %collective-permute-start.9 = (bf16[512,640]{1,0:T(8,128)(2,1)}, bf16[512,640]{1,0:T(8,128)(2,1)}, u32[]{:S(2)}, u32[]{:S(2)}) collective-permute-start(bf16[512,640]{1,0:T(8,128)(2,1)} %get-tuple-element.33), channel_id=1, source_target_pairs={{0,2},{1,5},{2,0},{3,7},{4,6},{5,1},{6,4},{7,3},{8,10},{9,13},{10,... | collective-permute-start | bytes 1966088 | tf_op jit(solution)/shard_map/ppermute | solution.py:393
  10.3 14.1 %collective-permute-start.10 = (bf16[512,640]{1,0:T(8,128)(2,1)}, bf16[512,640]{1,0:T(8,128)(2,1)}, u32[]{:S(2)}, u32[]{:S(2)}) collective-permute-start(bf16[512,640]{1,0:T(8,128)(2,1)} %slice_bitcast_fusion), channel_id=1, source_target_pairs={{0,2},{1,5},{2,0},{3,7},{4,6},{5,1},{6,4},{7,3},{8,10},{9,13},{10,... | collective-permute-start | bytes 1966088 | tf_op jit(solution)/shard_map/ppermute | solution.py:393
  12.7 1.5 %collective-permute-start = (bf16[64,128]{1,0:T(8,128)(2,1)S(1)}, bf16[64,128]{1,0:T(8,128)(2,1)S(1)}, u32[]{:S(2)}, u32[]{:S(2)}) collective-permute-start(bf16[64,128]{1,0:T(8,128)(2,1)S(1)} %get-tuple-element.44), channel_id=1, source_target_pairs={{0,1},{1,0},{2,3},{3,2},{4,5},{5,4},{6,7},{7,6},{8,9},{9,8},{10,11... | collective-permute-start | bytes 49160 | tf_op jit(solution)/shard_map/ppermute | solution.py:393
  14.2 4.2 %collective-permute-start.1 = (bf16[2,64,128]{2,1,0:T(8,128)(2,1)S(1)}, bf16[2,64,128]{2,1,0:T(8,128)(2,1)S(1)}, u32[]{:S(2)}, u32[]{:S(2)}) collective-permute-start(bf16[2,64,128]{2,1,0:T(8,128)(2,1)S(1)} %pad_maximum_fusion.near_ref), channel_id=1, source_target_pairs={{3,0},{4,1},{1,2},{6,3},{7,4},{0,5},{5,6},{2,7},{11,8},{12,9},{9,1... | collective-permute-start | bytes 98312 | tf_op jit(solution)/shard_map/ppermute | solution.py:393
  15.3 24.5 %collective-permute-start.6 = (bf16[512,640]{1,0:T(8,128)(2,1)}, bf16[512,640]{1,0:T(8,128)(2,1)S(1)}, u32[]{:S(2)}, u32[]{:S(2)}) collective-permute-start(bf16[512,640]{1,0:T(8,128)(2,1)} %get-tuple-element.28), channel_id=1, source_target_pairs={{0,2},{1,5},{2,0},{3,7},{4,6},{5,1},{6,4},{7,3},{8,10},{9,13},{10,... | collective-permute-start | bytes 1966088 | tf_op jit(solution)/shard_map/ppermute | solution.py:393
  16.1 8.3 %copy-start.4 = (bf16[512,640]{1,0:T(8,128)(2,1)S(1)}, bf16[512,640]{1,0:T(8,128)(2,1)}, u32[]{:S(2)}) copy-start(bf16[512,640]{1,0:T(8,128)(2,1)} %copy-done.3) | copy-start | bytes 1966084
  18.8 3.5 %collective-permute-start.2 = (f32[48,128]{1,0:T(8,128)S(1)}, f32[48,128]{1,0:T(8,128)S(1)}, u32[]{:S(2)}, u32[]{:S(2)}) collective-permute-start(f32[48,128]{1,0:T(8,128)S(1)} %get-tuple-element.24.near_ref), channel_id=1, source_target_pairs={{0,4},{1,3},{2,6},{3,1},{4,0},{5,7},{6,2},{7,5},{8,12},{9,11},{10,... | collective-permute-start | bytes 73736 | tf_op jit(solution)/shard_map/ppermute | solution.py:393
  19.9 26.8 %collective-permute-start.7 = (bf16[512,640]{1,0:T(8,128)(2,1)S(1)}, bf16[512,640]{1,0:T(8,128)(2,1)S(1)}, u32[]{:S(2)}, u32[]{:S(2)}) collective-permute-start(bf16[512,640]{1,0:T(8,128)(2,1)S(1)} %slice_bitcast_fusion.1), channel_id=1, source_target_pairs={{0,2},{1,5},{2,0},{3,7},{4,6},{5,1},{6,4},{7,3},{8,10},{9,13},{10,... | collective-permute-start | bytes 1966088 | tf_op jit(solution)/shard_map/ppermute | solution.py:393
  22.3 0.7 collective-permute-start.3
  26.7 9.9 %collective-permute-start.12 = (f32[1,128,640]{2,1,0:T(8,128)S(1)}, f32[1,128,640]{2,1,0:T(8,128)S(1)}, u32[]{:S(2)}, u32[]{:S(2)}) collective-permute-start(f32[1,128,640]{2,1,0:T(8,128)S(1)} %get-tuple-element.38), channel_id=1, source_target_pairs={{0,4},{1,3},{2,6},{3,1},{4,0},{5,7},{6,2},{7,5},{8,12},{9,11},{10,... | collective-permute-start | bytes 983048 | tf_op jit(solution)/shard_map/ppermute | solution.py:393
  28.2 15.4 %collective-permute-start.11 = (f32[1,128,640]{2,1,0:T(8,128)S(1)}, f32[1,128,640]{2,1,0:T(8,128)S(1)}, u32[]{:S(2)}, u32[]{:S(2)}) collective-permute-start(f32[1,128,640]{2,1,0:T(8,128)S(1)} %get-tuple-element.36), channel_id=1, source_target_pairs={{0,4},{1,3},{2,6},{3,1},{4,0},{5,7},{6,2},{7,5},{8,12},{9,11},{10,... | collective-permute-start | bytes 983048 | tf_op jit(solution)/shard_map/ppermute | solution.py:393
  28.3 7.9 %collective-permute-start.4 = (f32[48,128]{1,0:T(8,128)S(1)}, f32[48,128]{1,0:T(8,128)S(1)}, u32[]{:S(2)}, u32[]{:S(2)}) collective-permute-start(f32[48,128]{1,0:T(8,128)S(1)} %add.10.here_ref.refs_5_), channel_id=1, source_target_pairs={{0,1},{2,3},{4,5},{6,7},{8,9},{10,11},{12,13},{14,15},{16,17},{18,... | collective-permute-start | bytes 73736 | tf_op jit(solution)/shard_map/ppermute | solution.py:393
  36.6 10.2 %copy-start.2 = (bf16[512,640]{1,0:T(8,128)(2,1)S(1)}, bf16[512,640]{1,0:T(8,128)(2,1)}, u32[]{:S(2)}) copy-start(bf16[512,640]{1,0:T(8,128)(2,1)} %copy-done.1) | copy-start | bytes 1966084
  37.2 19.5 %collective-permute-start.15 = (f32[1,112,640]{2,1,0:T(8,128)S(1)}, f32[1,112,640]{2,1,0:T(8,128)S(1)}, u32[]{:S(2)}, u32[]{:S(2)}) collective-permute-start(f32[1,112,640]{2,1,0:T(8,128)S(1)} %meet.3.refs_8_), channel_id=1, source_target_pairs={{0,8},{1,9},{2,10},{3,11},{4,12},{5,13},{6,14},{7,15},{8,0},{9,1},... | collective-permute-start | bytes 860168 | tf_op jit(solution)/shard_map/ppermute | solution.py:393
  44.2 26.6 %collective-permute-start.13 = (f32[1,112,640]{2,1,0:T(8,128)S(1)}, f32[1,112,640]{2,1,0:T(8,128)S(1)}, u32[]{:S(2)}, u32[]{:S(2)}) collective-permute-start(f32[1,112,640]{2,1,0:T(8,128)S(1)} %meet.2.refs_7_), channel_id=1, source_target_pairs={{0,8},{1,9},{2,10},{3,11},{4,12},{5,13},{6,14},{7,15},{8,0},{9,1},... | collective-permute-start | bytes 860168 | tf_op jit(solution)/shard_map/ppermute | solution.py:393
  47.9 17.0 %collective-permute-start.14 = (f32[112,640]{1,0:T(8,128)S(1)}, f32[112,640]{1,0:T(8,128)S(1)}, u32[]{:S(2)}, u32[]{:S(2)}) collective-permute-start(f32[112,640]{1,0:T(8,128)S(1)} %get-tuple-element.40), channel_id=1, source_target_pairs={{0,4},{1,3},{2,6},{3,1},{4,0},{5,7},{6,2},{7,5},{8,12},{9,11},{10,... | collective-permute-start | bytes 860168 | tf_op jit(solution)/shard_map/ppermute | solution.py:393
  49.2 21.7 %collective-permute-start.17 = (f32[112,640]{1,0:T(8,128)S(1)}, f32[112,640]{1,0:T(8,128)S(1)}, u32[]{:S(2)}, u32[]{:S(2)}) collective-permute-start(f32[112,640]{1,0:T(8,128)S(1)} %get-tuple-element.42), channel_id=1, source_target_pairs={{0,5},{1,2},{2,7},{3,0},{4,1},{5,6},{6,3},{7,4},{8,13},{9,10},{10,... | collective-permute-start | bytes 860168 | tf_op jit(solution)/shard_map/ppermute | solution.py:393
  56.7 14.2 %collective-permute-start.16 = (f32[112,640]{1,0:T(8,128)S(1)}, f32[112,640]{1,0:T(8,128)S(1)}, u32[]{:S(2)}, u32[]{:S(2)}) collective-permute-start(f32[112,640]{1,0:T(8,128)S(1)} %bitcast_add_fusion), channel_id=1, source_target_pairs={{0,1},{1,0},{2,3},{3,2},{4,5},{5,4},{6,7},{7,6},{8,9},{9,8},{10,11... | collective-permute-start | bytes 860168 | tf_op jit(solution)/shard_map/ppermute | solution.py:393
  (2 other events, 10.0 us)

commit v14 on v13

--- a/solution.py
+++ b/solution.py
@@ -389,6 +389,24 @@
     )(pick_column, stats, *operands)
 
 
+def hold_kernel(*refs):
+    del refs
+
+
+def hold(array, after):
+    any_space = pl.BlockSpec(memory_space=pl.ANY)
+    return pl.pallas_call(
+        hold_kernel,
+        in_specs=[any_space] * (1 + len(after)),
+        out_specs=any_space,
+        out_shape=jax.ShapeDtypeStruct(array.shape, array.dtype),
+        input_output_aliases={0: 0},
+        compiler_params=pltpu.CompilerParams(vmem_limit_bytes=1 << 20),
+        cost_estimate=pl.CostEstimate(flops=0, bytes_accessed=0, transcendentals=0),
+        name="hold",
+    )(array, *after)
+
+
 def swap(array, pairs):
     return lax.ppermute(array, "pat", pairs)
 
@@ -407,12 +425,12 @@
     far = swap(near, [(pair ^ 1, d) for d, pair in plan.by_rows()])
 
     kept0, kept1, sent0, sent1, other0, other1 = pack(covariates, plan)
-    rows_here = {}
+    rows_here, forward = {}, {}
     for chunk, kept, sent, other in ((1, kept1, sent1, other1), (0, kept0, sent0, other0)):
         passed = swap(other, to_other_side)
-        rows_here[chunk] = [
-            kept, passed, swap(sent, plan.by_rows()), swap(passed[1], plan.by_rows())
-        ]
+        rows_here[chunk] = [kept, passed, swap(sent, plan.by_rows())]
+        forward[chunk] = passed[1]
+    rows_here[1].append(swap(forward[1], plan.by_rows()))
 
     near_totals, panel = make_group(near, far, pick_column, weightings)
     far_totals = swap(near_totals, plan.by_sums())
@@ -422,15 +440,17 @@
     told = swap(totals, to_other_side[0::2])
     first, second, stats = make_panels(near, far, totals, told, pick_column, weightings)
 
-    across, top, after = [], [], [rows_here[0][2]]
+    across, top, came = [], [], []
     for even, odd in group_moments(plan, rows_here[1], panel, [totals]):
         arrived = swap(odd, plan.by_sums())
-        met = meet(pick_column, near_totals, far_totals, stats, even, arrived, after)
+        met = meet(pick_column, near_totals, far_totals, stats, even, arrived, [rows_here[0][2]])
+        came.append(arrived)
         for bit in plan.middle_bits:
             met = met[0::2] + swap(met[1::2], plan.by_mask(1 << bit))
         across.append(met)
         top.append(swap(met, plan.by_mask(1 << plan.top_bit))[0])
-        after = []
+
+    rows_here[0].append(swap(hold(forward[0], [across[1]]), plan.by_rows()))
 
     last = not plan.middle_bits
     sums = moments(plan, rows_here[0], first, second, stats, last, across)

time: 72.7 us -> 79.4 us (1.092)
  waiting for transfers between devices: 24 us -> 38 us
  starting transfers between devices: 35 us -> 26.5 us
  local copies, waits for them, and re-layouts: 3.52 us -> 4.6 us
    ppermute x18, waiting for transfers between devices: 24 us -> 38 us  [swap(): return lax.ppermute(array, 'pat', pairs)]
    ppermute x18, starting transfers between devices: 35 us -> 26.5 us  [swap(): return lax.ppermute(array, 'pat', pairs)]
    unnamed x16, local copies, waits for them, and re-layouts: 2.48 us -> 3.56 us
  transfers between devices with their start and end apart: 18 -> 18, of which waited for: 9 -> 11; matrix products, arithmetic and copies ran while one was open for 2% -> 1% of each run, Pallas kernels for 8% -> 6%
where the time goes in v14:
time: 79.4 us; the launch traced here: 79 us
  waiting for transfers between devices  38 us (48%)
  starting transfers between devices  26.5 us (33%)
  Pallas kernels  9.72 us (12%)
  local copies, waits for them, and re-layouts  4.6 us (6%)
    ppermute x18, waiting for transfers between devices, swap(): return lax.ppermute(array, 'pat', pairs)  38 us
    ppermute x18, starting transfers between devices, swap(): return lax.ppermute(array, 'pat', pairs)  26.5 us
    unnamed x16, local copies, waits for them, and re-layouts  3.56 us
    pallas_call x1, Pallas kernels, pack(): pl.pallas_call(functools.partial(pack_kernel, plan), grid=(plan.places,),...  2.7 us
    pallas_call x1, Pallas kernels, group_moments(): pl.pallas_call(functools.partial(group_moments_kernel, rows, 2), in_specs...  2.36 us
    pallas_call x4, Pallas kernels, small_call(): pl.pallas_call(kernel, in_specs=[vmem] * len(operands) + [pl.BlockSpec(me...  1.95 us
    pallas_call x1, Pallas kernels, finish(): pl.pallas_call(functools.partial(finish_kernel, plan, weightings, [len(pa...  1.61 us
  transfers between devices with their start and end apart: 18, of which 11 were waited for; matrix products, arithmetic and copies ran while one was open for 1% of the time, Pallas kernels for 6%

profile of v14, /device:TPU:1, one launch (start us, length us, event | category | flops | bytes accessed | tf_op | source)
XLA Modules:
  0.0 79.0 jit_solution(6291849234672551438)
XLA Ops:
  0.0 2.4 %copy-done = bf16[128,19968]{1,0:T(8,128)(2,1)S(1)} copy-done((bf16[128,19968]{1,0:T(8,128)(2,1)S(1)}, bf16[128,19968]{1,0:T(8,128)(2,1)}, u32[]{:S(2)}) %copy-start) | copy-done | bytes 5111832
  2.5 2.7 %pack.1 = (bf16[512,640]{1,0:T(8,128)(2,1)S(1)}, bf16[512,640]{1,0:T(8,128)(2,1)S(1)}, bf16[512,640]{1,0:T(8,128)(2,1)}, bf16[512,640]{1,0:T(8,128)(2,1)}, bf16[...) custom-call(bf16[128,19968]{1,0:T(8,128)(2,1)S(1)} %copy-done), custom_call_target="tpu_custom_call" | custom-call | bytes 10223616 | tf_op jit(solution)/shard_map/pack/pallas_call | solution.py:88
  5.8 2.4 %collective-permute-start.8 = (bf16[512,640]{1,0:T(8,128)(2,1)}, bf16[512,640]{1,0:T(8,128)(2,1)}, u32[]{:S(2)}, u32[]{:S(2)}) collective-permute-start(bf16[512,640]{1,0:T(8,128)(2,1)} %get-tuple-element.31), channel_id=1, source_target_pairs={{0,2},{1,5},{2,0},{3,7},{4,6},{5,1},{6,4},{7,3},{8,10},{9,13},{10,... | collective-permute-start | bytes 1966088 | tf_op jit(solution)/shard_map/ppermute | solution.py:411
  8.1 1.2 %collective-permute-done.7.refs_1_ = bf16[2,512,640]{2,1,0:T(8,128)(2,1)S(1)} collective-permute-done((bf16[2,512,640]{2,1,0:T(8,128)(2,1)S(1)}, bf16[2,512,640]{2,1,0:T(8,128)(2,1)S(1)}, u32[]{:S(2)}, u32[]{:S(2)}) %collective-permute-start.7) | collective-permute-done | bytes 1310752 | tf_op jit(solution)/shard_map/ppermute | solution.py:411
  10.3 2.4 %collective-permute-start.9 = (bf16[512,640]{1,0:T(8,128)(2,1)}, bf16[512,640]{1,0:T(8,128)(2,1)}, u32[]{:S(2)}, u32[]{:S(2)}) collective-permute-start(bf16[512,640]{1,0:T(8,128)(2,1)} %slice_bitcast_fusion), channel_id=1, source_target_pairs={{0,2},{1,5},{2,0},{3,7},{4,6},{5,1},{6,4},{7,3},{8,10},{9,13},{10,... | collective-permute-start | bytes 1966088 | tf_op jit(solution)/shard_map/ppermute | solution.py:411
  14.2 1.9 %collective-permute-start.1 = (bf16[2,64,128]{2,1,0:T(8,128)(2,1)S(1)}, bf16[2,64,128]{2,1,0:T(8,128)(2,1)S(1)}, u32[]{:S(2)}, u32[]{:S(2)}) collective-permute-start(bf16[2,64,128]{2,1,0:T(8,128)(2,1)S(1)} %pad_maximum_fusion.near_ref), channel_id=1, source_target_pairs={{3,0},{4,1},{1,2},{6,3},{7,4},{0,5},{5,6},{2,7},{11,8},{12,9},{9,1... | collective-permute-start | bytes 98312 | tf_op jit(solution)/shard_map/ppermute | solution.py:411
  16.3 2.4 %collective-permute-done.1.far_ref = bf16[2,64,128]{2,1,0:T(8,128)(2,1)S(1)} collective-permute-done((bf16[2,64,128]{2,1,0:T(8,128)(2,1)S(1)}, bf16[2,64,128]{2,1,0:T(8,128)(2,1)S(1)}, u32[]{:S(2)}, u32[]{:S(2)}) %collective-permute-start.1) | collective-permute-done | bytes 32800 | tf_op jit(solution)/shard_map/ppermute | solution.py:411
  19.1 1.5 %collective-permute-start.2 = (f32[48,128]{1,0:T(8,128)S(1)}, f32[48,128]{1,0:T(8,128)S(1)}, u32[]{:S(2)}, u32[]{:S(2)}) collective-permute-start(f32[48,128]{1,0:T(8,128)S(1)} %get-tuple-element.24.near_ref), channel_id=1, source_target_pairs={{0,4},{1,3},{2,6},{3,1},{4,0},{5,7},{6,2},{7,5},{8,12},{9,11},{10,... | collective-permute-start | bytes 73736 | tf_op jit(solution)/shard_map/ppermute | solution.py:411
  20.6 1.9 %collective-permute-done.2.far_ref = f32[48,128]{1,0:T(8,128)S(1)} collective-permute-done((f32[48,128]{1,0:T(8,128)S(1)}, f32[48,128]{1,0:T(8,128)S(1)}, u32[]{:S(2)}, u32[]{:S(2)}) %collective-permute-start.2) | collective-permute-done | bytes 24608 | tf_op jit(solution)/shard_map/ppermute | solution.py:411
  25.4 2.4 %group_moments.1 = (f32[1,128,640]{2,1,0:T(8,128)S(1)}, f32[1,128,640]{2,1,0:T(8,128)S(1)}, f32[1,128,640]{2,1,0:T(8,128)S(1)}, f32[1,128,640]{2,1,0:T(8,128)S(1)}) custom-call(bf16[512,640]{1,0:T(8,128)(2,1)S(1)} %copy-done.4, bf16[2,512,640]{2,1,0:T(8,128)(2,1)S(1)} %collective-permute-done.7.refs_1_, bf16[512,640]{1,0:T(8,128)(2,1)} %collective-permute-done.8.refs_2_, ...), custom_call_target="tpu_custom_call" | custom-call | bytes 6291456 | tf_op jit(solution)/shard_map/group_moments/pallas_call | solution.py:312
  27.8 1.5 %collective-permute-start.10 = (f32[1,128,640]{2,1,0:T(8,128)S(1)}, f32[1,128,640]{2,1,0:T(8,128)S(1)}, u32[]{:S(2)}, u32[]{:S(2)}) collective-permute-start(f32[1,128,640]{2,1,0:T(8,128)S(1)} %get-tuple-element.34), channel_id=1, source_target_pairs={{0,4},{1,3},{2,6},{3,1},{4,0},{5,7},{6,2},{7,5},{8,12},{9,11},{10,... | collective-permute-start | bytes 983048 | tf_op jit(solution)/shard_map/ppermute | solution.py:411
  29.3 1.3 %collective-permute-start.4 = (f32[48,128]{1,0:T(8,128)S(1)}, f32[48,128]{1,0:T(8,128)S(1)}, u32[]{:S(2)}, u32[]{:S(2)}) collective-permute-start(f32[48,128]{1,0:T(8,128)S(1)} %add.10.here_ref.refs_5_), channel_id=1, source_target_pairs={{0,1},{2,3},{4,5},{6,7},{8,9},{10,11},{12,13},{14,15},{16,17},{18,... | collective-permute-start | bytes 73736 | tf_op jit(solution)/shard_map/ppermute | solution.py:411
  30.6 6.9 %collective-permute-done.4.told_ref = f32[48,128]{1,0:T(8,128)S(1)} collective-permute-done((f32[48,128]{1,0:T(8,128)S(1)}, f32[48,128]{1,0:T(8,128)S(1)}, u32[]{:S(2)}, u32[]{:S(2)}) %collective-permute-start.4) | collective-permute-done | bytes 24608 | tf_op jit(solution)/shard_map/ppermute | solution.py:411
  38.6 1.3 %collective-permute-start.12 = (f32[1,128,640]{2,1,0:T(8,128)S(1)}, f32[1,128,640]{2,1,0:T(8,128)S(1)}, u32[]{:S(2)}, u32[]{:S(2)}) collective-permute-start(f32[1,128,640]{2,1,0:T(8,128)S(1)} %get-tuple-element.38), channel_id=1, source_target_pairs={{0,4},{1,3},{2,6},{3,1},{4,0},{5,7},{6,2},{7,5},{8,12},{9,11},{10,... | collective-permute-start | bytes 983048 | tf_op jit(solution)/shard_map/ppermute | solution.py:411
  39.9 2.4 %collective-permute-start.15 = (f32[1,112,640]{2,1,0:T(8,128)S(1)}, f32[1,112,640]{2,1,0:T(8,128)S(1)}, u32[]{:S(2)}, u32[]{:S(2)}) collective-permute-start(f32[1,112,640]{2,1,0:T(8,128)S(1)} %meet.2.refs_1_.refs_8_), channel_id=1, source_target_pairs={{0,8},{1,9},{2,10},{3,11},{4,12},{5,13},{6,14},{7,15},{8,0},{9,1},... | collective-permute-start | bytes 860168 | tf_op jit(solution)/shard_map/ppermute | solution.py:411
  42.3 2.7 %collective-permute-done.12.right_ref = f32[1,128,640]{2,1,0:T(8,128)S(1)} collective-permute-done((f32[1,128,640]{2,1,0:T(8,128)S(1)}, f32[1,128,640]{2,1,0:T(8,128)S(1)}, u32[]{:S(2)}, u32[]{:S(2)}) %collective-permute-start.12) | collective-permute-done | bytes 327712 | tf_op jit(solution)/shard_map/ppermute | solution.py:411
  45.7 2.0 %collective-permute-start.13 = (f32[1,112,640]{2,1,0:T(8,128)S(1)}, f32[1,112,640]{2,1,0:T(8,128)S(1)}, u32[]{:S(2)}, u32[]{:S(2)}) collective-permute-start(f32[1,112,640]{2,1,0:T(8,128)S(1)} %meet.3.refs_7_), channel_id=1, source_target_pairs={{0,8},{1,9},{2,10},{3,11},{4,12},{5,13},{6,14},{7,15},{8,0},{9,1},... | collective-permute-start | bytes 860168 | tf_op jit(solution)/shard_map/ppermute | solution.py:411
  47.7 11.7 %collective-permute-done.11.refs_3_ = bf16[512,640]{1,0:T(8,128)(2,1)S(1)} collective-permute-done((bf16[512,640]{1,0:T(8,128)(2,1)S(1)}, bf16[512,640]{1,0:T(8,128)(2,1)S(1)}, u32[]{:S(2)}, u32[]{:S(2)}) %collective-permute-start.11) | collective-permute-done | bytes 655392 | tf_op jit(solution)/shard_map/ppermute | solution.py:411
  59.4 1.1 %moments.1 = (f32[112,640]{1,0:T(8,128)S(1)}, f32[112,640]{1,0:T(8,128)S(1)}, f32[112,640]{1,0:T(8,128)S(1)}, f32[112,640]{1,0:T(8,128)S(1)}) custom-call(bf16[512,640]{1,0:T(8,128)(2,1)S(1)} %copy-done.2, bf16[2,512,640]{2,1,0:T(8,128)(2,1)S(1)} %collective-permute-done.5.refs_1_, bf16[512,640]{1,0:T(8,128)(2,1)S(1)} %collective-permute-done.6.refs_0_.refs_2_, ...), custom_call_target="tpu_custom_call" | custom-call | bytes 6291456 | tf_op jit(solution)/shard_map/moments/pallas_call | solution.py:332
  60.6 7.7 %collective-permute-start.16 = (f32[112,640]{1,0:T(8,128)S(1)}, f32[112,640]{1,0:T(8,128)S(1)}, u32[]{:S(2)}, u32[]{:S(2)}) collective-permute-start(f32[112,640]{1,0:T(8,128)S(1)} %bitcast_add_fusion), channel_id=1, source_target_pairs={{0,1},{1,0},{2,3},{3,2},{4,5},{5,4},{6,7},{7,6},{8,9},{9,8},{10,11... | collective-permute-start | bytes 860168 | tf_op jit(solution)/shard_map/ppermute | solution.py:411
  68.3 1.2 %collective-permute-done.16.refs_3_ = f32[112,640]{1,0:T(8,128)S(1)} collective-permute-done((f32[112,640]{1,0:T(8,128)S(1)}, f32[112,640]{1,0:T(8,128)S(1)}, u32[]{:S(2)}, u32[]{:S(2)}) %collective-permute-start.16) | collective-permute-done | bytes 286752 | tf_op jit(solution)/shard_map/ppermute | solution.py:411
  69.5 4.6 %collective-permute-done.14.refs_2_ = f32[112,640]{1,0:T(8,128)S(1)} collective-permute-done((f32[112,640]{1,0:T(8,128)S(1)}, f32[112,640]{1,0:T(8,128)S(1)}, u32[]{:S(2)}, u32[]{:S(2)}) %collective-permute-start.14) | collective-permute-done | bytes 286752 | tf_op jit(solution)/shard_map/ppermute | solution.py:411
  74.1 3.3 %collective-permute-done.17.refs_4_ = f32[112,640]{1,0:T(8,128)S(1)} collective-permute-done((f32[112,640]{1,0:T(8,128)S(1)}, f32[112,640]{1,0:T(8,128)S(1)}, u32[]{:S(2)}, u32[]{:S(2)}) %collective-permute-start.17) | collective-permute-done | bytes 286752 | tf_op jit(solution)/shard_map/ppermute | solution.py:411
  77.4 1.6 %finish.1 = f32[48,1,1248]{2,1,0:T(1,128)} custom-call(s32[48,1]{1,0:T(8,128)S(1)} %copy.10.pick_ref, f32[3,48,128]{2,1,0:T(8,128)S(1)} %get-tuple-element.25.stats_ref.refs_6_, f32[112,640]{1,0:T(8,128)S(1)} %get-tuple-element.39.refs_0_, f32[112,640]{1,0:T(8,128)S(1)} %bitcast.14, f32[112,640]{1,0:T(8,128)S(1)} %collective-permute-done.14.refs_2_, ...), custom_call_target="tpu_custom_call" | custom-call | bytes 16384 | tf_op jit(solution)/shard_map/finish/pallas_call | solution.py:380
  (46 shorter events, 8.1 us)
Async XLA Ops:
  5.1 11.0 %copy-start.1 = (bf16[512,640]{1,0:T(8,128)(2,1)}, bf16[512,640]{1,0:T(8,128)(2,1)S(1)}, u32[]{:S(2)}) copy-start(bf16[512,640]{1,0:T(8,128)(2,1)S(1)} %get-tuple-element.26.refs_0_) | copy-start | bytes 1966084
  5.2 11.0 %copy-start.3 = (bf16[512,640]{1,0:T(8,128)(2,1)}, bf16[512,640]{1,0:T(8,128)(2,1)S(1)}, u32[]{:S(2)}) copy-start(bf16[512,640]{1,0:T(8,128)(2,1)S(1)} %get-tuple-element.29.refs_0_) | copy-start | bytes 1966084
  5.2 7.6 %copy-start.5 = (s32[128,48]{0,1:T(8,128)S(1)}, s32[128,48]{0,1:T(8,128)}, u32[]{:S(2)}) copy-start(s32[128,48]{0,1:T(8,128)} %param.6) | copy-start | bytes 73732
  5.2 7.6 %copy-start.6 = (bf16[128,16]{0,1:T(8,128)(2,1)S(1)}, bf16[128,16]{0,1:T(8,128)(2,1)}, u32[]{:S(2)}) copy-start(bf16[128,16]{0,1:T(8,128)(2,1)} %param.5) | copy-start | bytes 12292
  5.2 11.0 %copy-start.7 = (s32[48]{0:T(128)S(1)}, s32[48]{0:T(128)}, u32[]{:S(2)}) copy-start(s32[48]{0:T(128)} %param.7) | copy-start | bytes 580
  5.2 4.2 %collective-permute-start.7 = (bf16[2,512,640]{2,1,0:T(8,128)(2,1)S(1)}, bf16[2,512,640]{2,1,0:T(8,128)(2,1)S(1)}, u32[]{:S(2)}, u32[]{:S(2)}) collective-permute-start(bf16[2,512,640]{2,1,0:T(8,128)(2,1)S(1)} %get-tuple-element.30), channel_id=1, source_target_pairs={{0,1},{1,0},{2,3},{3,2},{4,5},{5,4},{6,7},{7,6},{8,9},{9,8},{10,11... | collective-permute-start | bytes 3932168 | tf_op jit(solution)/shard_map/ppermute | solution.py:411
  5.3 32.4 %collective-permute-start.5 = (bf16[2,512,640]{2,1,0:T(8,128)(2,1)}, bf16[2,512,640]{2,1,0:T(8,128)(2,1)S(1)}, u32[]{:S(2)}, u32[]{:S(2)}) collective-permute-start(bf16[2,512,640]{2,1,0:T(8,128)(2,1)} %get-tuple-element.27), channel_id=1, source_target_pairs={{0,1},{1,0},{2,3},{3,2},{4,5},{5,4},{6,7},{7,6},{8,9},{9,8},{10,11... | collective-permute-start | bytes 3932168 | tf_op jit(solution)/shard_map/ppermute | solution.py:411
  5.8 17.5 %collective-permute-start.8 = (bf16[512,640]{1,0:T(8,128)(2,1)}, bf16[512,640]{1,0:T(8,128)(2,1)}, u32[]{:S(2)}, u32[]{:S(2)}) collective-permute-start(bf16[512,640]{1,0:T(8,128)(2,1)} %get-tuple-element.31), channel_id=1, source_target_pairs={{0,2},{1,5},{2,0},{3,7},{4,6},{5,1},{6,4},{7,3},{8,10},{9,13},{10,... | collective-permute-start | bytes 1966088 | tf_op jit(solution)/shard_map/ppermute | solution.py:411
  10.3 14.1 %collective-permute-start.9 = (bf16[512,640]{1,0:T(8,128)(2,1)}, bf16[512,640]{1,0:T(8,128)(2,1)}, u32[]{:S(2)}, u32[]{:S(2)}) collective-permute-start(bf16[512,640]{1,0:T(8,128)(2,1)} %slice_bitcast_fusion), channel_id=1, source_target_pairs={{0,2},{1,5},{2,0},{3,7},{4,6},{5,1},{6,4},{7,3},{8,10},{9,13},{10,... | collective-permute-start | bytes 1966088 | tf_op jit(solution)/shard_map/ppermute | solution.py:411
  12.7 25.1 %collective-permute-start.6 = (bf16[512,640]{1,0:T(8,128)(2,1)}, bf16[512,640]{1,0:T(8,128)(2,1)S(1)}, u32[]{:S(2)}, u32[]{:S(2)}) collective-permute-start(bf16[512,640]{1,0:T(8,128)(2,1)} %get-tuple-element.28), channel_id=1, source_target_pairs={{0,2},{1,5},{2,0},{3,7},{4,6},{5,1},{6,4},{7,3},{8,10},{9,13},{10,... | collective-permute-start | bytes 1966088 | tf_op jit(solution)/shard_map/ppermute | solution.py:411
  12.7 1.5 %collective-permute-start = (bf16[64,128]{1,0:T(8,128)(2,1)S(1)}, bf16[64,128]{1,0:T(8,128)(2,1)S(1)}, u32[]{:S(2)}, u32[]{:S(2)}) collective-permute-start(bf16[64,128]{1,0:T(8,128)(2,1)S(1)} %get-tuple-element.44), channel_id=1, source_target_pairs={{0,1},{1,0},{2,3},{3,2},{4,5},{5,4},{6,7},{7,6},{8,9},{9,8},{10,11... | collective-permute-start | bytes 49160 | tf_op jit(solution)/shard_map/ppermute | solution.py:411
  14.2 4.4 %collective-permute-start.1 = (bf16[2,64,128]{2,1,0:T(8,128)(2,1)S(1)}, bf16[2,64,128]{2,1,0:T(8,128)(2,1)S(1)}, u32[]{:S(2)}, u32[]{:S(2)}) collective-permute-start(bf16[2,64,128]{2,1,0:T(8,128)(2,1)S(1)} %pad_maximum_fusion.near_ref), channel_id=1, source_target_pairs={{3,0},{4,1},{1,2},{6,3},{7,4},{0,5},{5,6},{2,7},{11,8},{12,9},{9,1... | collective-permute-start | bytes 98312 | tf_op jit(solution)/shard_map/ppermute | solution.py:411
  19.1 3.5 %collective-permute-start.2 = (f32[48,128]{1,0:T(8,128)S(1)}, f32[48,128]{1,0:T(8,128)S(1)}, u32[]{:S(2)}, u32[]{:S(2)}) collective-permute-start(f32[48,128]{1,0:T(8,128)S(1)} %get-tuple-element.24.near_ref), channel_id=1, source_target_pairs={{0,4},{1,3},{2,6},{3,1},{4,0},{5,7},{6,2},{7,5},{8,12},{9,11},{10,... | collective-permute-start | bytes 73736 | tf_op jit(solution)/shard_map/ppermute | solution.py:411
  22.6 0.7 collective-permute-start.3
  27.8 10.0 %collective-permute-start.10 = (f32[1,128,640]{2,1,0:T(8,128)S(1)}, f32[1,128,640]{2,1,0:T(8,128)S(1)}, u32[]{:S(2)}, u32[]{:S(2)}) collective-permute-start(f32[1,128,640]{2,1,0:T(8,128)S(1)} %get-tuple-element.34), channel_id=1, source_target_pairs={{0,4},{1,3},{2,6},{3,1},{4,0},{5,7},{6,2},{7,5},{8,12},{9,11},{10,... | collective-permute-start | bytes 983048 | tf_op jit(solution)/shard_map/ppermute | solution.py:411
  29.3 8.2 %collective-permute-start.4 = (f32[48,128]{1,0:T(8,128)S(1)}, f32[48,128]{1,0:T(8,128)S(1)}, u32[]{:S(2)}, u32[]{:S(2)}) collective-permute-start(f32[48,128]{1,0:T(8,128)S(1)} %add.10.here_ref.refs_5_), channel_id=1, source_target_pairs={{0,1},{2,3},{4,5},{6,7},{8,9},{10,11},{12,13},{14,15},{16,17},{18,... | collective-permute-start | bytes 73736 | tf_op jit(solution)/shard_map/ppermute | solution.py:411
  38.5 21.0 %copy-start.2 = (bf16[512,640]{1,0:T(8,128)(2,1)S(1)}, bf16[512,640]{1,0:T(8,128)(2,1)}, u32[]{:S(2)}) copy-start(bf16[512,640]{1,0:T(8,128)(2,1)} %copy-done.1) | copy-start | bytes 1966084
  38.5 20.9 %collective-permute-start.11 = (bf16[512,640]{1,0:T(8,128)(2,1)S(1)}, bf16[512,640]{1,0:T(8,128)(2,1)S(1)}, u32[]{:S(2)}, u32[]{:S(2)}) collective-permute-start(bf16[512,640]{1,0:T(8,128)(2,1)S(1)} %hold.1), channel_id=1, source_target_pairs={{0,2},{1,5},{2,0},{3,7},{4,6},{5,1},{6,4},{7,3},{8,10},{9,13},{10,... | collective-permute-start | bytes 1966088 | tf_op jit(solution)/shard_map/ppermute | solution.py:411
  38.6 6.4 %collective-permute-start.12 = (f32[1,128,640]{2,1,0:T(8,128)S(1)}, f32[1,128,640]{2,1,0:T(8,128)S(1)}, u32[]{:S(2)}, u32[]{:S(2)}) collective-permute-start(f32[1,128,640]{2,1,0:T(8,128)S(1)} %get-tuple-element.38), channel_id=1, source_target_pairs={{0,4},{1,3},{2,6},{3,1},{4,0},{5,7},{6,2},{7,5},{8,12},{9,11},{10,... | collective-permute-start | bytes 983048 | tf_op jit(solution)/shard_map/ppermute | solution.py:411
  39.9 20.7 %collective-permute-start.15 = (f32[1,112,640]{2,1,0:T(8,128)S(1)}, f32[1,112,640]{2,1,0:T(8,128)S(1)}, u32[]{:S(2)}, u32[]{:S(2)}) collective-permute-start(f32[1,112,640]{2,1,0:T(8,128)S(1)} %meet.2.refs_1_.refs_8_), channel_id=1, source_target_pairs={{0,8},{1,9},{2,10},{3,11},{4,12},{5,13},{6,14},{7,15},{8,0},{9,1},... | collective-permute-start | bytes 860168 | tf_op jit(solution)/shard_map/ppermute | solution.py:411
  45.7 22.7 %collective-permute-start.13 = (f32[1,112,640]{2,1,0:T(8,128)S(1)}, f32[1,112,640]{2,1,0:T(8,128)S(1)}, u32[]{:S(2)}, u32[]{:S(2)}) collective-permute-start(f32[1,112,640]{2,1,0:T(8,128)S(1)} %meet.3.refs_7_), channel_id=1, source_target_pairs={{0,8},{1,9},{2,10},{3,11},{4,12},{5,13},{6,14},{7,15},{8,0},{9,1},... | collective-permute-start | bytes 860168 | tf_op jit(solution)/shard_map/ppermute | solution.py:411
  60.6 8.9 %collective-permute-start.16 = (f32[112,640]{1,0:T(8,128)S(1)}, f32[112,640]{1,0:T(8,128)S(1)}, u32[]{:S(2)}, u32[]{:S(2)}) collective-permute-start(f32[112,640]{1,0:T(8,128)S(1)} %bitcast_add_fusion), channel_id=1, source_target_pairs={{0,1},{1,0},{2,3},{3,2},{4,5},{5,4},{6,7},{7,6},{8,9},{9,8},{10,11... | collective-permute-start | bytes 860168 | tf_op jit(solution)/shard_map/ppermute | solution.py:411
  68.3 5.8 %collective-permute-start.14 = (f32[112,640]{1,0:T(8,128)S(1)}, f32[112,640]{1,0:T(8,128)S(1)}, u32[]{:S(2)}, u32[]{:S(2)}) collective-permute-start(f32[112,640]{1,0:T(8,128)S(1)} %get-tuple-element.40), channel_id=1, source_target_pairs={{0,4},{1,3},{2,6},{3,1},{4,0},{5,7},{6,2},{7,5},{8,12},{9,11},{10,... | collective-permute-start | bytes 860168 | tf_op jit(solution)/shard_map/ppermute | solution.py:411
  68.3 9.1 %collective-permute-start.17 = (f32[112,640]{1,0:T(8,128)S(1)}, f32[112,640]{1,0:T(8,128)S(1)}, u32[]{:S(2)}, u32[]{:S(2)}) collective-permute-start(f32[112,640]{1,0:T(8,128)S(1)} %get-tuple-element.42), channel_id=1, source_target_pairs={{0,5},{1,2},{2,7},{3,0},{4,1},{5,6},{6,3},{7,4},{8,13},{9,10},{10,... | collective-permute-start | bytes 860168 | tf_op jit(solution)/shard_map/ppermute | solution.py:411
  (2 other events, 3.5 us)

commit v15 on v13

--- a/solution.py
+++ b/solution.py
@@ -315,7 +315,7 @@
         + [pl.BlockSpec(memory_space=pl.ANY)] * len(after),
         out_specs=[pl.BlockSpec(memory_space=pltpu.VMEM)] * 4,
         out_shape=[out] * 4,
-        compiler_params=pltpu.CompilerParams(vmem_limit_bytes=20 << 20),
+        compiler_params=pltpu.CompilerParams(vmem_limit_bytes=10 << 20),
         cost_estimate=pl.CostEstimate(flops=0, bytes_accessed=6 << 20, transcendentals=0),
         name="group_moments",
     )(*rows_here, panel, *after)
@@ -335,7 +335,7 @@
         + [pl.BlockSpec(memory_space=pl.ANY)] * len(after),
         out_specs=[pl.BlockSpec(memory_space=pltpu.VMEM)] * len(out_shape),
         out_shape=out_shape,
-        compiler_params=pltpu.CompilerParams(vmem_limit_bytes=20 << 20),
+        compiler_params=pltpu.CompilerParams(vmem_limit_bytes=10 << 20),
         cost_estimate=pl.CostEstimate(flops=0, bytes_accessed=6 << 20, transcendentals=0),
         name="moments",
     )(*rows_here, first, second, stats, *after)

time: 72.7 us -> 72.7 us (level)
  transfers between devices with their start and end apart: 18 -> 18, of which waited for: 9 -> 9; matrix products, arithmetic and copies ran while one was open for 2% -> 2% of each run, Pallas kernels for 8% -> 7%
where the time goes in v15:
time: 72.7 us; the launch traced here: 72.5 us
  starting transfers between devices  35 us (48%)
  waiting for transfers between devices  24 us (33%)
  Pallas kernels  9.72 us (13%)
  local copies, waits for them, and re-layouts  3.52 us (5%)
    ppermute x18, starting transfers between devices, swap(): return lax.ppermute(array, 'pat', pairs)  35 us
    ppermute x18, waiting for transfers between devices, swap(): return lax.ppermute(array, 'pat', pairs)  24 us
    pallas_call x1, Pallas kernels, pack(): pl.pallas_call(functools.partial(pack_kernel, plan), grid=(plan.places,),...  2.7 us
    unnamed x16, local copies, waits for them, and re-layouts  2.48 us
    pallas_call x1, Pallas kernels, group_moments(): pl.pallas_call(functools.partial(group_moments_kernel, rows, 2), in_specs...  2.36 us
    pallas_call x4, Pallas kernels, small_call(): pl.pallas_call(kernel, in_specs=[vmem] * len(operands) + [pl.BlockSpec(me...  1.95 us
    pallas_call x1, Pallas kernels, finish(): pl.pallas_call(functools.partial(finish_kernel, plan, weightings, [len(pa...  1.61 us
  transfers between devices with their start and end apart: 18, of which 9 were waited for; matrix products, arithmetic and copies ran while one was open for 2% of the time, Pallas kernels for 7%

profile of v15, /device:TPU:1, one launch (start us, length us, event | category | flops | bytes accessed | tf_op | source)
XLA Modules:
  0.0 72.5 jit_solution(2244757420094123192)
XLA Ops:
  0.0 2.4 %copy-done = bf16[128,19968]{1,0:T(8,128)(2,1)S(1)} copy-done((bf16[128,19968]{1,0:T(8,128)(2,1)S(1)}, bf16[128,19968]{1,0:T(8,128)(2,1)}, u32[]{:S(2)}) %copy-start) | copy-done | bytes 5111832
  2.5 2.7 %pack.1 = (bf16[512,640]{1,0:T(8,128)(2,1)S(1)}, bf16[512,640]{1,0:T(8,128)(2,1)S(1)}, bf16[512,640]{1,0:T(8,128)(2,1)}, bf16[512,640]{1,0:T(8,128)(2,1)}, bf16[...) custom-call(bf16[128,19968]{1,0:T(8,128)(2,1)S(1)} %copy-done), custom_call_target="tpu_custom_call" | custom-call | bytes 10223616 | tf_op jit(solution)/shard_map/pack/pallas_call | solution.py:88
  5.8 2.4 %collective-permute-start.9 = (bf16[512,640]{1,0:T(8,128)(2,1)}, bf16[512,640]{1,0:T(8,128)(2,1)}, u32[]{:S(2)}, u32[]{:S(2)}) collective-permute-start(bf16[512,640]{1,0:T(8,128)(2,1)} %get-tuple-element.33), channel_id=1, source_target_pairs={{0,2},{1,5},{2,0},{3,7},{4,6},{5,1},{6,4},{7,3},{8,10},{9,13},{10,... | collective-permute-start | bytes 1966088 | tf_op jit(solution)/shard_map/ppermute | solution.py:393
  8.1 1.2 %collective-permute-done.8.refs_1_ = bf16[2,512,640]{2,1,0:T(8,128)(2,1)S(1)} collective-permute-done((bf16[2,512,640]{2,1,0:T(8,128)(2,1)S(1)}, bf16[2,512,640]{2,1,0:T(8,128)(2,1)S(1)}, u32[]{:S(2)}, u32[]{:S(2)}) %collective-permute-start.8) | collective-permute-done | bytes 1310752 | tf_op jit(solution)/shard_map/ppermute | solution.py:393
  9.4 0.9 %slice_bitcast_fusion = bf16[512,640]{1,0:T(8,128)(2,1)} fusion(bf16[2,512,640]{2,1,0:T(8,128)(2,1)S(1)} %collective-permute-done.8.refs_1_), kind=kLoop, calls=%fused_computation | loop fusion | bytes 1310720 | tf_op jit(solution)/shard_map/squeeze | solution.py:414
  10.3 2.4 %collective-permute-start.10 = (bf16[512,640]{1,0:T(8,128)(2,1)}, bf16[512,640]{1,0:T(8,128)(2,1)}, u32[]{:S(2)}, u32[]{:S(2)}) collective-permute-start(bf16[512,640]{1,0:T(8,128)(2,1)} %slice_bitcast_fusion), channel_id=1, source_target_pairs={{0,2},{1,5},{2,0},{3,7},{4,6},{5,1},{6,4},{7,3},{8,10},{9,13},{10,... | collective-permute-start | bytes 1966088 | tf_op jit(solution)/shard_map/ppermute | solution.py:393
  14.2 1.0 %collective-permute-start.1 = (bf16[2,64,128]{2,1,0:T(8,128)(2,1)S(1)}, bf16[2,64,128]{2,1,0:T(8,128)(2,1)S(1)}, u32[]{:S(2)}, u32[]{:S(2)}) collective-permute-start(bf16[2,64,128]{2,1,0:T(8,128)(2,1)S(1)} %pad_maximum_fusion.near_ref), channel_id=1, source_target_pairs={{3,0},{4,1},{1,2},{6,3},{7,4},{0,5},{5,6},{2,7},{11,8},{12,9},{9,1... | collective-permute-start | bytes 98312 | tf_op jit(solution)/shard_map/ppermute | solution.py:393
  16.1 2.3 %collective-permute-done.1.far_ref = bf16[2,64,128]{2,1,0:T(8,128)(2,1)S(1)} collective-permute-done((bf16[2,64,128]{2,1,0:T(8,128)(2,1)S(1)}, bf16[2,64,128]{2,1,0:T(8,128)(2,1)S(1)}, u32[]{:S(2)}, u32[]{:S(2)}) %collective-permute-start.1) | collective-permute-done | bytes 32800 | tf_op jit(solution)/shard_map/ppermute | solution.py:393
  18.8 1.0 %collective-permute-start.2 = (f32[48,128]{1,0:T(8,128)S(1)}, f32[48,128]{1,0:T(8,128)S(1)}, u32[]{:S(2)}, u32[]{:S(2)}) collective-permute-start(f32[48,128]{1,0:T(8,128)S(1)} %get-tuple-element.24.near_ref), channel_id=1, source_target_pairs={{0,4},{1,3},{2,6},{3,1},{4,0},{5,7},{6,2},{7,5},{8,12},{9,11},{10,... | collective-permute-start | bytes 73736 | tf_op jit(solution)/shard_map/ppermute | solution.py:393
  20.5 1.8 %collective-permute-done.2.far_ref = f32[48,128]{1,0:T(8,128)S(1)} collective-permute-done((f32[48,128]{1,0:T(8,128)S(1)}, f32[48,128]{1,0:T(8,128)S(1)}, u32[]{:S(2)}, u32[]{:S(2)}) %collective-permute-start.2) | collective-permute-done | bytes 24608 | tf_op jit(solution)/shard_map/ppermute | solution.py:393
  23.0 1.3 %collective-permute-done.10.refs_3_ = bf16[512,640]{1,0:T(8,128)(2,1)} collective-permute-done((bf16[512,640]{1,0:T(8,128)(2,1)}, bf16[512,640]{1,0:T(8,128)(2,1)}, u32[]{:S(2)}, u32[]{:S(2)}) %collective-permute-start.10) | collective-permute-done | bytes 655392 | tf_op jit(solution)/shard_map/ppermute | solution.py:393
  24.3 2.4 %group_moments.1 = (f32[1,128,640]{2,1,0:T(8,128)S(1)}, f32[1,128,640]{2,1,0:T(8,128)S(1)}, f32[1,128,640]{2,1,0:T(8,128)S(1)}, f32[1,128,640]{2,1,0:T(8,128)S(1)}) custom-call(bf16[512,640]{1,0:T(8,128)(2,1)S(1)} %copy-done.4, bf16[2,512,640]{2,1,0:T(8,128)(2,1)S(1)} %collective-permute-done.8.refs_1_, bf16[512,640]{1,0:T(8,128)(2,1)} %collective-permute-done.9.refs_2_, ...), custom_call_target="tpu_custom_call" | custom-call | bytes 6291456 | tf_op jit(solution)/shard_map/group_moments/pallas_call | solution.py:312
  26.7 1.5 %collective-permute-start.12 = (f32[1,128,640]{2,1,0:T(8,128)S(1)}, f32[1,128,640]{2,1,0:T(8,128)S(1)}, u32[]{:S(2)}, u32[]{:S(2)}) collective-permute-start(f32[1,128,640]{2,1,0:T(8,128)S(1)} %get-tuple-element.38), channel_id=1, source_target_pairs={{0,4},{1,3},{2,6},{3,1},{4,0},{5,7},{6,2},{7,5},{8,12},{9,11},{10,... | collective-permute-start | bytes 983048 | tf_op jit(solution)/shard_map/ppermute | solution.py:393
  28.3 1.3 %collective-permute-start.4 = (f32[48,128]{1,0:T(8,128)S(1)}, f32[48,128]{1,0:T(8,128)S(1)}, u32[]{:S(2)}, u32[]{:S(2)}) collective-permute-start(f32[48,128]{1,0:T(8,128)S(1)} %add.10.here_ref.refs_5_), channel_id=1, source_target_pairs={{0,1},{2,3},{4,5},{6,7},{8,9},{10,11},{12,13},{14,15},{16,17},{18,... | collective-permute-start | bytes 73736 | tf_op jit(solution)/shard_map/ppermute | solution.py:393
  29.5 6.6 %collective-permute-done.4.told_ref = f32[48,128]{1,0:T(8,128)S(1)} collective-permute-done((f32[48,128]{1,0:T(8,128)S(1)}, f32[48,128]{1,0:T(8,128)S(1)}, u32[]{:S(2)}, u32[]{:S(2)}) %collective-permute-start.4) | collective-permute-done | bytes 24608 | tf_op jit(solution)/shard_map/ppermute | solution.py:393
  37.2 2.5 %collective-permute-start.15 = (f32[1,112,640]{2,1,0:T(8,128)S(1)}, f32[1,112,640]{2,1,0:T(8,128)S(1)}, u32[]{:S(2)}, u32[]{:S(2)}) collective-permute-start(f32[1,112,640]{2,1,0:T(8,128)S(1)} %meet.3.refs_8_), channel_id=1, source_target_pairs={{0,8},{1,9},{2,10},{3,11},{4,12},{5,13},{6,14},{7,15},{8,0},{9,1},... | collective-permute-start | bytes 860168 | tf_op jit(solution)/shard_map/ppermute | solution.py:393
  39.8 3.8 %collective-permute-done.11.right_ref = f32[1,128,640]{2,1,0:T(8,128)S(1)} collective-permute-done((f32[1,128,640]{2,1,0:T(8,128)S(1)}, f32[1,128,640]{2,1,0:T(8,128)S(1)}, u32[]{:S(2)}, u32[]{:S(2)}) %collective-permute-start.11) | collective-permute-done | bytes 327712 | tf_op jit(solution)/shard_map/ppermute | solution.py:393
  44.2 2.5 %collective-permute-start.13 = (f32[1,112,640]{2,1,0:T(8,128)S(1)}, f32[1,112,640]{2,1,0:T(8,128)S(1)}, u32[]{:S(2)}, u32[]{:S(2)}) collective-permute-start(f32[1,112,640]{2,1,0:T(8,128)S(1)} %meet.2.refs_7_), channel_id=1, source_target_pairs={{0,8},{1,9},{2,10},{3,11},{4,12},{5,13},{6,14},{7,15},{8,0},{9,1},... | collective-permute-start | bytes 860168 | tf_op jit(solution)/shard_map/ppermute | solution.py:393
  46.8 1.1 %moments.1 = (f32[112,640]{1,0:T(8,128)S(1)}, f32[112,640]{1,0:T(8,128)S(1)}, f32[112,640]{1,0:T(8,128)S(1)}, f32[112,640]{1,0:T(8,128)S(1)}) custom-call(bf16[512,640]{1,0:T(8,128)(2,1)S(1)} %copy-done.2, bf16[2,512,640]{2,1,0:T(8,128)(2,1)S(1)} %collective-permute-done.5.refs_1_, bf16[512,640]{1,0:T(8,128)(2,1)S(1)} %collective-permute-done.6.refs_0_.refs_2_, ...), custom_call_target="tpu_custom_call" | custom-call | bytes 6291456 | tf_op jit(solution)/shard_map/moments/pallas_call | solution.py:332
  47.9 1.3 %collective-permute-start.14 = (f32[112,640]{1,0:T(8,128)S(1)}, f32[112,640]{1,0:T(8,128)S(1)}, u32[]{:S(2)}, u32[]{:S(2)}) collective-permute-start(f32[112,640]{1,0:T(8,128)S(1)} %get-tuple-element.40), channel_id=1, source_target_pairs={{0,4},{1,3},{2,6},{3,1},{4,0},{5,7},{6,2},{7,5},{8,12},{9,11},{10,... | collective-permute-start | bytes 860168 | tf_op jit(solution)/shard_map/ppermute | solution.py:393
  49.2 7.5 %collective-permute-start.17 = (f32[112,640]{1,0:T(8,128)S(1)}, f32[112,640]{1,0:T(8,128)S(1)}, u32[]{:S(2)}, u32[]{:S(2)}) collective-permute-start(f32[112,640]{1,0:T(8,128)S(1)} %get-tuple-element.42), channel_id=1, source_target_pairs={{0,5},{1,2},{2,7},{3,0},{4,1},{5,6},{6,3},{7,4},{8,13},{9,10},{10,... | collective-permute-start | bytes 860168 | tf_op jit(solution)/shard_map/ppermute | solution.py:393
  56.7 8.3 %collective-permute-start.16 = (f32[112,640]{1,0:T(8,128)S(1)}, f32[112,640]{1,0:T(8,128)S(1)}, u32[]{:S(2)}, u32[]{:S(2)}) collective-permute-start(f32[112,640]{1,0:T(8,128)S(1)} %bitcast_add_fusion), channel_id=1, source_target_pairs={{0,1},{1,0},{2,3},{3,2},{4,5},{5,4},{6,7},{7,6},{8,9},{9,8},{10,11... | collective-permute-start | bytes 860168 | tf_op jit(solution)/shard_map/ppermute | solution.py:393
  65.0 5.9 %collective-permute-done.17.refs_4_ = f32[112,640]{1,0:T(8,128)S(1)} collective-permute-done((f32[112,640]{1,0:T(8,128)S(1)}, f32[112,640]{1,0:T(8,128)S(1)}, u32[]{:S(2)}, u32[]{:S(2)}) %collective-permute-start.17) | collective-permute-done | bytes 286752 | tf_op jit(solution)/shard_map/ppermute | solution.py:393
  70.9 1.6 %finish.1 = f32[48,1,1248]{2,1,0:T(1,128)} custom-call(s32[48,1]{1,0:T(8,128)S(1)} %copy.9.pick_ref, f32[3,48,128]{2,1,0:T(8,128)S(1)} %get-tuple-element.25.stats_ref.refs_6_, f32[112,640]{1,0:T(8,128)S(1)} %get-tuple-element.39.refs_0_, f32[112,640]{1,0:T(8,128)S(1)} %bitcast.14, f32[112,640]{1,0:T(8,128)S(1)} %collective-permute-done.14.refs_2_, ...), custom_call_target="tpu_custom_call" | custom-call | bytes 16384 | tf_op jit(solution)/shard_map/finish/pallas_call | solution.py:380
  (45 shorter events, 6.5 us)
Async XLA Ops:
  5.1 10.8 %copy-start.1 = (bf16[512,640]{1,0:T(8,128)(2,1)}, bf16[512,640]{1,0:T(8,128)(2,1)S(1)}, u32[]{:S(2)}) copy-start(bf16[512,640]{1,0:T(8,128)(2,1)S(1)} %get-tuple-element.26.refs_0_) | copy-start | bytes 1966084
  5.2 10.8 %copy-start.3 = (bf16[512,640]{1,0:T(8,128)(2,1)}, bf16[512,640]{1,0:T(8,128)(2,1)S(1)}, u32[]{:S(2)}) copy-start(bf16[512,640]{1,0:T(8,128)(2,1)S(1)} %get-tuple-element.31.refs_0_) | copy-start | bytes 1966084
  5.2 7.5 %copy-start.6 = (bf16[128,16]{0,1:T(8,128)(2,1)S(1)}, bf16[128,16]{0,1:T(8,128)(2,1)}, u32[]{:S(2)}) copy-start(bf16[128,16]{0,1:T(8,128)(2,1)} %param.5) | copy-start | bytes 12292
  5.2 10.8 %copy-start.7 = (s32[48]{0:T(128)S(1)}, s32[48]{0:T(128)}, u32[]{:S(2)}) copy-start(s32[48]{0:T(128)} %param.7) | copy-start | bytes 580
  5.2 4.2 %collective-permute-start.8 = (bf16[2,512,640]{2,1,0:T(8,128)(2,1)S(1)}, bf16[2,512,640]{2,1,0:T(8,128)(2,1)S(1)}, u32[]{:S(2)}, u32[]{:S(2)}) collective-permute-start(bf16[2,512,640]{2,1,0:T(8,128)(2,1)S(1)} %get-tuple-element.32), channel_id=1, source_target_pairs={{0,1},{1,0},{2,3},{3,2},{4,5},{5,4},{6,7},{7,6},{8,9},{9,8},{10,11... | collective-permute-start | bytes 3932168 | tf_op jit(solution)/shard_map/ppermute | solution.py:393
  5.3 14.6 %collective-permute-start.5 = (bf16[2,512,640]{2,1,0:T(8,128)(2,1)}, bf16[2,512,640]{2,1,0:T(8,128)(2,1)S(1)}, u32[]{:S(2)}, u32[]{:S(2)}) collective-permute-start(bf16[2,512,640]{2,1,0:T(8,128)(2,1)} %get-tuple-element.27), channel_id=1, source_target_pairs={{0,1},{1,0},{2,3},{3,2},{4,5},{5,4},{6,7},{7,6},{8,9},{9,8},{10,11... | collective-permute-start | bytes 3932168 | tf_op jit(solution)/shard_map/ppermute | solution.py:393
  5.8 17.2 %collective-permute-start.9 = (bf16[512,640]{1,0:T(8,128)(2,1)}, bf16[512,640]{1,0:T(8,128)(2,1)}, u32[]{:S(2)}, u32[]{:S(2)}) collective-permute-start(bf16[512,640]{1,0:T(8,128)(2,1)} %get-tuple-element.33), channel_id=1, source_target_pairs={{0,2},{1,5},{2,0},{3,7},{4,6},{5,1},{6,4},{7,3},{8,10},{9,13},{10,... | collective-permute-start | bytes 1966088 | tf_op jit(solution)/shard_map/ppermute | solution.py:393
  10.3 14.1 %collective-permute-start.10 = (bf16[512,640]{1,0:T(8,128)(2,1)}, bf16[512,640]{1,0:T(8,128)(2,1)}, u32[]{:S(2)}, u32[]{:S(2)}) collective-permute-start(bf16[512,640]{1,0:T(8,128)(2,1)} %slice_bitcast_fusion), channel_id=1, source_target_pairs={{0,2},{1,5},{2,0},{3,7},{4,6},{5,1},{6,4},{7,3},{8,10},{9,13},{10,... | collective-permute-start | bytes 1966088 | tf_op jit(solution)/shard_map/ppermute | solution.py:393
  12.7 1.5 %collective-permute-start = (bf16[64,128]{1,0:T(8,128)(2,1)S(1)}, bf16[64,128]{1,0:T(8,128)(2,1)S(1)}, u32[]{:S(2)}, u32[]{:S(2)}) collective-permute-start(bf16[64,128]{1,0:T(8,128)(2,1)S(1)} %get-tuple-element.44), channel_id=1, source_target_pairs={{0,1},{1,0},{2,3},{3,2},{4,5},{5,4},{6,7},{7,6},{8,9},{9,8},{10,11... | collective-permute-start | bytes 49160 | tf_op jit(solution)/shard_map/ppermute | solution.py:393
  14.2 4.2 %collective-permute-start.1 = (bf16[2,64,128]{2,1,0:T(8,128)(2,1)S(1)}, bf16[2,64,128]{2,1,0:T(8,128)(2,1)S(1)}, u32[]{:S(2)}, u32[]{:S(2)}) collective-permute-start(bf16[2,64,128]{2,1,0:T(8,128)(2,1)S(1)} %pad_maximum_fusion.near_ref), channel_id=1, source_target_pairs={{3,0},{4,1},{1,2},{6,3},{7,4},{0,5},{5,6},{2,7},{11,8},{12,9},{9,1... | collective-permute-start | bytes 98312 | tf_op jit(solution)/shard_map/ppermute | solution.py:393
  15.3 24.5 %collective-permute-start.6 = (bf16[512,640]{1,0:T(8,128)(2,1)}, bf16[512,640]{1,0:T(8,128)(2,1)S(1)}, u32[]{:S(2)}, u32[]{:S(2)}) collective-permute-start(bf16[512,640]{1,0:T(8,128)(2,1)} %get-tuple-element.28), channel_id=1, source_target_pairs={{0,2},{1,5},{2,0},{3,7},{4,6},{5,1},{6,4},{7,3},{8,10},{9,13},{10,... | collective-permute-start | bytes 1966088 | tf_op jit(solution)/shard_map/ppermute | solution.py:393
  16.1 8.3 %copy-start.4 = (bf16[512,640]{1,0:T(8,128)(2,1)S(1)}, bf16[512,640]{1,0:T(8,128)(2,1)}, u32[]{:S(2)}) copy-start(bf16[512,640]{1,0:T(8,128)(2,1)} %copy-done.3) | copy-start | bytes 1966084
  18.8 3.5 %collective-permute-start.2 = (f32[48,128]{1,0:T(8,128)S(1)}, f32[48,128]{1,0:T(8,128)S(1)}, u32[]{:S(2)}, u32[]{:S(2)}) collective-permute-start(f32[48,128]{1,0:T(8,128)S(1)} %get-tuple-element.24.near_ref), channel_id=1, source_target_pairs={{0,4},{1,3},{2,6},{3,1},{4,0},{5,7},{6,2},{7,5},{8,12},{9,11},{10,... | collective-permute-start | bytes 73736 | tf_op jit(solution)/shard_map/ppermute | solution.py:393
  19.9 26.8 %collective-permute-start.7 = (bf16[512,640]{1,0:T(8,128)(2,1)S(1)}, bf16[512,640]{1,0:T(8,128)(2,1)S(1)}, u32[]{:S(2)}, u32[]{:S(2)}) collective-permute-start(bf16[512,640]{1,0:T(8,128)(2,1)S(1)} %slice_bitcast_fusion.1), channel_id=1, source_target_pairs={{0,2},{1,5},{2,0},{3,7},{4,6},{5,1},{6,4},{7,3},{8,10},{9,13},{10,... | collective-permute-start | bytes 1966088 | tf_op jit(solution)/shard_map/ppermute | solution.py:393
  22.3 0.7 collective-permute-start.3
  26.7 9.9 %collective-permute-start.12 = (f32[1,128,640]{2,1,0:T(8,128)S(1)}, f32[1,128,640]{2,1,0:T(8,128)S(1)}, u32[]{:S(2)}, u32[]{:S(2)}) collective-permute-start(f32[1,128,640]{2,1,0:T(8,128)S(1)} %get-tuple-element.38), channel_id=1, source_target_pairs={{0,4},{1,3},{2,6},{3,1},{4,0},{5,7},{6,2},{7,5},{8,12},{9,11},{10,... | collective-permute-start | bytes 983048 | tf_op jit(solution)/shard_map/ppermute | solution.py:393
  28.2 15.4 %collective-permute-start.11 = (f32[1,128,640]{2,1,0:T(8,128)S(1)}, f32[1,128,640]{2,1,0:T(8,128)S(1)}, u32[]{:S(2)}, u32[]{:S(2)}) collective-permute-start(f32[1,128,640]{2,1,0:T(8,128)S(1)} %get-tuple-element.36), channel_id=1, source_target_pairs={{0,4},{1,3},{2,6},{3,1},{4,0},{5,7},{6,2},{7,5},{8,12},{9,11},{10,... | collective-permute-start | bytes 983048 | tf_op jit(solution)/shard_map/ppermute | solution.py:393
  28.3 7.9 %collective-permute-start.4 = (f32[48,128]{1,0:T(8,128)S(1)}, f32[48,128]{1,0:T(8,128)S(1)}, u32[]{:S(2)}, u32[]{:S(2)}) collective-permute-start(f32[48,128]{1,0:T(8,128)S(1)} %add.10.here_ref.refs_5_), channel_id=1, source_target_pairs={{0,1},{2,3},{4,5},{6,7},{8,9},{10,11},{12,13},{14,15},{16,17},{18,... | collective-permute-start | bytes 73736 | tf_op jit(solution)/shard_map/ppermute | solution.py:393
  36.6 10.2 %copy-start.2 = (bf16[512,640]{1,0:T(8,128)(2,1)S(1)}, bf16[512,640]{1,0:T(8,128)(2,1)}, u32[]{:S(2)}) copy-start(bf16[512,640]{1,0:T(8,128)(2,1)} %copy-done.1) | copy-start | bytes 1966084
  37.2 19.4 %collective-permute-start.15 = (f32[1,112,640]{2,1,0:T(8,128)S(1)}, f32[1,112,640]{2,1,0:T(8,128)S(1)}, u32[]{:S(2)}, u32[]{:S(2)}) collective-permute-start(f32[1,112,640]{2,1,0:T(8,128)S(1)} %meet.3.refs_8_), channel_id=1, source_target_pairs={{0,8},{1,9},{2,10},{3,11},{4,12},{5,13},{6,14},{7,15},{8,0},{9,1},... | collective-permute-start | bytes 860168 | tf_op jit(solution)/shard_map/ppermute | solution.py:393
  44.2 26.6 %collective-permute-start.13 = (f32[1,112,640]{2,1,0:T(8,128)S(1)}, f32[1,112,640]{2,1,0:T(8,128)S(1)}, u32[]{:S(2)}, u32[]{:S(2)}) collective-permute-start(f32[1,112,640]{2,1,0:T(8,128)S(1)} %meet.2.refs_7_), channel_id=1, source_target_pairs={{0,8},{1,9},{2,10},{3,11},{4,12},{5,13},{6,14},{7,15},{8,0},{9,1},... | collective-permute-start | bytes 860168 | tf_op jit(solution)/shard_map/ppermute | solution.py:393
  47.9 17.1 %collective-permute-start.14 = (f32[112,640]{1,0:T(8,128)S(1)}, f32[112,640]{1,0:T(8,128)S(1)}, u32[]{:S(2)}, u32[]{:S(2)}) collective-permute-start(f32[112,640]{1,0:T(8,128)S(1)} %get-tuple-element.40), channel_id=1, source_target_pairs={{0,4},{1,3},{2,6},{3,1},{4,0},{5,7},{6,2},{7,5},{8,12},{9,11},{10,... | collective-permute-start | bytes 860168 | tf_op jit(solution)/shard_map/ppermute | solution.py:393
  49.2 21.7 %collective-permute-start.17 = (f32[112,640]{1,0:T(8,128)S(1)}, f32[112,640]{1,0:T(8,128)S(1)}, u32[]{:S(2)}, u32[]{:S(2)}) collective-permute-start(f32[112,640]{1,0:T(8,128)S(1)} %get-tuple-element.42), channel_id=1, source_target_pairs={{0,5},{1,2},{2,7},{3,0},{4,1},{5,6},{6,3},{7,4},{8,13},{9,10},{10,... | collective-permute-start | bytes 860168 | tf_op jit(solution)/shard_map/ppermute | solution.py:393
  56.7 14.2 %collective-permute-start.16 = (f32[112,640]{1,0:T(8,128)S(1)}, f32[112,640]{1,0:T(8,128)S(1)}, u32[]{:S(2)}, u32[]{:S(2)}) collective-permute-start(f32[112,640]{1,0:T(8,128)S(1)} %bitcast_add_fusion), channel_id=1, source_target_pairs={{0,1},{1,0},{2,3},{3,2},{4,5},{5,4},{6,7},{7,6},{8,9},{9,8},{10,11... | collective-permute-start | bytes 860168 | tf_op jit(solution)/shard_map/ppermute | solution.py:393
  (2 other events, 10.0 us)

commit v16 on v15

--- a/solution.py
+++ b/solution.py
@@ -35,7 +35,7 @@
 
 
 def pack_kernel(
-    plan, x_ref, kept0_ref, kept1_ref, sent0_ref, sent1_ref, other0_ref, other1_ref
+    plan, x_ref, kept0_ref, kept1_ref, sent0_ref, sent1_ref, other0_ref, stay1_ref, pass1_ref
 ):
     step = pl.program_id(0)
     me = lax.axis_index("pat")
@@ -66,7 +66,7 @@
                 tail = x_ref[:, tile(first + plan.tiles)]
                 folded = jnp.where(lane >= edge, head.astype(jnp.float32), tail.astype(jnp.float32))
                 if away:
-                    target = (other0_ref, other1_ref)[chunk].at[sent]
+                    target = (stay1_ref, pass1_ref)[sent] if chunk else other0_ref.at[sent]
                 elif sent:
                     target = (sent0_ref, sent1_ref)[chunk]
                 else:
@@ -89,8 +89,8 @@
         functools.partial(pack_kernel, plan),
         grid=(plan.places,),
         in_specs=[pl.BlockSpec(memory_space=pltpu.VMEM)],
-        out_specs=[mine_spec] * 4 + [other_spec] * 2,
-        out_shape=[mine] * 4 + [other] * 2,
+        out_specs=[mine_spec] * 4 + [other_spec] + [mine_spec] * 2,
+        out_shape=[mine] * 4 + [other] + [mine] * 2,
         compiler_params=pltpu.CompilerParams(vmem_limit_bytes=12 << 20),
         cost_estimate=pl.CostEstimate(
             flops=0, bytes_accessed=4 * covariates.size, transcendentals=0
@@ -406,13 +406,20 @@
     near = jnp.stack([mine, swap(mine, to_other_side)])
     far = swap(near, [(pair ^ 1, d) for d, pair in plan.by_rows()])
 
-    kept0, kept1, sent0, sent1, other0, other1 = pack(covariates, plan)
-    rows_here = {}
-    for chunk, kept, sent, other in ((1, kept1, sent1, other1), (0, kept0, sent0, other0)):
-        passed = swap(other, to_other_side)
-        rows_here[chunk] = [
-            kept, passed, swap(sent, plan.by_rows()), swap(passed[1], plan.by_rows())
+    kept0, kept1, sent0, sent1, other0, stay1, pass1 = pack(covariates, plan)
+    forward = swap(pass1, to_other_side)
+    rows_here = {
+        1: [
+            kept1,
+            swap(stay1[None], to_other_side),
+            swap(sent1, plan.by_rows()),
+            swap(forward, plan.by_rows()),
         ]
+    }
+    passed = swap(other0, to_other_side)
+    rows_here[0] = [
+        kept0, passed, swap(sent0, plan.by_rows()), swap(passed[1], plan.by_rows())
+    ]
 
     near_totals, panel = make_group(near, far, pick_column, weightings)
     far_totals = swap(near_totals, plan.by_sums())

time: 72.7 us -> 76.9 us (1.058)
  waiting for transfers between devices: 24 us -> 26.1 us
  starting transfers between devices: 35 us -> 37 us
    ppermute x18 -> x19, waiting for transfers between devices: 24 us -> 26.1 us  [swap(): return lax.ppermute(array, 'pat', pairs)]
    ppermute x18 -> x19, starting transfers between devices: 35 us -> 37 us  [swap(): return lax.ppermute(array, 'pat', pairs)]
    squeeze x2 -> x1, local copies, waits for them, and re-layouts: 0.95 us -> 0.06 us  [on_device(): passed[1]]
    unnamed x16 -> x10, local copies, waits for them, and re-layouts: 2.48 us -> 3.32 us
  transfers between devices with their start and end apart: 18 -> 19, of which waited for: 9 -> 9; matrix products, arithmetic and copies ran while one was open for 2% -> 0% of each run, Pallas kernels for 7% -> 7%
where the time goes in v16:
time: 76.9 us; the launch traced here: 76.6 us
  starting transfers between devices  37 us (48%)
  waiting for transfers between devices  26.1 us (34%)
  Pallas kernels  9.93 us (13%)
  local copies, waits for them, and re-layouts  3.47 us (5%)
    ppermute x19, starting transfers between devices, swap(): return lax.ppermute(array, 'pat', pairs)  37 us
    ppermute x19, waiting for transfers between devices, swap(): return lax.ppermute(array, 'pat', pairs)  26.1 us
    unnamed x10, local copies, waits for them, and re-layouts  3.32 us
    pallas_call x1, Pallas kernels, pack(): pl.pallas_call(functools.partial(pack_kernel, plan), grid=(plan.places,),...  2.8 us
    pallas_call x1, Pallas kernels, group_moments(): pl.pallas_call(functools.partial(group_moments_kernel, rows, 2), in_specs...  2.38 us
    pallas_call x4, Pallas kernels, small_call(): pl.pallas_call(kernel, in_specs=[vmem] * len(operands) + [pl.BlockSpec(me...  1.95 us
    pallas_call x1, Pallas kernels, finish(): pl.pallas_call(functools.partial(finish_kernel, plan, weightings, [len(pa...  1.62 us
  transfers between devices with their start and end apart: 19, of which 9 were waited for; matrix products, arithmetic and copies ran while one was open for 0% of the time, Pallas kernels for 7%

profile of v16, /device:TPU:1, one launch (start us, length us, event | category | flops | bytes accessed | tf_op | source)
XLA Modules:
  0.0 76.6 jit_solution(1322638964518116250)
XLA Ops:
  0.0 2.4 %copy-done = bf16[128,19968]{1,0:T(8,128)(2,1)S(1)} copy-done((bf16[128,19968]{1,0:T(8,128)(2,1)S(1)}, bf16[128,19968]{1,0:T(8,128)(2,1)}, u32[]{:S(2)}) %copy-start) | copy-done | bytes 5111832
  2.5 2.8 %pack.1 = (bf16[512,640]{1,0:T(8,128)(2,1)S(1)}, bf16[512,640]{1,0:T(8,128)(2,1)S(1)}, bf16[512,640]{1,0:T(8,128)(2,1)S(1)}, bf16[512,640]{1,0:T(8,128)(2,1)}, b...) custom-call(bf16[128,19968]{1,0:T(8,128)(2,1)S(1)} %copy-done), custom_call_target="tpu_custom_call" | custom-call | bytes 10223616 | tf_op jit(solution)/shard_map/pack/pallas_call | solution.py:88
  5.3 0.9 %copy-done.1 = bf16[512,640]{1,0:T(8,128)(2,1)} copy-done((bf16[512,640]{1,0:T(8,128)(2,1)}, bf16[512,640]{1,0:T(8,128)(2,1)S(1)}, u32[]{:S(2)}) %copy-start.1) | copy-done | bytes 655384
  6.7 2.7 %collective-permute-start.9 = (bf16[512,640]{1,0:T(8,128)(2,1)}, bf16[512,640]{1,0:T(8,128)(2,1)}, u32[]{:S(2)}, u32[]{:S(2)}) collective-permute-start(bf16[512,640]{1,0:T(8,128)(2,1)} %get-tuple-element.34), channel_id=1, source_target_pairs={{0,2},{1,5},{2,0},{3,7},{4,6},{5,1},{6,4},{7,3},{8,10},{9,13},{10,... | collective-permute-start | bytes 1966088 | tf_op jit(solution)/shard_map/ppermute | solution.py:393
  9.4 1.4 %collective-permute-done.10 = bf16[512,640]{1,0:T(8,128)(2,1)} collective-permute-done((bf16[512,640]{1,0:T(8,128)(2,1)S(1)}, bf16[512,640]{1,0:T(8,128)(2,1)}, u32[]{:S(2)}, u32[]{:S(2)}) %collective-permute-start.10) | collective-permute-done | bytes 655392 | tf_op jit(solution)/shard_map/ppermute | solution.py:393
  10.8 2.6 %collective-permute-start.11 = (bf16[512,640]{1,0:T(8,128)(2,1)}, bf16[512,640]{1,0:T(8,128)(2,1)}, u32[]{:S(2)}, u32[]{:S(2)}) collective-permute-start(bf16[512,640]{1,0:T(8,128)(2,1)} %collective-permute-done.10), channel_id=1, source_target_pairs={{0,2},{1,5},{2,0},{3,7},{4,6},{5,1},{6,4},{7,3},{8,10},{9,13},{10,... | collective-permute-start | bytes 1966088 | tf_op jit(solution)/shard_map/ppermute | solution.py:393
  14.7 1.3 %collective-permute-start.1 = (bf16[2,64,128]{2,1,0:T(8,128)(2,1)S(1)}, bf16[2,64,128]{2,1,0:T(8,128)(2,1)S(1)}, u32[]{:S(2)}, u32[]{:S(2)}) collective-permute-start(bf16[2,64,128]{2,1,0:T(8,128)(2,1)S(1)} %pad_maximum_fusion.near_ref), channel_id=1, source_target_pairs={{3,0},{4,1},{1,2},{6,3},{7,4},{0,5},{5,6},{2,7},{11,8},{12,9},{9,1... | collective-permute-start | bytes 98312 | tf_op jit(solution)/shard_map/ppermute | solution.py:393
  16.1 2.8 %collective-permute-done.1.far_ref = bf16[2,64,128]{2,1,0:T(8,128)(2,1)S(1)} collective-permute-done((bf16[2,64,128]{2,1,0:T(8,128)(2,1)S(1)}, bf16[2,64,128]{2,1,0:T(8,128)(2,1)S(1)}, u32[]{:S(2)}, u32[]{:S(2)}) %collective-permute-start.1) | collective-permute-done | bytes 32800 | tf_op jit(solution)/shard_map/ppermute | solution.py:393
  19.4 1.3 %collective-permute-start.2 = (f32[48,128]{1,0:T(8,128)S(1)}, f32[48,128]{1,0:T(8,128)S(1)}, u32[]{:S(2)}, u32[]{:S(2)}) collective-permute-start(f32[48,128]{1,0:T(8,128)S(1)} %get-tuple-element.25.near_ref), channel_id=1, source_target_pairs={{0,4},{1,3},{2,6},{3,1},{4,0},{5,7},{6,2},{7,5},{8,12},{9,11},{10,... | collective-permute-start | bytes 73736 | tf_op jit(solution)/shard_map/ppermute | solution.py:393
  20.6 2.2 %collective-permute-done.2.far_ref = f32[48,128]{1,0:T(8,128)S(1)} collective-permute-done((f32[48,128]{1,0:T(8,128)S(1)}, f32[48,128]{1,0:T(8,128)S(1)}, u32[]{:S(2)}, u32[]{:S(2)}) %collective-permute-start.2) | collective-permute-done | bytes 24608 | tf_op jit(solution)/shard_map/ppermute | solution.py:393
  22.8 1.3 %collective-permute-start.6 = (bf16[512,640]{1,0:T(8,128)(2,1)}, bf16[512,640]{1,0:T(8,128)(2,1)S(1)}, u32[]{:S(2)}, u32[]{:S(2)}) collective-permute-start(bf16[512,640]{1,0:T(8,128)(2,1)} %copy-done.1), channel_id=1, source_target_pairs={{0,2},{1,5},{2,0},{3,7},{4,6},{5,1},{6,4},{7,3},{8,10},{9,13},{10,... | collective-permute-start | bytes 1966088 | tf_op jit(solution)/shard_map/ppermute | solution.py:393
  25.6 2.4 %group_moments.1 = (f32[1,128,640]{2,1,0:T(8,128)S(1)}, f32[1,128,640]{2,1,0:T(8,128)S(1)}, f32[1,128,640]{2,1,0:T(8,128)S(1)}, f32[1,128,640]{2,1,0:T(8,128)S(1)}) custom-call(bf16[512,640]{1,0:T(8,128)(2,1)S(1)} %get-tuple-element.32.refs_0_, bf16[1,512,640]{2,1,0:T(8,128)(2,1)S(1)} %collective-permute-done.8.refs_1_, ...), custom_call_target="tpu_custom_call" | custom-call | bytes 6291456 | tf_op jit(solution)/shard_map/group_moments/pallas_call | solution.py:312
  28.0 1.5 %collective-permute-start.13 = (f32[1,128,640]{2,1,0:T(8,128)S(1)}, f32[1,128,640]{2,1,0:T(8,128)S(1)}, u32[]{:S(2)}, u32[]{:S(2)}) collective-permute-start(f32[1,128,640]{2,1,0:T(8,128)S(1)} %get-tuple-element.40), channel_id=1, source_target_pairs={{0,4},{1,3},{2,6},{3,1},{4,0},{5,7},{6,2},{7,5},{8,12},{9,11},{10,... | collective-permute-start | bytes 983048 | tf_op jit(solution)/shard_map/ppermute | solution.py:393
  29.6 1.3 %collective-permute-start.4 = (f32[48,128]{1,0:T(8,128)S(1)}, f32[48,128]{1,0:T(8,128)S(1)}, u32[]{:S(2)}, u32[]{:S(2)}) collective-permute-start(f32[48,128]{1,0:T(8,128)S(1)} %add.10.here_ref.refs_5_), channel_id=1, source_target_pairs={{0,1},{2,3},{4,5},{6,7},{8,9},{10,11},{12,13},{14,15},{16,17},{18,... | collective-permute-start | bytes 73736 | tf_op jit(solution)/shard_map/ppermute | solution.py:393
  30.9 7.9 %collective-permute-done.4.told_ref = f32[48,128]{1,0:T(8,128)S(1)} collective-permute-done((f32[48,128]{1,0:T(8,128)S(1)}, f32[48,128]{1,0:T(8,128)S(1)}, u32[]{:S(2)}, u32[]{:S(2)}) %collective-permute-start.4) | collective-permute-done | bytes 24608 | tf_op jit(solution)/shard_map/ppermute | solution.py:393
  39.6 2.6 %collective-permute-start.16 = (f32[1,112,640]{2,1,0:T(8,128)S(1)}, f32[1,112,640]{2,1,0:T(8,128)S(1)}, u32[]{:S(2)}, u32[]{:S(2)}) collective-permute-start(f32[1,112,640]{2,1,0:T(8,128)S(1)} %meet.3.refs_8_), channel_id=1, source_target_pairs={{0,8},{1,9},{2,10},{3,11},{4,12},{5,13},{6,14},{7,15},{8,0},{9,1},... | collective-permute-start | bytes 860168 | tf_op jit(solution)/shard_map/ppermute | solution.py:393
  42.2 2.7 %collective-permute-done.12.right_ref = f32[1,128,640]{2,1,0:T(8,128)S(1)} collective-permute-done((f32[1,128,640]{2,1,0:T(8,128)S(1)}, f32[1,128,640]{2,1,0:T(8,128)S(1)}, u32[]{:S(2)}, u32[]{:S(2)}) %collective-permute-start.12) | collective-permute-done | bytes 327712 | tf_op jit(solution)/shard_map/ppermute | solution.py:393
  45.6 2.5 %collective-permute-start.14 = (f32[1,112,640]{2,1,0:T(8,128)S(1)}, f32[1,112,640]{2,1,0:T(8,128)S(1)}, u32[]{:S(2)}, u32[]{:S(2)}) collective-permute-start(f32[1,112,640]{2,1,0:T(8,128)S(1)} %meet.2.refs_7_), channel_id=1, source_target_pairs={{0,8},{1,9},{2,10},{3,11},{4,12},{5,13},{6,14},{7,15},{8,0},{9,1},... | collective-permute-start | bytes 860168 | tf_op jit(solution)/shard_map/ppermute | solution.py:393
  48.1 1.2 %moments.1 = (f32[112,640]{1,0:T(8,128)S(1)}, f32[112,640]{1,0:T(8,128)S(1)}, f32[112,640]{1,0:T(8,128)S(1)}, f32[112,640]{1,0:T(8,128)S(1)}) custom-call(bf16[512,640]{1,0:T(8,128)(2,1)S(1)} %get-tuple-element.27.refs_0_, bf16[2,512,640]{2,1,0:T(8,128)(2,1)S(1)} %collective-permute-done.5.refs_1_, ...), custom_call_target="tpu_custom_call" | custom-call | bytes 6291456 | tf_op jit(solution)/shard_map/moments/pallas_call | solution.py:332
  49.3 16.6 %collective-permute-start.17 = (f32[112,640]{1,0:T(8,128)S(1)}, f32[112,640]{1,0:T(8,128)S(1)}, u32[]{:S(2)}, u32[]{:S(2)}) collective-permute-start(f32[112,640]{1,0:T(8,128)S(1)} %bitcast_add_fusion), channel_id=1, source_target_pairs={{0,1},{1,0},{2,3},{3,2},{4,5},{5,4},{6,7},{7,6},{8,9},{9,8},{10,11... | collective-permute-start | bytes 860168 | tf_op jit(solution)/shard_map/ppermute | solution.py:393
  65.9 1.0 %collective-permute-start.15 = (f32[112,640]{1,0:T(8,128)S(1)}, f32[112,640]{1,0:T(8,128)S(1)}, u32[]{:S(2)}, u32[]{:S(2)}) collective-permute-start(f32[112,640]{1,0:T(8,128)S(1)} %get-tuple-element.42), channel_id=1, source_target_pairs={{0,4},{1,3},{2,6},{3,1},{4,0},{5,7},{6,2},{7,5},{8,12},{9,11},{10,... | collective-permute-start | bytes 860168 | tf_op jit(solution)/shard_map/ppermute | solution.py:393
  67.3 4.4 %collective-permute-done.15.refs_2_ = f32[112,640]{1,0:T(8,128)S(1)} collective-permute-done((f32[112,640]{1,0:T(8,128)S(1)}, f32[112,640]{1,0:T(8,128)S(1)}, u32[]{:S(2)}, u32[]{:S(2)}) %collective-permute-start.15) | collective-permute-done | bytes 286752 | tf_op jit(solution)/shard_map/ppermute | solution.py:393
  71.7 3.3 %collective-permute-done.18.refs_4_ = f32[112,640]{1,0:T(8,128)S(1)} collective-permute-done((f32[112,640]{1,0:T(8,128)S(1)}, f32[112,640]{1,0:T(8,128)S(1)}, u32[]{:S(2)}, u32[]{:S(2)}) %collective-permute-start.18) | collective-permute-done | bytes 286752 | tf_op jit(solution)/shard_map/ppermute | solution.py:393
  75.0 1.6 %finish.1 = f32[48,1,1248]{2,1,0:T(1,128)} custom-call(s32[48,1]{1,0:T(8,128)S(1)} %copy.9.pick_ref, f32[3,48,128]{2,1,0:T(8,128)S(1)} %get-tuple-element.26.stats_ref.refs_6_, f32[112,640]{1,0:T(8,128)S(1)} %get-tuple-element.41.refs_0_, f32[112,640]{1,0:T(8,128)S(1)} %bitcast.13, f32[112,640]{1,0:T(8,128)S(1)} %collective-permute-done.15.refs_2_, ...), custom_call_target="tpu_custom_call" | custom-call | bytes 16384 | tf_op jit(solution)/shard_map/finish/pallas_call | solution.py:380
  (40 shorter events, 5.9 us)
Async XLA Ops:
  0.0 2.4 %copy-start = (bf16[128,19968]{1,0:T(8,128)(2,1)S(1)}, bf16[128,19968]{1,0:T(8,128)(2,1)}, u32[]{:S(2)}) copy-start(bf16[128,19968]{1,0:T(8,128)(2,1)} %x_ref.1) | copy-start | bytes 15335428
  2.5 11.0 %copy-start.2 = (s32[128,48]{0,1:T(8,128)S(1)}, s32[128,48]{0,1:T(8,128)}, u32[]{:S(2)}) copy-start(s32[128,48]{0,1:T(8,128)} %param.6) | copy-start | bytes 73732
  2.5 11.0 %copy-start.3 = (bf16[128,16]{0,1:T(8,128)(2,1)S(1)}, bf16[128,16]{0,1:T(8,128)(2,1)}, u32[]{:S(2)}) copy-start(bf16[128,16]{0,1:T(8,128)(2,1)} %param.5) | copy-start | bytes 12292
  2.5 13.6 %copy-start.4 = (s32[48]{0:T(128)S(1)}, s32[48]{0:T(128)}, u32[]{:S(2)}) copy-start(s32[48]{0:T(128)} %param.7) | copy-start | bytes 580
  5.3 0.9 %copy-start.1 = (bf16[512,640]{1,0:T(8,128)(2,1)}, bf16[512,640]{1,0:T(8,128)(2,1)S(1)}, u32[]{:S(2)}) copy-start(bf16[512,640]{1,0:T(8,128)(2,1)S(1)} %get-tuple-element.29) | copy-start | bytes 1966084
  6.1 18.0 %collective-permute-start.5 = (bf16[2,512,640]{2,1,0:T(8,128)(2,1)}, bf16[2,512,640]{2,1,0:T(8,128)(2,1)S(1)}, u32[]{:S(2)}, u32[]{:S(2)}) collective-permute-start(bf16[2,512,640]{2,1,0:T(8,128)(2,1)} %get-tuple-element.28), channel_id=1, source_target_pairs={{0,1},{1,0},{2,3},{3,2},{4,5},{5,4},{6,7},{7,6},{8,9},{9,8},{10,11... | collective-permute-start | bytes 3932168 | tf_op jit(solution)/shard_map/ppermute | solution.py:393
  6.2 4.7 %collective-permute-start.10 = (bf16[512,640]{1,0:T(8,128)(2,1)S(1)}, bf16[512,640]{1,0:T(8,128)(2,1)}, u32[]{:S(2)}, u32[]{:S(2)}) collective-permute-start(bf16[512,640]{1,0:T(8,128)(2,1)S(1)} %get-tuple-element.35), channel_id=1, source_target_pairs={{0,1},{1,0},{2,3},{3,2},{4,5},{5,4},{6,7},{7,6},{8,9},{9,8},{10,11... | collective-permute-start | bytes 1966088 | tf_op jit(solution)/shard_map/ppermute | solution.py:393
  6.6 18.5 %collective-permute-start.8 = (bf16[1,512,640]{2,1,0:T(8,128)(2,1)}, bf16[1,512,640]{2,1,0:T(8,128)(2,1)S(1)}, u32[]{:S(2)}, u32[]{:S(2)}) collective-permute-start(bf16[1,512,640]{2,1,0:T(8,128)(2,1)} %bitcast.6), channel_id=1, source_target_pairs={{0,1},{1,0},{2,3},{3,2},{4,5},{5,4},{6,7},{7,6},{8,9},{9,8},{10,11... | collective-permute-start | bytes 1966088 | tf_op jit(solution)/shard_map/ppermute | solution.py:393
  6.7 18.4 %collective-permute-start.9 = (bf16[512,640]{1,0:T(8,128)(2,1)}, bf16[512,640]{1,0:T(8,128)(2,1)}, u32[]{:S(2)}, u32[]{:S(2)}) collective-permute-start(bf16[512,640]{1,0:T(8,128)(2,1)} %get-tuple-element.34), channel_id=1, source_target_pairs={{0,2},{1,5},{2,0},{3,7},{4,6},{5,1},{6,4},{7,3},{8,10},{9,13},{10,... | collective-permute-start | bytes 1966088 | tf_op jit(solution)/shard_map/ppermute | solution.py:393
  10.8 14.8 %collective-permute-start.11 = (bf16[512,640]{1,0:T(8,128)(2,1)}, bf16[512,640]{1,0:T(8,128)(2,1)}, u32[]{:S(2)}, u32[]{:S(2)}) collective-permute-start(bf16[512,640]{1,0:T(8,128)(2,1)} %collective-permute-done.10), channel_id=1, source_target_pairs={{0,2},{1,5},{2,0},{3,7},{4,6},{5,1},{6,4},{7,3},{8,10},{9,13},{10,... | collective-permute-start | bytes 1966088 | tf_op jit(solution)/shard_map/ppermute | solution.py:393
  13.5 1.3 %collective-permute-start = (bf16[64,128]{1,0:T(8,128)(2,1)S(1)}, bf16[64,128]{1,0:T(8,128)(2,1)S(1)}, u32[]{:S(2)}, u32[]{:S(2)}) collective-permute-start(bf16[64,128]{1,0:T(8,128)(2,1)S(1)} %get-tuple-element.46), channel_id=1, source_target_pairs={{0,1},{1,0},{2,3},{3,2},{4,5},{5,4},{6,7},{7,6},{8,9},{9,8},{10,11... | collective-permute-start | bytes 49160 | tf_op jit(solution)/shard_map/ppermute | solution.py:393
  14.7 4.2 %collective-permute-start.1 = (bf16[2,64,128]{2,1,0:T(8,128)(2,1)S(1)}, bf16[2,64,128]{2,1,0:T(8,128)(2,1)S(1)}, u32[]{:S(2)}, u32[]{:S(2)}) collective-permute-start(bf16[2,64,128]{2,1,0:T(8,128)(2,1)S(1)} %pad_maximum_fusion.near_ref), channel_id=1, source_target_pairs={{3,0},{4,1},{1,2},{6,3},{7,4},{0,5},{5,6},{2,7},{11,8},{12,9},{9,1... | collective-permute-start | bytes 98312 | tf_op jit(solution)/shard_map/ppermute | solution.py:393
  19.4 3.5 %collective-permute-start.2 = (f32[48,128]{1,0:T(8,128)S(1)}, f32[48,128]{1,0:T(8,128)S(1)}, u32[]{:S(2)}, u32[]{:S(2)}) collective-permute-start(f32[48,128]{1,0:T(8,128)S(1)} %get-tuple-element.25.near_ref), channel_id=1, source_target_pairs={{0,4},{1,3},{2,6},{3,1},{4,0},{5,7},{6,2},{7,5},{8,12},{9,11},{10,... | collective-permute-start | bytes 73736 | tf_op jit(solution)/shard_map/ppermute | solution.py:393
  22.8 19.4 %collective-permute-start.6 = (bf16[512,640]{1,0:T(8,128)(2,1)}, bf16[512,640]{1,0:T(8,128)(2,1)S(1)}, u32[]{:S(2)}, u32[]{:S(2)}) collective-permute-start(bf16[512,640]{1,0:T(8,128)(2,1)} %copy-done.1), channel_id=1, source_target_pairs={{0,2},{1,5},{2,0},{3,7},{4,6},{5,1},{6,4},{7,3},{8,10},{9,13},{10,... | collective-permute-start | bytes 1966088 | tf_op jit(solution)/shard_map/ppermute | solution.py:393
  24.1 0.7 collective-permute-start.3
  24.9 23.2 %collective-permute-start.7 = (bf16[512,640]{1,0:T(8,128)(2,1)S(1)}, bf16[512,640]{1,0:T(8,128)(2,1)S(1)}, u32[]{:S(2)}, u32[]{:S(2)}) collective-permute-start(bf16[512,640]{1,0:T(8,128)(2,1)S(1)} %slice_bitcast_fusion), channel_id=1, source_target_pairs={{0,2},{1,5},{2,0},{3,7},{4,6},{5,1},{6,4},{7,3},{8,10},{9,13},{10,... | collective-permute-start | bytes 1966088 | tf_op jit(solution)/shard_map/ppermute | solution.py:393
  28.0 10.9 %collective-permute-start.13 = (f32[1,128,640]{2,1,0:T(8,128)S(1)}, f32[1,128,640]{2,1,0:T(8,128)S(1)}, u32[]{:S(2)}, u32[]{:S(2)}) collective-permute-start(f32[1,128,640]{2,1,0:T(8,128)S(1)} %get-tuple-element.40), channel_id=1, source_target_pairs={{0,4},{1,3},{2,6},{3,1},{4,0},{5,7},{6,2},{7,5},{8,12},{9,11},{10,... | collective-permute-start | bytes 983048 | tf_op jit(solution)/shard_map/ppermute | solution.py:393
  29.5 15.4 %collective-permute-start.12 = (f32[1,128,640]{2,1,0:T(8,128)S(1)}, f32[1,128,640]{2,1,0:T(8,128)S(1)}, u32[]{:S(2)}, u32[]{:S(2)}) collective-permute-start(f32[1,128,640]{2,1,0:T(8,128)S(1)} %get-tuple-element.38), channel_id=1, source_target_pairs={{0,4},{1,3},{2,6},{3,1},{4,0},{5,7},{6,2},{7,5},{8,12},{9,11},{10,... | collective-permute-start | bytes 983048 | tf_op jit(solution)/shard_map/ppermute | solution.py:393
  29.6 9.2 %collective-permute-start.4 = (f32[48,128]{1,0:T(8,128)S(1)}, f32[48,128]{1,0:T(8,128)S(1)}, u32[]{:S(2)}, u32[]{:S(2)}) collective-permute-start(f32[48,128]{1,0:T(8,128)S(1)} %add.10.here_ref.refs_5_), channel_id=1, source_target_pairs={{0,1},{2,3},{4,5},{6,7},{8,9},{10,11},{12,13},{14,15},{16,17},{18,... | collective-permute-start | bytes 73736 | tf_op jit(solution)/shard_map/ppermute | solution.py:393
  39.6 9.7 %collective-permute-start.16 = (f32[1,112,640]{2,1,0:T(8,128)S(1)}, f32[1,112,640]{2,1,0:T(8,128)S(1)}, u32[]{:S(2)}, u32[]{:S(2)}) collective-permute-start(f32[1,112,640]{2,1,0:T(8,128)S(1)} %meet.3.refs_8_), channel_id=1, source_target_pairs={{0,8},{1,9},{2,10},{3,11},{4,12},{5,13},{6,14},{7,15},{8,0},{9,1},... | collective-permute-start | bytes 860168 | tf_op jit(solution)/shard_map/ppermute | solution.py:393
  45.6 21.7 %collective-permute-start.14 = (f32[1,112,640]{2,1,0:T(8,128)S(1)}, f32[1,112,640]{2,1,0:T(8,128)S(1)}, u32[]{:S(2)}, u32[]{:S(2)}) collective-permute-start(f32[1,112,640]{2,1,0:T(8,128)S(1)} %meet.2.refs_7_), channel_id=1, source_target_pairs={{0,8},{1,9},{2,10},{3,11},{4,12},{5,13},{6,14},{7,15},{8,0},{9,1},... | collective-permute-start | bytes 860168 | tf_op jit(solution)/shard_map/ppermute | solution.py:393
  49.3 17.9 %collective-permute-start.17 = (f32[112,640]{1,0:T(8,128)S(1)}, f32[112,640]{1,0:T(8,128)S(1)}, u32[]{:S(2)}, u32[]{:S(2)}) collective-permute-start(f32[112,640]{1,0:T(8,128)S(1)} %bitcast_add_fusion), channel_id=1, source_target_pairs={{0,1},{1,0},{2,3},{3,2},{4,5},{5,4},{6,7},{7,6},{8,9},{9,8},{10,11... | collective-permute-start | bytes 860168 | tf_op jit(solution)/shard_map/ppermute | solution.py:393
  65.9 5.8 %collective-permute-start.15 = (f32[112,640]{1,0:T(8,128)S(1)}, f32[112,640]{1,0:T(8,128)S(1)}, u32[]{:S(2)}, u32[]{:S(2)}) collective-permute-start(f32[112,640]{1,0:T(8,128)S(1)} %get-tuple-element.42), channel_id=1, source_target_pairs={{0,4},{1,3},{2,6},{3,1},{4,0},{5,7},{6,2},{7,5},{8,12},{9,11},{10,... | collective-permute-start | bytes 860168 | tf_op jit(solution)/shard_map/ppermute | solution.py:393
  66.9 8.1 %collective-permute-start.18 = (f32[112,640]{1,0:T(8,128)S(1)}, f32[112,640]{1,0:T(8,128)S(1)}, u32[]{:S(2)}, u32[]{:S(2)}) collective-permute-start(f32[112,640]{1,0:T(8,128)S(1)} %get-tuple-element.44), channel_id=1, source_target_pairs={{0,5},{1,2},{2,7},{3,0},{4,1},{5,6},{6,3},{7,4},{8,13},{9,10},{10,... | collective-permute-start | bytes 860168 | tf_op jit(solution)/shard_map/ppermute | solution.py:393
